TPU v7x, 32 devices: a whole 2x2x4 slice. The times are simulated.
32 devices in a mesh: seq: 8 (over z, x), mp: 4 (over y, core).
Axes of the slice: x: 2, y: 2, z: 4, core: 2. Of those that a mesh axis runs over, the one named last changes fastest.
Arguments:
- inputs: float32 [2, 2048, 1024], P(None, 'seq', 'mp'), may hold values from -6 to 6
- row_starts: int32 [2, 8], P(None, 'seq'), may hold values from 0 to 1, as said below
- norm_gain: float32 [1024], replicated, may hold values from 0.5 to 1.5
- in_weight: float32 [2, 1024, 2048], P(None, None, 'mp'), may hold values from -0.1875 to 0.1875
- conv_weight: float32 [4, 2048], P(None, 'mp'), may hold values from -3 to 3
- conv_bias: float32 [2048], P('mp'), may hold values from -0.5 to 0.5
- xproj_weight: float32 [2048, 96], P('mp'), may hold values from -0.125 to 0.125
- dtproj_weight: float32 [64, 2048], P(None, 'mp'), may hold values from -0.75 to 0.75
- dt_bias: float32 [2048], P('mp'), may hold values from -9 to -3
- decay_log: float32 [16, 2048], P(None, 'mp'), may hold values from 0 to 2.77
- skip_gain: float32 [2048], P('mp'), may hold values from 0.5 to 1.5
- out_weight: float32 [2048, 1024], P('mp'), may hold values from -0.25 to 0.25
- output_grad: float32 [2, 2048, 1024], P(None, 'seq', 'mp'), may hold values from -6 to 6
Outputs:
- output: float32 [2, 2048, 1024], P(None, 'seq', 'mp')
- input_grad: float32 [2, 2048, 1024], P(None, 'seq', 'mp')
- grad_norm_gain: float32 [1024], P('mp')
- grad_in_weight: float32 [2, 1024, 2048], P(None, None, 'mp')
- grad_conv_weight: float32 [4, 2048], P(None, 'mp')
- grad_conv_bias: float32 [2048], P('mp')
- grad_xproj_weight: float32 [2048, 96], P('mp')
- grad_dtproj_weight: float32 [64, 2048], P(None, 'mp')
- grad_dt_bias: float32 [2048], P('mp')
- grad_decay_log: float32 [16, 2048], P(None, 'mp')
- grad_skip_gain: float32 [2048], P('mp')
- grad_out_weight: float32 [2048, 1024], P('mp')
Inputs may be any that keep to these rules, and one draw needn't show every extreme that they name: `row_starts`: in every lane group 0 begins a row and each row spans a multiple of 2 groups; in one lane, drawn from the seed, a single row spans all 8 groups.
All inputs are finite; a program needn't handle non-finite values.
Results may differ from a plain program's by a relative error of at most 0.024.
Values may be sent and summed in bfloat16 or wider, within the bound.
No kernel may reach another device: no remote copies, remote signals or barrier semaphores. Data moves between devices by JAX's collectives and lax.ppermute only.
A program may use at most 192 MiB of HBM per device.

v0:
```python
import functools

import jax
import jax.numpy as jnp
from jax import lax
from jax.experimental import pallas as pl
from jax.experimental.pallas import tpu as pltpu
from jax.sharding import PartitionSpec as P

F32 = jnp.float32
BF16 = jnp.bfloat16
LOG2E = 1.4426950408889634
CHUNK = 16
LANE = 128
FAR = 1.0e4


def swap(block, axis, bit):
    devices = lax.axis_size(axis)
    return lax.ppermute(block, axis, [(i, i ^ bit) for i in range(devices)])


def from_behind(block, axis, distance):
    devices = range(lax.axis_size(axis))
    route = [(i - distance, i) for i in devices if i - distance in devices]
    return lax.ppermute(block, axis, route)


def bits_of(axis):
    count = lax.axis_size(axis)
    bits = []
    while (1 << len(bits)) < count:
        bits.append(1 << len(bits))
    return bits


def gather_last(block, axis):
    index = lax.axis_index(axis)
    whole = block
    for bit in reversed(bits_of(axis)):
        other = swap(whole, axis, bit)
        upper = (index & bit) != 0
        first = jnp.where(upper, other, whole)
        second = jnp.where(upper, whole, other)
        whole = jnp.stack([first, second], axis=0)
    count = len(bits_of(axis))
    order = tuple(reversed(range(count)))
    lead = whole.ndim - count
    whole = jnp.transpose(whole, order + tuple(range(count, whole.ndim)))
    whole = whole.reshape((lax.axis_size(axis),) + whole.shape[count:])
    moved = jnp.moveaxis(whole, 0, lead - 1)
    return moved.reshape(block.shape[:-1] + (-1,))


def sum_all(block, axis):
    total = block
    for bit in bits_of(axis):
        sent = total.astype(BF16)
        total = sent.astype(F32) + swap(sent, axis, bit).astype(F32)
    return total


def halves(block, upper):
    half = block.shape[0] // 2
    low, high = block[:half], block[half:]
    return jnp.where(upper, high, low), jnp.where(upper, low, high)


def scatter_sum(block, axis, bits):
    index = lax.axis_index(axis)
    total = block
    for bit in bits:
        kept, sent = halves(total, (index & bit) != 0)
        total = kept.astype(F32) + swap(sent.astype(BF16), axis, bit).astype(F32)
    return total


def spread(block, axis, bits):
    index = lax.axis_index(axis)
    whole = block
    for bit in reversed(bits):
        other = swap(whole, axis, bit)
        upper = (index & bit) != 0
        whole = jnp.concatenate(
            [jnp.where(upper, other, whole), jnp.where(upper, whole, other)], axis=0
        )
    return whole


def sum_rows(block, axis):
    bits = bits_of(axis)
    rows = block.shape[0]
    unit = 16 << len(bits)
    padded = -(-rows // unit) * unit
    if padded != rows:
        block = jnp.pad(block, ((0, padded - rows), (0, 0)))
    part = scatter_sum(block, axis, bits).astype(BF16)
    return spread(part, axis, bits)[:rows]


def silu_slope(values):
    logistic = jax.nn.sigmoid(values)
    return logistic * (1.0 + values * (1.0 - logistic))


def iota(shape, dim):
    return lax.broadcasted_iota(jnp.int32, shape, dim)


def widen(part, width):
    return jnp.concatenate([part] * (width // part.shape[1]), axis=1)


def ends_kernel(dt_ref, u_ref, gy_ref, b_ref, c_ref, a_ref, end_ref, pull_ref, prod):
    length, width = dt_ref.shape
    states = a_ref.shape[0]
    rate = a_ref[...] * LOG2E
    wide = CHUNK * states
    per_state = (iota((states, wide), 1) % states == iota((states, wide), 0)).astype(BF16)

    def chunk(i, carried):
        state, factor, pulled = carried
        for j in range(CHUNK):
            t = i * CHUNK + j

            def row(ref):
                return jnp.broadcast_to(ref[pl.ds(t, 1), :], (states, width))

            b, c = widen(b_ref[t], width), widen(c_ref[t], width)
            decay = jnp.exp2(row(dt_ref) * rate)
            state = decay * state + row(u_ref) * b
            factor = factor * decay
            prod[j * states : (j + 1) * states, :] = factor.astype(BF16) * (row(gy_ref) * c).astype(
                BF16
            )
        pulled = pulled + jnp.dot(per_state, prod[...], preferred_element_type=F32)
        return state, factor, pulled

    zero = jnp.zeros((states, width), F32)
    state, _, pulled = lax.fori_loop(0, length // CHUNK, chunk, (zero, zero + 1.0, zero))
    end_ref[...] = state
    pull_ref[...] = pulled


def scan_ends(dt, u, gy, b, c, rate):
    lanes, length, width = dt.shape
    states = rate.shape[0]
    token = pl.BlockSpec((None, length, width), lambda l: (l, 0, 0))
    column = pl.BlockSpec((None, length, states, LANE), lambda l: (l, 0, 0, 0))
    whole = pl.BlockSpec((states, width), lambda l: (0, 0))
    state = pl.BlockSpec((None, states, width), lambda l: (l, 0, 0))
    shape = jax.ShapeDtypeStruct((lanes, states, width), F32)
    return pl.pallas_call(
        ends_kernel,
        grid=(lanes,),
        in_specs=[token, token, token, column, column, whole],
        out_specs=[state, state],
        out_shape=[shape, shape],
        scratch_shapes=[pltpu.VMEM((CHUNK * states, width), BF16)],
        compiler_params=pltpu.CompilerParams(vmem_limit_bytes=40 << 20),
        name="scan_ends",
    )(dt, u, gy, b, c, rate)


def scan_kernel(
    dt_ref,
    u_ref,
    gy_ref,
    b_ref,
    c_ref,
    a_ref,
    begin_ref,
    last_ref,
    y_ref,
    gq_ref,
    gs_ref,
    ga_ref,
    gbc_ref,
    states_buf,
    p1,
    p2,
    p3,
    p4,
    p5,
):
    length, width = dt_ref.shape
    states = a_ref.shape[0]
    plain = a_ref[...]
    rate = plain * LOG2E
    rate_low = plain.astype(BF16)
    wide = CHUNK * states
    per_state = (iota((states, wide), 1) % states == iota((states, wide), 0)).astype(BF16)
    per_step = (iota((CHUNK, wide), 1) // states == iota((CHUNK, wide), 0)).astype(BF16)
    pick_b = (iota((wide, LANE), 0) % states + 64 == iota((wide, LANE), 1)).astype(F32)
    pick_c = (iota((wide, LANE), 0) % states + 80 == iota((wide, LANE), 1)).astype(F32)
    ones = jnp.ones((width, LANE), BF16)

    def row(ref, t):
        return jnp.broadcast_to(ref[pl.ds(t, 1), :], (states, width))

    def slot(t):
        return pl.ds(pl.multiple_of(t * states, states), states)

    begin = begin_ref[...]
    states_buf[0:states, :] = begin.astype(BF16)

    def forward(i, state):
        for j in range(CHUNK):
            t = i * CHUNK + j
            b, c = widen(b_ref[t], width), widen(c_ref[t].astype(BF16), width)
            state = jnp.exp2(row(dt_ref, t) * rate) * state + row(u_ref, t) * b
            low = state.astype(BF16)
            states_buf[slot(t + 1), :] = low
            p1[j * states : (j + 1) * states, :] = low * c
        y_ref[pl.ds(pl.multiple_of(i * CHUNK, CHUNK), CHUNK), :] = jnp.dot(
            per_step, p1[...], preferred_element_type=F32
        )
        return state

    lax.fori_loop(0, length // CHUNK, forward, begin)

    def backward(k, carried):
        carry, ga = carried
        i = length // CHUNK - 1 - k
        for j in reversed(range(CHUNK)):
            t = i * CHUNK + j
            b, c = widen(b_ref[t].astype(BF16), width), widen(c_ref[t], width)
            dt, gy, u = row(dt_ref, t), row(gy_ref, t), row(u_ref, t)
            grad = carry + gy * c
            carry = jnp.exp2(dt * rate) * grad
            low = grad.astype(BF16)
            turn = carry.astype(BF16) * states_buf[slot(t), :]
            s = slice(j * states, (j + 1) * states)
            p1[s, :] = turn * rate_low
            p2[s, :] = turn * dt.astype(BF16)
            p3[s, :] = low * b
            p4[s, :] = states_buf[slot(t + 1), :] * gy.astype(BF16)
            p5[s, :] = low * u.astype(BF16)
        o = pl.ds(pl.multiple_of(i * CHUNK, CHUNK), CHUNK)
        gq_ref[o, :] = jnp.dot(per_step, p1[...], preferred_element_type=F32)
        ga = ga + jnp.dot(per_state, p2[...], preferred_element_type=F32)
        gs_ref[o, :] = jnp.dot(per_step, p3[...], preferred_element_type=F32)
        sum_c = jnp.dot(p4[...], ones, preferred_element_type=F32)
        sum_b = jnp.dot(p5[...], ones, preferred_element_type=F32)
        picked = (sum_b * pick_b + sum_c * pick_c).astype(BF16)
        gbc_ref[o, :] = jnp.dot(per_step, picked, preferred_element_type=F32)
        return carry, ga

    zero = jnp.zeros((states, width), F32)
    _, ga = lax.fori_loop(0, length // CHUNK, backward, (last_ref[...], zero))
    ga_ref[...] = ga


def scan_all(dt, u, gy, b, c, rate, begin, last):
    lanes, length, width = dt.shape
    states = rate.shape[0]
    token = pl.BlockSpec((None, length, width), lambda l: (l, 0, 0))
    column = pl.BlockSpec((None, length, states, LANE), lambda l: (l, 0, 0, 0))
    whole = pl.BlockSpec((states, width), lambda l: (0, 0))
    state = pl.BlockSpec((None, states, width), lambda l: (l, 0, 0))
    narrow = pl.BlockSpec((None, length, LANE), lambda l: (l, 0, 0))
    shape = jax.ShapeDtypeStruct
    return pl.pallas_call(
        scan_kernel,
        grid=(lanes,),
        in_specs=[token, token, token, column, column, whole, state, state],
        out_specs=[token, token, token, state, narrow],
        out_shape=[shape((lanes, length, width), F32)] * 3
        + [shape((lanes, states, width), F32), shape((lanes, length, LANE), F32)],
        scratch_shapes=[pltpu.VMEM(((length + 1) * states, width), BF16)]
        + [pltpu.VMEM((CHUNK * states, width), BF16)] * 5,
        compiler_params=pltpu.CompilerParams(vmem_limit_bytes=40 << 20),
        name="scan_all",
    )(dt, u, gy, b, c, rate, begin, last)


def entering(end, pulled, reach, rate):
    index, count = lax.axis_index("seq"), lax.axis_size("seq")
    own = (end.astype(BF16), pulled.astype(BF16))
    got = {}
    for k in range(1, count):
        to_later = (index ^ k) > index
        sent = jnp.where(to_later, own[0], own[1])
        got[k] = (swap(sent, "seq", k), swap(reach, "seq", k))
    states = jnp.stack([jnp.zeros_like(own[0])] + [got[k][0] for k in range(1, count)])
    spans = jnp.stack([jnp.zeros_like(reach)] + [got[k][1] for k in range(1, count)])
    order = jnp.arange(count) ^ index
    states, spans = states[order], spans[order]
    begin = jnp.zeros(end.shape, F32)
    last = jnp.zeros(end.shape, F32)
    for g in range(count):
        factor = jnp.exp(spans[g][:, None, :] * rate)
        begin = jnp.where(g < index, begin * factor + states[g].astype(F32), begin)
        h = count - 1 - g
        factor = jnp.exp(spans[h][:, None, :] * rate)
        last = jnp.where(h > index, last * factor + states[h].astype(F32), last)
    return begin, last


def per_device(
    inputs,
    row_starts,
    norm_gain,
    in_weight,
    conv_weight,
    conv_bias,
    xproj_weight,
    dtproj_weight,
    dt_bias,
    decay_log,
    skip_gain,
    out_weight,
    output_grad,
):
    lane_count, length, shard_width = inputs.shape
    low_rank = dtproj_weight.shape[0]
    state_count = decay_log.shape[0]
    tap_count = conv_weight.shape[0]
    inner_width = conv_bias.shape[0]
    model_width = norm_gain.shape[0]
    starts = row_starts.astype(F32)
    carry_mask = (1.0 - starts)[:, :, None]
    mp_index = lax.axis_index("mp")
    gathered = gather_last(inputs.astype(BF16), "mp").astype(F32)
    inv_rms = lax.rsqrt(jnp.mean(gathered * gathered, axis=2, keepdims=True) + 1e-05)
    normed = (gathered * inv_rms * norm_gain).astype(BF16)
    grad_whole = gather_last(output_grad.astype(BF16), "mp")
    w_in = in_weight.astype(BF16)
    inner_act = jnp.einsum("ltd,de->lte", normed, w_in[0], preferred_element_type=F32).astype(BF16)
    rim_rows = from_behind(inner_act[:, length - (tap_count - 1) :, :], "seq", 1)
    gate_in = jnp.einsum("ltd,de->lte", normed, w_in[1], preferred_element_type=F32)
    rim_rows = rim_rows.astype(F32) * carry_mask
    padded = jnp.concatenate([rim_rows, inner_act.astype(F32)], axis=1)
    conv_sum = conv_bias + conv_weight[0] * padded[:, 0:length]
    for tap in range(1, tap_count):
        conv_sum = conv_sum + conv_weight[tap] * padded[:, tap : tap + length]
    mixed = jax.nn.silu(conv_sum)
    mixed_low = mixed.astype(BF16)
    w_x = xproj_weight.astype(BF16)
    projected = sum_all(
        jnp.einsum("lte,er->ltr", mixed_low, w_x, preferred_element_type=F32), "mp"
    )
    dt_low = projected[:, :, :low_rank].astype(BF16)
    input_mat = projected[:, :, low_rank : low_rank + state_count]
    read_mat = projected[:, :, low_rank + state_count :]
    w_dt = dtproj_weight.astype(BF16)
    dt_pre = jnp.einsum("ltr,re->lte", dt_low, w_dt, preferred_element_type=F32) + dt_bias
    step_size = jax.nn.softplus(dt_pre)
    decay_rate = -jnp.exp(decay_log)
    w_out = out_weight.astype(BF16)
    gate_act = jax.nn.silu(gate_in)
    grad_gated = jnp.einsum("ltd,ed->lte", grad_whole, w_out, preferred_element_type=F32)
    grad_scan = grad_gated * gate_act
    source = step_size * mixed
    wide = input_mat.shape + (LANE,)
    b_wide = jnp.broadcast_to(input_mat[..., None], wide)
    c_wide = jnp.broadcast_to(read_mat[..., None], wide)
    end_state, pulled = scan_ends(step_size, source, grad_scan, b_wide, c_wide, decay_rate)
    reach = jnp.sum(step_size, axis=1) + FAR * starts
    begin, last = entering(end_state, pulled * carry_mask, reach, decay_rate)
    y, turn_sum, pull_sum, grad_rate, grad_bc = scan_all(
        step_size, source, grad_scan, b_wide, c_wide, decay_rate, begin * carry_mask, last
    )
    scan_out = y + skip_gain * mixed
    gated = (scan_out * gate_act).astype(BF16)
    out_part = jnp.einsum("lte,ed->ltd", gated, w_out, preferred_element_type=F32)
    blocks = jnp.moveaxis(
        out_part.reshape(lane_count, length, -1, shard_width), 2, 0
    )
    mp_bits = bits_of("mp")
    branch = scatter_sum(blocks, "mp", mp_bits[::-1])[0]
    output = inputs + branch
    grad_out_w = jnp.einsum("lte,ltd->ed", gated, grad_whole, preferred_element_type=F32)
    grad_gate = grad_gated * scan_out * silu_slope(gate_in)
    grad_skip = jnp.sum(grad_scan * mixed, axis=(0, 1))
    grad_step = turn_sum + pull_sum * mixed
    grad_mixed = pull_sum * step_size + grad_scan * skip_gain
    grad_log = jnp.sum(grad_rate, axis=0) * decay_rate
    slope_pre = grad_step * jax.nn.sigmoid(dt_pre)
    grad_bias_dt = jnp.sum(slope_pre, axis=(0, 1))
    grad_pre = slope_pre.astype(BF16)
    grad_dt_w = jnp.einsum("ltr,lte->re", dt_low, grad_pre, preferred_element_type=F32)
    grad_dt_low = jnp.einsum("lte,re->ltr", grad_pre, w_dt, preferred_element_type=F32)
    narrow = low_rank + 2 * state_count
    grad_proj_part = jnp.concatenate([grad_dt_low, grad_bc[:, :, low_rank:narrow]], axis=2)
    grad_projected = sum_all(grad_proj_part, "mp").astype(BF16)
    grad_x_w = jnp.einsum("ltr,lte->re", grad_projected, mixed_low, preferred_element_type=F32)
    grad_mixed = grad_mixed + jnp.einsum(
        "ltr,er->lte", grad_projected, w_x, preferred_element_type=F32
    )
    grad_conv = grad_mixed * silu_slope(conv_sum)
    grad_conv_b = jnp.sum(grad_conv, axis=(0, 1))
    grad_conv_w = jnp.stack(
        [
            jnp.sum(grad_conv * padded[:, tap : tap + length], axis=(0, 1))
            for tap in range(tap_count)
        ]
    )
    grad_padded = jnp.pad(conv_weight[0] * grad_conv, ((0, 0), (0, tap_count - 1), (0, 0)))
    for tap in range(1, tap_count):
        grad_padded = grad_padded + jnp.pad(
            conv_weight[tap] * grad_conv, ((0, 0), (tap, tap_count - 1 - tap), (0, 0))
        )
    rim_back = from_behind(grad_padded[:, : tap_count - 1] * carry_mask, "seq", -1)
    tail_zeros = jnp.zeros((lane_count, length - (tap_count - 1), inner_width), F32)
    grad_inner = grad_padded[:, tap_count - 1 :] + jnp.concatenate([tail_zeros, rim_back], axis=1)
    grad_inner_low = grad_inner.astype(BF16)
    grad_gate_low = grad_gate.astype(BF16)
    grad_in_w = [
        jnp.einsum("ltd,lte->de", normed, part, preferred_element_type=F32)
        for part in (grad_inner_low, grad_gate_low)
    ]
    grad_normed = jnp.einsum(
        "lte,de->ltd", grad_inner_low, w_in[0], preferred_element_type=F32
    ) + jnp.einsum("lte,de->ltd", grad_gate_low, w_in[1], preferred_element_type=F32)
    row_part = jnp.sum(
        grad_inner_low.astype(F32) * inner_act.astype(F32)
        + grad_gate_low.astype(F32) * gate_in,
        axis=2,
    )
    row_dot = row_part
    for bit in mp_bits:
        row_dot = row_dot + swap(row_dot, "mp", bit)
    blocks = jnp.moveaxis(grad_normed.reshape(lane_count, length, -1, shard_width), 2, 0)
    grad_own = scatter_sum(blocks, "mp", mp_bits[::-1])[0]
    own_gain = lax.dynamic_slice_in_dim(norm_gain, mp_index * shard_width, shard_width, 0)
    unit_own = inputs * inv_rms
    grad_gain = jnp.sum(grad_own * unit_own, axis=(0, 1))
    input_grad = output_grad + inv_rms * (
        grad_own * own_gain - unit_own * (row_dot[:, :, None] / model_width)
    )
    gain_rows = jnp.pad(grad_gain, (0, -shard_width % inner_width)).reshape(-1, inner_width)
    small = jnp.concatenate(
        [
            grad_conv_w,
            grad_conv_b[None],
            grad_bias_dt[None],
            grad_skip[None],
            grad_log,
            grad_dt_w,
            grad_x_w,
            gain_rows,
        ],
        axis=0,
    )
    sum_out_w = sum_rows(grad_out_w, "seq").astype(F32)
    sum_gate_w = sum_rows(grad_in_w[1], "seq").astype(F32)
    sum_inner_w = sum_rows(grad_in_w[0], "seq").astype(F32)
    small = sum_rows(small, "seq").astype(F32)
    cuts = [tap_count, 1, 1, 1, state_count, low_rank, narrow, gain_rows.shape[0]]
    parts, at = [], 0
    for size in cuts:
        parts.append(small[at : at + size])
        at += size
    return (
        output,
        input_grad,
        parts[7].reshape(-1)[:shard_width],
        jnp.stack([sum_inner_w, sum_gate_w]),
        parts[0],
        parts[1][0],
        parts[6].T,
        parts[5],
        parts[2][0],
        parts[4],
        parts[3][0],
        sum_out_w,
    )


def solution(mesh):
    in_specs = (
        P(None, "seq", "mp"),
        P(None, "seq"),
        P(),
        P(None, None, "mp"),
        P(None, "mp"),
        P("mp"),
        P("mp", None),
        P(None, "mp"),
        P("mp"),
        P(None, "mp"),
        P("mp"),
        P("mp", None),
        P(None, "seq", "mp"),
    )
    out_specs = (
        P(None, "seq", "mp"),
        P(None, "seq", "mp"),
        P("mp"),
        P(None, None, "mp"),
        P(None, "mp"),
        P("mp"),
        P("mp", None),
        P(None, "mp"),
        P("mp"),
        P(None, "mp"),
        P("mp"),
        P("mp", None),
    )
    return jax.shard_map(
        per_device, mesh=mesh, in_specs=in_specs, out_specs=out_specs, check_vma=False
    )
```

profile of v0, /device:TPU:0, one launch (start us, length us, event | category | flops | bytes accessed | tf_op | source)
XLA Modules:
  0.0 301.6 jit_solution(18130109844697163420)
XLA Ops:
  1.7 3.0 %collective-permute-start.5 = (bf16[2,256,256]{2,1,0:T(8,128)(2,1)S(1)}, bf16[2,256,256]{2,1,0:T(8,128)(2,1)S(1)}, u32[]{:S(2)}, u32[]{:S(2)}) collective-permute-start(bf16[2,256,256]{2,1,0:T(8,128)(2,1)S(1)} %convert_element_type.343), channel_id=1, source_target_pairs={{0,2},{1,3},{2,0},{3,1},{4,6},{5,7},{6,4},{7,5},{8,10},{9,11},{10,... | collective-permute-start | bytes 786440 | tf_op jit(solution)/shard_map/ppermute | solution.py:20
  9.1 3.9 %convert_element_type.329 = bf16[2,1024,512]{2,1,0:T(8,128)(2,1)} convert(f32[2,1024,512]{2,1,0:T(8,128)} %param.16) | non-fusion elementwise | flops 1048576 | bytes 6291456 | tf_op jit(solution)/shard_map/convert_element_type | solution.py:328
  13.1 3.6 %collective-permute-done = bf16[2,256,256]{2,1,0:T(8,128)(2,1)S(1)} collective-permute-done((bf16[2,256,256]{2,1,0:T(8,128)(2,1)S(1)}, bf16[2,256,256]{2,1,0:T(8,128)(2,1)S(1)}, u32[]{:S(2)}, u32[]{:S(2)}) %collective-permute-start) | collective-permute-done | bytes 262176 | tf_op jit(solution)/shard_map/ppermute | solution.py:20
  23.3 3.9 %collective-permute-start.2 = (bf16[2,3,512]{2,1,0:T(4,128)(2,1)S(1)}, bf16[2,3,512]{2,1,0:T(4,128)(2,1)S(1)}, u32[]{:S(2)}, u32[]{:S(2)}) collective-permute-start(bf16[2,3,512]{2,1,0:T(4,128)(2,1)S(1)} %slice.332), channel_id=1, source_target_pairs={{0,4},{4,8},{8,12},{12,16},{16,20},{20,24},{24,28},{1,5},{5,9},{9,... | collective-permute-start | bytes 18440 | tf_op jit(solution)/shard_map/ppermute | solution.py:26
  31.6 3.0 multiply_reduce_fusion
  40.6 2.8 fusion.1
  47.1 2.4 collective-permute-start.13
  61.3 9.3 %scan_ends.1 = (f32[2,16,512]{2,1,0:T(8,128)S(1)}, f32[2,16,512]{2,1,0:T(8,128)S(1)}) custom-call(f32[2,256,512]{2,1,0:T(8,128)S(1)} %get-tuple-element.60.dt_ref, f32[2,256,512]{2,1,0:T(8,128)S(1)} %get-tuple-element.59.u_ref, f32[2,256,512]{2,1,0:T(8,128)S(1)} %get-tuple-element.36.gy_ref, f32[2,256,16,128]{3,2,1,0:T(8,128)S(1)} %broadcast_in_dim.10.b_ref, ...), custom_call_target="tpu_custom_call" | custom-call | tf_op jit(solution)/shard_map/scan_ends/pallas_call | solution.py:153
  72.3 2.9 collective-permute-done.8
  76.4 3.6 %collective-permute-done.9 = f32[2,512]{1,0:T(2,128)S(1)} collective-permute-done((f32[2,512]{1,0:T(2,128)}, f32[2,512]{1,0:T(2,128)S(1)}, u32[]{:S(2)}, u32[]{:S(2)}) %collective-permute-start.9) | collective-permute-done | bytes 4128 | tf_op jit(solution)/shard_map/ppermute | solution.py:20
  80.0 3.5 %collective-permute-start.20 = (bf16[2,16,512]{2,1,0:T(8,128)(2,1)S(1)}, bf16[2,16,512]{2,1,0:T(8,128)(2,1)S(1)}, u32[]{:S(2)}, u32[]{:S(2)}) collective-permute-start(bf16[2,16,512]{2,1,0:T(8,128)(2,1)S(1)} %get-tuple-element.42), channel_id=1, source_target_pairs={{0,28},{4,24},{8,20},{12,16},{16,12},{20,8},{24,4},{28,0},{1,29},{... | collective-permute-start | bytes 98312 | tf_op jit(solution)/shard_map/ppermute | solution.py:20
  85.4 3.6 %collective-permute-start.17 = (bf16[2,16,512]{2,1,0:T(8,128)(2,1)}, bf16[2,16,512]{2,1,0:T(8,128)(2,1)S(1)}, u32[]{:S(2)}, u32[]{:S(2)}) collective-permute-start(bf16[2,16,512]{2,1,0:T(8,128)(2,1)} %get-tuple-element.95), channel_id=1, source_target_pairs={{0,16},{4,20},{8,24},{12,28},{16,0},{20,4},{24,8},{28,12},{1,17},{... | collective-permute-start | bytes 98312 | tf_op jit(solution)/shard_map/ppermute | solution.py:20
  94.6 3.3 %collective-permute-done.15 = bf16[2,16,512]{2,1,0:T(8,128)(2,1)S(1)} collective-permute-done((bf16[2,16,512]{2,1,0:T(8,128)(2,1)}, bf16[2,16,512]{2,1,0:T(8,128)(2,1)S(1)}, u32[]{:S(2)}, u32[]{:S(2)}) %collective-permute-start.15) | collective-permute-done | bytes 32800 | tf_op jit(solution)/shard_map/ppermute | solution.py:20
  99.7 3.3 %collective-permute-done.16 = bf16[2,16,512]{2,1,0:T(8,128)(2,1)S(1)} collective-permute-done((bf16[2,16,512]{2,1,0:T(8,128)(2,1)}, bf16[2,16,512]{2,1,0:T(8,128)(2,1)S(1)}, u32[]{:S(2)}, u32[]{:S(2)}) %collective-permute-start.16) | collective-permute-done | bytes 32800 | tf_op jit(solution)/shard_map/ppermute | solution.py:20
  110.8 29.8 %scan_all.1 = (f32[2,256,512]{2,1,0:T(8,128)S(1)}, f32[2,256,512]{2,1,0:T(8,128)S(1)}, f32[2,256,512]{2,1,0:T(8,128)S(1)}, f32[2,16,512]{2,1,0:T(8,128)S(1)}, f32[2,256,128]{2,1,0:T(8,128)S(1)}) custom-call(f32[2,256,512]{2,1,0:T(8,128)S(1)} %get-tuple-element.60.dt_ref, f32[2,256,512]{2,1,0:T(8,128)S(1)} %get-tuple-element.59.u_ref, ...), custom_call_target="tpu_custom_call" | custom-call | tf_op jit(solution)/shard_map/scan_all/pallas_call | solution.py:263
  143.7 3.4 %fusion.62 = (f32[512]{0:T(512)}, bf16[2,256,512]{2,1,0:T(8,128)(2,1)S(1)}) fusion(f32[2,256,512]{2,1,0:T(8,128)} %get-tuple-element.116, f32[2,256,512]{2,1,0:T(8,128)} %copy-done.5, f32[2,256,512]{2,1,0:T(8,128)} %copy-done.3, f32[2,256,512]{2,1,0:T(8,128)} %copy-done.24), kind=kLoop, calls=%fused_computation.272 | loop fusion | flops 3145216 | bytes 4720640 | tf_op jit(solution)/shard_map/reduce_sum | solution.py:380
  150.7 3.1 %collective-permute-done.24 = bf16[2,256,96]{1,2,0:T(8,128)(2,1)S(1)} collective-permute-done((bf16[2,256,96]{1,2,0:T(8,128)(2,1)S(1)}, bf16[2,256,96]{1,2,0:T(8,128)(2,1)S(1)}, u32[]{:S(2)}, u32[]{:S(2)}) %collective-permute-start.24) | collective-permute-done | bytes 98336 | tf_op jit(solution)/shard_map/ppermute | solution.py:20
  153.8 2.8 broadcast_multiply_fusion.3
  159.4 3.1 %collective-permute-done.25 = f32[2,3,512]{2,1,0:T(4,128)S(1)} collective-permute-done((f32[2,3,512]{2,1,0:T(4,128)S(1)}, f32[2,3,512]{2,1,0:T(4,128)S(1)}, u32[]{:S(2)}, u32[]{:S(2)}) %collective-permute-start.25) | collective-permute-done | bytes 12320 | tf_op jit(solution)/shard_map/ppermute | solution.py:26
  191.1 3.6 %collective-permute-done.36 = bf16[512,512]{1,0:T(8,128)(2,1)} collective-permute-done((bf16[512,512]{1,0:T(8,128)(2,1)}, bf16[512,512]{1,0:T(8,128)(2,1)}, u32[]{:S(2)}, u32[]{:S(2)}) %collective-permute-start.36) | collective-permute-done | bytes 524320 | tf_op jit(solution)/shard_map/ppermute | solution.py:20
  197.3 7.7 %collective-permute-done.42 = bf16[512,512]{1,0:T(8,128)(2,1)} collective-permute-done((bf16[512,512]{1,0:T(8,128)(2,1)S(1)}, bf16[512,512]{1,0:T(8,128)(2,1)}, u32[]{:S(2)}, u32[]{:S(2)}) %collective-permute-start.42) | collective-permute-done | bytes 524320 | tf_op jit(solution)/shard_map/ppermute | solution.py:20
  211.9 4.5 %collective-permute-done.43 = bf16[256,512]{1,0:T(8,128)(2,1)S(1)} collective-permute-done((bf16[256,512]{1,0:T(8,128)(2,1)S(1)}, bf16[256,512]{1,0:T(8,128)(2,1)S(1)}, u32[]{:S(2)}, u32[]{:S(2)}) %collective-permute-start.43) | collective-permute-done | bytes 262176 | tf_op jit(solution)/shard_map/ppermute | solution.py:20
  221.7 3.6 %collective-permute-done.50 = bf16[64,1024]{1,0:T(8,128)(2,1)} collective-permute-done((bf16[64,1024]{1,0:T(8,128)(2,1)S(1)}, bf16[64,1024]{1,0:T(8,128)(2,1)}, u32[]{:S(2)}, u32[]{:S(2)}) %collective-permute-start.50) | collective-permute-done | bytes 131104 | tf_op jit(solution)/shard_map/ppermute | solution.py:20
  226.4 2.7 collective-permute-start.31
  231.4 2.8 collective-permute-start.32
  234.5 10.3 %collective-permute-done.32 = bf16[32,512]{1,0:T(8,128)(2,1)S(1)} collective-permute-done((bf16[32,512]{1,0:T(8,128)(2,1)S(1)}, bf16[32,512]{1,0:T(8,128)(2,1)S(1)}, u32[]{:S(2)}, u32[]{:S(2)}) %collective-permute-start.32) | collective-permute-done | bytes 32800 | tf_op jit(solution)/shard_map/ppermute | solution.py:20
  245.0 2.7 collective-permute-start.52
  252.1 4.6 %collective-permute-done.34 = bf16[64,512]{1,0:T(8,128)(2,1)S(1)} collective-permute-done((bf16[64,512]{1,0:T(8,128)(2,1)S(1)}, bf16[64,512]{1,0:T(8,128)(2,1)S(1)}, u32[]{:S(2)}, u32[]{:S(2)}) %collective-permute-start.34) | collective-permute-done | bytes 65568 | tf_op jit(solution)/shard_map/ppermute | solution.py:20
  269.9 10.8 %collective-permute-done.53 = bf16[256,1024]{1,0:T(8,128)(2,1)S(1)} collective-permute-done((bf16[256,1024]{1,0:T(8,128)(2,1)S(1)}, bf16[256,1024]{1,0:T(8,128)(2,1)S(1)}, u32[]{:S(2)}, u32[]{:S(2)}) %collective-permute-start.53) | collective-permute-done | bytes 524320 | tf_op jit(solution)/shard_map/ppermute | solution.py:20
  282.5 9.4 %collective-permute-done.41 = bf16[512,512]{1,0:T(8,128)(2,1)S(1)} collective-permute-done((bf16[512,512]{1,0:T(8,128)(2,1)S(1)}, bf16[512,512]{1,0:T(8,128)(2,1)S(1)}, u32[]{:S(2)}, u32[]{:S(2)}) %collective-permute-start.41) | collective-permute-done | bytes 524320 | tf_op jit(solution)/shard_map/ppermute | solution.py:20
  292.2 6.6 %collective-permute-done.47 = bf16[512,512]{1,0:T(8,128)(2,1)S(1)} collective-permute-done((bf16[512,512]{1,0:T(8,128)(2,1)S(1)}, bf16[512,512]{1,0:T(8,128)(2,1)S(1)}, u32[]{:S(2)}, u32[]{:S(2)}) %collective-permute-start.47) | collective-permute-done | bytes 524320 | tf_op jit(solution)/shard_map/ppermute | solution.py:20
  299.0 2.6 maximum_convert_fusion
  (368 shorter events, 133.3 us)
Async XLA Ops:
  1.7 11.3 %collective-permute-start.5 = (bf16[2,256,256]{2,1,0:T(8,128)(2,1)S(1)}, bf16[2,256,256]{2,1,0:T(8,128)(2,1)S(1)}, u32[]{:S(2)}, u32[]{:S(2)}) collective-permute-start(bf16[2,256,256]{2,1,0:T(8,128)(2,1)S(1)} %convert_element_type.343), channel_id=1, source_target_pairs={{0,2},{1,3},{2,0},{3,1},{4,6},{5,7},{6,4},{7,5},{8,10},{9,11},{10,... | collective-permute-start | bytes 786440 | tf_op jit(solution)/shard_map/ppermute | solution.py:20
  5.8 10.9 %collective-permute-start = (bf16[2,256,256]{2,1,0:T(8,128)(2,1)S(1)}, bf16[2,256,256]{2,1,0:T(8,128)(2,1)S(1)}, u32[]{:S(2)}, u32[]{:S(2)}) collective-permute-start(bf16[2,256,256]{2,1,0:T(8,128)(2,1)S(1)} %convert_element_type.324), channel_id=1, source_target_pairs={{0,2},{1,3},{2,0},{3,1},{4,6},{5,7},{6,4},{7,5},{8,10},{9,11},{10,... | collective-permute-start | bytes 786440 | tf_op jit(solution)/shard_map/ppermute | solution.py:20
  47.1 42.6 %collective-permute-start.13 = (f32[2,512]{1,0:T(2,128)}, f32[2,512]{1,0:T(2,128)}, u32[]{:S(2)}, u32[]{:S(2)}) collective-permute-start(f32[2,512]{1,0:T(2,128)} %broadcast_add_fusion), channel_id=1, source_target_pairs={{0,28},{4,24},{8,20},{12,16},{16,12},{20,8},{24,4},{28,0},{1,29},{... | collective-permute-start | bytes 12296 | tf_op jit(solution)/shard_map/ppermute | solution.py:20
  49.5 35.9 %collective-permute-start.12 = (f32[2,512]{1,0:T(2,128)}, f32[2,512]{1,0:T(2,128)}, u32[]{:S(2)}, u32[]{:S(2)}) collective-permute-start(f32[2,512]{1,0:T(2,128)} %broadcast_add_fusion), channel_id=1, source_target_pairs={{0,24},{4,28},{8,16},{12,20},{16,8},{20,12},{24,0},{28,4},{1,25},{... | collective-permute-start | bytes 12296 | tf_op jit(solution)/shard_map/ppermute | solution.py:20
  51.9 32.5 %collective-permute-start.11 = (f32[2,512]{1,0:T(2,128)}, f32[2,512]{1,0:T(2,128)}, u32[]{:S(2)}, u32[]{:S(2)}) collective-permute-start(f32[2,512]{1,0:T(2,128)} %broadcast_add_fusion), channel_id=1, source_target_pairs={{0,20},{4,16},{8,28},{12,24},{16,4},{20,0},{24,12},{28,8},{1,21},{... | collective-permute-start | bytes 12296 | tf_op jit(solution)/shard_map/ppermute | solution.py:20
  52.6 30.9 %collective-permute-start.10 = (f32[2,512]{1,0:T(2,128)}, f32[2,512]{1,0:T(2,128)}, u32[]{:S(2)}, u32[]{:S(2)}) collective-permute-start(f32[2,512]{1,0:T(2,128)} %broadcast_add_fusion), channel_id=1, source_target_pairs={{0,16},{4,20},{8,24},{12,28},{16,0},{20,4},{24,8},{28,12},{1,17},{... | collective-permute-start | bytes 12296 | tf_op jit(solution)/shard_map/ppermute | solution.py:20
  54.7 16.7 %collective-permute-start.7 = (f32[2,512]{1,0:T(2,128)}, f32[2,512]{1,0:T(2,128)}, u32[]{:S(2)}, u32[]{:S(2)}) collective-permute-start(f32[2,512]{1,0:T(2,128)} %broadcast_add_fusion), channel_id=1, source_target_pairs={{0,4},{4,0},{8,12},{12,8},{16,20},{20,16},{24,28},{28,24},{1,5},{5... | collective-permute-start | bytes 12296 | tf_op jit(solution)/shard_map/ppermute | solution.py:20
  80.0 25.4 %collective-permute-start.20 = (bf16[2,16,512]{2,1,0:T(8,128)(2,1)S(1)}, bf16[2,16,512]{2,1,0:T(8,128)(2,1)S(1)}, u32[]{:S(2)}, u32[]{:S(2)}) collective-permute-start(bf16[2,16,512]{2,1,0:T(8,128)(2,1)S(1)} %get-tuple-element.42), channel_id=1, source_target_pairs={{0,28},{4,24},{8,20},{12,16},{16,12},{20,8},{24,4},{28,0},{1,29},{... | collective-permute-start | bytes 98312 | tf_op jit(solution)/shard_map/ppermute | solution.py:20
  83.4 21.3 %collective-permute-start.19 = (bf16[2,16,512]{2,1,0:T(8,128)(2,1)S(1)}, bf16[2,16,512]{2,1,0:T(8,128)(2,1)S(1)}, u32[]{:S(2)}, u32[]{:S(2)}) collective-permute-start(bf16[2,16,512]{2,1,0:T(8,128)(2,1)S(1)} %get-tuple-element.93), channel_id=1, source_target_pairs={{0,24},{4,28},{8,16},{12,20},{16,8},{20,12},{24,0},{28,4},{1,25},{... | collective-permute-start | bytes 98312 | tf_op jit(solution)/shard_map/ppermute | solution.py:20
  84.3 19.8 %collective-permute-start.18 = (bf16[2,16,512]{2,1,0:T(8,128)(2,1)S(1)}, bf16[2,16,512]{2,1,0:T(8,128)(2,1)S(1)}, u32[]{:S(2)}, u32[]{:S(2)}) collective-permute-start(bf16[2,16,512]{2,1,0:T(8,128)(2,1)S(1)} %get-tuple-element.94), channel_id=1, source_target_pairs={{0,20},{4,16},{8,28},{12,24},{16,4},{20,0},{24,12},{28,8},{1,21},{... | collective-permute-start | bytes 98312 | tf_op jit(solution)/shard_map/ppermute | solution.py:20
  85.4 18.1 %collective-permute-start.17 = (bf16[2,16,512]{2,1,0:T(8,128)(2,1)}, bf16[2,16,512]{2,1,0:T(8,128)(2,1)S(1)}, u32[]{:S(2)}, u32[]{:S(2)}) collective-permute-start(bf16[2,16,512]{2,1,0:T(8,128)(2,1)} %get-tuple-element.95), channel_id=1, source_target_pairs={{0,16},{4,20},{8,24},{12,28},{16,0},{20,4},{24,8},{28,12},{1,17},{... | collective-permute-start | bytes 98312 | tf_op jit(solution)/shard_map/ppermute | solution.py:20
  166.8 13.1 %collective-permute-start.28 = (f32[2,256]{1,0:T(2,128)S(1)}, f32[2,256]{1,0:T(2,128)S(1)}, u32[]{:S(2)}, u32[]{:S(2)}) collective-permute-start(f32[2,256]{1,0:T(2,128)S(1)} %get-tuple-element.34), channel_id=1, source_target_pairs={{0,1},{1,0},{2,3},{3,2},{4,5},{5,4},{6,7},{7,6},{8,9},{9,8},{10,11... | collective-permute-start | bytes 6152 | tf_op jit(solution)/shard_map/ppermute | solution.py:20
  168.4 17.8 %collective-permute-start.48 = (bf16[256,1024]{1,0:T(8,128)(2,1)}, bf16[256,1024]{1,0:T(8,128)(2,1)}, u32[]{:S(2)}, u32[]{:S(2)}) collective-permute-start(bf16[256,1024]{1,0:T(8,128)(2,1)} %select_convert_fusion), channel_id=1, source_target_pairs={{0,4},{4,0},{8,12},{12,8},{16,20},{20,16},{24,28},{28,24},{1,5},{5... | collective-permute-start | bytes 1572872 | tf_op jit(solution)/shard_map/ppermute | solution.py:20
  170.8 18.9 %collective-permute-start.21 = (bf16[2,2,256,256]{3,2,1,0:T(8,128)(2,1)}, bf16[2,2,256,256]{3,2,1,0:T(8,128)(2,1)}, u32[]{:S(2)}, u32[]{:S(2)}) collective-permute-start(bf16[2,2,256,256]{3,2,1,0:T(8,128)(2,1)} %select_convert_fusion.4), channel_id=1, source_target_pairs={{0,2},{1,3},{2,0},{3,1},{4,6},{5,7},{6,4},{7,5},{8,10},{9,11},{10,... | collective-permute-start | bytes 1572872 | tf_op jit(solution)/shard_map/ppermute | solution.py:20
  176.8 17.9 %collective-permute-start.36 = (bf16[512,512]{1,0:T(8,128)(2,1)}, bf16[512,512]{1,0:T(8,128)(2,1)}, u32[]{:S(2)}, u32[]{:S(2)}) collective-permute-start(bf16[512,512]{1,0:T(8,128)(2,1)} %select_convert_fusion.2), channel_id=1, source_target_pairs={{0,4},{4,0},{8,12},{12,8},{16,20},{20,16},{24,28},{28,24},{1,5},{5... | collective-permute-start | bytes 1572872 | tf_op jit(solution)/shard_map/ppermute | solution.py:20
  177.6 27.4 %collective-permute-start.42 = (bf16[512,512]{1,0:T(8,128)(2,1)S(1)}, bf16[512,512]{1,0:T(8,128)(2,1)}, u32[]{:S(2)}, u32[]{:S(2)}) collective-permute-start(bf16[512,512]{1,0:T(8,128)(2,1)S(1)} %select_convert_fusion.1), channel_id=1, source_target_pairs={{0,4},{4,0},{8,12},{12,8},{16,20},{20,16},{24,28},{28,24},{1,5},{5... | collective-permute-start | bytes 1572872 | tf_op jit(solution)/shard_map/ppermute | solution.py:20
  184.7 22.8 %collective-permute-start.26 = (bf16[2,2,256,256]{3,2,1,0:T(8,128)(2,1)}, bf16[2,2,256,256]{3,2,1,0:T(8,128)(2,1)S(1)}, u32[]{:S(2)}, u32[]{:S(2)}) collective-permute-start(bf16[2,2,256,256]{3,2,1,0:T(8,128)(2,1)} %select_convert_fusion.3), channel_id=1, source_target_pairs={{0,2},{1,3},{2,0},{3,1},{4,6},{5,7},{6,4},{7,5},{8,10},{9,11},{10,... | collective-permute-start | bytes 1572872 | tf_op jit(solution)/shard_map/ppermute | solution.py:20
  188.4 19.5 %collective-permute-start.49 = (bf16[128,1024]{1,0:T(8,128)(2,1)S(1)}, bf16[128,1024]{1,0:T(8,128)(2,1)S(1)}, u32[]{:S(2)}, u32[]{:S(2)}) collective-permute-start(bf16[128,1024]{1,0:T(8,128)(2,1)S(1)} %select_convert_fusion.5), channel_id=1, source_target_pairs={{0,8},{4,12},{8,0},{12,4},{16,24},{20,28},{24,16},{28,20},{1,9},{5... | collective-permute-start | bytes 786440 | tf_op jit(solution)/shard_map/ppermute | solution.py:20
  191.0 26.7 %collective-permute-start.22 = (bf16[1,2,256,256]{3,2,1,0:T(8,128)(2,1)S(1)}, bf16[1,2,256,256]{3,2,1,0:T(8,128)(2,1)S(1)}, u32[]{:S(2)}, u32[]{:S(2)}) collective-permute-start(bf16[1,2,256,256]{3,2,1,0:T(8,128)(2,1)S(1)} %select_convert_fusion.9), channel_id=1, source_target_pairs={{0,1},{1,0},{2,3},{3,2},{4,5},{5,4},{6,7},{7,6},{8,9},{9,8},{10,11... | collective-permute-start | bytes 786440 | tf_op jit(solution)/shard_map/ppermute | solution.py:20
  196.1 14.2 %collective-permute-start.37 = (bf16[256,512]{1,0:T(8,128)(2,1)S(1)}, bf16[256,512]{1,0:T(8,128)(2,1)S(1)}, u32[]{:S(2)}, u32[]{:S(2)}) collective-permute-start(bf16[256,512]{1,0:T(8,128)(2,1)S(1)} %select_convert_fusion.7), channel_id=1, source_target_pairs={{0,8},{4,12},{8,0},{12,4},{16,24},{20,28},{24,16},{28,20},{1,9},{5... | collective-permute-start | bytes 786440 | tf_op jit(solution)/shard_map/ppermute | solution.py:20
  208.0 17.2 %collective-permute-start.50 = (bf16[64,1024]{1,0:T(8,128)(2,1)S(1)}, bf16[64,1024]{1,0:T(8,128)(2,1)}, u32[]{:S(2)}, u32[]{:S(2)}) collective-permute-start(bf16[64,1024]{1,0:T(8,128)(2,1)S(1)} %select_convert_fusion.10), channel_id=1, source_target_pairs={{0,16},{4,20},{8,24},{12,28},{16,0},{20,4},{24,8},{28,12},{1,17},{... | collective-permute-start | bytes 393224 | tf_op jit(solution)/shard_map/ppermute | solution.py:20
  211.1 18.0 %collective-permute-start.38 = (bf16[128,512]{1,0:T(8,128)(2,1)}, bf16[128,512]{1,0:T(8,128)(2,1)}, u32[]{:S(2)}, u32[]{:S(2)}) collective-permute-start(bf16[128,512]{1,0:T(8,128)(2,1)} %select_convert_fusion.12), channel_id=1, source_target_pairs={{0,16},{4,20},{8,24},{12,28},{16,0},{20,4},{24,8},{28,12},{1,17},{... | collective-permute-start | bytes 393224 | tf_op jit(solution)/shard_map/ppermute | solution.py:20
  216.5 17.7 %collective-permute-start.44 = (bf16[128,512]{1,0:T(8,128)(2,1)S(1)}, bf16[128,512]{1,0:T(8,128)(2,1)S(1)}, u32[]{:S(2)}, u32[]{:S(2)}) collective-permute-start(bf16[128,512]{1,0:T(8,128)(2,1)S(1)} %select_convert_fusion.11), channel_id=1, source_target_pairs={{0,16},{4,20},{8,24},{12,28},{16,0},{20,4},{24,8},{28,12},{1,17},{... | collective-permute-start | bytes 393224 | tf_op jit(solution)/shard_map/ppermute | solution.py:20
  226.2 18.7 %collective-permute-start.51 = (bf16[64,1024]{1,0:T(8,128)(2,1)S(1)}, bf16[64,1024]{1,0:T(8,128)(2,1)S(1)}, u32[]{:S(2)}, u32[]{:S(2)}) collective-permute-start(bf16[64,1024]{1,0:T(8,128)(2,1)S(1)} %add_convert_fusion), channel_id=1, source_target_pairs={{0,16},{4,20},{8,24},{12,28},{16,0},{20,4},{24,8},{28,12},{1,17},{... | collective-permute-start | bytes 393224 | tf_op jit(solution)/shard_map/ppermute | solution.py:20
  230.1 19.9 %collective-permute-start.39 = (bf16[128,512]{1,0:T(8,128)(2,1)S(1)}, bf16[128,512]{1,0:T(8,128)(2,1)S(1)}, u32[]{:S(2)}, u32[]{:S(2)}) collective-permute-start(bf16[128,512]{1,0:T(8,128)(2,1)S(1)} %add_convert_fusion.2), channel_id=1, source_target_pairs={{0,16},{4,20},{8,24},{12,28},{16,0},{20,4},{24,8},{28,12},{1,17},{... | collective-permute-start | bytes 393224 | tf_op jit(solution)/shard_map/ppermute | solution.py:20
  231.4 13.4 %collective-permute-start.32 = (bf16[32,512]{1,0:T(8,128)(2,1)S(1)}, bf16[32,512]{1,0:T(8,128)(2,1)S(1)}, u32[]{:S(2)}, u32[]{:S(2)}) collective-permute-start(bf16[32,512]{1,0:T(8,128)(2,1)S(1)} %select_convert_fusion.15), channel_id=1, source_target_pairs={{0,16},{4,20},{8,24},{12,28},{16,0},{20,4},{24,8},{28,12},{1,17},{... | collective-permute-start | bytes 98312 | tf_op jit(solution)/shard_map/ppermute | solution.py:20
  234.3 24.2 %collective-permute-start.45 = (bf16[128,512]{1,0:T(8,128)(2,1)S(1)}, bf16[128,512]{1,0:T(8,128)(2,1)S(1)}, u32[]{:S(2)}, u32[]{:S(2)}) collective-permute-start(bf16[128,512]{1,0:T(8,128)(2,1)S(1)} %add_convert_fusion.1), channel_id=1, source_target_pairs={{0,16},{4,20},{8,24},{12,28},{16,0},{20,4},{24,8},{28,12},{1,17},{... | collective-permute-start | bytes 393224 | tf_op jit(solution)/shard_map/ppermute | solution.py:20
  245.0 20.6 %collective-permute-start.52 = (bf16[128,1024]{1,0:T(8,128)(2,1)S(1)}, bf16[128,1024]{1,0:T(8,128)(2,1)S(1)}, u32[]{:S(2)}, u32[]{:S(2)}) collective-permute-start(bf16[128,1024]{1,0:T(8,128)(2,1)S(1)} %pad_maximum_fusion.8), channel_id=1, source_target_pairs={{0,8},{4,12},{8,0},{12,4},{16,24},{20,28},{24,16},{28,20},{1,9},{5... | collective-permute-start | bytes 786440 | tf_op jit(solution)/shard_map/ppermute | solution.py:20
  250.0 17.4 %collective-permute-start.40 = (bf16[256,512]{1,0:T(8,128)(2,1)S(1)}, bf16[256,512]{1,0:T(8,128)(2,1)S(1)}, u32[]{:S(2)}, u32[]{:S(2)}) collective-permute-start(bf16[256,512]{1,0:T(8,128)(2,1)S(1)} %pad_maximum_fusion.6), channel_id=1, source_target_pairs={{0,8},{4,12},{8,0},{12,4},{16,24},{20,28},{24,16},{28,20},{1,9},{5... | collective-permute-start | bytes 786440 | tf_op jit(solution)/shard_map/ppermute | solution.py:20
  265.8 14.9 %collective-permute-start.53 = (bf16[256,1024]{1,0:T(8,128)(2,1)S(1)}, bf16[256,1024]{1,0:T(8,128)(2,1)S(1)}, u32[]{:S(2)}, u32[]{:S(2)}) collective-permute-start(bf16[256,1024]{1,0:T(8,128)(2,1)S(1)} %pad_maximum_fusion.5), channel_id=1, source_target_pairs={{0,4},{4,0},{8,12},{12,8},{16,20},{20,16},{24,28},{28,24},{1,5},{5... | collective-permute-start | bytes 1572872 | tf_op jit(solution)/shard_map/ppermute | solution.py:20
  267.6 24.4 %collective-permute-start.41 = (bf16[512,512]{1,0:T(8,128)(2,1)S(1)}, bf16[512,512]{1,0:T(8,128)(2,1)S(1)}, u32[]{:S(2)}, u32[]{:S(2)}) collective-permute-start(bf16[512,512]{1,0:T(8,128)(2,1)S(1)} %pad_maximum_fusion.3), channel_id=1, source_target_pairs={{0,4},{4,0},{8,12},{12,8},{16,20},{20,16},{24,28},{28,24},{1,5},{5... | collective-permute-start | bytes 1572872 | tf_op jit(solution)/shard_map/ppermute | solution.py:20
  268.2 30.5 %collective-permute-start.47 = (bf16[512,512]{1,0:T(8,128)(2,1)S(1)}, bf16[512,512]{1,0:T(8,128)(2,1)S(1)}, u32[]{:S(2)}, u32[]{:S(2)}) collective-permute-start(bf16[512,512]{1,0:T(8,128)(2,1)S(1)} %pad_maximum_fusion.4), channel_id=1, source_target_pairs={{0,4},{4,0},{8,12},{12,8},{16,20},{20,16},{24,28},{28,24},{1,5},{5... | collective-permute-start | bytes 1572872 | tf_op jit(solution)/shard_map/ppermute | solution.py:20
  (92 other events, 524.8 us)
where the time goes:
time: 303 us; the launch traced here: 302 us
  waiting for transfers between devices  95 us (31%)
  starting transfers between devices  68.5 us (23%)
  other arithmetic  45.2 us (15%)
  Pallas kernels  39 us (13%)
  local copies, waits for them, and re-layouts  35.2 us (12%)
  matrix products  16.6 us (5%)
    ppermute x52, waiting for transfers between devices, swap(): return lax.ppermute(block, axis, [(i, i ^ bit) for i in range(devices)])  91.9 us
    ppermute x52, starting transfers between devices, swap(): return lax.ppermute(block, axis, [(i, i ^ bit) for i in range(devices)])  63 us
    pallas_call x1, Pallas kernels, scan_all(): pl.pallas_call(scan_kernel, grid=(lanes,), in_specs=[token, token, token,...  29.8 us
    unnamed x154, local copies, waits for them, and re-layouts  18.7 us
    pallas_call x1, Pallas kernels, scan_ends(): pl.pallas_call(ends_kernel, grid=(lanes,), in_specs=[token, token, token,...  9.26 us
    add x10, other arithmetic, scatter_sum(): total = kept.astype(F32) + swap(sent.astype(BF16), axis, bit).astype(F32)  6.55 us
  transfers between devices with their start and end apart: 54, of which 23 were waited for; matrix products, arithmetic and copies ran while one was open for 20% of the time, Pallas kernels for 3%

commit v1 on v0

v1 whole, which is shorter than its diff:
```python
import functools

import jax
import jax.numpy as jnp
from jax import lax
from jax.experimental import pallas as pl
from jax.experimental.pallas import tpu as pltpu
from jax.sharding import PartitionSpec as P

F32 = jnp.float32
BF16 = jnp.bfloat16
LOG2E = 1.4426950408889634
CHUNK = 32
LANE = 128
FAR = 1.0e4
VMEM = pl.BlockSpec(memory_space=pltpu.VMEM)


def swap(block, axis, bit):
    devices = lax.axis_size(axis)
    return lax.ppermute(block, axis, [(i, i ^ bit) for i in range(devices)])


def from_behind(block, axis, distance):
    devices = range(lax.axis_size(axis))
    route = [(i - distance, i) for i in devices if i - distance in devices]
    return lax.ppermute(block, axis, route)


def bits_of(axis):
    count = lax.axis_size(axis)
    bits = []
    while (1 << len(bits)) < count:
        bits.append(1 << len(bits))
    return bits


def after(array, *others):
    return lax.optimization_barrier((array, *others))[0]


def hop(kept, sent, axis, bit):
    total = kept.astype(F32) + swap(sent, axis, bit).astype(F32)
    half = total.shape[-1] // 2
    return total[..., :half], total[..., half:].astype(BF16)


class Reduction:
    def __init__(self):
        self.bits = bits_of("seq")
        self.orders = [list(self.bits), list(self.bits)]
        if len(self.bits) > 1:
            self.orders[1][:2] = self.bits[1], self.bits[0]
        self.index = lax.axis_index("seq")
        self.odd = lax.axis_index("mp") % 2
        self.mp = lax.axis_size("mp")
        self.count = lax.axis_size("seq")

    def own(self, step):
        even = (self.index & self.orders[0][step]) != 0
        odd = (self.index & self.orders[1][step]) != 0
        return jnp.where(self.odd == 1, odd, even).astype(jnp.int32)

    def swap(self, block, step):
        route = []
        for s in range(self.count):
            for m in range(self.mp):
                route.append((s * self.mp + m, (s ^ self.orders[m % 2][step]) * self.mp + m))
        return lax.ppermute(block, ("seq", "mp"), route)

    def halves(self, block, step):
        half = block.shape[0] // 2
        up = self.own(step)
        kept = lax.dynamic_slice_in_dim(block, up * half, half, 0)
        sent = lax.dynamic_slice_in_dim(block, (1 - up) * half, half, 0)
        return kept, sent

    def part(self, left, right, up):
        half = left.shape[2] // 2
        cut = lax.dynamic_slice_in_dim(left, up * half, half, 2)
        return jnp.einsum("lta,ltb->ab", cut, right, preferred_element_type=F32)

    def sent(self, left, right):
        return self.part(left, right, 1 - self.own(0)).astype(BF16)

    def kept(self, left, right):
        return self.part(left, right, self.own(0))

    def place(self):
        place = jnp.int32(0)
        for step in range(1, len(self.bits)):
            place = place * 2 + self.own(step)
        return place

    def order(self, per, turn):
        blocks = self.count // 2
        pieces = blocks // per
        at = jnp.arange(blocks)
        low, high = turn % pieces, turn // pieces
        source = (((at // per) ^ low) * per + at % per) ^ self.place()
        up = self.own(0) ^ high
        return jnp.concatenate([jnp.stack([up * blocks, (1 - up) * blocks]), source]).astype(jnp.int32)


class Sum:
    def __init__(self, over, sent, count):
        self.over, self.count, self.kept = over, count, None
        self.step, self.down = 0, False
        self.sent = sent
        self.got = over.swap(sent, 0)

    def split(self, block):
        rows = block.shape[0] // self.count
        return [block[k * rows : (k + 1) * rows] for k in range(self.count)]

    def over_now(self):
        return self.down and self.step == 0

    def next(self, *earlier):
        over, steps = self.over, len(self.over.bits)
        if earlier:
            self.got = after(self.got, *earlier)
        got = self.split(self.got)
        if not self.down:
            self.step += 1
            if self.step < steps:
                sent = []
                for k in range(self.count):
                    own, other = over.halves(self.kept[k], self.step), over.halves(got[k], self.step)
                    self.kept[k] = own[0].astype(F32) + other[0].astype(F32)
                    sent.append((own[1].astype(F32) + other[1].astype(F32)).astype(BF16))
                self.sent = jnp.concatenate(sent, axis=0)
            else:
                self.down = True
                self.whole = [(a.astype(F32) + b.astype(F32)).astype(BF16) for a, b in zip(self.kept, got, strict=True)]
                self.step -= 1
        else:
            self.whole = [jnp.concatenate(pair, axis=0) for pair in zip(self.whole, got, strict=True)]
            self.step -= 1
        if self.down:
            self.sent = jnp.concatenate(self.whole, axis=0)
        self.got = over.swap(self.sent, self.step)
        return self.sent

    def finish(self):
        while not self.over_now():
            self.next()
        return self.whole, self.split(self.got)


def silu_slope(values):
    logistic = jax.nn.sigmoid(values)
    return logistic * (1.0 + values * (1.0 - logistic))


def cost(ops, lanes, length, width, states):
    work = lanes * length * width * states
    return pl.CostEstimate(flops=ops * work * 16, bytes_accessed=work * 2, transcendentals=work)


def settle_kernel(names, layout, order_ref, *refs):
    parts, outs = refs[: len(layout)], refs[-2 - names : -2]
    wide, sems = refs[-2:]
    copies, at = [], 0
    for part, (out, lead, which, first, blocks, turned) in zip(parts, layout, strict=True):
        size = part.shape[0] // blocks
        for b in range(blocks):
            source = order_ref[which + 2 + b]
            rows = part[pl.ds(pl.multiple_of(source * size, size), size), :].astype(F32)
            goal = pl.multiple_of((order_ref[which + first] + b) * size, size)
            ref = outs[out] if lead is None else outs[out].at[lead]
            if turned:
                rows = jnp.transpose(rows)
                spot = wide.at[at : at + rows.shape[0], 0:size]
                target = ref.at[:, pl.ds(goal, size)]
            else:
                spot = wide.at[at : at + size, 0 : part.shape[1]]
                target = ref.at[pl.ds(goal, size), :]
            spot[...] = rows
            at += rows.shape[0]
            copies.append(pltpu.make_async_copy(spot, target, sems.at[len(copies)]))
            copies[-1].start()
    for copy in copies:
        copy.wait()


def settle(orders, parts, layout, shapes, into=()):
    any_space = pl.BlockSpec(memory_space=pl.ANY)
    rows = sum(p.shape[1] * l[4] if l[5] else p.shape[0] for p, l in zip(parts, layout, strict=True))
    width = max(p.shape[0] // l[4] if l[5] else p.shape[1] for p, l in zip(parts, layout, strict=True))
    count = sum(l[4] for l in layout)
    return pl.pallas_call(
        functools.partial(settle_kernel, len(shapes), layout),
        in_specs=[pl.BlockSpec(memory_space=pltpu.SMEM)] + [VMEM] * len(parts) + [any_space] * len(into),
        out_specs=[any_space] * len(shapes),
        out_shape=[jax.ShapeDtypeStruct(s, F32) for s in shapes],
        input_output_aliases={1 + len(parts) + k: k for k in range(len(into))},
        scratch_shapes=[pltpu.VMEM((rows, width), F32), pltpu.SemaphoreType.DMA((count,))],
        compiler_params=pltpu.CompilerParams(vmem_limit_bytes=16 << 20),
        name="settle",
    )(orders, *parts, *into)


def iota(shape, dim):
    return lax.broadcasted_iota(jnp.int32, shape, dim)


def widen(part, width):
    return jnp.concatenate([part] * (width // part.shape[1]), axis=1)


def dot(a, b):
    return jnp.dot(a, b, preferred_element_type=F32)


def dot_t(a, b):
    return lax.dot_general(a, b, (((1,), (1,)), ((), ())), preferred_element_type=F32)


def row_of(ref, t, count):
    return jnp.broadcast_to(ref[pl.ds(t, 1), :], (count, ref.shape[1]))


def rows_of(i, count):
    return pl.ds(pl.multiple_of(i * count, count), count)


def chunk_columns(ref, i):
    per = LANE // CHUNK
    tile = ref[:, rows_of(i // per, LANE)]
    return pltpu.roll(tile, LANE - (i % per) * CHUNK, 1)


def spread_column(tile, j, width):
    part = jnp.broadcast_to(tile[:, j : j + 1], (tile.shape[0], LANE))
    return widen(part, width)


def selectors(states):
    wide = CHUNK * states
    per_state = iota((states, wide), 1) % states == iota((states, wide), 0)
    per_step = iota((CHUNK, wide), 1) // states == iota((CHUNK, wide), 0)
    return per_state.astype(F32), per_step.astype(F32)


def from_lanes(first, states):
    shape = (LANE, CHUNK * states)
    return (iota(shape, 0) == first + iota(shape, 1) % states).astype(BF16)


def to_lanes(first, states):
    shape = (CHUNK * states, LANE)
    return (iota(shape, 1) == first + iota(shape, 0) % states).astype(BF16)


def by_step(proj, lanes, per_step):
    spread = dot(proj, lanes)
    return spread * jnp.concatenate([per_step] * (spread.shape[0] // CHUNK), axis=0)


def ends_kernel(
    low_rank, sent_ref, got_ref, wdt_ref, bias_ref, log_ref, mixed_ref, gy_ref,
    end_ref, pull_ref, span_ref, dt_ref, u_ref, sig_ref, proj_ref,
    ahead, behind, left_b, left_c, xa, xb, ya, yb,
):
    length, width = dt_ref.shape
    states = log_ref.shape[0]
    rate = -jnp.exp(log_ref[...]) * LOG2E
    per_state, per_step = selectors(states)
    chunks = length // CHUNK
    upto = (iota((length, length), 1) <= iota((length, length), 0)).astype(BF16)
    after = (iota((length, length), 1) > iota((length, length), 0)).astype(BF16)
    proj = sent_ref[...].astype(F32) + got_ref[...].astype(F32)
    proj_ref[...] = proj
    proj = proj.astype(BF16)
    for first, left in ((low_rank, left_b), (low_rank + states, left_c)):
        spread = by_step(proj, from_lanes(first, states), per_step)
        for i in range(chunks):
            flat = jnp.sum(spread[i * CHUNK : (i + 1) * CHUNK], axis=0, keepdims=True)
            left[i * states : (i + 1) * states, :] = (flat * per_state).astype(BF16)
    block = min(128, length)
    for i in range(length // block):
        o = slice(i * block, (i + 1) * block)
        pre = dot(proj[o], wdt_ref[...]) + bias_ref[...]
        small = jnp.exp(-jnp.abs(pre))
        one = 1.0 + small
        series = small * (1.0 - small * (0.5 - small * (1.0 / 3.0)))
        dt = jnp.maximum(pre, 0.0) + jnp.where(small < 1e-3, series, jnp.log(one))
        dt_ref[o, :] = dt
        u_ref[o, :] = dt * mixed_ref[o, :]
        sig_ref[o, :] = jnp.where(pre >= 0.0, 1.0, small) / one
    dt = dt_ref[...]
    high = dt.astype(BF16)
    low = (dt - high.astype(F32)).astype(BF16)
    ahead[...] = dot(upto, high) + dot(upto, low)
    behind[...] = dot(after, high) + dot(after, low)
    span_ref[...] = ahead[length - 1 : length, :]
    xb[...] = jnp.zeros(xb.shape, BF16)
    yb[...] = jnp.zeros(yb.shape, BF16)

    def flush(i, x, y, sums):
        o = rows_of(jnp.maximum(i, 0), states)
        return sums[0] + dot(left_b[o, :], x[...]), sums[1] + dot(left_c[o, :], y[...])

    def fill(i, x, y):
        for j in range(CHUNK):
            t = i * CHUNK + j
            s = slice(j * states, (j + 1) * states)
            to_end = jnp.exp2(row_of(behind, t, states) * rate)
            x[s, :] = (to_end * row_of(u_ref, t, states)).astype(BF16)
            to_here = jnp.exp2(row_of(ahead, t, states) * rate)
            y[s, :] = (to_here * row_of(gy_ref, t, states)).astype(BF16)

    def body(k, sums):
        sums = flush(2 * k - 1, xb, yb, sums)
        fill(2 * k, xa, ya)
        sums = flush(2 * k, xa, ya, sums)
        fill(2 * k + 1, xb, yb)
        return sums

    zero = jnp.zeros((states, width), F32)
    sums = lax.fori_loop(0, chunks // 2, body, (zero, zero))
    sums = flush(chunks - 1, xb, yb, sums)
    end_ref[...] = sums[0]
    pull_ref[...] = sums[1]


def lane_spec(*shape):
    return pl.BlockSpec((None, *shape), lambda l: (l,) + (0,) * len(shape))


def whole_spec(*shape):
    return pl.BlockSpec(shape, lambda l: (0,) * len(shape))


def scan_ends(low_rank, sent, got, w_dt, bias, log, mixed, gy):
    lanes, length, width = mixed.shape
    states = log.shape[0]
    shape = jax.ShapeDtypeStruct
    token = shape((lanes, length, width), F32)
    state = shape((lanes, states, width), F32)
    tokens, state_spec, narrow = lane_spec(length, width), lane_spec(states, width), lane_spec(length, LANE)
    return pl.pallas_call(
        functools.partial(ends_kernel, low_rank),
        grid=(lanes,),
        in_specs=[
            narrow,
            narrow,
            whole_spec(*w_dt.shape),
            whole_spec(1, width),
            whole_spec(states, width),
            tokens,
            tokens,
        ],
        out_specs=[state_spec, state_spec, lane_spec(1, width), tokens, tokens, tokens, narrow],
        out_shape=[state, state, shape((lanes, 1, width), F32), token, token, token, shape(sent.shape, F32)],
        scratch_shapes=[pltpu.VMEM((length, width), F32)] * 2
        + [pltpu.VMEM((length // CHUNK * states, CHUNK * states), BF16)] * 2
        + [pltpu.VMEM((CHUNK * states, width), BF16)] * 4,
        compiler_params=pltpu.CompilerParams(vmem_limit_bytes=24 << 20),
        cost_estimate=cost(8, lanes, length, width, states),
        name="scan_ends",
    )(sent, got, w_dt, bias, log, mixed, gy)


def forward_kernel(
    low_rank, lanes, place_ref, proj_ref, log_ref, dt_ref, u_ref, gy_ref, got_ref,
    y_ref, gc_ref, last_ref, hs_ref,
    pa, pb, p0, cols, left_c, masked, sems,
):
    length, width = dt_ref.shape
    states = log_ref.shape[0]
    l = pl.program_id(0)
    rate = -jnp.exp(log_ref[...]) * LOG2E
    _, per_step = selectors(states)
    wide = CHUNK * states
    chunks = length // CHUNK
    groups = got_ref.shape[0]
    place = place_ref[0]

    def leave(i, p, at):
        rows = pl.ds(pl.multiple_of((i * CHUNK + 1) * states, states), wide)
        return pltpu.make_async_copy(p, hs_ref.at[l, rows, :], sems.at[at])

    zero = jnp.zeros((states, width), F32)

    def join(g, total, use):
        at = lanes * states
        spans = got_ref[g, at : at + lanes, :].astype(F32)
        span = jnp.sum(jnp.where(iota(spans.shape, 0) == l, spans, 0.0), axis=0, keepdims=True)
        factor = jnp.exp2(span * rate)
        return jnp.where(use, total * factor + got_ref[g, rows_of(l, states), :].astype(F32), total)

    begin = last = zero
    for g in range(groups):
        begin = join(g, begin, g < place)
        h = groups - 1 - g
        last = join(h, last, h > place)
    last_ref[...] = last
    begin = jnp.where(place_ref[1 + l] != 0, 0.0, begin)
    p0[...] = begin.astype(BF16)
    first = pltpu.make_async_copy(p0, hs_ref.at[l, pl.ds(0, states), :], sems.at[2])
    first.start()
    proj = proj_ref[...]
    cols[...] = jnp.transpose(proj)[low_rank : low_rank + states]
    spread = by_step(proj.astype(BF16), from_lanes(low_rank + states, states), per_step)
    left_c[...] = spread.astype(BF16)

    def flush(i, p):
        o = rows_of(jnp.maximum(i, 0), CHUNK)
        h = p[...]
        y_ref[o, :] = dot(left_c[o, :], h)
        masked[o, :] = (dot_t(gy_ref[o, :].astype(BF16), h) * per_step).astype(BF16)

    def fill(i, state, p):
        b_tile = chunk_columns(cols, i)
        for j in range(CHUNK):
            t = i * CHUNK + j
            b = spread_column(b_tile, j, width)
            decay = jnp.exp2(row_of(dt_ref, t, states) * rate)
            state = decay * state + row_of(u_ref, t, states) * b
            p[j * states : (j + 1) * states, :] = state.astype(BF16)
        return state

    def body(k, state):
        @pl.when(k > 0)
        def _():
            leave(2 * k - 2, pa, 0).wait()

        flush(2 * k - 1, pb)
        state = fill(2 * k, state, pa)
        leave(2 * k, pa, 0).start()

        @pl.when(k > 0)
        def _():
            leave(2 * k - 1, pb, 1).wait()

        flush(2 * k, pa)
        state = fill(2 * k + 1, state, pb)
        leave(2 * k + 1, pb, 1).start()
        return state

    lax.fori_loop(0, chunks // 2, body, begin)
    flush(chunks - 1, pb)
    gc_ref[...] = dot(masked[...], to_lanes(low_rank + states, states))
    leave(chunks - 2, pa, 0).wait()
    leave(chunks - 1, pb, 1).wait()
    first.wait()


def scan_forward(low_rank, place, proj, log, dt, u, gy, got):
    lanes, length, width = dt.shape
    states = log.shape[0]
    shape = jax.ShapeDtypeStruct
    tokens, state_spec, narrow = lane_spec(length, width), lane_spec(states, width), lane_spec(length, LANE)
    return pl.pallas_call(
        functools.partial(forward_kernel, low_rank, lanes),
        grid=(lanes,),
        in_specs=[
            pl.BlockSpec(memory_space=pltpu.SMEM),
            narrow,
            whole_spec(states, width),
            tokens,
            tokens,
            tokens,
            whole_spec(*got.shape),
        ],
        out_specs=[tokens, narrow, state_spec, pl.BlockSpec(memory_space=pltpu.HBM)],
        out_shape=[
            shape((lanes, length, width), F32),
            shape(proj.shape, F32),
            shape((lanes, states, width), F32),
            shape((lanes, (length + 1) * states, width), BF16),
        ],
        scratch_shapes=[pltpu.VMEM((CHUNK * states, width), BF16)] * 2
        + [
            pltpu.VMEM((states, width), BF16),
            pltpu.VMEM((states, length), F32),
            pltpu.VMEM((length, CHUNK * states), BF16),
            pltpu.VMEM((length, CHUNK * states), BF16),
            pltpu.SemaphoreType.DMA((3,)),
        ],
        compiler_params=pltpu.CompilerParams(vmem_limit_bytes=24 << 20),
        cost_estimate=cost(8, lanes, length, width, states),
        name="scan_forward",
    )(place, proj, log, dt, u, gy, got)


def backward_kernel(
    low_rank, proj_ref, log_ref, dt_ref, u_ref, gy_ref, last_ref, gc_ref, hs_ref, *refs
):
    (turn_ref, pull_ref, gbc_ref, ga_ref,
     ha, hb, pa, pb, qa, qb, ra, rb, cols, left_b, masked, sems) = refs[-16:]
    length, width = dt_ref.shape
    states = log_ref.shape[0]
    l = pl.program_id(0)
    plain = -jnp.exp(log_ref[...])
    rate = plain * LOG2E
    rate_low = plain.astype(BF16)
    per_state, per_step = selectors(states)
    per_state_low, per_step_low = per_state.astype(BF16), per_step.astype(BF16)
    chunks = length // CHUNK
    wide = CHUNK * states

    def enter(i, h, at):
        return pltpu.make_async_copy(hs_ref.at[l, rows_of(i, wide), :], h, sems.at[at])

    enter(chunks - 1, ha, 0).start()
    for ref in (pb, qb, rb):
        ref[...] = jnp.zeros(ref.shape, BF16)
    proj = proj_ref[...]
    cols[...] = jnp.transpose(proj)[low_rank + states : low_rank + 2 * states]
    left_b[...] = by_step(proj.astype(BF16), from_lanes(low_rank, states), per_step).astype(BF16)

    def flush(i, p, q, r, ga):
        o = rows_of(jnp.minimum(i, chunks - 1), CHUNK)
        grad = p[...]
        pull_ref[o, :] = dot(left_b[o, :], grad)
        masked[o, :] = (dot_t(u_ref[o, :].astype(BF16), grad) * per_step).astype(BF16)
        turn_ref[o, :] = dot(per_step_low, q[...])
        return ga + dot(per_state_low, r[...])

    def fill(i, carry, h, p, q, r):
        c_tile = chunk_columns(cols, i)
        for j in reversed(range(CHUNK)):
            t = i * CHUNK + j
            s = slice(j * states, (j + 1) * states)
            c = spread_column(c_tile, j, width)
            dt = row_of(dt_ref, t, states)
            grad = carry + row_of(gy_ref, t, states) * c
            carry = jnp.exp2(dt * rate) * grad
            p[s, :] = grad.astype(BF16)
            turn = carry.astype(BF16) * h[s, :] * rate_low
            q[s, :] = turn
            r[s, :] = turn * dt.astype(BF16)
        return carry

    def body(k, carried):
        carry, ga = carried
        i = chunks - 1 - 2 * k
        enter(i, ha, 0).wait()
        enter(i - 1, hb, 1).start()
        ga = flush(i + 1, pb, qb, rb, ga)
        carry = fill(i, carry, ha, pa, qa, ra)
        enter(i - 1, hb, 1).wait()

        @pl.when(i > 1)
        def _():
            enter(i - 2, ha, 0).start()

        ga = flush(i, pa, qa, ra, ga)
        carry = fill(i - 1, carry, hb, pb, qb, rb)
        return carry, ga

    zero = jnp.zeros((states, width), F32)
    _, ga = lax.fori_loop(0, chunks // 2, body, (last_ref[...], zero))
    ga_ref[...] = flush(0, pb, qb, rb, ga)
    gbc_ref[...] = gc_ref[...] + dot(masked[...], to_lanes(low_rank, states))


def scan_backward(low_rank, proj, log, dt, u, gy, last, gc, hs, *earlier):
    lanes, length, width = dt.shape
    states = log.shape[0]
    shape = jax.ShapeDtypeStruct
    tokens, state_spec, narrow = lane_spec(length, width), lane_spec(states, width), lane_spec(length, LANE)
    token = shape((lanes, length, width), F32)
    return pl.pallas_call(
        functools.partial(backward_kernel, low_rank),
        grid=(lanes,),
        in_specs=[narrow, whole_spec(states, width), tokens, tokens, tokens, state_spec, narrow]
        + [pl.BlockSpec(memory_space=pltpu.HBM)]
        + [pl.BlockSpec(memory_space=pl.ANY)] * len(earlier),
        out_specs=[tokens, tokens, narrow, state_spec],
        out_shape=[token, token, shape(proj.shape, F32), shape((lanes, states, width), F32)],
        scratch_shapes=[pltpu.VMEM((CHUNK * states, width), BF16)] * 8
        + [
            pltpu.VMEM((states, length), F32),
            pltpu.VMEM((length, CHUNK * states), BF16),
            pltpu.VMEM((length, CHUNK * states), BF16),
            pltpu.SemaphoreType.DMA((2,)),
        ],
        compiler_params=pltpu.CompilerParams(vmem_limit_bytes=24 << 20),
        cost_estimate=cost(12, lanes, length, width, states),
        name="scan_backward",
    )(proj, log, dt, u, gy, last, gc, hs, *earlier)


def per_device(
    inputs,
    row_starts,
    norm_gain,
    in_weight,
    conv_weight,
    conv_bias,
    xproj_weight,
    dtproj_weight,
    dt_bias,
    decay_log,
    skip_gain,
    out_weight,
    output_grad,
):
    lane_count, length, shard_width = inputs.shape
    low_rank = dtproj_weight.shape[0]
    state_count = decay_log.shape[0]
    tap_count = conv_weight.shape[0]
    inner_width = conv_bias.shape[0]
    model_width = norm_gain.shape[0]
    starts = row_starts.astype(F32)
    carry_mask = (1.0 - starts)[:, :, None]
    mp_index, mp_size = lax.axis_index("mp"), lax.axis_size("mp")
    seq_index, seq_size = lax.axis_index("seq"), lax.axis_size("seq")
    mp_bits, seq_bits = bits_of("mp"), bits_of("seq")
    near_first = [int(format(k, "0%db" % len(mp_bits))[::-1], 2) for k in range(mp_size)]

    def blocks(array, axis, order):
        parts = [
            lax.dynamic_slice_in_dim(array, (mp_index ^ k) * shard_width, shard_width, axis) for k in order
        ]
        return jnp.concatenate(parts, axis=axis)

    x_parts, grad_parts = {0: inputs.astype(BF16)}, {}
    square = jnp.sum(jnp.square(inputs), axis=2)
    for bit in reversed(mp_bits):
        for k in list(x_parts):
            x_parts[k | bit] = swap(x_parts[k], "mp", bit)
        square = square + swap(square, "mp", bit)
    grad_parts[0] = after(output_grad.astype(BF16), x_parts[mp_bits[-1]])
    for bit in reversed(mp_bits):
        for k in list(grad_parts):
            grad_parts[k | bit] = swap(grad_parts[k], "mp", bit)
    near = list(range(mp_size))
    w_in = blocks(in_weight, 1, near).astype(BF16)
    w_back = blocks(in_weight, 1, near_first).astype(BF16)
    w_out = out_weight.astype(BF16)
    w_spread = blocks(out_weight, 1, near_first).astype(BF16)
    gain = blocks(norm_gain, 0, near)
    w_x = jnp.pad(xproj_weight.astype(BF16), ((0, 0), (0, -xproj_weight.shape[1] % LANE)))
    w_dt = jnp.pad(dtproj_weight.astype(BF16), ((0, -low_rank % LANE), (0, 0)))
    inv_rms = lax.rsqrt(square[:, :, None] / model_width + 1e-05)
    x_whole = jnp.concatenate([x_parts[k] for k in near], axis=2)
    normed = (x_whole.astype(F32) * inv_rms * gain).astype(BF16)
    inner_act = jnp.einsum("ltd,de->lte", normed, w_in[0], preferred_element_type=F32).astype(BF16)
    rim_rows = from_behind(inner_act[:, length - (tap_count - 1) :, :], "seq", 1)
    gate_in = jnp.einsum("ltd,de->lte", normed, w_in[1], preferred_element_type=F32)
    rim_rows = rim_rows.astype(F32) * carry_mask
    padded = jnp.concatenate([rim_rows, inner_act.astype(F32)], axis=1)
    conv_sum = conv_bias + conv_weight[0] * padded[:, 0:length]
    for tap in range(1, tap_count):
        conv_sum = conv_sum + conv_weight[tap] * padded[:, tap : tap + length]
    mixed = jax.nn.silu(conv_sum)
    mixed_low = mixed.astype(BF16)
    sent = jnp.einsum("lte,er->ltr", mixed_low, w_x, preferred_element_type=F32).astype(BF16)
    for bit in mp_bits[:-1]:
        sent = (sent.astype(F32) + swap(sent, "mp", bit).astype(F32)).astype(BF16)
    got = swap(sent, "mp", mp_bits[-1])
    grad_whole = jnp.concatenate(
        [
            sum(jnp.where(k == (mp_index ^ block), grad_parts[k], 0) for k in range(mp_size))
            for block in range(mp_size)
        ],
        axis=2,
    )
    grad_gated = jnp.einsum("ltd,ed->lte", grad_whole, w_out, preferred_element_type=F32)
    grad_scan = grad_gated * jax.nn.silu(gate_in)
    end_state, pulled, span, dt, source, slope_dt, projected = scan_ends(
        low_rank, sent, got, w_dt, dt_bias[None], decay_log, mixed, grad_scan
    )
    span = span + FAR * starts[:, :, None]
    to_later = (jnp.arange(seq_size) > seq_index)[:, None, None]
    flat = (1, lane_count * state_count, inner_width)
    edge = jnp.where(to_later, end_state.reshape(flat), (pulled * carry_mask).reshape(flat))
    spans = jnp.broadcast_to(
        span.reshape(1, lane_count, inner_width), (seq_size, lane_count, inner_width)
    )
    message = jnp.concatenate([edge, spans], axis=1).astype(BF16)
    message = jnp.pad(message, ((0, 0), (0, -message.shape[1] % 8), (0, 0)))
    groups = lax.all_to_all(message, "seq", 0, 0, tiled=True)
    place = jnp.concatenate([seq_index[None].astype(jnp.int32), row_starts[:, 0]])
    y, grad_read, last, states_all = scan_forward(
        low_rank, place, projected, decay_log, dt, source, grad_scan, groups
    )
    scan_out = y + skip_gain * mixed
    gated = (scan_out * jax.nn.silu(gate_in)).astype(BF16)
    grad_gate = (grad_gated * scan_out * silu_slope(gate_in)).astype(BF16)
    over = Reduction()
    half_width = model_width // 2
    first_sent = over.sent(normed, grad_gate)
    sum_first = Sum(over, jnp.concatenate([first_sent, over.sent(grad_whole, gated)], axis=0), 2)
    out_sent = jnp.einsum(
        "lte,ed->ltd", after(gated, sum_first.sent), w_spread[:, half_width:], preferred_element_type=F32
    ).astype(BF16)
    turn, pull, part, grad_log = scan_backward(
        low_rank, projected, decay_log, dt, source, grad_scan, last, grad_read, states_all,
        sum_first.sent, out_sent,
    )
    grad_slope = (turn + pull * mixed) * slope_dt
    grad_pre = grad_slope.astype(BF16)
    part = part + jnp.einsum("lte,re->ltr", grad_pre, w_dt, preferred_element_type=F32)
    sent = part.astype(BF16)
    for bit in mp_bits[:-1]:
        got = swap(sent, "mp", bit)
        if bit == 1:
            kept = over.kept(after(normed, sent), grad_gate)
            sent = after(sent, kept)
        sent = (sent.astype(F32) + got.astype(F32)).astype(BF16)
    got = swap(sent, "mp", mp_bits[-1])
    sum_first.kept = [kept, over.kept(after(grad_whole, sent), gated)]
    step = sum_first.next(sent)
    grad_dt_w = jnp.einsum(
        "ltr,lte->re", projected.astype(BF16), after(grad_pre, step), preferred_element_type=F32
    )[:low_rank]
    grad_projected = after(sent, grad_dt_w).astype(F32) + got.astype(F32)
    grad_projected = grad_projected.astype(BF16)
    grad_mixed = pull * dt + grad_scan * skip_gain + jnp.einsum(
        "ltr,er->lte", grad_projected, w_x, preferred_element_type=F32
    )
    grad_conv = grad_mixed * silu_slope(conv_sum)
    grad_conv_b = jnp.sum(grad_conv, axis=(0, 1))
    grad_conv_w = jnp.stack(
        [
            jnp.sum(grad_conv * padded[:, tap : tap + length], axis=(0, 1))
            for tap in range(tap_count)
        ]
    )
    grad_padded = jnp.pad(conv_weight[0] * grad_conv, ((0, 0), (0, tap_count - 1), (0, 0)))
    for tap in range(1, tap_count):
        grad_padded = grad_padded + jnp.pad(
            conv_weight[tap] * grad_conv, ((0, 0), (tap, tap_count - 1 - tap), (0, 0))
        )
    rim_sent = grad_padded[:, : tap_count - 1] * carry_mask
    rim_back = from_behind(rim_sent, "seq", -1)
    grad_x_w = jnp.einsum(
        "ltr,lte->re", grad_projected, after(mixed_low, rim_sent), preferred_element_type=F32
    )[: low_rank + 2 * state_count]
    step = grad_x_w
    tail_zeros = jnp.zeros((lane_count, length - (tap_count - 1), inner_width), F32)
    grad_inner = after(grad_padded, step)[:, tap_count - 1 :] + jnp.concatenate(
        [tail_zeros, rim_back], axis=1
    )
    grad_inner = grad_inner.astype(BF16)
    sum_inner = Sum(over, over.sent(normed, grad_inner), 1)
    sum_inner.kept = [over.kept(normed, after(grad_inner, sum_inner.sent))]
    step = sum_first.next(sum_inner.kept[0])

    def back(part, cut):
        return jnp.einsum("lte,de->ltd", part[0], w_back[0, cut], preferred_element_type=F32) + jnp.einsum(
            "lte,de->ltd", part[1], w_back[1, cut], preferred_element_type=F32
        )

    grads = (after(grad_inner, step), grad_gate)
    back_sent = back(grads, slice(half_width, None)).astype(BF16)
    back_kept = back((after(grad_inner, back_sent), grad_gate), slice(0, half_width))
    step = sum_inner.next(back_sent)
    row_dot = jnp.sum(
        after(grad_inner, step).astype(F32) * inner_act.astype(F32) + grad_gate.astype(F32) * gate_in,
        axis=2,
    )
    for bit in mp_bits:
        row_dot = row_dot + swap(row_dot, "mp", bit)
    for bit in mp_bits[:-1]:
        back_kept, back_sent = hop(back_kept, back_sent, "mp", bit)
    grad_own = back_kept + swap(back_sent, "mp", mp_bits[-1]).astype(F32)
    step = sum_first.next(back_sent)
    out_kept = jnp.einsum(
        "lte,ed->ltd", after(gated, step), w_spread[:, :half_width], preferred_element_type=F32
    )
    for bit in mp_bits[:-1]:
        out_kept, out_sent = hop(out_kept, out_sent, "mp", bit)
    output = inputs + (out_kept + swap(out_sent, "mp", mp_bits[-1]).astype(F32))
    step = sum_inner.next(out_sent)
    unit_own = inputs * inv_rms
    grad_gain = jnp.sum(grad_own * unit_own, axis=(0, 1))
    input_grad = output_grad + inv_rms * (
        grad_own * gain[:shard_width] - unit_own * (row_dot[:, :, None] / model_width)
    )
    gain_rows = jnp.pad(grad_gain, (0, -shard_width % inner_width)).reshape(-1, inner_width)
    small = jnp.concatenate(
        [
            grad_conv_w,
            grad_conv_b[None],
            jnp.sum(grad_slope, axis=(0, 1))[None],
            jnp.sum(grad_scan * mixed, axis=(0, 1))[None],
            jnp.sum(grad_log, axis=0),
            grad_dt_w,
            grad_x_w,
            gain_rows,
        ],
        axis=0,
    )
    small = jnp.pad(small, ((0, -small.shape[0] % 16), (0, 0)))
    step = sum_first.next(step)
    step = sum_inner.next(step)
    for bit in seq_bits:
        low = after(small, step).astype(BF16)
        small = low.astype(F32) + swap(low, "seq", bit).astype(F32)
        step = sum_first.next(step) if not sum_first.over_now() else step
        step = sum_inner.next(step) if not sum_inner.over_now() else step
    per = shard_width * seq_size // model_width
    blocks = seq_size // 2
    orders = jnp.concatenate([over.order(per, mp_index), over.order(1, 0)])
    second = 2 + blocks
    in_shape, out_shape = (2, model_width, inner_width), out_weight.shape
    early, late = sum_first.finish()
    layout = [(0, 1, 0, 0, blocks, False), (0, 1, 0, 1, blocks, False)]
    shapes, pieces = [in_shape], [early[0], late[0]]
    aligned = model_width // seq_size % LANE == 0
    if aligned:
        layout += [(1, None, second, 0, blocks, True), (1, None, second, 1, blocks, True)]
        shapes, pieces = [in_shape, out_shape], [*pieces, early[1], late[1]]
    in_w, *out_w = settle(orders, pieces, layout, shapes)
    if not aligned:
        source = orders[second + 2 :]
        halves = [p.reshape(blocks, -1, inner_width)[source].reshape(-1, inner_width) for p in (early[1], late[1])]
        up = over.own(0) == 1
        halves = [jnp.where(up, halves[1], halves[0]), jnp.where(up, halves[0], halves[1])]
        out_w = [jnp.concatenate(halves, axis=0).astype(F32).T]
    early, late = sum_inner.finish()
    (in_w,) = settle(orders, early, [(0, 0, 0, 0, blocks, False)], [in_shape], [in_w])
    (in_w,) = settle(orders, late, [(0, 0, 0, 1, blocks, False)], [in_shape], [in_w])
    (out_w,) = out_w
    sizes = [tap_count, 1, 1, 1, state_count, low_rank, low_rank + 2 * state_count, gain_rows.shape[0]]
    parts, at = [], 0
    for size in sizes:
        parts.append(small[at : at + size])
        at += size
    return (
        output,
        input_grad,
        parts[7].reshape(-1)[:shard_width],
        in_w,
        parts[0],
        parts[1][0],
        parts[6].T,
        parts[5],
        parts[2][0],
        parts[4],
        parts[3][0],
        out_w,
    )


def solution(mesh):
    in_specs = (
        P(None, "seq", "mp"),
        P(None, "seq"),
        P(),
        P(None, None, "mp"),
        P(None, "mp"),
        P("mp"),
        P("mp", None),
        P(None, "mp"),
        P("mp"),
        P(None, "mp"),
        P("mp"),
        P("mp", None),
        P(None, "seq", "mp"),
    )
    out_specs = (
        P(None, "seq", "mp"),
        P(None, "seq", "mp"),
        P("mp"),
        P(None, None, "mp"),
        P(None, "mp"),
        P("mp"),
        P("mp", None),
        P(None, "mp"),
        P("mp"),
        P(None, "mp"),
        P("mp"),
        P("mp", None),
    )
    return jax.shard_map(
        per_device, mesh=mesh, in_specs=in_specs, out_specs=out_specs, check_vma=False
    )
```

time: 303 us -> 207 us (0.68)
  starting transfers between devices: 68.5 us -> 39.2 us
  other arithmetic: 45.2 us -> 17.5 us
  waiting for transfers between devices: 95 us -> 71.1 us
  local copies, waits for them, and re-layouts: 35.2 us -> 24.3 us
    ppermute x52 -> x21, waiting for transfers between devices: 91.9 us -> 28.5 us  [swap(): return lax.ppermute(block, axis, [(i, i ^ bit) for i in range(devices)])]
    ppermute x52 -> x21, starting transfers between devices: 63 us -> 14.8 us  [swap(): return lax.ppermute(block, axis, [(i, i ^ bit) for i in range(devices)])]
    ppermute x0 -> x12, waiting for transfers between devices: none -> 33.2 us  [swap(): return lax.ppermute(block, ('seq', 'mp'), route)]
    convert_element_type x29 -> x16, other arithmetic: 18.3 us -> 3.83 us  [the longest x1 1.24 us: per_device(): normed = (x_whole.astype(F32) * inv_rms * gain).astype(BF16)]
    ppermute x0 -> x12, starting transfers between devices: none -> 13.5 us  [swap(): return lax.ppermute(block, ('seq', 'mp'), route)]
    unnamed x154 -> x171, local copies, waits for them, and re-layouts: 18.7 us -> 12.1 us
    add x13 -> x7, other arithmetic: 7.76 us -> 1.31 us  [the longest x1 0.88 us: next(): self.kept[k] = own[0].astype(F32) + other[0].astype(F32)]
    all_to_all x0 -> x1, starting transfers between devices: none -> 5.98 us  [per_device(): groups = lax.all_to_all(message, 'seq', 0, 0, tiled=True)]
  transfers between devices with their start and end apart: 54 -> 36, of which waited for: 23 -> 18; matrix products, arithmetic and copies ran while one was open for 20% -> 19% of each run, Pallas kernels for 3% -> 8%
where the time goes in v1:
time: 207 us; the launch traced here: 206 us
  waiting for transfers between devices  71.1 us (34%)
  starting transfers between devices  39.2 us (19%)
  Pallas kernels  36.7 us (18%)
  local copies, waits for them, and re-layouts  24.3 us (12%)
  other arithmetic  17.5 us (8%)
  matrix products  14.9 us (7%)
  between operations  2.28 us (1%)
    ppermute x12, waiting for transfers between devices, swap(): return lax.ppermute(block, ('seq', 'mp'), route)  33.2 us
    ppermute x21, waiting for transfers between devices, swap(): return lax.ppermute(block, axis, [(i, i ^ bit) for i in range(devices)])  28.5 us
    ppermute x21, starting transfers between devices, swap(): return lax.ppermute(block, axis, [(i, i ^ bit) for i in range(devices)])  14.8 us
    ppermute x12, starting transfers between devices, swap(): return lax.ppermute(block, ('seq', 'mp'), route)  13.5 us
    pallas_call x1, Pallas kernels, scan_backward(): pl.pallas_call(functools.partial(backward_kernel, low_rank), grid=(lanes,...  12.6 us
    unnamed x171, local copies, waits for them, and re-layouts  12.1 us
    pallas_call x1, Pallas kernels, scan_forward(): pl.pallas_call(functools.partial(forward_kernel, low_rank, lanes), grid=(...  9.76 us
    pallas_call x1, Pallas kernels, scan_ends(): pl.pallas_call(functools.partial(ends_kernel, low_rank), grid=(lanes,), i...  8.41 us
  transfers between devices with their start and end apart: 36, of which 18 were waited for; matrix products, arithmetic and copies ran while one was open for 19% of the time, Pallas kernels for 8%

profile of v1, /device:TPU:0, one launch (start us, length us, event | category | flops | bytes accessed | tf_op | source)
XLA Modules:
  0.0 205.9 jit_solution(13859679925726734602)
XLA Ops:
  1.8 3.0 %collective-permute-start.1 = (bf16[2,256,256]{1,2,0:T(8,128)(2,1)S(1)}, bf16[2,256,256]{1,2,0:T(8,128)(2,1)S(1)}, u32[]{:S(2)}, u32[]{:S(2)}) collective-permute-start(bf16[2,256,256]{1,2,0:T(8,128)(2,1)S(1)} %copy.43), channel_id=1, source_target_pairs={{0,2},{1,3},{2,0},{3,1},{4,6},{5,7},{6,4},{7,5},{8,10},{9,11},{10,... | collective-permute-start | bytes 786440 | tf_op jit(solution)/shard_map/ppermute | solution.py:21
  8.3 2.5 %dynamic-slice_convert_fusion.3 = (bf16[2,256,512]{2,1,0:T(8,128)(2,1)S(1)}, bf16[2,256,512]{2,1,0:T(8,128)(2,1)S(1)}, bf16[2,256,512]{2,1,0:T(8,128)(2,1)S(1)}, bf16[2,256,512]{2,1,0:T(8,128)(2,1)S(1)}) fusion(f32[2,1024,512]{2,1,0:T(8,128)} %param.16, s32[]{:T(128)S(6)} %select_n.219, s32[]{:T(128)S(6)} %select_n.220, s32[]{:T(128)S(6)} %select_n.222, ...), kind=kLoop, calls=%fused_computation.59 | loop fusion | bytes 4194320 | tf_op jit(solution)/shard_map/convert.12
  14.5 1.9 collective-permute-start.9
  18.5 3.4 %collective-permute-start.5 = (bf16[2,3,512]{2,1,0:T(4,128)(2,1)S(1)}, bf16[2,3,512]{2,1,0:T(4,128)(2,1)S(1)}, u32[]{:S(2)}, u32[]{:S(2)}) collective-permute-start(bf16[2,3,512]{2,1,0:T(4,128)(2,1)S(1)} %slice.192), channel_id=1, source_target_pairs={{0,4},{4,8},{8,12},{12,16},{16,20},{20,24},{24,28},{1,5},{5,9},{9,... | collective-permute-start | bytes 18440 | tf_op jit(solution)/shard_map/ppermute | solution.py:27
  26.0 3.1 %multiply_reduce_fusion = (f32[512]{0:T(512)}, f32[2,256,512]{2,1,0:T(8,128)S(1)}, f32[2,256,512]{2,1,0:T(8,128)S(1)}, f32[2,256,512]{2,1,0:T(8,128)}, f32[2,256,512]{2,1,0:T(8,128)}) fusion(f32[2,256,512]{2,1,0:T(8,128)S(1)} %fusion.6, f32[2,256,512]{2,1,0:T(8,128)S(1)} %get-tuple-element.168, f32[512]{0:T(512)S(1)} %bitcast.142, ...), kind=kOutput, calls=%fused_computation.36 | convolution fusion | flops 547356160 | bytes 9461760 | tf_op jit(solution)/shard_map/ltd,ed->lte/dot_general | solution.py:664
  31.5 1.8 collective-permute-start.7
  33.3 4.0 %collective-permute-done.7.got_ref = bf16[2,256,128]{2,1,0:T(8,128)(2,1)S(1)} collective-permute-done((bf16[2,256,128]{2,1,0:T(8,128)(2,1)S(1)}, bf16[2,256,128]{2,1,0:T(8,128)(2,1)S(1)}, u32[]{:S(2)}, u32[]{:S(2)}) %collective-permute-start.7) | collective-permute-done | bytes 131104 | tf_op jit(solution)/shard_map/ppermute | solution.py:21
  39.7 8.4 %scan_ends.1 = (f32[2,16,512]{2,1,0:T(8,128)S(1)}, f32[2,16,512]{2,1,0:T(8,128)S(1)}, f32[2,1,512]{2,1,0:T(1,128)S(1)}, f32[2,256,512]{2,1,0:T(8,128)S(1)}, f32[...) custom-call(bf16[2,256,128]{2,1,0:T(8,128)(2,1)S(1)} %add_convert_fusion.13.sent_ref, ...), custom_call_target="tpu_custom_call" | custom-call | flops 536870912 | bytes 8388608 | tf_op jit(solution)/shard_map/scan_ends/pallas_call | solution.py:343
  51.1 6.0 %all-to-all-start = ((bf16[8,40,512]{2,1,0:T(8,128)(2,1)}), bf16[8,40,512]{2,1,0:T(8,128)(2,1)}, u32[]{:S(2)}, u32[]{:S(2)}) async-start(bf16[8,40,512]{2,1,0:T(8,128)(2,1)} %fusion.42), calls=%async_computation | async-start | bytes 655360 | tf_op jit(solution)/shard_map/all_to_all | solution.py:678
  58.0 2.6 %dynamic-slice_convert_fusion.5 = (bf16[512,256]{1,0:T(8,128)(2,1)}, bf16[512,256]{1,0:T(8,128)(2,1)}, bf16[512,256]{1,0:T(8,128)(2,1)}, bf16[512,256]{1,0:T(8,128)(2,1)}) fusion(f32[512,1024]{1,0:T(8,128)} %param.24, s32[]{:T(128)S(6)} %select_n.219, s32[]{:T(128)S(6)} %select_n.222, s32[]{:T(128)S(6)} %select_n.220, s32[]{:T(128)S(6)} %select_n.221), kind=kLoop, calls=%fused_computation.98 | loop fusion | bytes 2097168 | tf_op jit(solution)/shard_map/convert.6
  61.7 5.6 %all-to-all-done.got_ref = bf16[8,40,512]{2,1,0:T(8,128)(2,1)} async-done(((bf16[8,40,512]{2,1,0:T(8,128)(2,1)}), bf16[8,40,512]{2,1,0:T(8,128)(2,1)}, u32[]{:S(2)}, u32[]{:S(2)}) %all-to-all-start) | async-done | bytes 327712 | tf_op jit(solution)/shard_map/all_to_all | solution.py:678
  68.5 9.8 %scan_forward.1 = (f32[2,256,512]{2,1,0:T(8,128)S(1)}, f32[2,256,128]{2,1,0:T(8,128)S(1)}, f32[2,16,512]{2,1,0:T(8,128)S(1)}, bf16[2,4112,512]{2,1,0:T(8,128)(2,1)S(1)}) custom-call(s32[3]{0:T(128)S(1)} %pad_add_fusion.1.place_ref, f32[2,256,128]{2,1,0:T(8,128)S(1)} %get-tuple-element.57.proj_ref, f32[16,512]{1,0:T(8,128)S(1)} %copy-done.8, ...), custom_call_target="tpu_custom_call" | custom-call | flops 536870912 | bytes 8388608 | tf_op jit(solution)/shard_map/scan_forward/pallas_call | solution.py:456
  82.5 12.6 %scan_backward.1 = (f32[2,256,512]{2,1,0:T(8,128)S(1)}, f32[2,256,512]{2,1,0:T(8,128)S(1)}, f32[2,256,128]{2,1,0:T(8,128)S(1)}, f32[2,16,512]{2,1,0:T(8,128)S(1)}) custom-call(f32[2,256,128]{2,1,0:T(8,128)S(1)} %get-tuple-element.57.proj_ref, f32[16,512]{1,0:T(8,128)S(1)} %copy-done.8, f32[2,256,512]{2,1,0:T(8,128)S(1)} %get-tuple-element.58.dt_ref, ...), custom_call_target="tpu_custom_call" | custom-call | flops 805306368 | bytes 8388608 | tf_op jit(solution)/shard_map/scan_backward/pallas_call | solution.py:567
  97.8 1.6 collective-permute-start.14
  101.0 2.4 %collective-permute-done.14 = bf16[2,256,128]{2,1,0:T(8,128)(2,1)S(1)} collective-permute-done((bf16[2,256,128]{2,1,0:T(8,128)(2,1)S(1)}, bf16[2,256,128]{2,1,0:T(8,128)(2,1)S(1)}, u32[]{:S(2)}, u32[]{:S(2)}) %collective-permute-start.14) | collective-permute-done | bytes 131104 | tf_op jit(solution)/shard_map/ppermute | solution.py:21
  106.7 3.8 %collective-permute-done.15 = f32[2,3,512]{2,1,0:T(4,128)S(1)} collective-permute-done((f32[2,3,512]{2,1,0:T(4,128)S(1)}, f32[2,3,512]{2,1,0:T(4,128)S(1)}, u32[]{:S(2)}, u32[]{:S(2)}) %collective-permute-start.15) | collective-permute-done | bytes 12320 | tf_op jit(solution)/shard_map/ppermute | solution.py:27
  111.1 1.6 collective-permute-start.21
  115.8 4.5 %collective-permute-done.21 = bf16[512,512]{1,0:T(8,128)(2,1)S(1)} collective-permute-done((bf16[512,512]{1,0:T(8,128)(2,1)S(1)}, bf16[512,512]{1,0:T(8,128)(2,1)S(1)}, u32[]{:S(2)}, u32[]{:S(2)}) %collective-permute-start.21) | collective-permute-done | bytes 524320 | tf_op jit(solution)/shard_map/ppermute | solution.py:69
  127.3 1.6 convert_add_fusion.1
  129.0 9.1 %collective-permute-done.16 = bf16[256,512]{1,0:T(8,128)(2,1)S(1)} collective-permute-done((bf16[256,512]{1,0:T(8,128)(2,1)}, bf16[256,512]{1,0:T(8,128)(2,1)S(1)}, u32[]{:S(2)}, u32[]{:S(2)}) %collective-permute-start.16) | collective-permute-done | bytes 262176 | tf_op jit(solution)/shard_map/ppermute | solution.py:69
  139.0 1.6 collective-permute-start.20
  140.6 1.6 convert_add_fusion
  142.8 2.9 %collective-permute-start.25 = (bf16[128,512]{1,0:T(8,128)(2,1)S(1)}, bf16[128,512]{1,0:T(8,128)(2,1)S(1)}, u32[]{:S(2)}, u32[]{:S(2)}) collective-permute-start(bf16[128,512]{1,0:T(8,128)(2,1)S(1)} %add_convert_fusion.5), channel_id=1, source_target_pairs={{0,16},{1,17},{2,18},{3,19},{4,20},{5,21},{6,22},{7,23},{8,24},{9,... | collective-permute-start | bytes 393224 | tf_op jit(solution)/shard_map/ppermute | solution.py:69
  145.7 9.7 %collective-permute-done.26 = bf16[256,512]{1,0:T(8,128)(2,1)S(1)} collective-permute-done((bf16[256,512]{1,0:T(8,128)(2,1)S(1)}, bf16[256,512]{1,0:T(8,128)(2,1)S(1)}, u32[]{:S(2)}, u32[]{:S(2)}) %collective-permute-start.26) | collective-permute-done | bytes 262176 | tf_op jit(solution)/shard_map/ppermute | solution.py:69
  160.7 2.5 %collective-permute-start.28 = (bf16[128,512]{1,0:T(8,128)(2,1)S(1)}, bf16[128,512]{1,0:T(8,128)(2,1)S(1)}, u32[]{:S(2)}, u32[]{:S(2)}) collective-permute-start(bf16[128,512]{1,0:T(8,128)(2,1)S(1)} %add_convert_fusion.4), channel_id=1, source_target_pairs={{0,16},{1,17},{2,18},{3,19},{4,20},{5,21},{6,22},{7,23},{8,24},{9,... | collective-permute-start | bytes 393224 | tf_op jit(solution)/shard_map/ppermute | solution.py:69
  163.2 4.9 %collective-permute-done.27 = bf16[192,512]{1,0:T(8,128)(2,1)S(1)} collective-permute-done((bf16[192,512]{1,0:T(8,128)(2,1)S(1)}, bf16[192,512]{1,0:T(8,128)(2,1)S(1)}, u32[]{:S(2)}, u32[]{:S(2)}) %collective-permute-start.27) | collective-permute-done | bytes 196640 | tf_op jit(solution)/shard_map/ppermute | solution.py:21
  172.1 2.0 collective-permute-start.31
  174.2 5.6 %collective-permute-done.30 = bf16[192,512]{1,0:T(8,128)(2,1)S(1)} collective-permute-done((bf16[192,512]{1,0:T(8,128)(2,1)S(1)}, bf16[192,512]{1,0:T(8,128)(2,1)S(1)}, u32[]{:S(2)}, u32[]{:S(2)}) %collective-permute-start.30) | collective-permute-done | bytes 196640 | tf_op jit(solution)/shard_map/ppermute | solution.py:21
  179.9 7.7 %collective-permute-done.31 = bf16[256,512]{1,0:T(8,128)(2,1)S(1)} collective-permute-done((bf16[256,512]{1,0:T(8,128)(2,1)S(1)}, bf16[256,512]{1,0:T(8,128)(2,1)S(1)}, u32[]{:S(2)}, u32[]{:S(2)}) %collective-permute-start.31) | collective-permute-done | bytes 262176 | tf_op jit(solution)/shard_map/ppermute | solution.py:69
  188.3 7.6 %collective-permute-done.32 = bf16[192,512]{1,0:T(8,128)(2,1)S(1)} collective-permute-done((bf16[192,512]{1,0:T(8,128)(2,1)S(1)}, bf16[192,512]{1,0:T(8,128)(2,1)S(1)}, u32[]{:S(2)}, u32[]{:S(2)}) %collective-permute-start.32) | collective-permute-done | bytes 196640 | tf_op jit(solution)/shard_map/ppermute | solution.py:21
  199.8 2.7 %settle.3 = (f32[2,1024,512]{2,1,0:T(8,128)}, f32[512,1024]{1,0:T(8,128)}) custom-call(s32[12]{0:T(128)S(1)} %concatenate.108.order_ref, bf16[512,512]{1,0:T(8,128)(2,1)S(1)} %pad_maximum_fusion.10.refs_0_, bf16[512,512]{1,0:T(8,128)(2,1)S(1)} %get-tuple-element.136.refs_1_, bf16[512,512]{1,0:T(8,128)(2,1)S(1)} %pad_maximum_fusion.11.refs_2_, ...), custom_call_target="tpu_custom_call" | custom-call | tf_op jit(solution)/shard_map/settle/pallas_call | solution.py:192
  204.2 1.6 settle.5
  (320 shorter events, 63.9 us)
Async XLA Ops:
  1.8 10.9 %collective-permute-start.1 = (bf16[2,256,256]{1,2,0:T(8,128)(2,1)S(1)}, bf16[2,256,256]{1,2,0:T(8,128)(2,1)S(1)}, u32[]{:S(2)}, u32[]{:S(2)}) collective-permute-start(bf16[2,256,256]{1,2,0:T(8,128)(2,1)S(1)} %copy.43), channel_id=1, source_target_pairs={{0,2},{1,3},{2,0},{3,1},{4,6},{5,7},{6,4},{7,5},{8,10},{9,11},{10,... | collective-permute-start | bytes 786440 | tf_op jit(solution)/shard_map/ppermute | solution.py:21
  4.9 11.6 %collective-permute-start = (bf16[2,256,256]{1,2,0:T(8,128)(2,1)S(1)}, bf16[2,256,256]{1,2,0:T(8,128)(2,1)S(1)}, u32[]{:S(2)}, u32[]{:S(2)}) collective-permute-start(bf16[2,256,256]{1,2,0:T(8,128)(2,1)S(1)} %copy.43), channel_id=1, source_target_pairs={{0,1},{1,0},{2,3},{3,2},{4,5},{5,4},{6,7},{7,6},{8,9},{9,8},{10,11... | collective-permute-start | bytes 786440 | tf_op jit(solution)/shard_map/ppermute | solution.py:21
  6.0 6.2 %collective-permute-start.3 = (f32[2,256]{1,0:T(2,128)S(1)}, f32[2,256]{1,0:T(2,128)S(1)}, u32[]{:S(2)}, u32[]{:S(2)}) collective-permute-start(f32[2,256]{1,0:T(2,128)S(1)} %multiply_reduce_fusion.6), channel_id=1, source_target_pairs={{0,2},{1,3},{2,0},{3,1},{4,6},{5,7},{6,4},{7,5},{8,10},{9,11},{10,... | collective-permute-start | bytes 6152 | tf_op jit(solution)/shard_map/ppermute | solution.py:21
  12.7 3.7 %collective-permute-start.2 = (bf16[2,256,256]{1,2,0:T(8,128)(2,1)S(1)}, bf16[2,256,256]{1,2,0:T(8,128)(2,1)}, u32[]{:S(2)}, u32[]{:S(2)}) collective-permute-start(bf16[2,256,256]{1,2,0:T(8,128)(2,1)S(1)} %collective-permute-done.1), channel_id=1, source_target_pairs={{0,1},{1,0},{2,3},{3,2},{4,5},{5,4},{6,7},{7,6},{8,9},{9,8},{10,11... | collective-permute-start | bytes 786440 | tf_op jit(solution)/shard_map/ppermute | solution.py:21
  14.5 8.7 %collective-permute-start.9 = (bf16[2,256,256]{2,1,0:T(8,128)(2,1)S(1)}, bf16[2,256,256]{2,1,0:T(8,128)(2,1)S(1)}, u32[]{:S(2)}, u32[]{:S(2)}) collective-permute-start(bf16[2,256,256]{2,1,0:T(8,128)(2,1)S(1)} %convert_element_type.302), channel_id=1, source_target_pairs={{0,2},{1,3},{2,0},{3,1},{4,6},{5,7},{6,4},{7,5},{8,10},{9,11},{10,... | collective-permute-start | bytes 786440 | tf_op jit(solution)/shard_map/ppermute | solution.py:21
  16.4 7.6 %collective-permute-start.8 = (bf16[2,256,256]{2,1,0:T(8,128)(2,1)S(1)}, bf16[2,256,256]{2,1,0:T(8,128)(2,1)S(1)}, u32[]{:S(2)}, u32[]{:S(2)}) collective-permute-start(bf16[2,256,256]{2,1,0:T(8,128)(2,1)S(1)} %convert_element_type.302), channel_id=1, source_target_pairs={{0,1},{1,0},{2,3},{3,2},{4,5},{5,4},{6,7},{7,6},{8,9},{9,8},{10,11... | collective-permute-start | bytes 786440 | tf_op jit(solution)/shard_map/ppermute | solution.py:21
  18.5 5.5 %collective-permute-start.5 = (bf16[2,3,512]{2,1,0:T(4,128)(2,1)S(1)}, bf16[2,3,512]{2,1,0:T(4,128)(2,1)S(1)}, u32[]{:S(2)}, u32[]{:S(2)}) collective-permute-start(bf16[2,3,512]{2,1,0:T(4,128)(2,1)S(1)} %slice.192), channel_id=1, source_target_pairs={{0,4},{4,8},{8,12},{12,16},{16,20},{20,24},{24,28},{1,5},{5,9},{9,... | collective-permute-start | bytes 18440 | tf_op jit(solution)/shard_map/ppermute | solution.py:27
  29.6 1.8 collective-permute-start.6
  31.5 5.8 %collective-permute-start.7 = (bf16[2,256,128]{2,1,0:T(8,128)(2,1)S(1)}, bf16[2,256,128]{2,1,0:T(8,128)(2,1)S(1)}, u32[]{:S(2)}, u32[]{:S(2)}) collective-permute-start(bf16[2,256,128]{2,1,0:T(8,128)(2,1)S(1)} %add_convert_fusion.13.sent_ref), channel_id=1, source_target_pairs={{0,2},{1,3},{2,0},{3,1},{4,6},{5,7},{6,4},{7,5},{8,10},{9,11},{10,... | collective-permute-start | bytes 393224 | tf_op jit(solution)/shard_map/ppermute | solution.py:21
  51.1 16.1 %all-to-all-start = ((bf16[8,40,512]{2,1,0:T(8,128)(2,1)}), bf16[8,40,512]{2,1,0:T(8,128)(2,1)}, u32[]{:S(2)}, u32[]{:S(2)}) async-start(bf16[8,40,512]{2,1,0:T(8,128)(2,1)} %fusion.42), calls=%async_computation | async-start | bytes 655360 | tf_op jit(solution)/shard_map/all_to_all | solution.py:678
  80.5 19.3 %collective-permute-start.11 = (bf16[1024,512]{1,0:T(8,128)(2,1)S(1)}, bf16[1024,512]{1,0:T(8,128)(2,1)S(1)}, u32[]{:S(2)}, u32[]{:S(2)}) collective-permute-start(bf16[1024,512]{1,0:T(8,128)(2,1)S(1)} %pad_maximum_fusion.3.refs_0_), channel_id=1, source_target_pairs={{0,4},{1,9},{2,6},{3,11},{4,0},{5,13},{6,2},{7,15},{8,12},{9,1},{1... | collective-permute-start | bytes 3145736 | tf_op jit(solution)/shard_map/ppermute | solution.py:69
  97.8 5.6 %collective-permute-start.14 = (bf16[2,256,128]{2,1,0:T(8,128)(2,1)S(1)}, bf16[2,256,128]{2,1,0:T(8,128)(2,1)S(1)}, u32[]{:S(2)}, u32[]{:S(2)}) collective-permute-start(bf16[2,256,128]{2,1,0:T(8,128)(2,1)S(1)} %add_convert_fusion.11), channel_id=1, source_target_pairs={{0,2},{1,3},{2,0},{3,1},{4,6},{5,7},{6,4},{7,5},{8,10},{9,11},{10,... | collective-permute-start | bytes 393224 | tf_op jit(solution)/shard_map/ppermute | solution.py:21
  100.5 12.6 %collective-permute-start.13 = (bf16[512,512]{1,0:T(8,128)(2,1)S(1)}, bf16[512,512]{1,0:T(8,128)(2,1)S(1)}, u32[]{:S(2)}, u32[]{:S(2)}) collective-permute-start(bf16[512,512]{1,0:T(8,128)(2,1)S(1)} %pad_maximum_fusion.6), channel_id=1, source_target_pairs={{0,8},{1,5},{2,10},{3,7},{4,12},{5,1},{6,14},{7,3},{8,0},{9,13},{1... | collective-permute-start | bytes 1572872 | tf_op jit(solution)/shard_map/ppermute | solution.py:69
  104.9 5.6 %collective-permute-start.15 = (f32[2,3,512]{2,1,0:T(4,128)S(1)}, f32[2,3,512]{2,1,0:T(4,128)S(1)}, u32[]{:S(2)}, u32[]{:S(2)}) collective-permute-start(f32[2,3,512]{2,1,0:T(4,128)S(1)} %slice_multiply_fusion), channel_id=1, source_target_pairs={{4,0},{8,4},{12,8},{16,12},{20,16},{24,20},{28,24},{5,1},{9,5},{13... | collective-permute-start | bytes 36872 | tf_op jit(solution)/shard_map/ppermute | solution.py:27
  111.1 9.2 %collective-permute-start.21 = (bf16[512,512]{1,0:T(8,128)(2,1)S(1)}, bf16[512,512]{1,0:T(8,128)(2,1)S(1)}, u32[]{:S(2)}, u32[]{:S(2)}) collective-permute-start(bf16[512,512]{1,0:T(8,128)(2,1)S(1)} %fusion.2), channel_id=1, source_target_pairs={{0,4},{1,9},{2,6},{3,11},{4,0},{5,13},{6,2},{7,15},{8,12},{9,1},{1... | collective-permute-start | bytes 1572872 | tf_op jit(solution)/shard_map/ppermute | solution.py:69
  115.8 11.5 %collective-permute-start.17 = (bf16[2,256,512]{2,1,0:T(8,128)(2,1)}, bf16[2,256,512]{2,1,0:T(8,128)(2,1)}, u32[]{:S(2)}, u32[]{:S(2)}) collective-permute-start(bf16[2,256,512]{2,1,0:T(8,128)(2,1)} %fusion.3), channel_id=1, source_target_pairs={{0,1},{1,0},{2,3},{3,2},{4,5},{5,4},{6,7},{7,6},{8,9},{9,8},{10,11... | collective-permute-start | bytes 1572872 | tf_op jit(solution)/shard_map/ppermute | solution.py:21
  122.6 18.0 %collective-permute-start.18 = (bf16[2,256,512]{2,1,0:T(8,128)(2,1)S(1)}, bf16[2,256,512]{2,1,0:T(8,128)(2,1)}, u32[]{:S(2)}, u32[]{:S(2)}) collective-permute-start(bf16[2,256,512]{2,1,0:T(8,128)(2,1)S(1)} %copy-done.6), channel_id=1, source_target_pairs={{0,1},{1,0},{2,3},{3,2},{4,5},{5,4},{6,7},{7,6},{8,9},{9,8},{10,11... | collective-permute-start | bytes 1572872 | tf_op jit(solution)/shard_map/ppermute | solution.py:21
  123.1 15.0 %collective-permute-start.16 = (bf16[256,512]{1,0:T(8,128)(2,1)}, bf16[256,512]{1,0:T(8,128)(2,1)S(1)}, u32[]{:S(2)}, u32[]{:S(2)}) collective-permute-start(bf16[256,512]{1,0:T(8,128)(2,1)} %pad_maximum_fusion.12), channel_id=1, source_target_pairs={{0,16},{1,17},{2,18},{3,19},{4,20},{5,21},{6,22},{7,23},{8,24},{9,... | collective-permute-start | bytes 786440 | tf_op jit(solution)/shard_map/ppermute | solution.py:69
  123.7 3.6 %collective-permute-start.23 = (f32[2,256]{1,0:T(2,128)S(1)}, f32[2,256]{1,0:T(2,128)S(1)}, u32[]{:S(2)}, u32[]{:S(2)}) collective-permute-start(f32[2,256]{1,0:T(2,128)S(1)} %add.383), channel_id=1, source_target_pairs={{0,2},{1,3},{2,0},{3,1},{4,6},{5,7},{6,4},{7,5},{8,10},{9,11},{10,... | collective-permute-start | bytes 6152 | tf_op jit(solution)/shard_map/ppermute | solution.py:21
  125.7 17.1 %collective-permute-start.24 = (bf16[256,512]{1,0:T(8,128)(2,1)S(1)}, bf16[256,512]{1,0:T(8,128)(2,1)S(1)}, u32[]{:S(2)}, u32[]{:S(2)}) collective-permute-start(bf16[256,512]{1,0:T(8,128)(2,1)S(1)} %copy-done.63), channel_id=1, source_target_pairs={{0,8},{1,5},{2,10},{3,7},{4,12},{5,1},{6,14},{7,3},{8,0},{9,13},{1... | collective-permute-start | bytes 786440 | tf_op jit(solution)/shard_map/ppermute | solution.py:69
  138.9 16.6 %collective-permute-start.26 = (bf16[256,512]{1,0:T(8,128)(2,1)S(1)}, bf16[256,512]{1,0:T(8,128)(2,1)S(1)}, u32[]{:S(2)}, u32[]{:S(2)}) collective-permute-start(bf16[256,512]{1,0:T(8,128)(2,1)S(1)} %pad_maximum_fusion.13), channel_id=1, source_target_pairs={{0,16},{1,17},{2,18},{3,19},{4,20},{5,21},{6,22},{7,23},{8,24},{9,... | collective-permute-start | bytes 786440 | tf_op jit(solution)/shard_map/ppermute | solution.py:69
  139.0 19.2 %collective-permute-start.20 = (bf16[2,256,256]{2,1,0:T(8,128)(2,1)S(1)}, bf16[2,256,256]{2,1,0:T(8,128)(2,1)S(1)}, u32[]{:S(2)}, u32[]{:S(2)}) collective-permute-start(bf16[2,256,256]{2,1,0:T(8,128)(2,1)S(1)} %slice.287), channel_id=1, source_target_pairs={{0,2},{1,3},{2,0},{3,1},{4,6},{5,7},{6,4},{7,5},{8,10},{9,11},{10,... | collective-permute-start | bytes 786440 | tf_op jit(solution)/shard_map/ppermute | solution.py:21
  142.2 16.0 %collective-permute-start.19 = (bf16[2,256,256]{2,1,0:T(8,128)(2,1)S(1)}, bf16[2,256,256]{2,1,0:T(8,128)(2,1)S(1)}, u32[]{:S(2)}, u32[]{:S(2)}) collective-permute-start(bf16[2,256,256]{2,1,0:T(8,128)(2,1)S(1)} %slice.286), channel_id=1, source_target_pairs={{0,2},{1,3},{2,0},{3,1},{4,6},{5,7},{6,4},{7,5},{8,10},{9,11},{10,... | collective-permute-start | bytes 786440 | tf_op jit(solution)/shard_map/ppermute | solution.py:21
  142.8 15.4 %collective-permute-start.25 = (bf16[128,512]{1,0:T(8,128)(2,1)S(1)}, bf16[128,512]{1,0:T(8,128)(2,1)S(1)}, u32[]{:S(2)}, u32[]{:S(2)}) collective-permute-start(bf16[128,512]{1,0:T(8,128)(2,1)S(1)} %add_convert_fusion.5), channel_id=1, source_target_pairs={{0,16},{1,17},{2,18},{3,19},{4,20},{5,21},{6,22},{7,23},{8,24},{9,... | collective-permute-start | bytes 393224 | tf_op jit(solution)/shard_map/ppermute | solution.py:69
  157.0 12.2 %collective-permute-start.29 = (bf16[512,512]{1,0:T(8,128)(2,1)}, bf16[512,512]{1,0:T(8,128)(2,1)S(1)}, u32[]{:S(2)}, u32[]{:S(2)}) collective-permute-start(bf16[512,512]{1,0:T(8,128)(2,1)} %pad_maximum_fusion.7), channel_id=1, source_target_pairs={{0,8},{1,5},{2,10},{3,7},{4,12},{5,1},{6,14},{7,3},{8,0},{9,13},{1... | collective-permute-start | bytes 1572872 | tf_op jit(solution)/shard_map/ppermute | solution.py:69
  160.2 7.9 %collective-permute-start.27 = (bf16[192,512]{1,0:T(8,128)(2,1)S(1)}, bf16[192,512]{1,0:T(8,128)(2,1)S(1)}, u32[]{:S(2)}, u32[]{:S(2)}) collective-permute-start(bf16[192,512]{1,0:T(8,128)(2,1)S(1)} %pad.45), channel_id=1, source_target_pairs={{0,4},{4,0},{8,12},{12,8},{16,20},{20,16},{24,28},{28,24},{1,5},{5... | collective-permute-start | bytes 589832 | tf_op jit(solution)/shard_map/ppermute | solution.py:21
  160.7 11.3 %collective-permute-start.28 = (bf16[128,512]{1,0:T(8,128)(2,1)S(1)}, bf16[128,512]{1,0:T(8,128)(2,1)S(1)}, u32[]{:S(2)}, u32[]{:S(2)}) collective-permute-start(bf16[128,512]{1,0:T(8,128)(2,1)S(1)} %add_convert_fusion.4), channel_id=1, source_target_pairs={{0,16},{1,17},{2,18},{3,19},{4,20},{5,21},{6,22},{7,23},{8,24},{9,... | collective-permute-start | bytes 393224 | tf_op jit(solution)/shard_map/ppermute | solution.py:69
  172.0 7.8 %collective-permute-start.30 = (bf16[192,512]{1,0:T(8,128)(2,1)S(1)}, bf16[192,512]{1,0:T(8,128)(2,1)S(1)}, u32[]{:S(2)}, u32[]{:S(2)}) collective-permute-start(bf16[192,512]{1,0:T(8,128)(2,1)S(1)} %convert_add_fusion.7), channel_id=1, source_target_pairs={{0,8},{4,12},{8,0},{12,4},{16,24},{20,28},{24,16},{28,20},{1,9},{5... | collective-permute-start | bytes 589832 | tf_op jit(solution)/shard_map/ppermute | solution.py:21
  172.1 15.4 %collective-permute-start.31 = (bf16[256,512]{1,0:T(8,128)(2,1)S(1)}, bf16[256,512]{1,0:T(8,128)(2,1)S(1)}, u32[]{:S(2)}, u32[]{:S(2)}) collective-permute-start(bf16[256,512]{1,0:T(8,128)(2,1)S(1)} %pad_maximum_fusion.14), channel_id=1, source_target_pairs={{0,8},{1,5},{2,10},{3,7},{4,12},{5,1},{6,14},{7,3},{8,0},{9,13},{1... | collective-permute-start | bytes 786440 | tf_op jit(solution)/shard_map/ppermute | solution.py:69
  174.2 25.6 %collective-permute-start.34 = (bf16[1024,512]{1,0:T(8,128)(2,1)}, bf16[1024,512]{1,0:T(8,128)(2,1)S(1)}, u32[]{:S(2)}, u32[]{:S(2)}) collective-permute-start(bf16[1024,512]{1,0:T(8,128)(2,1)} %constant_dynamic-update-slice_fusion), channel_id=1, source_target_pairs={{0,4},{1,9},{2,6},{3,11},{4,0},{5,13},{6,2},{7,15},{8,12},{9,1},{1... | collective-permute-start | bytes 3145736 | tf_op jit(solution)/shard_map/ppermute | solution.py:69
  187.6 8.4 %collective-permute-start.32 = (bf16[192,512]{1,0:T(8,128)(2,1)S(1)}, bf16[192,512]{1,0:T(8,128)(2,1)S(1)}, u32[]{:S(2)}, u32[]{:S(2)}) collective-permute-start(bf16[192,512]{1,0:T(8,128)(2,1)S(1)} %convert_add_fusion.6), channel_id=1, source_target_pairs={{0,16},{4,20},{8,24},{12,28},{16,0},{20,4},{24,8},{28,12},{1,17},{... | collective-permute-start | bytes 589832 | tf_op jit(solution)/shard_map/ppermute | solution.py:21
  187.8 16.4 %collective-permute-start.33 = (bf16[512,512]{1,0:T(8,128)(2,1)S(1)}, bf16[512,512]{1,0:T(8,128)(2,1)S(1)}, u32[]{:S(2)}, u32[]{:S(2)}) collective-permute-start(bf16[512,512]{1,0:T(8,128)(2,1)S(1)} %pad_maximum_fusion.9.refs_0_), channel_id=1, source_target_pairs={{0,4},{1,9},{2,6},{3,11},{4,0},{5,13},{6,2},{7,15},{8,12},{9,1},{1... | collective-permute-start | bytes 1572872 | tf_op jit(solution)/shard_map/ppermute | solution.py:69
  (89 other events, 551.6 us)

commit v2 on v1

--- a/solution.py
+++ b/solution.py
@@ -11,6 +11,7 @@
 BF16 = jnp.bfloat16
 LOG2E = 1.4426950408889634
 CHUNK = 32
+ROUND = 4
 LANE = 128
 FAR = 1.0e4
 VMEM = pl.BlockSpec(memory_space=pltpu.VMEM)
@@ -37,12 +38,6 @@
 
 def after(array, *others):
     return lax.optimization_barrier((array, *others))[0]
-
-
-def hop(kept, sent, axis, bit):
-    total = kept.astype(F32) + swap(sent, axis, bit).astype(F32)
-    half = total.shape[-1] // 2
-    return total[..., :half], total[..., half:].astype(BF16)
 
 
 class Reduction:
@@ -101,51 +96,115 @@
         up = self.own(0) ^ high
         return jnp.concatenate([jnp.stack([up * blocks, (1 - up) * blocks]), source]).astype(jnp.int32)
 
+    def flat_order(self):
+        blocks = self.count // 2
+        place = jnp.int32(0)
+        for step in range(len(self.bits) - 1):
+            place = place * 2 + self.own(step)
+        return (jnp.arange(blocks) ^ place).astype(jnp.int32)
+
+
+def advance_kernel(plan, flag_ref, *refs):
+    refs = list(refs)
+    sent_ref, got_ref = refs.pop(0), refs.pop(0)
+    inputs, outputs = refs[: plan["inputs"]], refs[plan["inputs"] :]
+    message = outputs.pop(0)
+    up = flag_ref[0]
+    at = 0
+    for mode, rows, first in plan["blocks"]:
+        if mode == "half":
+            kept, new = inputs.pop(0), outputs.pop(0)
+            half = rows // 2
+            own = pl.multiple_of(up * half, half)
+            other = pl.multiple_of((1 - up) * half, half)
+            new[...] = kept[pl.ds(own, half), :].astype(F32) + got_ref[pl.ds(first + own, half), :].astype(F32)
+            send = kept[pl.ds(other, half), :].astype(F32) + got_ref[pl.ds(first + other, half), :].astype(F32)
+            message[at : at + half, :] = send.astype(BF16)
+            at += half
+        elif mode in ("flat", "sum", "hold"):
+            kept = inputs.pop(0)
+            total = (kept[...].astype(F32) + got_ref[first : first + rows, :].astype(F32)).astype(BF16)
+            if mode != "sum":
+                outputs.pop(0)[...] = total
+            if mode != "hold":
+                message[at : at + rows, :] = total
+                at += rows
+        elif mode == "enter":
+            message[at : at + rows, :] = inputs.pop(0)[...].astype(BF16)
+            at += rows
+        elif mode == "grow":
+            message[at : at + rows, :] = sent_ref[first : first + rows, :]
+            message[at + rows : at + 2 * rows, :] = got_ref[first : first + rows, :]
+            at += 2 * rows
+        else:
+            total = sent_ref[first : first + rows, :].astype(F32) + got_ref[first : first + rows, :].astype(F32)
+            message[at : at + rows, :] = total.astype(BF16)
+            at += rows
+
+
+def advance(flag, sent, got, blocks, inputs):
+    width = sent.shape[1]
+    grown = {"half": 0.5, "hold": 0, "grow": 2}
+    total = int(sum(rows * grown.get(mode, 1) for mode, rows, _ in blocks))
+    shapes = [jax.ShapeDtypeStruct((total, width), BF16)]
+    for mode, rows, _ in blocks:
+        if mode == "half":
+            shapes.append(jax.ShapeDtypeStruct((rows // 2, width), F32))
+        elif mode in ("flat", "hold"):
+            shapes.append(jax.ShapeDtypeStruct((rows, width), BF16))
+    return pl.pallas_call(
+        functools.partial(advance_kernel, {"inputs": len(inputs), "blocks": blocks}),
+        in_specs=[pl.BlockSpec(memory_space=pltpu.SMEM)] + [VMEM] * (2 + len(inputs)),
+        out_specs=[VMEM] * len(shapes),
+        out_shape=shapes,
+        compiler_params=pltpu.CompilerParams(vmem_limit_bytes=12 << 20),
+        name="advance",
+    )(flag, sent, got, *inputs)
+
 
 class Sum:
-    def __init__(self, over, sent, count):
-        self.over, self.count, self.kept = over, count, None
-        self.step, self.down = 0, False
-        self.sent = sent
-        self.got = over.swap(sent, 0)
-
-    def split(self, block):
-        rows = block.shape[0] // self.count
-        return [block[k * rows : (k + 1) * rows] for k in range(self.count)]
-
-    def over_now(self):
-        return self.down and self.step == 0
+    def __init__(self, over, sent, flat, flags):
+        self.over, self.flat, self.flags = over, flat, flags
+        self.kept, self.rider, self.count = None, None, 0
+        self.rows = [block.shape[0] for block in sent]
+        self.message = jnp.concatenate([block.astype(BF16) for block in sent], axis=0)
+        self.got = over.swap(self.message, 0)
 
     def next(self, *earlier):
-        over, steps = self.over, len(self.over.bits)
-        if earlier:
-            self.got = after(self.got, *earlier)
-        got = self.split(self.got)
-        if not self.down:
-            self.step += 1
-            if self.step < steps:
-                sent = []
-                for k in range(self.count):
-                    own, other = over.halves(self.kept[k], self.step), over.halves(got[k], self.step)
-                    self.kept[k] = own[0].astype(F32) + other[0].astype(F32)
-                    sent.append((own[1].astype(F32) + other[1].astype(F32)).astype(BF16))
-                self.sent = jnp.concatenate(sent, axis=0)
-            else:
-                self.down = True
-                self.whole = [(a.astype(F32) + b.astype(F32)).astype(BF16) for a, b in zip(self.kept, got, strict=True)]
-                self.step -= 1
-        else:
-            self.whole = [jnp.concatenate(pair, axis=0) for pair in zip(self.whole, got, strict=True)]
-            self.step -= 1
-        if self.down:
-            self.sent = jnp.concatenate(self.whole, axis=0)
-        self.got = over.swap(self.sent, self.step)
-        return self.sent
-
-    def finish(self):
-        while not self.over_now():
+        steps = len(self.over.bits)
+        k = self.count
+        got = after(self.got, *earlier) if earlier else self.got
+        blocks, inputs, rows, kept, first = [], [], [], [], 0
+        for m, size in enumerate(self.rows):
+            mode = "half" if k < steps - 1 else "sum" if k == steps - 1 else "grow"
+            if self.flat[m]:
+                mode = {steps - 2: "flat", steps - 1: "hold", steps: "enter"}.get(k, mode)
+            if mode == "enter":
+                size = self.kept[m].shape[0]
+            blocks.append((mode, size, first))
+            if mode != "grow":
+                inputs.append(self.kept[m])
+            first += 0 if mode == "enter" else size
+            rows.append({"half": size // 2, "hold": 0, "grow": 2 * size}.get(mode, size))
+        if self.rider is not None and k == steps - 1:
+            blocks.append(("enter", self.rider.shape[0], 0))
+            inputs.append(self.rider)
+        elif self.rider is not None and k >= steps:
+            blocks.append(("ride", self.rider.shape[0], first))
+        flag = self.flags[min(k + 1, steps - 1)]
+        self.message, *kept = advance(flag, self.message, got, blocks, inputs)
+        for m, (mode, _, _) in enumerate(blocks[: len(rows)]):
+            if mode in ("half", "flat", "hold"):
+                self.kept[m] = kept.pop(0)
+        self.rows = rows
+        self.count = k + 1
+        step = self.count if self.count < steps else 2 * steps - 1 - self.count
+        self.got = self.over.swap(self.message, step)
+        return self.message
+
+    def run_out(self):
+        while self.count < 2 * len(self.over.bits) - 1:
             self.next()
-        return self.whole, self.split(self.got)
 
 
 def silu_slope(values):
@@ -162,11 +221,11 @@
     parts, outs = refs[: len(layout)], refs[-2 - names : -2]
     wide, sems = refs[-2:]
     copies, at = [], 0
-    for part, (out, lead, which, first, blocks, turned) in zip(parts, layout, strict=True):
-        size = part.shape[0] // blocks
+    for part, (out, lead, which, first, blocks, turned, offset, count) in zip(parts, layout, strict=True):
+        size = count // blocks
         for b in range(blocks):
             source = order_ref[which + 2 + b]
-            rows = part[pl.ds(pl.multiple_of(source * size, size), size), :].astype(F32)
+            rows = part[pl.ds(pl.multiple_of(offset + source * size, size), size), :].astype(F32)
             goal = pl.multiple_of((order_ref[which + first] + b) * size, size)
             ref = outs[out] if lead is None else outs[out].at[lead]
             if turned:
@@ -186,8 +245,8 @@
 
 def settle(orders, parts, layout, shapes, into=()):
     any_space = pl.BlockSpec(memory_space=pl.ANY)
-    rows = sum(p.shape[1] * l[4] if l[5] else p.shape[0] for p, l in zip(parts, layout, strict=True))
-    width = max(p.shape[0] // l[4] if l[5] else p.shape[1] for p, l in zip(parts, layout, strict=True))
+    rows = sum(p.shape[1] * l[4] if l[5] else l[7] for p, l in zip(parts, layout, strict=True))
+    width = max(l[7] // l[4] if l[5] else p.shape[1] for p, l in zip(parts, layout, strict=True))
     count = sum(l[4] for l in layout)
     return pl.pallas_call(
         functools.partial(settle_kernel, len(shapes), layout),
@@ -199,6 +258,77 @@
         compiler_params=pltpu.CompilerParams(vmem_limit_bytes=16 << 20),
         name="settle",
     )(orders, *parts, *into)
+
+
+def deal_kernel(sizes, offset, order_ref, own_ref, late_ref, *refs):
+    outs, rows = refs[:-1], refs[-1]
+    blocks = order_ref.shape[0]
+    size = rows.shape[0] // blocks
+    for b in range(blocks):
+        source = order_ref[b]
+        for part, first in ((own_ref, 0), (late_ref, blocks // 2)):
+
+            @pl.when(jnp.logical_and(source >= first, source < first + blocks // 2))
+            def _():
+                at = pl.ds(pl.multiple_of(offset + (source - first) * size, size), size)
+                rows[b * size : (b + 1) * size, :] = part[at, :].astype(F32)
+
+    at = 0
+    for out, count in zip(outs, sizes, strict=True):
+        out[...] = rows[at : at + count, :]
+        at += count
+
+
+def deal(order, own, late, offset, count, sizes):
+    width = own.shape[1]
+    return pl.pallas_call(
+        functools.partial(deal_kernel, sizes, offset),
+        in_specs=[pl.BlockSpec(memory_space=pltpu.SMEM), VMEM, VMEM],
+        out_shape=[jax.ShapeDtypeStruct((count, width), F32) for count in sizes],
+        scratch_shapes=[pltpu.VMEM((2 * count, width), F32)],
+        compiler_params=pltpu.CompilerParams(vmem_limit_bytes=8 << 20),
+        name="deal",
+    )(order, own, late)
+
+
+def hop_kernel(got_ref, *refs):
+    kept, (row_ref, message), outs = refs[:2], refs[2:4], refs[4:]
+    lanes, length, width = kept[0].shape
+    half = width // 2
+    for l in range(lanes):
+        for m in range(2):
+            o = slice(m * length, (m + 1) * length)
+            outs[m][l] = kept[m][l, :, :half] + got_ref[l, o, :half].astype(F32)
+            send = kept[m][l, :, half:] + got_ref[l, o, half:].astype(F32)
+            message[l, o, :] = send.astype(BF16)
+        rows = got_ref[l, 2 * length :, :].astype(F32)
+        came = jnp.concatenate([rows[r : r + 1] for r in range(2 * length // width)], axis=1)
+        total = row_ref[l : l + 1, :] + came[:, :length] + came[:, length:]
+        outs[2][l : l + 1, :] = total
+        high = total.astype(BF16).astype(F32)
+        both = jnp.concatenate([high, total - high], axis=1)
+        pieces = [both[:, at : at + half] for at in range(0, 2 * length, half)]
+        pieces.append(jnp.zeros((message.shape[1] - 2 * length - len(pieces), half), F32))
+        message[l, 2 * length :, :] = jnp.concatenate(pieces, axis=0).astype(BF16)
+
+
+def hop(got, out_kept, back_kept, row_dot):
+    lanes, length, width = out_kept.shape
+    shape = jax.ShapeDtypeStruct
+    half = shape((lanes, length, width // 2), F32)
+    rows = 2 * length - (-(4 * length // width) // 16) * 16
+    return pl.pallas_call(
+        hop_kernel_entry,
+        in_specs=[VMEM] * 4,
+        out_specs=[VMEM] * 4,
+        out_shape=[shape((lanes, rows, width // 2), BF16), half, half, shape(row_dot.shape, F32)],
+        compiler_params=pltpu.CompilerParams(vmem_limit_bytes=12 << 20),
+        name="hop",
+    )(got, out_kept, back_kept, row_dot)
+
+
+def hop_kernel_entry(got_ref, out_ref, back_ref, row_ref, message, *outs):
+    hop_kernel(got_ref, out_ref, back_ref, row_ref, message, *outs)
 
 
 def iota(shape, dim):
@@ -312,14 +442,16 @@
             y[s, :] = (to_here * row_of(gy_ref, t, states)).astype(BF16)
 
     def body(k, sums):
-        sums = flush(2 * k - 1, xb, yb, sums)
-        fill(2 * k, xa, ya)
-        sums = flush(2 * k, xa, ya, sums)
-        fill(2 * k + 1, xb, yb)
+        for i in range(0, ROUND, 2):
+            at = ROUND * k + i
+            sums = flush(at - 1, xb, yb, sums)
+            fill(at, xa, ya)
+            sums = flush(at, xa, ya, sums)
+            fill(at + 1, xb, yb)
         return sums
 
     zero = jnp.zeros((states, width), F32)
-    sums = lax.fori_loop(0, chunks // 2, body, (zero, zero))
+    sums = lax.fori_loop(0, chunks // ROUND, body, (zero, zero))
     sums = flush(chunks - 1, xb, yb, sums)
     end_ref[...] = sums[0]
     pull_ref[...] = sums[1]
@@ -353,11 +485,13 @@
             tokens,
         ],
         out_specs=[state_spec, state_spec, lane_spec(1, width), tokens, tokens, tokens, narrow],
-        out_shape=[state, state, shape((lanes, 1, width), F32), token, token, token, shape(sent.shape, F32)],
+        out_shape=[state, state, shape((lanes, 1, width), F32)]
+        + [pltpu.HBM((lanes, length, width), F32)] * 3
+        + [shape(sent.shape, F32)],
         scratch_shapes=[pltpu.VMEM((length, width), F32)] * 2
         + [pltpu.VMEM((length // CHUNK * states, CHUNK * states), BF16)] * 2
         + [pltpu.VMEM((CHUNK * states, width), BF16)] * 4,
-        compiler_params=pltpu.CompilerParams(vmem_limit_bytes=24 << 20),
+        compiler_params=pltpu.CompilerParams(vmem_limit_bytes=14 << 20),
         cost_estimate=cost(8, lanes, length, width, states),
         name="scan_ends",
     )(sent, got, w_dt, bias, log, mixed, gy)
@@ -366,7 +500,7 @@
 def forward_kernel(
     low_rank, lanes, place_ref, proj_ref, log_ref, dt_ref, u_ref, gy_ref, got_ref,
     y_ref, gc_ref, last_ref, hs_ref,
-    pa, pb, p0, cols, left_c, masked, sems,
+    kept, pa, pb, cols, left_c, masked, sems,
 ):
     length, width = dt_ref.shape
     states = log_ref.shape[0]
@@ -378,9 +512,11 @@
     groups = got_ref.shape[0]
     place = place_ref[0]
 
-    def leave(i, p, at):
-        rows = pl.ds(pl.multiple_of((i * CHUNK + 1) * states, states), wide)
-        return pltpu.make_async_copy(p, hs_ref.at[l, rows, :], sems.at[at])
+    half = chunks // 2 * wide
+
+    def leave(slot, part):
+        rows = pl.ds(part * half, half)
+        return pltpu.make_async_copy(kept.at[slot, rows, :], hs_ref.at[slot, rows, :], sems.at[slot, part])
 
     zero = jnp.zeros((states, width), F32)
 
@@ -398,9 +534,6 @@
         last = join(h, last, h > place)
     last_ref[...] = last
     begin = jnp.where(place_ref[1 + l] != 0, 0.0, begin)
-    p0[...] = begin.astype(BF16)
-    first = pltpu.make_async_copy(p0, hs_ref.at[l, pl.ds(0, states), :], sems.at[2])
-    first.start()
     proj = proj_ref[...]
     cols[...] = jnp.transpose(proj)[low_rank : low_rank + states]
     spread = by_step(proj.astype(BF16), from_lanes(low_rank + states, states), per_step)
@@ -414,38 +547,39 @@
 
     def fill(i, state, p):
         b_tile = chunk_columns(cols, i)
+        low = state.astype(BF16)
         for j in range(CHUNK):
             t = i * CHUNK + j
             b = spread_column(b_tile, j, width)
             decay = jnp.exp2(row_of(dt_ref, t, states) * rate)
             state = decay * state + row_of(u_ref, t, states) * b
-            p[j * states : (j + 1) * states, :] = state.astype(BF16)
+            kept[l, rows_of(t, states), :] = low
+            low = state.astype(BF16)
+            p[j * states : (j + 1) * states, :] = low
         return state
 
     def body(k, state):
-        @pl.when(k > 0)
-        def _():
-            leave(2 * k - 2, pa, 0).wait()
-
-        flush(2 * k - 1, pb)
-        state = fill(2 * k, state, pa)
-        leave(2 * k, pa, 0).start()
-
-        @pl.when(k > 0)
-        def _():
-            leave(2 * k - 1, pb, 1).wait()
-
-        flush(2 * k, pa)
-        state = fill(2 * k + 1, state, pb)
-        leave(2 * k + 1, pb, 1).start()
+        for i in range(0, ROUND, 2):
+            at = ROUND * k + i
+            flush(at - 1, pb)
+            state = fill(at, state, pa)
+            flush(at, pa)
+            state = fill(at + 1, state, pb)
         return state
 
-    lax.fori_loop(0, chunks // 2, body, begin)
+    rounds = chunks // ROUND
+    state = lax.fori_loop(0, rounds // 2, body, begin)
+    leave(l, 0).start()
+    lax.fori_loop(rounds // 2, rounds, body, state)
+    leave(l, 1).start()
     flush(chunks - 1, pb)
     gc_ref[...] = dot(masked[...], to_lanes(low_rank + states, states))
-    leave(chunks - 2, pa, 0).wait()
-    leave(chunks - 1, pb, 1).wait()
-    first.wait()
+
+    @pl.when(l == lanes - 1)
+    def _():
+        for slot in range(lanes):
+            for part in range(2):
+                leave(slot, part).wait()
 
 
 def scan_forward(low_rank, place, proj, log, dt, u, gy, got):
@@ -470,27 +604,27 @@
             shape((lanes, length, width), F32),
             shape(proj.shape, F32),
             shape((lanes, states, width), F32),
-            shape((lanes, (length + 1) * states, width), BF16),
+            shape((lanes, length * states, width), BF16),
         ],
-        scratch_shapes=[pltpu.VMEM((CHUNK * states, width), BF16)] * 2
+        scratch_shapes=[pltpu.VMEM((lanes, length * states, width), BF16)]
+        + [pltpu.VMEM((CHUNK * states, width), BF16)] * 2
         + [
-            pltpu.VMEM((states, width), BF16),
             pltpu.VMEM((states, length), F32),
             pltpu.VMEM((length, CHUNK * states), BF16),
             pltpu.VMEM((length, CHUNK * states), BF16),
-            pltpu.SemaphoreType.DMA((3,)),
+            pltpu.SemaphoreType.DMA((lanes, 2)),
         ],
-        compiler_params=pltpu.CompilerParams(vmem_limit_bytes=24 << 20),
+        compiler_params=pltpu.CompilerParams(vmem_limit_bytes=20 << 20),
         cost_estimate=cost(8, lanes, length, width, states),
         name="scan_forward",
     )(place, proj, log, dt, u, gy, got)
 
 
 def backward_kernel(
-    low_rank, proj_ref, log_ref, dt_ref, u_ref, gy_ref, last_ref, gc_ref, hs_ref, *refs
+    low_rank, lanes, proj_ref, log_ref, dt_ref, u_ref, gy_ref, last_ref, gc_ref, hs_ref, *refs
 ):
     (turn_ref, pull_ref, gbc_ref, ga_ref,
-     ha, hb, pa, pb, qa, qb, ra, rb, cols, left_b, masked, sems) = refs[-16:]
+     kept, pa, pb, qa, qb, ra, rb, cols, left_b, masked, sems) = refs[-15:]
     length, width = dt_ref.shape
     states = log_ref.shape[0]
     l = pl.program_id(0)
@@ -500,12 +634,19 @@
     per_state, per_step = selectors(states)
     per_state_low, per_step_low = per_state.astype(BF16), per_step.astype(BF16)
     chunks = length // CHUNK
-    wide = CHUNK * states
-
-    def enter(i, h, at):
-        return pltpu.make_async_copy(hs_ref.at[l, rows_of(i, wide), :], h, sems.at[at])
-
-    enter(chunks - 1, ha, 0).start()
+
+    half = length // 2 * states
+
+    def enter(slot, part):
+        rows = pl.ds(part * half, half)
+        return pltpu.make_async_copy(hs_ref.at[slot, rows, :], kept.at[slot, rows, :], sems.at[slot, part])
+
+    @pl.when(l == 0)
+    def _():
+        for slot in range(lanes):
+            for part in (1, 0):
+                enter(slot, part).start()
+
     for ref in (pb, qb, rb):
         ref[...] = jnp.zeros(ref.shape, BF16)
     proj = proj_ref[...]
@@ -520,7 +661,7 @@
         turn_ref[o, :] = dot(per_step_low, q[...])
         return ga + dot(per_state_low, r[...])
 
-    def fill(i, carry, h, p, q, r):
+    def fill(i, carry, p, q, r):
         c_tile = chunk_columns(cols, i)
         for j in reversed(range(CHUNK)):
             t = i * CHUNK + j
@@ -530,30 +671,27 @@
             grad = carry + row_of(gy_ref, t, states) * c
             carry = jnp.exp2(dt * rate) * grad
             p[s, :] = grad.astype(BF16)
-            turn = carry.astype(BF16) * h[s, :] * rate_low
+            turn = carry.astype(BF16) * kept[l, rows_of(t, states), :] * rate_low
             q[s, :] = turn
             r[s, :] = turn * dt.astype(BF16)
         return carry
 
     def body(k, carried):
         carry, ga = carried
-        i = chunks - 1 - 2 * k
-        enter(i, ha, 0).wait()
-        enter(i - 1, hb, 1).start()
-        ga = flush(i + 1, pb, qb, rb, ga)
-        carry = fill(i, carry, ha, pa, qa, ra)
-        enter(i - 1, hb, 1).wait()
-
-        @pl.when(i > 1)
-        def _():
-            enter(i - 2, ha, 0).start()
-
-        ga = flush(i, pa, qa, ra, ga)
-        carry = fill(i - 1, carry, hb, pb, qb, rb)
+        for i in range(0, ROUND, 2):
+            at = chunks - 1 - ROUND * k - i
+            ga = flush(at + 1, pb, qb, rb, ga)
+            carry = fill(at, carry, pa, qa, ra)
+            ga = flush(at, pa, qa, ra, ga)
+            carry = fill(at - 1, carry, pb, qb, rb)
         return carry, ga
 
-    zero = jnp.zeros((states, width), F32)
-    _, ga = lax.fori_loop(0, chunks // 2, body, (last_ref[...], zero))
+    rounds = chunks // ROUND
+    carried = (last_ref[...], jnp.zeros((states, width), F32))
+    enter(l, 1).wait()
+    carried = lax.fori_loop(0, rounds // 2, body, carried)
+    enter(l, 0).wait()
+    _, ga = lax.fori_loop(rounds // 2, rounds, body, carried)
     ga_ref[...] = flush(0, pb, qb, rb, ga)
     gbc_ref[...] = gc_ref[...] + dot(masked[...], to_lanes(low_rank, states))
 
@@ -565,21 +703,22 @@
     tokens, state_spec, narrow = lane_spec(length, width), lane_spec(states, width), lane_spec(length, LANE)
     token = shape((lanes, length, width), F32)
     return pl.pallas_call(
-        functools.partial(backward_kernel, low_rank),
+        functools.partial(backward_kernel, low_rank, lanes),
         grid=(lanes,),
         in_specs=[narrow, whole_spec(states, width), tokens, tokens, tokens, state_spec, narrow]
         + [pl.BlockSpec(memory_space=pltpu.HBM)]
         + [pl.BlockSpec(memory_space=pl.ANY)] * len(earlier),
         out_specs=[tokens, tokens, narrow, state_spec],
         out_shape=[token, token, shape(proj.shape, F32), shape((lanes, states, width), F32)],
-        scratch_shapes=[pltpu.VMEM((CHUNK * states, width), BF16)] * 8
+        scratch_shapes=[pltpu.VMEM((lanes, length * states, width), BF16)]
+        + [pltpu.VMEM((CHUNK * states, width), BF16)] * 6
         + [
             pltpu.VMEM((states, length), F32),
             pltpu.VMEM((length, CHUNK * states), BF16),
             pltpu.VMEM((length, CHUNK * states), BF16),
-            pltpu.SemaphoreType.DMA((2,)),
+            pltpu.SemaphoreType.DMA((lanes, 2)),
         ],
-        compiler_params=pltpu.CompilerParams(vmem_limit_bytes=24 << 20),
+        compiler_params=pltpu.CompilerParams(vmem_limit_bytes=22 << 20),
         cost_estimate=cost(12, lanes, length, width, states),
         name="scan_backward",
     )(proj, log, dt, u, gy, last, gc, hs, *earlier)
@@ -626,10 +765,19 @@
             x_parts[k | bit] = swap(x_parts[k], "mp", bit)
         square = square + swap(square, "mp", bit)
     grad_parts[0] = after(output_grad.astype(BF16), x_parts[mp_bits[-1]])
-    for bit in reversed(mp_bits):
+    for bit in reversed(mp_bits[1:]):
         for k in list(grad_parts):
             grad_parts[k | bit] = swap(grad_parts[k], "mp", bit)
     near = list(range(mp_size))
+    over = Reduction()
+    per = shard_width * seq_size // model_width
+    halves = seq_size // 2
+    place = jnp.concatenate([seq_index[None].astype(jnp.int32), row_starts[:, 0]])
+    orders = jnp.concatenate([over.order(per, mp_index), over.order(1, 0)])
+    flat_order = over.flat_order()
+    flags = [over.own(step)[None] for step in range(len(seq_bits))]
+    span_more = FAR * starts[:, :, None]
+    to_later = (jnp.arange(seq_size) > seq_index)[:, None, None]
     w_in = blocks(in_weight, 1, near).astype(BF16)
     w_back = blocks(in_weight, 1, near_first).astype(BF16)
     w_out = out_weight.astype(BF16)
@@ -638,12 +786,16 @@
     w_x = jnp.pad(xproj_weight.astype(BF16), ((0, 0), (0, -xproj_weight.shape[1] % LANE)))
     w_dt = jnp.pad(dtproj_weight.astype(BF16), ((0, -low_rank % LANE), (0, 0)))
     inv_rms = lax.rsqrt(square[:, :, None] / model_width + 1e-05)
+    x_parts[near[-1]] = after(x_parts[near[-1]], place, orders, flat_order, span_more, *flags)
     x_whole = jnp.concatenate([x_parts[k] for k in near], axis=2)
     normed = (x_whole.astype(F32) * inv_rms * gain).astype(BF16)
+    rim_count = 8
+    rim_normed = from_behind(normed[:, length - rim_count :, :], "seq", 1)
     inner_act = jnp.einsum("ltd,de->lte", normed, w_in[0], preferred_element_type=F32).astype(BF16)
-    rim_rows = from_behind(inner_act[:, length - (tap_count - 1) :, :], "seq", 1)
     gate_in = jnp.einsum("ltd,de->lte", normed, w_in[1], preferred_element_type=F32)
-    rim_rows = rim_rows.astype(F32) * carry_mask
+    rim_rows = jnp.einsum("ltd,de->lte", rim_normed, w_in[0], preferred_element_type=F32).astype(BF16)
+    rim_rows = after(rim_rows, *grad_parts.values())
+    rim_rows = (rim_rows.astype(F32) * carry_mask)[:, rim_count - (tap_count - 1) :]
     padded = jnp.concatenate([rim_rows, inner_act.astype(F32)], axis=1)
     conv_sum = conv_bias + conv_weight[0] * padded[:, 0:length]
     for tap in range(1, tap_count):
@@ -654,6 +806,11 @@
     for bit in mp_bits[:-1]:
         sent = (sent.astype(F32) + swap(sent, "mp", bit).astype(F32)).astype(BF16)
     got = swap(sent, "mp", mp_bits[-1])
+    for k in list(grad_parts):
+        grad_parts[k] = after(grad_parts[k], sent)
+        grad_parts[k | 1] = swap(grad_parts[k], "mp", 1)
+    rim_pad = jnp.zeros((lane_count, rim_count, model_width), BF16)
+    normed_more = jnp.concatenate([after(normed, sent), rim_normed, rim_pad], axis=1)
     grad_whole = jnp.concatenate(
         [
             sum(jnp.where(k == (mp_index ^ block), grad_parts[k], 0) for k in range(mp_size))
@@ -666,8 +823,7 @@
     end_state, pulled, span, dt, source, slope_dt, projected = scan_ends(
         low_rank, sent, got, w_dt, dt_bias[None], decay_log, mixed, grad_scan
     )
-    span = span + FAR * starts[:, :, None]
-    to_later = (jnp.arange(seq_size) > seq_index)[:, None, None]
+    span = span + span_more
     flat = (1, lane_count * state_count, inner_width)
     edge = jnp.where(to_later, end_state.reshape(flat), (pulled * carry_mask).reshape(flat))
     spans = jnp.broadcast_to(
@@ -676,23 +832,20 @@
     message = jnp.concatenate([edge, spans], axis=1).astype(BF16)
     message = jnp.pad(message, ((0, 0), (0, -message.shape[1] % 8), (0, 0)))
     groups = lax.all_to_all(message, "seq", 0, 0, tiled=True)
-    place = jnp.concatenate([seq_index[None].astype(jnp.int32), row_starts[:, 0]])
     y, grad_read, last, states_all = scan_forward(
         low_rank, place, projected, decay_log, dt, source, grad_scan, groups
     )
     scan_out = y + skip_gain * mixed
     gated = (scan_out * jax.nn.silu(gate_in)).astype(BF16)
     grad_gate = (grad_gated * scan_out * silu_slope(gate_in)).astype(BF16)
-    over = Reduction()
     half_width = model_width // 2
-    first_sent = over.sent(normed, grad_gate)
-    sum_first = Sum(over, jnp.concatenate([first_sent, over.sent(grad_whole, gated)], axis=0), 2)
-    out_sent = jnp.einsum(
-        "lte,ed->ltd", after(gated, sum_first.sent), w_spread[:, half_width:], preferred_element_type=F32
-    ).astype(BF16)
+    first = [over.sent(normed, grad_gate)]
+    first.append(over.sent(grad_whole, after(gated, first[0])))
+    sum_first = Sum(over, first, (False, False), flags)
+    sum_first.kept = [over.kept(after(normed, sum_first.message), grad_gate)]
+    sum_first.kept.append(over.kept(grad_whole, after(gated, sum_first.kept[0])))
     turn, pull, part, grad_log = scan_backward(
-        low_rank, projected, decay_log, dt, source, grad_scan, last, grad_read, states_all,
-        sum_first.sent, out_sent,
+        low_rank, projected, decay_log, dt, source, grad_scan, last, grad_read, states_all, *sum_first.kept
     )
     grad_slope = (turn + pull * mixed) * slope_dt
     grad_pre = grad_slope.astype(BF16)
@@ -701,14 +854,11 @@
     for bit in mp_bits[:-1]:
         got = swap(sent, "mp", bit)
         if bit == 1:
-            kept = over.kept(after(normed, sent), grad_gate)
-            sent = after(sent, kept)
+            got = after(got, sum_first.next(sent))
         sent = (sent.astype(F32) + got.astype(F32)).astype(BF16)
     got = swap(sent, "mp", mp_bits[-1])
-    sum_first.kept = [kept, over.kept(after(grad_whole, sent), gated)]
-    step = sum_first.next(sent)
     grad_dt_w = jnp.einsum(
-        "ltr,lte->re", projected.astype(BF16), after(grad_pre, step), preferred_element_type=F32
+        "ltr,lte->re", projected.astype(BF16), after(grad_pre, sent), preferred_element_type=F32
     )[:low_rank]
     grad_projected = after(sent, grad_dt_w).astype(F32) + got.astype(F32)
     grad_projected = grad_projected.astype(BF16)
@@ -729,52 +879,12 @@
             conv_weight[tap] * grad_conv, ((0, 0), (tap, tap_count - 1 - tap), (0, 0))
         )
     rim_sent = grad_padded[:, : tap_count - 1] * carry_mask
-    rim_back = from_behind(rim_sent, "seq", -1)
-    grad_x_w = jnp.einsum(
-        "ltr,lte->re", grad_projected, after(mixed_low, rim_sent), preferred_element_type=F32
-    )[: low_rank + 2 * state_count]
-    step = grad_x_w
-    tail_zeros = jnp.zeros((lane_count, length - (tap_count - 1), inner_width), F32)
-    grad_inner = after(grad_padded, step)[:, tap_count - 1 :] + jnp.concatenate(
-        [tail_zeros, rim_back], axis=1
-    )
-    grad_inner = grad_inner.astype(BF16)
-    sum_inner = Sum(over, over.sent(normed, grad_inner), 1)
-    sum_inner.kept = [over.kept(normed, after(grad_inner, sum_inner.sent))]
-    step = sum_first.next(sum_inner.kept[0])
-
-    def back(part, cut):
-        return jnp.einsum("lte,de->ltd", part[0], w_back[0, cut], preferred_element_type=F32) + jnp.einsum(
-            "lte,de->ltd", part[1], w_back[1, cut], preferred_element_type=F32
-        )
-
-    grads = (after(grad_inner, step), grad_gate)
-    back_sent = back(grads, slice(half_width, None)).astype(BF16)
-    back_kept = back((after(grad_inner, back_sent), grad_gate), slice(0, half_width))
-    step = sum_inner.next(back_sent)
-    row_dot = jnp.sum(
-        after(grad_inner, step).astype(F32) * inner_act.astype(F32) + grad_gate.astype(F32) * gate_in,
-        axis=2,
-    )
-    for bit in mp_bits:
-        row_dot = row_dot + swap(row_dot, "mp", bit)
-    for bit in mp_bits[:-1]:
-        back_kept, back_sent = hop(back_kept, back_sent, "mp", bit)
-    grad_own = back_kept + swap(back_sent, "mp", mp_bits[-1]).astype(F32)
-    step = sum_first.next(back_sent)
-    out_kept = jnp.einsum(
-        "lte,ed->ltd", after(gated, step), w_spread[:, :half_width], preferred_element_type=F32
-    )
-    for bit in mp_bits[:-1]:
-        out_kept, out_sent = hop(out_kept, out_sent, "mp", bit)
-    output = inputs + (out_kept + swap(out_sent, "mp", mp_bits[-1]).astype(F32))
-    step = sum_inner.next(out_sent)
-    unit_own = inputs * inv_rms
-    grad_gain = jnp.sum(grad_own * unit_own, axis=(0, 1))
-    input_grad = output_grad + inv_rms * (
-        grad_own * gain[:shard_width] - unit_own * (row_dot[:, :, None] / model_width)
-    )
-    gain_rows = jnp.pad(grad_gain, (0, -shard_width % inner_width)).reshape(-1, inner_width)
+    rim_fill = jnp.zeros((lane_count, rim_count - (tap_count - 1), inner_width), F32)
+    rim_tail = jnp.zeros((lane_count, rim_count, inner_width), F32)
+    grad_more = jnp.concatenate(
+        [grad_padded[:, tap_count - 1 :], rim_fill, rim_sent, rim_tail], axis=1
+    ).astype(BF16)
+    grad_x_w = jnp.einsum("ltr,lte->re", grad_projected, after(mixed_low, rim_sent), preferred_element_type=F32)
     small = jnp.concatenate(
         [
             grad_conv_w,
@@ -783,51 +893,101 @@
             jnp.sum(grad_scan * mixed, axis=(0, 1))[None],
             jnp.sum(grad_log, axis=0),
             grad_dt_w,
-            grad_x_w,
-            gain_rows,
+            grad_x_w[: low_rank + 2 * state_count],
         ],
         axis=0,
     )
-    small = jnp.pad(small, ((0, -small.shape[0] % 16), (0, 0)))
+    small = jnp.pad(small, ((0, -small.shape[0] % (8 * seq_size)), (0, 0)))
+    small_kept, small_sent = over.halves(small, 0)
+    inner_sent = over.sent(normed_more, after(grad_more, grad_x_w))
+    sum_inner = Sum(over, [inner_sent, small_sent], (False, True), flags)
+    step = sum_first.next(sum_inner.message)
+    sum_inner.kept = [over.kept(normed_more, after(grad_more, step)), small_kept]
+    rim_back = from_behind(after(rim_sent, step), "seq", -1)
+    out_sent = jnp.einsum(
+        "lte,ed->ltd", after(gated, sum_inner.kept[0]), w_spread[:, half_width:], preferred_element_type=F32
+    ).astype(BF16)
+    out_kept = jnp.einsum(
+        "lte,ed->ltd", after(gated, out_sent), w_spread[:, :half_width], preferred_element_type=F32
+    )
+    tail_zeros = jnp.zeros((lane_count, length - (tap_count - 1), inner_width), F32)
+    grad_inner = grad_padded[:, tap_count - 1 :] + jnp.concatenate(
+        [tail_zeros, after(rim_back, out_kept)], axis=1
+    )
+    grad_inner = grad_inner.astype(BF16)
+
+    def back(part, cut):
+        return jnp.einsum("lte,de->ltd", part[0], w_back[0, cut], preferred_element_type=F32) + jnp.einsum(
+            "lte,de->ltd", part[1], w_back[1, cut], preferred_element_type=F32
+        )
+
+    back_sent = back((grad_inner, grad_gate), slice(half_width, None)).astype(BF16)
+    back_kept = back((after(grad_inner, back_sent), grad_gate), slice(0, half_width))
+    row_dot = jnp.sum(
+        after(grad_inner, back_kept).astype(F32) * inner_act.astype(F32) + grad_gate.astype(F32) * gate_in,
+        axis=2,
+    )
+
+    def as_rows(values, width):
+        high = values.astype(BF16)
+        low = (values - high.astype(F32)).astype(BF16)
+        rows = jnp.concatenate([high, low], axis=1).reshape(lane_count, -1, width)
+        return jnp.pad(rows, ((0, 0), (0, -rows.shape[1] % 16), (0, 0)))
+
+    message = jnp.concatenate([out_sent, back_sent, as_rows(row_dot, half_width)], axis=1)
+    step = sum_inner.next(message)
     step = sum_first.next(step)
+    got = swap(after(message, step), "mp", 1)
+    for bit in mp_bits[:-1]:
+        if bit == 1:
+            step = sum_inner.next(message)
+            step = sum_first.next(step)
+        message, out_kept, back_kept, row_dot = hop(after(got, step), out_kept, back_kept, row_dot)
+        got = swap(message, "mp", 2 * bit)
+    got = after(got, message)
+    rows = got[:, 2 * length :][:, : 2 * length // shard_width].reshape(lane_count, 2 * length).astype(F32)
+    row_dot = row_dot + rows[:, :length] + rows[:, length:]
+    grad_own = back_kept + got[:, length : 2 * length].astype(F32)
+    output = inputs + (out_kept + got[:, :length].astype(F32))
+    unit_own = inputs * inv_rms
+    grad_gain = jnp.sum(grad_own * unit_own, axis=(0, 1))
+    input_grad = output_grad + inv_rms * (
+        grad_own * gain[:shard_width] - unit_own * (row_dot[:, :, None] / model_width)
+    )
+    grad_gain = jnp.pad(grad_gain, (0, -shard_width % inner_width)).reshape(-1, inner_width)
+    sum_inner.rider = jnp.pad(grad_gain, ((0, -grad_gain.shape[0] % 16), (0, 0)))
+    step = sum_inner.next(grad_gain)
+    step = sum_first.next(step)
+    output, input_grad = after(output, step), after(input_grad, step)
     step = sum_inner.next(step)
-    for bit in seq_bits:
-        low = after(small, step).astype(BF16)
-        small = low.astype(F32) + swap(low, "seq", bit).astype(F32)
-        step = sum_first.next(step) if not sum_first.over_now() else step
-        step = sum_inner.next(step) if not sum_inner.over_now() else step
-    per = shard_width * seq_size // model_width
-    blocks = seq_size // 2
-    orders = jnp.concatenate([over.order(per, mp_index), over.order(1, 0)])
-    second = 2 + blocks
+    step = sum_inner.next(step)
+    sum_first.run_out()
+    second = 2 + halves
     in_shape, out_shape = (2, model_width, inner_width), out_weight.shape
-    early, late = sum_first.finish()
-    layout = [(0, 1, 0, 0, blocks, False), (0, 1, 0, 1, blocks, False)]
-    shapes, pieces = [in_shape], [early[0], late[0]]
-    aligned = model_width // seq_size % LANE == 0
-    if aligned:
-        layout += [(1, None, second, 0, blocks, True), (1, None, second, 1, blocks, True)]
-        shapes, pieces = [in_shape, out_shape], [*pieces, early[1], late[1]]
-    in_w, *out_w = settle(orders, pieces, layout, shapes)
-    if not aligned:
-        source = orders[second + 2 :]
-        halves = [p.reshape(blocks, -1, inner_width)[source].reshape(-1, inner_width) for p in (early[1], late[1])]
+    half = model_width // 2
+    layout = [(0, 1, 0, 0, halves, False, 0, half), (0, 1, 0, 1, halves, False, 0, half)]
+    ends = (sum_first.message, after(sum_first.got, step))
+    if model_width // seq_size % LANE == 0:
+        layout += [(1, None, second, 0, halves, True, half, half), (1, None, second, 1, halves, True, half, half)]
+        in_w, out_w = settle(orders, [*ends, *ends], layout, [in_shape, out_shape])
+    else:
+        (in_w,) = settle(orders, [*ends], layout, [in_shape])
+        rows = [p[half:].reshape(halves, -1, inner_width)[orders[second + 2 :]].reshape(half, -1) for p in ends]
         up = over.own(0) == 1
-        halves = [jnp.where(up, halves[1], halves[0]), jnp.where(up, halves[0], halves[1])]
-        out_w = [jnp.concatenate(halves, axis=0).astype(F32).T]
-    early, late = sum_inner.finish()
-    (in_w,) = settle(orders, early, [(0, 0, 0, 0, blocks, False)], [in_shape], [in_w])
-    (in_w,) = settle(orders, late, [(0, 0, 0, 1, blocks, False)], [in_shape], [in_w])
-    (out_w,) = out_w
-    sizes = [tap_count, 1, 1, 1, state_count, low_rank, low_rank + 2 * state_count, gain_rows.shape[0]]
-    parts, at = [], 0
-    for size in sizes:
-        parts.append(small[at : at + size])
-        at += size
+        rows = [jnp.where(up, rows[1], rows[0]), jnp.where(up, rows[0], rows[1])]
+        out_w = jnp.concatenate(rows, axis=0).astype(F32).T
+    sizes = [tap_count, 1, 1, 1, state_count, low_rank, low_rank + 2 * state_count]
+    sum_inner.run_out()
+    ends = (sum_inner.message, sum_inner.got)
+    in_w = settle(orders, ends[:1], [(0, 0, 0, 0, halves, False, 0, half)], [in_shape], [in_w])
+    parts = deal(flat_order, *ends, half, small.shape[0] // 2, sizes)
+    (in_w,) = settle(orders, ends[1:], [(0, 0, 0, 1, halves, False, 0, half)], [in_shape], in_w)
+    last = half + small.shape[0] // 2
+    grad_gain = ends[0][last : last + 1].astype(F32) + ends[1][last : last + 1].astype(F32)
     return (
         output,
         input_grad,
-        parts[7].reshape(-1)[:shard_width],
+        grad_gain.reshape(-1)[:shard_width],
         in_w,
         parts[0],
         parts[1][0],

time: 207 us -> 190 us (0.918)
  local copies, waits for them, and re-layouts: 24.3 us -> 13.7 us
  waiting for transfers between devices: 71.1 us -> 63.2 us
  starting transfers between devices: 39.2 us -> 35.2 us
  Pallas kernels: 36.7 us -> 40.3 us
  other arithmetic: 17.5 us -> 19.6 us
    ppermute x21 -> x14, waiting for transfers between devices: 28.5 us -> 15.6 us  [swap(): return lax.ppermute(block, axis, [(i, i ^ bit) for i in range(devices)])]
    unnamed x171 -> x179, local copies, waits for them, and re-layouts: 12.1 us -> 5.57 us
    ppermute x21 -> x14, starting transfers between devices: 14.8 us -> 9.23 us  [swap(): return lax.ppermute(block, axis, [(i, i ^ bit) for i in range(devices)])]
    ppermute x12, waiting for transfers between devices: 33.2 us -> 37.9 us  [swap(): return lax.ppermute(block, ('seq', 'mp'), route)]
    pallas_call x1 -> x13, Pallas kernels: 12.6 us -> 17.1 us  [the longest x1 11 us: scan_backward(): pl.pallas_call(functools.partial(backward_kernel, low_rank, lanes), grid=...]
    slice x16 -> x7, local copies, waits for them, and re-layouts: 4.07 us -> 0.17 us  [the longest x1 0.13 us: per_device(): grad_padded[:, tap_count - 1:]]
    reduce_sum x2 -> x1, other arithmetic: 2.45 us -> 0.28 us  [per_device(): jnp.sum(after(grad_inner, back_kept).astype(F32) * inner_act.astype(F32)...]
  transfers between devices with their start and end apart: 36 -> 29, of which waited for: 18 -> 13; matrix products, arithmetic and copies ran while one was open for 19% -> 18% of each run, Pallas kernels for 8% -> 10%
where the time goes in v2:
time: 190 us; the launch traced here: 189 us
  waiting for transfers between devices  63.2 us (33%)
  Pallas kernels  40.3 us (21%)
  starting transfers between devices  35.2 us (19%)
  other arithmetic  19.6 us (10%)
  matrix products  14.7 us (8%)
  local copies, waits for them, and re-layouts  13.7 us (7%)
  between operations  2.39 us (1%)
    ppermute x12, waiting for transfers between devices, swap(): return lax.ppermute(block, ('seq', 'mp'), route)  37.9 us
    ppermute x14, waiting for transfers between devices, swap(): return lax.ppermute(block, axis, [(i, i ^ bit) for i in range(devices)])  15.6 us
    ppermute x12, starting transfers between devices, swap(): return lax.ppermute(block, ('seq', 'mp'), route)  14.6 us
    pallas_call x1, Pallas kernels, scan_backward(): pl.pallas_call(functools.partial(backward_kernel, low_rank, lanes), grid=...  11 us
    ppermute x14, starting transfers between devices, swap(): return lax.ppermute(block, axis, [(i, i ^ bit) for i in range(devices)])  9.23 us
    pallas_call x1, Pallas kernels, scan_ends(): pl.pallas_call(functools.partial(ends_kernel, low_rank), grid=(lanes,), i...  9.08 us
    pallas_call x1, Pallas kernels, scan_forward(): pl.pallas_call(functools.partial(forward_kernel, low_rank, lanes), grid=(...  8.34 us
    all_to_all x1, starting transfers between devices, per_device(): groups = lax.all_to_all(message, 'seq', 0, 0, tiled=True)  6.63 us
  transfers between devices with their start and end apart: 29, of which 13 were waited for; matrix products, arithmetic and copies ran while one was open for 18% of the time, Pallas kernels for 10%

profile of v2, /device:TPU:0, one launch (start us, length us, event | category | flops | bytes accessed | tf_op | source)
XLA Modules:
  0.0 189.2 jit_solution(9898809056986522898)
XLA Ops:
  2.0 3.0 %collective-permute-start.1 = (bf16[2,256,256]{2,1,0:T(8,128)(2,1)S(1)}, bf16[2,256,256]{2,1,0:T(8,128)(2,1)S(1)}, u32[]{:S(2)}, u32[]{:S(2)}) collective-permute-start(bf16[2,256,256]{2,1,0:T(8,128)(2,1)S(1)} %get-tuple-element.207), channel_id=1, source_target_pairs={{0,2},{1,3},{2,0},{3,1},{4,6},{5,7},{6,4},{7,5},{8,10},{9,11},{10,... | collective-permute-start | bytes 786440 | tf_op jit(solution)/shard_map/ppermute | solution.py:22
  6.1 2.5 %dynamic-slice_convert_fusion.3 = (bf16[2,256,512]{2,1,0:T(8,128)(2,1)S(1)}, bf16[2,256,512]{2,1,0:T(8,128)(2,1)S(1)}, bf16[2,256,512]{2,1,0:T(8,128)(2,1)S(1)}, bf16[2,256,512]{2,1,0:T(8,128)(2,1)S(1)}) fusion(f32[2,1024,512]{2,1,0:T(8,128)} %param.16, s32[]{:T(128)S(6)} %select_n.195, s32[]{:T(128)S(6)} %select_n.196, s32[]{:T(128)S(6)} %select_n.198, ...), kind=kLoop, calls=%fused_computation.63 | loop fusion | bytes 4194320 | tf_op jit(solution)/shard_map/convert.15
  13.1 1.8 collective-permute-start.6
  16.2 3.5 %collective-permute-start.5 = (bf16[2,8,1024]{2,1,0:T(8,128)(2,1)S(1)}, bf16[2,8,1024]{2,1,0:T(8,128)(2,1)S(1)}, u32[]{:S(2)}, u32[]{:S(2)}) collective-permute-start(bf16[2,8,1024]{2,1,0:T(8,128)(2,1)S(1)} %slice.131), channel_id=1, source_target_pairs={{0,4},{4,8},{8,12},{12,16},{16,20},{20,24},{24,28},{1,5},{5,9},{9,... | collective-permute-start | bytes 98312 | tf_op jit(solution)/shard_map/ppermute | solution.py:28
  21.7 1.6 fusion.80
  25.7 1.9 %fusion.9 = f32[2,256,512]{2,1,0:T(8,128)S(1)} fusion(bf16[2,256,1024]{2,1,0:T(8,128)(2,1)S(1)} %multiply_convert_fusion, bf16[2,1024,512]{2,1,0:T(8,128)(2,1)} %pad_maximum_fusion), kind=kOutput, calls=%fused_computation.31 | convolution fusion | flops 536870912 | bytes 3145728 | tf_op jit(solution)/shard_map/ltd,de->lte/dot_general | solution.py:795
  27.7 1.7 collective-permute-start.8
  29.8 2.4 %multiply_reduce_fusion = (f32[512]{0:T(512)}, f32[2,256,512]{2,1,0:T(8,128)S(1)}, f32[2,256,512]{2,1,0:T(8,128)}) fusion(f32[2,256,512]{2,1,0:T(8,128)S(1)} %get-tuple-element.184.mixed_ref, f32[2,256,512]{2,1,0:T(8,128)S(1)} %fusion.9, f32[512,1024]{1,0:T(8,128)S(1)} %copy-done.59, bf16[2,256,256]{2,1,0:T(8,128)(2,1)S(1)} %get-tuple-element.204, ...), kind=kOutput, calls=%fused_computation.44 | convolution fusion | flops 543424000 | bytes 7342080 | tf_op jit(solution)/shard_map/ltd,ed->lte/dot_general | solution.py:821
  33.6 9.1 %scan_ends.1 = (f32[2,16,512]{2,1,0:T(8,128)S(1)}, f32[2,16,512]{2,1,0:T(8,128)S(1)}, f32[2,1,512]{2,1,0:T(1,128)S(1)}, f32[2,256,512]{2,1,0:T(8,128)}, f32[2,25...) custom-call(bf16[2,256,128]{2,1,0:T(8,128)(2,1)S(1)} %add_convert_fusion.4.sent_ref, ...), custom_call_target="tpu_custom_call" | custom-call | flops 536870912 | bytes 8388608 | tf_op jit(solution)/shard_map/scan_ends/pallas_call | solution.py:475
  43.8 6.6 %all-to-all-start = ((bf16[8,40,512]{2,1,0:T(8,128)(2,1)}), bf16[8,40,512]{2,1,0:T(8,128)(2,1)}, u32[]{:S(2)}, u32[]{:S(2)}) async-start(bf16[8,40,512]{2,1,0:T(8,128)(2,1)} %fusion.42), calls=%async_computation | async-start | bytes 655360 | tf_op jit(solution)/shard_map/all_to_all | solution.py:834
  51.6 2.6 %dynamic-slice_convert_fusion.5 = (bf16[512,256]{1,0:T(8,128)(2,1)}, bf16[512,256]{1,0:T(8,128)(2,1)}, bf16[512,256]{1,0:T(8,128)(2,1)}, bf16[512,256]{1,0:T(8,128)(2,1)}) fusion(f32[512,1024]{1,0:T(8,128)} %param.24, s32[]{:T(128)S(6)} %select_n.195, s32[]{:T(128)S(6)} %select_n.198, s32[]{:T(128)S(6)} %select_n.196, s32[]{:T(128)S(6)} %select_n.197), kind=kLoop, calls=%fused_computation.96 | loop fusion | bytes 2097168 | tf_op jit(solution)/shard_map/convert.5
  54.2 2.3 %pad_maximum_fusion.2 = bf16[2,256,1024]{2,1,0:T(8,128)(2,1)} fusion(bf16[2,256,256]{2,1,0:T(8,128)(2,1)} %copy-done.53, bf16[2,256,256]{2,1,0:T(8,128)(2,1)} %copy-done.54, bf16[2,256,256]{2,1,0:T(8,128)(2,1)} %copy-done.51, bf16[2,256,256]{2,1,0:T(8,128)(2,1)} %copy-done.52), kind=kLoop, calls=%fused_computation.34 | loop fusion | flops 4194304 | bytes 2097152 | tf_op jit(solution)/shard_map/concatenate | solution.py:814
  56.5 4.1 %all-to-all-done.got_ref = bf16[8,40,512]{2,1,0:T(8,128)(2,1)} async-done(((bf16[8,40,512]{2,1,0:T(8,128)(2,1)}), bf16[8,40,512]{2,1,0:T(8,128)(2,1)}, u32[]{:S(2)}, u32[]{:S(2)}) %all-to-all-start) | async-done | bytes 327712 | tf_op jit(solution)/shard_map/all_to_all | solution.py:834
  61.9 8.3 %scan_forward.1 = (f32[2,256,512]{2,1,0:T(8,128)S(1)}, f32[2,256,128]{2,1,0:T(8,128)S(1)}, f32[2,16,512]{2,1,0:T(8,128)S(1)}, bf16[2,4096,512]{2,1,0:T(8,128)(2,1)S(1)}) custom-call(s32[3]{0:T(128)S(1)} %pad_add_fusion.1.place_ref, f32[2,256,128]{2,1,0:T(8,128)S(1)} %get-tuple-element.96.proj_ref, f32[16,512]{1,0:T(8,128)S(1)} %copy-done.14, ...), custom_call_target="tpu_custom_call" | custom-call | flops 536870912 | bytes 8388608 | tf_op jit(solution)/shard_map/scan_forward/pallas_call | solution.py:590
  75.9 11.0 %scan_backward.1 = (f32[2,256,512]{2,1,0:T(8,128)S(1)}, f32[2,256,512]{2,1,0:T(8,128)S(1)}, f32[2,256,128]{2,1,0:T(8,128)S(1)}, f32[2,16,512]{2,1,0:T(8,128)S(1)}) custom-call(f32[2,256,128]{2,1,0:T(8,128)S(1)} %get-tuple-element.96.proj_ref, f32[16,512]{1,0:T(8,128)S(1)} %copy-done.14, f32[2,256,512]{2,1,0:T(8,128)S(1)} %copy-done.4, ...), custom_call_target="tpu_custom_call" | custom-call | flops 805306368 | bytes 8388608 | tf_op jit(solution)/shard_map/scan_backward/pallas_call | solution.py:705
  90.0 2.7 %advance.10 = (bf16[512,512]{1,0:T(8,128)(2,1)}, f32[256,512]{1,0:T(8,128)S(1)}, f32[256,512]{1,0:T(8,128)S(1)}) custom-call(s32[1]{0:T(128)} %bitcast.7.flag_ref, bf16[1024,512]{1,0:T(8,128)(2,1)} %pad_maximum_fusion.3.refs_0_, bf16[1024,512]{1,0:T(8,128)(2,1)} %collective-permute-done.12.refs_1_, f32[512,512]{1,0:T(8,128)S(1)} %convolution_bitcast_fusion.3.refs_0_.refs_2_, ...), custom_call_target="tpu_custom_call" | custom-call | tf_op jit(solution)/shard_map/advance/pallas_call | solution.py:155
  94.2 4.4 %collective-permute-done.13 = bf16[2,256,128]{2,1,0:T(8,128)(2,1)S(1)} collective-permute-done((bf16[2,256,128]{2,1,0:T(8,128)(2,1)S(1)}, bf16[2,256,128]{2,1,0:T(8,128)(2,1)S(1)}, u32[]{:S(2)}, u32[]{:S(2)}) %collective-permute-start.13) | collective-permute-done | bytes 131104 | tf_op jit(solution)/shard_map/ppermute | solution.py:22
  103.5 1.8 fusion.3
  111.3 4.7 %collective-permute-done.15 = f32[2,3,512]{2,1,0:T(4,128)S(1)} collective-permute-done((f32[2,3,512]{2,1,0:T(4,128)S(1)}, f32[2,3,512]{2,1,0:T(4,128)S(1)}, u32[]{:S(2)}, u32[]{:S(2)}) %collective-permute-start.15) | collective-permute-done | bytes 12320 | tf_op jit(solution)/shard_map/ppermute | solution.py:28
  123.0 3.0 %collective-permute-start.19 = (bf16[256,512]{1,0:T(8,128)(2,1)S(1)}, bf16[256,512]{1,0:T(8,128)(2,1)S(1)}, u32[]{:S(2)}, u32[]{:S(2)}) collective-permute-start(bf16[256,512]{1,0:T(8,128)(2,1)S(1)} %advance.13.refs_0_), channel_id=1, source_target_pairs={{0,16},{1,17},{2,18},{3,19},{4,20},{5,21},{6,22},{7,23},{8,24},{9,... | collective-permute-start | bytes 786440 | tf_op jit(solution)/shard_map/ppermute | solution.py:64
  126.0 7.4 %collective-permute-done.20.refs_1_ = bf16[304,512]{1,0:T(8,128)(2,1)S(1)} collective-permute-done((bf16[304,512]{1,0:T(8,128)(2,1)S(1)}, bf16[304,512]{1,0:T(8,128)(2,1)S(1)}, u32[]{:S(2)}, u32[]{:S(2)}) %collective-permute-start.20) | collective-permute-done | bytes 311328 | tf_op jit(solution)/shard_map/ppermute | solution.py:64
  133.5 4.7 %collective-permute-done.19.refs_1_ = bf16[256,512]{1,0:T(8,128)(2,1)S(1)} collective-permute-done((bf16[256,512]{1,0:T(8,128)(2,1)S(1)}, bf16[256,512]{1,0:T(8,128)(2,1)S(1)}, u32[]{:S(2)}, u32[]{:S(2)}) %collective-permute-start.19) | collective-permute-done | bytes 262176 | tf_op jit(solution)/shard_map/ppermute | solution.py:64
  139.3 1.6 collective-permute-start.22
  140.9 3.3 %collective-permute-start.23 = (bf16[176,512]{1,0:T(8,128)(2,1)S(1)}, bf16[176,512]{1,0:T(8,128)(2,1)S(1)}, u32[]{:S(2)}, u32[]{:S(2)}) collective-permute-start(bf16[176,512]{1,0:T(8,128)(2,1)S(1)} %get-tuple-element.142.refs_0_), channel_id=1, source_target_pairs={{0,16},{1,17},{2,18},{3,19},{4,20},{5,21},{6,22},{7,23},{8,24},{9,... | collective-permute-start | bytes 540680 | tf_op jit(solution)/shard_map/ppermute | solution.py:64
  144.3 8.9 %collective-permute-done.21 = bf16[2,528,256]{2,1,0:T(8,128)(2,1)S(1)} collective-permute-done((bf16[2,528,256]{2,1,0:T(8,128)(2,1)S(1)}, bf16[2,528,256]{2,1,0:T(8,128)(2,1)S(1)}, u32[]{:S(2)}, u32[]{:S(2)}) %collective-permute-start.21) | collective-permute-done | bytes 540704 | tf_op jit(solution)/shard_map/ppermute | solution.py:22
  154.7 1.6 collective-permute-start.27
  156.3 7.9 %collective-permute-done.24.refs_1_ = bf16[144,512]{1,0:T(8,128)(2,1)S(1)} collective-permute-done((bf16[144,512]{1,0:T(8,128)(2,1)S(1)}, bf16[144,512]{1,0:T(8,128)(2,1)S(1)}, u32[]{:S(2)}, u32[]{:S(2)}) %collective-permute-start.24) | collective-permute-done | bytes 147488 | tf_op jit(solution)/shard_map/ppermute | solution.py:64
  164.3 10.6 %collective-permute-done.25.refs_1_ = bf16[320,512]{1,0:T(8,128)(2,1)S(1)} collective-permute-done((bf16[320,512]{1,0:T(8,128)(2,1)S(1)}, bf16[320,512]{1,0:T(8,128)(2,1)S(1)}, u32[]{:S(2)}, u32[]{:S(2)}) %collective-permute-start.25) | collective-permute-done | bytes 327712 | tf_op jit(solution)/shard_map/ppermute | solution.py:64
  175.1 2.7 %settle.3 = (f32[2,1024,512]{2,1,0:T(8,128)}, f32[512,1024]{1,0:T(8,128)}) custom-call(s32[12]{0:T(128)S(1)} %concatenate.70.order_ref, bf16[1024,512]{1,0:T(8,128)(2,1)S(1)} %advance.17.refs_0_.refs_2_, bf16[1024,512]{1,0:T(8,128)(2,1)S(1)} %collective-permute-done.27.refs_1_.refs_3_, bf16[1024,512]{1,0:T(8,128)(2,1)S(1)} %advance.17.refs_0_.refs_2_, ...), custom_call_target="tpu_custom_call" | custom-call | tf_op jit(solution)/shard_map/settle/pallas_call | solution.py:251
  177.8 1.6 settle.4.refs_1_
  179.4 6.1 %collective-permute-done.26.refs_0_.late_ref = bf16[624,512]{1,0:T(8,128)(2,1)S(1)} collective-permute-done((bf16[624,512]{1,0:T(8,128)(2,1)S(1)}, bf16[624,512]{1,0:T(8,128)(2,1)S(1)}, u32[]{:S(2)}, u32[]{:S(2)}) %collective-permute-start.26) | collective-permute-done | bytes 639008 | tf_op jit(solution)/shard_map/ppermute | solution.py:64
  187.5 1.6 settle.5
  (311 shorter events, 49.7 us)
Async XLA Ops:
  2.0 9.4 %collective-permute-start.1 = (bf16[2,256,256]{2,1,0:T(8,128)(2,1)S(1)}, bf16[2,256,256]{2,1,0:T(8,128)(2,1)S(1)}, u32[]{:S(2)}, u32[]{:S(2)}) collective-permute-start(bf16[2,256,256]{2,1,0:T(8,128)(2,1)S(1)} %get-tuple-element.207), channel_id=1, source_target_pairs={{0,2},{1,3},{2,0},{3,1},{4,6},{5,7},{6,4},{7,5},{8,10},{9,11},{10,... | collective-permute-start | bytes 786440 | tf_op jit(solution)/shard_map/ppermute | solution.py:22
  5.0 9.9 %collective-permute-start = (bf16[2,256,256]{2,1,0:T(8,128)(2,1)S(1)}, bf16[2,256,256]{2,1,0:T(8,128)(2,1)}, u32[]{:S(2)}, u32[]{:S(2)}) collective-permute-start(bf16[2,256,256]{2,1,0:T(8,128)(2,1)S(1)} %get-tuple-element.207), channel_id=1, source_target_pairs={{0,1},{1,0},{2,3},{3,2},{4,5},{5,4},{6,7},{7,6},{8,9},{9,8},{10,11... | collective-permute-start | bytes 786440 | tf_op jit(solution)/shard_map/ppermute | solution.py:22
  5.0 6.3 %collective-permute-start.3 = (f32[2,256]{1,0:T(2,128)S(1)}, f32[2,256]{1,0:T(2,128)S(1)}, u32[]{:S(2)}, u32[]{:S(2)}) collective-permute-start(f32[2,256]{1,0:T(2,128)S(1)} %get-tuple-element.206), channel_id=1, source_target_pairs={{0,2},{1,3},{2,0},{3,1},{4,6},{5,7},{6,4},{7,5},{8,10},{9,11},{10,... | collective-permute-start | bytes 6152 | tf_op jit(solution)/shard_map/ppermute | solution.py:22
  8.7 34.1 %copy-start.80 = (f32[2]{0:T(128)}, f32[2]{0:T(128)S(1)}, u32[]{:S(2)}) copy-start(f32[2]{0:T(128)S(1)} %get-tuple-element.217) | copy-start | bytes 28
  11.4 1.7 collective-permute-start.4
  11.4 3.5 %collective-permute-start.2 = (bf16[2,256,256]{2,1,0:T(8,128)(2,1)S(1)}, bf16[2,256,256]{2,1,0:T(8,128)(2,1)S(1)}, u32[]{:S(2)}, u32[]{:S(2)}) collective-permute-start(bf16[2,256,256]{2,1,0:T(8,128)(2,1)S(1)} %collective-permute-done.1), channel_id=1, source_target_pairs={{0,1},{1,0},{2,3},{3,2},{4,5},{5,4},{6,7},{7,6},{8,9},{9,8},{10,11... | collective-permute-start | bytes 786440 | tf_op jit(solution)/shard_map/ppermute | solution.py:22
  13.1 8.5 %collective-permute-start.6 = (bf16[2,256,256]{2,1,0:T(8,128)(2,1)S(1)}, bf16[2,256,256]{2,1,0:T(8,128)(2,1)S(1)}, u32[]{:S(2)}, u32[]{:S(2)}) collective-permute-start(bf16[2,256,256]{2,1,0:T(8,128)(2,1)S(1)} %convert_element_type.214), channel_id=1, source_target_pairs={{0,2},{1,3},{2,0},{3,1},{4,6},{5,7},{6,4},{7,5},{8,10},{9,11},{10,... | collective-permute-start | bytes 786440 | tf_op jit(solution)/shard_map/ppermute | solution.py:22
  16.2 5.1 %collective-permute-start.5 = (bf16[2,8,1024]{2,1,0:T(8,128)(2,1)S(1)}, bf16[2,8,1024]{2,1,0:T(8,128)(2,1)S(1)}, u32[]{:S(2)}, u32[]{:S(2)}) collective-permute-start(bf16[2,8,1024]{2,1,0:T(8,128)(2,1)S(1)} %slice.131), channel_id=1, source_target_pairs={{0,4},{4,8},{8,12},{12,16},{16,20},{20,24},{24,28},{1,5},{5,9},{9,... | collective-permute-start | bytes 98312 | tf_op jit(solution)/shard_map/ppermute | solution.py:28
  23.6 1.5 collective-permute-start.7
  25.2 4.2 %collective-permute-start.10 = (bf16[2,256,256]{2,1,0:T(8,128)(2,1)S(1)}, bf16[2,256,256]{2,1,0:T(8,128)(2,1)S(1)}, u32[]{:S(2)}, u32[]{:S(2)}) collective-permute-start(bf16[2,256,256]{2,1,0:T(8,128)(2,1)S(1)} %collective-permute-done.6), channel_id=1, source_target_pairs={{0,1},{1,0},{2,3},{3,2},{4,5},{5,4},{6,7},{7,6},{8,9},{9,8},{10,11... | collective-permute-start | bytes 786440 | tf_op jit(solution)/shard_map/ppermute | solution.py:22
  25.7 3.7 %collective-permute-start.9 = (bf16[2,256,256]{2,1,0:T(8,128)(2,1)S(1)}, bf16[2,256,256]{2,1,0:T(8,128)(2,1)S(1)}, u32[]{:S(2)}, u32[]{:S(2)}) collective-permute-start(bf16[2,256,256]{2,1,0:T(8,128)(2,1)S(1)} %convert_element_type.214), channel_id=1, source_target_pairs={{0,1},{1,0},{2,3},{3,2},{4,5},{5,4},{6,7},{7,6},{8,9},{9,8},{10,11... | collective-permute-start | bytes 786440 | tf_op jit(solution)/shard_map/ppermute | solution.py:22
  27.7 5.9 %collective-permute-start.8 = (bf16[2,256,128]{2,1,0:T(8,128)(2,1)S(1)}, bf16[2,256,128]{2,1,0:T(8,128)(2,1)S(1)}, u32[]{:S(2)}, u32[]{:S(2)}) collective-permute-start(bf16[2,256,128]{2,1,0:T(8,128)(2,1)S(1)} %add_convert_fusion.4.sent_ref), channel_id=1, source_target_pairs={{0,2},{1,3},{2,0},{3,1},{4,6},{5,7},{6,4},{7,5},{8,10},{9,11},{10,... | collective-permute-start | bytes 393224 | tf_op jit(solution)/shard_map/ppermute | solution.py:22
  32.1 28.5 %copy-start = (f32[2,256,512]{2,1,0:T(8,128)}, f32[2,256,512]{2,1,0:T(8,128)S(1)}, u32[]{:S(2)}) copy-start(f32[2,256,512]{2,1,0:T(8,128)S(1)} %get-tuple-element.180.gy_ref) | copy-start | bytes 3145732
  43.8 16.9 %all-to-all-start = ((bf16[8,40,512]{2,1,0:T(8,128)(2,1)}), bf16[8,40,512]{2,1,0:T(8,128)(2,1)}, u32[]{:S(2)}, u32[]{:S(2)}) async-start(bf16[8,40,512]{2,1,0:T(8,128)(2,1)} %fusion.42), calls=%async_computation | async-start | bytes 655360 | tf_op jit(solution)/shard_map/all_to_all | solution.py:834
  73.5 16.4 %collective-permute-start.12 = (bf16[1024,512]{1,0:T(8,128)(2,1)}, bf16[1024,512]{1,0:T(8,128)(2,1)}, u32[]{:S(2)}, u32[]{:S(2)}) collective-permute-start(bf16[1024,512]{1,0:T(8,128)(2,1)} %pad_maximum_fusion.3.refs_0_), channel_id=1, source_target_pairs={{0,4},{1,9},{2,6},{3,11},{4,0},{5,13},{6,2},{7,15},{8,12},{9,1},{1... | collective-permute-start | bytes 3145736 | tf_op jit(solution)/shard_map/ppermute | solution.py:64
  88.5 4.2 %collective-permute-start.11 = (bf16[2,256,128]{2,1,0:T(8,128)(2,1)S(1)}, bf16[2,256,128]{2,1,0:T(8,128)(2,1)S(1)}, u32[]{:S(2)}, u32[]{:S(2)}) collective-permute-start(bf16[2,256,128]{2,1,0:T(8,128)(2,1)S(1)} %add_convert_fusion.3), channel_id=1, source_target_pairs={{0,1},{1,0},{2,3},{3,2},{4,5},{5,4},{6,7},{7,6},{8,9},{9,8},{10,11... | collective-permute-start | bytes 393224 | tf_op jit(solution)/shard_map/ppermute | solution.py:22
  92.7 6.0 %collective-permute-start.13 = (bf16[2,256,128]{2,1,0:T(8,128)(2,1)S(1)}, bf16[2,256,128]{2,1,0:T(8,128)(2,1)S(1)}, u32[]{:S(2)}, u32[]{:S(2)}) collective-permute-start(bf16[2,256,128]{2,1,0:T(8,128)(2,1)S(1)} %add_convert_fusion.2), channel_id=1, source_target_pairs={{0,2},{1,3},{2,0},{3,1},{4,6},{5,7},{6,4},{7,5},{8,10},{9,11},{10,... | collective-permute-start | bytes 393224 | tf_op jit(solution)/shard_map/ppermute | solution.py:22
  93.5 12.7 %collective-permute-start.14 = (bf16[512,512]{1,0:T(8,128)(2,1)}, bf16[512,512]{1,0:T(8,128)(2,1)S(1)}, u32[]{:S(2)}, u32[]{:S(2)}) collective-permute-start(bf16[512,512]{1,0:T(8,128)(2,1)} %get-tuple-element.115.refs_0_), channel_id=1, source_target_pairs={{0,8},{1,5},{2,10},{3,7},{4,12},{5,1},{6,14},{7,3},{8,0},{9,13},{1... | collective-permute-start | bytes 1572872 | tf_op jit(solution)/shard_map/ppermute | solution.py:64
  105.3 14.9 %collective-permute-start.17 = (bf16[608,512]{1,0:T(8,128)(2,1)S(1)}, bf16[608,512]{1,0:T(8,128)(2,1)S(1)}, u32[]{:S(2)}, u32[]{:S(2)}) collective-permute-start(bf16[608,512]{1,0:T(8,128)(2,1)S(1)} %pad_maximum_fusion.4.refs_0_), channel_id=1, source_target_pairs={{0,4},{1,9},{2,6},{3,11},{4,0},{5,13},{6,2},{7,15},{8,12},{9,1},{1... | collective-permute-start | bytes 1867784 | tf_op jit(solution)/shard_map/ppermute | solution.py:64
  107.6 14.0 %collective-permute-start.16 = (bf16[256,512]{1,0:T(8,128)(2,1)S(1)}, bf16[256,512]{1,0:T(8,128)(2,1)S(1)}, u32[]{:S(2)}, u32[]{:S(2)}) collective-permute-start(bf16[256,512]{1,0:T(8,128)(2,1)S(1)} %get-tuple-element.125.refs_0_), channel_id=1, source_target_pairs={{0,16},{1,17},{2,18},{3,19},{4,20},{5,21},{6,22},{7,23},{8,24},{9,... | collective-permute-start | bytes 786440 | tf_op jit(solution)/shard_map/ppermute | solution.py:64
  108.4 7.6 %collective-permute-start.15 = (f32[2,3,512]{2,1,0:T(4,128)S(1)}, f32[2,3,512]{2,1,0:T(4,128)S(1)}, u32[]{:S(2)}, u32[]{:S(2)}) collective-permute-start(f32[2,3,512]{2,1,0:T(4,128)S(1)} %get-tuple-element.128), channel_id=1, source_target_pairs={{4,0},{8,4},{12,8},{16,12},{20,16},{24,20},{28,24},{5,1},{9,5},{13... | collective-permute-start | bytes 36872 | tf_op jit(solution)/shard_map/ppermute | solution.py:28
  121.6 16.6 %collective-permute-start.18 = (bf16[2,528,512]{2,1,0:T(8,128)(2,1)S(1)}, bf16[2,528,512]{2,1,0:T(8,128)(2,1)S(1)}, u32[]{:S(2)}, u32[]{:S(2)}) collective-permute-start(bf16[2,528,512]{2,1,0:T(8,128)(2,1)S(1)} %fusion.6), channel_id=1, source_target_pairs={{0,1},{1,0},{2,3},{3,2},{4,5},{5,4},{6,7},{7,6},{8,9},{9,8},{10,11... | collective-permute-start | bytes 3244040 | tf_op jit(solution)/shard_map/ppermute | solution.py:22
  121.7 11.7 %collective-permute-start.20 = (bf16[304,512]{1,0:T(8,128)(2,1)S(1)}, bf16[304,512]{1,0:T(8,128)(2,1)S(1)}, u32[]{:S(2)}, u32[]{:S(2)}) collective-permute-start(bf16[304,512]{1,0:T(8,128)(2,1)S(1)} %get-tuple-element.134.refs_0_), channel_id=1, source_target_pairs={{0,8},{1,5},{2,10},{3,7},{4,12},{5,1},{6,14},{7,3},{8,0},{9,13},{1... | collective-permute-start | bytes 933896 | tf_op jit(solution)/shard_map/ppermute | solution.py:64
  123.0 15.2 %collective-permute-start.19 = (bf16[256,512]{1,0:T(8,128)(2,1)S(1)}, bf16[256,512]{1,0:T(8,128)(2,1)S(1)}, u32[]{:S(2)}, u32[]{:S(2)}) collective-permute-start(bf16[256,512]{1,0:T(8,128)(2,1)S(1)} %advance.13.refs_0_), channel_id=1, source_target_pairs={{0,16},{1,17},{2,18},{3,19},{4,20},{5,21},{6,22},{7,23},{8,24},{9,... | collective-permute-start | bytes 786440 | tf_op jit(solution)/shard_map/ppermute | solution.py:64
  138.2 15.0 %copy-start.69 = (f32[256]{0:T(256)S(1)}, f32[256]{0:T(256)}, u32[]{:S(2)}) copy-start(f32[256]{0:T(256)} %copy-done.68) | copy-start | bytes 3076
  138.5 14.7 %collective-permute-start.21 = (bf16[2,528,256]{2,1,0:T(8,128)(2,1)S(1)}, bf16[2,528,256]{2,1,0:T(8,128)(2,1)S(1)}, u32[]{:S(2)}, u32[]{:S(2)}) collective-permute-start(bf16[2,528,256]{2,1,0:T(8,128)(2,1)S(1)} %get-tuple-element.146), channel_id=1, source_target_pairs={{0,2},{1,3},{2,0},{3,1},{4,6},{5,7},{6,4},{7,5},{8,10},{9,11},{10,... | collective-permute-start | bytes 1622024 | tf_op jit(solution)/shard_map/ppermute | solution.py:22
  139.3 15.3 %collective-permute-start.22 = (bf16[512,512]{1,0:T(8,128)(2,1)S(1)}, bf16[512,512]{1,0:T(8,128)(2,1)S(1)}, u32[]{:S(2)}, u32[]{:S(2)}) collective-permute-start(bf16[512,512]{1,0:T(8,128)(2,1)S(1)} %advance.15.refs_0_), channel_id=1, source_target_pairs={{0,8},{1,5},{2,10},{3,7},{4,12},{5,1},{6,14},{7,3},{8,0},{9,13},{1... | collective-permute-start | bytes 1572872 | tf_op jit(solution)/shard_map/ppermute | solution.py:64
  140.9 13.6 %collective-permute-start.23 = (bf16[176,512]{1,0:T(8,128)(2,1)S(1)}, bf16[176,512]{1,0:T(8,128)(2,1)S(1)}, u32[]{:S(2)}, u32[]{:S(2)}) collective-permute-start(bf16[176,512]{1,0:T(8,128)(2,1)S(1)} %get-tuple-element.142.refs_0_), channel_id=1, source_target_pairs={{0,16},{1,17},{2,18},{3,19},{4,20},{5,21},{6,22},{7,23},{8,24},{9,... | collective-permute-start | bytes 540680 | tf_op jit(solution)/shard_map/ppermute | solution.py:64
  154.6 9.6 %collective-permute-start.24 = (bf16[144,512]{1,0:T(8,128)(2,1)S(1)}, bf16[144,512]{1,0:T(8,128)(2,1)S(1)}, u32[]{:S(2)}, u32[]{:S(2)}) collective-permute-start(bf16[144,512]{1,0:T(8,128)(2,1)S(1)} %get-tuple-element.152.refs_0_), channel_id=1, source_target_pairs={{0,16},{1,17},{2,18},{3,19},{4,20},{5,21},{6,22},{7,23},{8,24},{9,... | collective-permute-start | bytes 442376 | tf_op jit(solution)/shard_map/ppermute | solution.py:64
  154.7 20.4 %collective-permute-start.27 = (bf16[1024,512]{1,0:T(8,128)(2,1)S(1)}, bf16[1024,512]{1,0:T(8,128)(2,1)S(1)}, u32[]{:S(2)}, u32[]{:S(2)}) collective-permute-start(bf16[1024,512]{1,0:T(8,128)(2,1)S(1)} %advance.17.refs_0_.refs_2_), channel_id=1, source_target_pairs={{0,4},{1,9},{2,6},{3,11},{4,0},{5,13},{6,2},{7,15},{8,12},{9,1},{1... | collective-permute-start | bytes 3145736 | tf_op jit(solution)/shard_map/ppermute | solution.py:64
  164.3 10.7 %collective-permute-start.25 = (bf16[320,512]{1,0:T(8,128)(2,1)S(1)}, bf16[320,512]{1,0:T(8,128)(2,1)S(1)}, u32[]{:S(2)}, u32[]{:S(2)}) collective-permute-start(bf16[320,512]{1,0:T(8,128)(2,1)S(1)} %advance.18.refs_0_), channel_id=1, source_target_pairs={{0,8},{1,5},{2,10},{3,7},{4,12},{5,1},{6,14},{7,3},{8,0},{9,13},{1... | collective-permute-start | bytes 983048 | tf_op jit(solution)/shard_map/ppermute | solution.py:64
  175.0 10.5 %collective-permute-start.26 = (bf16[624,512]{1,0:T(8,128)(2,1)S(1)}, bf16[624,512]{1,0:T(8,128)(2,1)S(1)}, u32[]{:S(2)}, u32[]{:S(2)}) collective-permute-start(bf16[624,512]{1,0:T(8,128)(2,1)S(1)} %advance.19.refs_0_.own_ref), channel_id=1, source_target_pairs={{0,4},{1,9},{2,6},{3,11},{4,0},{5,13},{6,2},{7,15},{8,12},{9,1},{1... | collective-permute-start | bytes 1916936 | tf_op jit(solution)/shard_map/ppermute | solution.py:64
  (86 other events, 414.0 us)

commit v3 on v2

--- a/solution.py
+++ b/solution.py
@@ -163,11 +163,11 @@
 
 
 class Sum:
-    def __init__(self, over, sent, flat, flags):
+    def __init__(self, over, sent, flat, flags, rows=None):
         self.over, self.flat, self.flags = over, flat, flags
         self.kept, self.rider, self.count = None, None, 0
-        self.rows = [block.shape[0] for block in sent]
-        self.message = jnp.concatenate([block.astype(BF16) for block in sent], axis=0)
+        self.rows = rows or [block.shape[0] for block in sent]
+        self.message = sent[0] if rows else jnp.concatenate([block.astype(BF16) for block in sent], axis=0)
         self.got = over.swap(self.message, 0)
 
     def next(self, *earlier):
@@ -217,7 +217,7 @@
     return pl.CostEstimate(flops=ops * work * 16, bytes_accessed=work * 2, transcendentals=work)
 
 
-def settle_kernel(names, layout, order_ref, *refs):
+def settle_kernel(names, layout, order_ref, *refs, starts=True, waits=True):
     parts, outs = refs[: len(layout)], refs[-2 - names : -2]
     wide, sems = refs[-2:]
     copies, at = [], 0
@@ -225,22 +225,23 @@
         size = count // blocks
         for b in range(blocks):
             source = order_ref[which + 2 + b]
-            rows = part[pl.ds(pl.multiple_of(offset + source * size, size), size), :].astype(F32)
             goal = pl.multiple_of((order_ref[which + first] + b) * size, size)
             ref = outs[out] if lead is None else outs[out].at[lead]
             if turned:
-                rows = jnp.transpose(rows)
-                spot = wide.at[at : at + rows.shape[0], 0:size]
+                spot = wide.at[at : at + part.shape[1], 0:size]
                 target = ref.at[:, pl.ds(goal, size)]
             else:
                 spot = wide.at[at : at + size, 0 : part.shape[1]]
                 target = ref.at[pl.ds(goal, size), :]
-            spot[...] = rows
-            at += rows.shape[0]
+            at += part.shape[1] if turned else size
             copies.append(pltpu.make_async_copy(spot, target, sems.at[len(copies)]))
-            copies[-1].start()
+            if starts:
+                rows = part[pl.ds(pl.multiple_of(offset + source * size, size), size), :].astype(F32)
+                spot[...] = jnp.transpose(rows) if turned else rows
+                copies[-1].start()
     for copy in copies:
-        copy.wait()
+        if waits:
+            copy.wait()
 
 
 def settle(orders, parts, layout, shapes, into=()):
@@ -260,8 +261,7 @@
     )(orders, *parts, *into)
 
 
-def deal_kernel(sizes, offset, order_ref, own_ref, late_ref, *refs):
-    outs, rows = refs[:-1], refs[-1]
+def deal_rows(sizes, offset, order_ref, own_ref, late_ref, outs, rows):
     blocks = order_ref.shape[0]
     size = rows.shape[0] // blocks
     for b in range(blocks):
@@ -279,56 +279,130 @@
         at += count
 
 
-def deal(order, own, late, offset, count, sizes):
+def finish_kernel(sizes, layout, offset, last, order_ref, flat_ref, own_ref, late_ref, into_ref, *refs):
+    out, small, (total, rows, wide, sems) = refs[0], refs[1:-4], refs[-4:]
+    settle_kernel(1, layout, order_ref, late_ref, out, wide, sems, waits=False)
+    deal_rows(sizes, offset, flat_ref, own_ref, late_ref, small, rows)
+    total[...] = own_ref[last : last + 16, :].astype(F32) + late_ref[last : last + 16, :].astype(F32)
+    settle_kernel(1, layout, order_ref, late_ref, out, wide, sems, starts=False)
+
+
+def finish(orders, flat_order, own, late, layout, offset, count, sizes, into):
     width = own.shape[1]
+    any_space, smem = pl.BlockSpec(memory_space=pl.ANY), pl.BlockSpec(memory_space=pltpu.SMEM)
+    shape = jax.ShapeDtypeStruct
     return pl.pallas_call(
-        functools.partial(deal_kernel, sizes, offset),
-        in_specs=[pl.BlockSpec(memory_space=pltpu.SMEM), VMEM, VMEM],
-        out_shape=[jax.ShapeDtypeStruct((count, width), F32) for count in sizes],
-        scratch_shapes=[pltpu.VMEM((2 * count, width), F32)],
-        compiler_params=pltpu.CompilerParams(vmem_limit_bytes=8 << 20),
-        name="deal",
-    )(order, own, late)
-
-
-def hop_kernel(got_ref, *refs):
-    kept, (row_ref, message), outs = refs[:2], refs[2:4], refs[4:]
-    lanes, length, width = kept[0].shape
+        functools.partial(finish_kernel, sizes, layout, offset, offset + count),
+        in_specs=[smem, smem, VMEM, VMEM, any_space],
+        out_specs=[any_space] + [VMEM] * (len(sizes) + 1),
+        out_shape=[shape(into.shape, F32)] + [shape((n, width), F32) for n in sizes] + [shape((16, width), F32)],
+        input_output_aliases={4: 0},
+        scratch_shapes=[
+            pltpu.VMEM((2 * count, width), F32),
+            pltpu.VMEM((layout[0][7], width), F32),
+            pltpu.SemaphoreType.DMA((layout[0][4],)),
+        ],
+        compiler_params=pltpu.CompilerParams(vmem_limit_bytes=16 << 20),
+        name="finish",
+    )(orders, flat_order, own, late, into)
+
+
+def hop_kernel(got_ref, out_ref, back_ref, row_ref, message, other, out_new, back_new, row_new):
+    lanes, length, width = out_ref.shape
     half = width // 2
     for l in range(lanes):
-        for m in range(2):
+        for m, (kept, new, sent) in enumerate(((out_ref, out_new, other), (back_ref, back_new, message))):
             o = slice(m * length, (m + 1) * length)
-            outs[m][l] = kept[m][l, :, :half] + got_ref[l, o, :half].astype(F32)
-            send = kept[m][l, :, half:] + got_ref[l, o, half:].astype(F32)
-            message[l, o, :] = send.astype(BF16)
+            new[l] = kept[l, :, :half] + got_ref[l, o, :half].astype(F32)
+            send = kept[l, :, half:] + got_ref[l, o, half:].astype(F32)
+            sent[l, :length, :] = send.astype(BF16)
         rows = got_ref[l, 2 * length :, :].astype(F32)
         came = jnp.concatenate([rows[r : r + 1] for r in range(2 * length // width)], axis=1)
         total = row_ref[l : l + 1, :] + came[:, :length] + came[:, length:]
-        outs[2][l : l + 1, :] = total
+        row_new[l : l + 1, :] = total
         high = total.astype(BF16).astype(F32)
         both = jnp.concatenate([high, total - high], axis=1)
         pieces = [both[:, at : at + half] for at in range(0, 2 * length, half)]
-        pieces.append(jnp.zeros((message.shape[1] - 2 * length - len(pieces), half), F32))
-        message[l, 2 * length :, :] = jnp.concatenate(pieces, axis=0).astype(BF16)
+        pieces.append(jnp.zeros((message.shape[1] - length - len(pieces), half), F32))
+        message[l, length:, :] = jnp.concatenate(pieces, axis=0).astype(BF16)
 
 
 def hop(got, out_kept, back_kept, row_dot):
     lanes, length, width = out_kept.shape
     shape = jax.ShapeDtypeStruct
     half = shape((lanes, length, width // 2), F32)
-    rows = 2 * length - (-(4 * length // width) // 16) * 16
+    rows = length - (-(4 * length // width) // 16) * 16
     return pl.pallas_call(
-        hop_kernel_entry,
+        hop_kernel,
         in_specs=[VMEM] * 4,
-        out_specs=[VMEM] * 4,
-        out_shape=[shape((lanes, rows, width // 2), BF16), half, half, shape(row_dot.shape, F32)],
+        out_specs=[VMEM] * 5,
+        out_shape=[
+            shape((lanes, rows, width // 2), BF16),
+            shape((lanes, length, width // 2), BF16),
+            half,
+            half,
+            shape(row_dot.shape, F32),
+        ],
         compiler_params=pltpu.CompilerParams(vmem_limit_bytes=12 << 20),
         name="hop",
     )(got, out_kept, back_kept, row_dot)
 
 
-def hop_kernel_entry(got_ref, out_ref, back_ref, row_ref, message, *outs):
-    hop_kernel(got_ref, out_ref, back_ref, row_ref, message, *outs)
+def product_kernel(flag_ref, left_ref, right_ref, more_ref, message):
+    half = message.shape[0] - more_ref.shape[0]
+    at = pl.multiple_of((1 - flag_ref[0]) * half, half)
+    for block in range(0, half, min(half, 256)):
+        size = min(half, 256)
+        cut = left_ref[:, pl.ds(pl.multiple_of(at + block, size), size)]
+        total = lax.dot_general(cut, right_ref[...], (((0,), (0,)), ((), ())), preferred_element_type=F32)
+        message[block : block + size, :] = total.astype(BF16)
+    message[half:, :] = more_ref[...].astype(BF16)
+
+
+def sent_product(flag, left, right, more):
+    half, width = left.shape[1] // 2, right.shape[1]
+    return pl.pallas_call(
+        product_kernel,
+        in_specs=[pl.BlockSpec(memory_space=pltpu.SMEM)] + [VMEM] * 3,
+        out_specs=VMEM,
+        out_shape=jax.ShapeDtypeStruct((half + more.shape[0], width), BF16),
+        compiler_params=pltpu.CompilerParams(vmem_limit_bytes=16 << 20),
+        name="sent_product",
+    )(flag, left, right, more)
+
+
+def pack_kernel(sizes, flag_ref, sent_ref, *refs):
+    parts, (message, kept, rows) = refs[:-3], refs[-3:]
+    at = 0
+    for part, size in zip(parts, sizes, strict=True):
+        if part.ndim == 3:
+            total = part[0]
+            for l in range(1, part.shape[0]):
+                total = total + part[l]
+            rows[at : at + size, :] = total
+        else:
+            rows[at : at + size, :] = part[0:size, :]
+        at += size
+    rows[at:, :] = jnp.zeros((rows.shape[0] - at, rows.shape[1]), F32)
+    half, first = kept.shape[0], sent_ref.shape[0]
+    up = flag_ref[0]
+    kept[...] = rows[pl.ds(pl.multiple_of(up * half, half), half), :]
+    message[0:first, :] = sent_ref[...]
+    message[first:, :] = rows[pl.ds(pl.multiple_of((1 - up) * half, half), half), :].astype(BF16)
+
+
+def pack(flag, sent, parts, sizes, half):
+    width = sent.shape[1]
+    shape = jax.ShapeDtypeStruct
+    return pl.pallas_call(
+        functools.partial(pack_kernel, sizes),
+        in_specs=[pl.BlockSpec(memory_space=pltpu.SMEM)] + [VMEM] * (1 + len(parts)),
+        out_specs=[VMEM] * 2,
+        out_shape=[shape((sent.shape[0] + half, width), BF16), shape((half, width), F32)],
+        scratch_shapes=[pltpu.VMEM((2 * half, width), F32)],
+        compiler_params=pltpu.CompilerParams(vmem_limit_bytes=8 << 20),
+        name="pack",
+    )(flag, sent, *parts)
 
 
 def iota(shape, dim):
@@ -809,8 +883,9 @@
     for k in list(grad_parts):
         grad_parts[k] = after(grad_parts[k], sent)
         grad_parts[k | 1] = swap(grad_parts[k], "mp", 1)
-    rim_pad = jnp.zeros((lane_count, rim_count, model_width), BF16)
-    normed_more = jnp.concatenate([after(normed, sent), rim_normed, rim_pad], axis=1)
+    normed_more = jnp.concatenate(
+        [after(normed, sent).reshape(-1, model_width), rim_normed.reshape(-1, model_width)], axis=0
+    )[None]
     grad_whole = jnp.concatenate(
         [
             sum(jnp.where(k == (mp_index ^ block), grad_parts[k], 0) for k in range(mp_size))
@@ -832,6 +907,9 @@
     message = jnp.concatenate([edge, spans], axis=1).astype(BF16)
     message = jnp.pad(message, ((0, 0), (0, -message.shape[1] % 8), (0, 0)))
     groups = lax.all_to_all(message, "seq", 0, 0, tiled=True)
+    projected, normed_more, w_back, w_spread = lax.optimization_barrier(
+        (projected, normed_more, w_back, w_spread)
+    )
     y, grad_read, last, states_all = scan_forward(
         low_rank, place, projected, decay_log, dt, source, grad_scan, groups
     )
@@ -859,7 +937,7 @@
     got = swap(sent, "mp", mp_bits[-1])
     grad_dt_w = jnp.einsum(
         "ltr,lte->re", projected.astype(BF16), after(grad_pre, sent), preferred_element_type=F32
-    )[:low_rank]
+    )
     grad_projected = after(sent, grad_dt_w).astype(F32) + got.astype(F32)
     grad_projected = grad_projected.astype(BF16)
     grad_mixed = pull * dt + grad_scan * skip_gain + jnp.einsum(
@@ -880,27 +958,26 @@
         )
     rim_sent = grad_padded[:, : tap_count - 1] * carry_mask
     rim_fill = jnp.zeros((lane_count, rim_count - (tap_count - 1), inner_width), F32)
-    rim_tail = jnp.zeros((lane_count, rim_count, inner_width), F32)
+    rim_rows = jnp.concatenate([rim_fill, rim_sent], axis=1).astype(BF16)
+    grad_main = grad_padded[:, tap_count - 1 :].astype(BF16)
     grad_more = jnp.concatenate(
-        [grad_padded[:, tap_count - 1 :], rim_fill, rim_sent, rim_tail], axis=1
-    ).astype(BF16)
+        [grad_main.reshape(-1, inner_width), rim_rows.reshape(-1, inner_width)], axis=0
+    )[None]
     grad_x_w = jnp.einsum("ltr,lte->re", grad_projected, after(mixed_low, rim_sent), preferred_element_type=F32)
-    small = jnp.concatenate(
-        [
-            grad_conv_w,
-            grad_conv_b[None],
-            jnp.sum(grad_slope, axis=(0, 1))[None],
-            jnp.sum(grad_scan * mixed, axis=(0, 1))[None],
-            jnp.sum(grad_log, axis=0),
-            grad_dt_w,
-            grad_x_w[: low_rank + 2 * state_count],
-        ],
-        axis=0,
-    )
-    small = jnp.pad(small, ((0, -small.shape[0] % (8 * seq_size)), (0, 0)))
-    small_kept, small_sent = over.halves(small, 0)
+    small = [
+        (grad_conv_w, tap_count),
+        (grad_conv_b[None], 1),
+        (jnp.sum(grad_slope, axis=(0, 1))[None], 1),
+        (jnp.sum(grad_scan * mixed, axis=(0, 1))[None], 1),
+        (grad_log, state_count),
+        (grad_dt_w, low_rank),
+        (grad_x_w, low_rank + 2 * state_count),
+    ]
+    sizes = [size for _, size in small]
+    small_half = -(-sum(sizes) // (8 * seq_size)) * 4 * seq_size
     inner_sent = over.sent(normed_more, after(grad_more, grad_x_w))
-    sum_inner = Sum(over, [inner_sent, small_sent], (False, True), flags)
+    inner_sent, small_kept = pack(flags[0], inner_sent, [part for part, _ in small], sizes, small_half)
+    sum_inner = Sum(over, [inner_sent], (False, True), flags, [half_width, small_half])
     step = sum_first.next(sum_inner.message)
     sum_inner.kept = [over.kept(normed_more, after(grad_more, step)), small_kept]
     rim_back = from_behind(after(rim_sent, step), "seq", -1)
@@ -938,17 +1015,22 @@
     step = sum_inner.next(message)
     step = sum_first.next(step)
     got = swap(after(message, step), "mp", 1)
+    far = mp_bits[-1]
     for bit in mp_bits[:-1]:
         if bit == 1:
             step = sum_inner.next(message)
             step = sum_first.next(step)
-        message, out_kept, back_kept, row_dot = hop(after(got, step), out_kept, back_kept, row_dot)
-        got = swap(message, "mp", 2 * bit)
+        message, other, out_kept, back_kept, row_dot = hop(after(got, step), out_kept, back_kept, row_dot)
+        if 2 * bit == far:
+            got = swap(message, "mp", far)
+            out_got = swap(after(other, message), "mp", far)
+        else:
+            message = jnp.concatenate([other, message], axis=1)
+            got = swap(message, "mp", 2 * bit)
     got = after(got, message)
-    rows = got[:, 2 * length :][:, : 2 * length // shard_width].reshape(lane_count, 2 * length).astype(F32)
+    rows = got[:, length:][:, : 2 * length // shard_width].reshape(lane_count, 2 * length).astype(F32)
     row_dot = row_dot + rows[:, :length] + rows[:, length:]
-    grad_own = back_kept + got[:, length : 2 * length].astype(F32)
-    output = inputs + (out_kept + got[:, :length].astype(F32))
+    grad_own = back_kept + got[:, :length].astype(F32)
     unit_own = inputs * inv_rms
     grad_gain = jnp.sum(grad_own * unit_own, axis=(0, 1))
     input_grad = output_grad + inv_rms * (
@@ -958,9 +1040,10 @@
     sum_inner.rider = jnp.pad(grad_gain, ((0, -grad_gain.shape[0] % 16), (0, 0)))
     step = sum_inner.next(grad_gain)
     step = sum_first.next(step)
-    output, input_grad = after(output, step), after(input_grad, step)
+    input_grad = after(input_grad, step)
     step = sum_inner.next(step)
-    step = sum_inner.next(step)
+    output = inputs + (out_kept + after(out_got, step).astype(F32))
+    step = sum_inner.next(output)
     sum_first.run_out()
     second = 2 + halves
     in_shape, out_shape = (2, model_width, inner_width), out_weight.shape
@@ -976,18 +1059,17 @@
         up = over.own(0) == 1
         rows = [jnp.where(up, rows[1], rows[0]), jnp.where(up, rows[0], rows[1])]
         out_w = jnp.concatenate(rows, axis=0).astype(F32).T
-    sizes = [tap_count, 1, 1, 1, state_count, low_rank, low_rank + 2 * state_count]
     sum_inner.run_out()
     ends = (sum_inner.message, sum_inner.got)
     in_w = settle(orders, ends[:1], [(0, 0, 0, 0, halves, False, 0, half)], [in_shape], [in_w])
-    parts = deal(flat_order, *ends, half, small.shape[0] // 2, sizes)
-    (in_w,) = settle(orders, ends[1:], [(0, 0, 0, 1, halves, False, 0, half)], [in_shape], in_w)
-    last = half + small.shape[0] // 2
-    grad_gain = ends[0][last : last + 1].astype(F32) + ends[1][last : last + 1].astype(F32)
+    count = small_half
+    in_w, *parts, grad_gain = finish(
+        orders, flat_order, *ends, [(0, 0, 0, 1, halves, False, 0, half)], half, count, sizes, in_w[0]
+    )
     return (
         output,
         input_grad,
-        grad_gain.reshape(-1)[:shard_width],
+        grad_gain[0, :shard_width],
         in_w,
         parts[0],
         parts[1][0],

time: 190 us -> 177 us (0.932)
  Pallas kernels: 40.3 us -> 36 us
  local copies, waits for them, and re-layouts: 13.7 us -> 10.5 us
  other arithmetic: 19.6 us -> 16.5 us
    ppermute x12, starting transfers between devices: 14.6 us -> 10.5 us  [swap(): return lax.ppermute(block, ('seq', 'mp'), route)]
    ppermute x14 -> x15, starting transfers between devices: 9.23 us -> 12.9 us  [swap(): return lax.ppermute(block, axis, [(i, i ^ bit) for i in range(devices)])]
    pallas_call x10, Pallas kernels: 4.4 us -> 0.73 us  [advance(): pl.pallas_call(functools.partial(advance_kernel, {'inputs': len(inputs),...]
    ppermute x14 -> x15, waiting for transfers between devices: 15.6 us -> 12 us  [swap(): return lax.ppermute(block, axis, [(i, i ^ bit) for i in range(devices)])]
    ppermute x12, waiting for transfers between devices: 37.9 us -> 41.1 us  [swap(): return lax.ppermute(block, ('seq', 'mp'), route)]
    concatenate x2 -> x0, other arithmetic: 2.32 us -> none  [the longest x1 1.24 us: per_device(): jnp.concatenate([after(normed, sent), rim_normed, rim_pad], axis=1)]
    unnamed x179 -> x115, local copies, waits for them, and re-layouts: 5.57 us -> 3.73 us
    pallas_call x3 -> x2, Pallas kernels: 5.84 us -> 4.28 us  [settle(): pl.pallas_call(functools.partial(settle_kernel, len(shapes), layout), in_...]
  transfers between devices with their start and end apart: 29 -> 30, of which waited for: 13 -> 20; matrix products, arithmetic and copies ran while one was open for 18% -> 17% of each run, Pallas kernels for 10% -> 9%
where the time goes in v3:
time: 177 us
  waiting for transfers between devices  64.8 us (37%)
  Pallas kernels  36 us (20%)
  starting transfers between devices  34.2 us (19%)
  other arithmetic  16.5 us (9%)
  matrix products  13 us (7%)
  local copies, waits for them, and re-layouts  10.5 us (6%)
  between operations  1.8 us (1%)
    ppermute x12, waiting for transfers between devices, swap(): return lax.ppermute(block, ('seq', 'mp'), route)  41.1 us
    ppermute x15, starting transfers between devices, swap(): return lax.ppermute(block, axis, [(i, i ^ bit) for i in range(devices)])  12.9 us
    ppermute x15, waiting for transfers between devices, swap(): return lax.ppermute(block, axis, [(i, i ^ bit) for i in range(devices)])  12 us
    pallas_call x1, Pallas kernels, scan_backward(): pl.pallas_call(functools.partial(backward_kernel, low_rank, lanes), grid=...  11 us
    ppermute x12, starting transfers between devices, swap(): return lax.ppermute(block, ('seq', 'mp'), route)  10.5 us
    pallas_call x1, Pallas kernels, scan_ends(): pl.pallas_call(functools.partial(ends_kernel, low_rank), grid=(lanes,), i...  9 us
    pallas_call x1, Pallas kernels, scan_forward(): pl.pallas_call(functools.partial(forward_kernel, low_rank, lanes), grid=(...  8.27 us
    ppermute x2, waiting for transfers between devices, from_behind(): return lax.ppermute(block, axis, route)  6.87 us
  transfers between devices with their start and end apart: 30, of which 20 were waited for; matrix products, arithmetic and copies ran while one was open for 17% of the time, Pallas kernels for 9%

profile of v3, /device:TPU:0, one launch (start us, length us, event | category | flops | bytes accessed | tf_op | source)
XLA Modules:
  0.0 176.7 jit_solution(881807195393857311)
XLA Ops:
  2.0 3.0 %collective-permute-start.1 = (bf16[2,256,256]{2,1,0:T(8,128)(2,1)S(1)}, bf16[2,256,256]{2,1,0:T(8,128)(2,1)S(1)}, u32[]{:S(2)}, u32[]{:S(2)}) collective-permute-start(bf16[2,256,256]{2,1,0:T(8,128)(2,1)S(1)} %get-tuple-element.228), channel_id=1, source_target_pairs={{0,2},{1,3},{2,0},{3,1},{4,6},{5,7},{6,4},{7,5},{8,10},{9,11},{10,... | collective-permute-start | bytes 786440 | tf_op jit(solution)/shard_map/ppermute | solution.py:22
  7.7 2.4 %dynamic-slice_convert_fusion.2 = (bf16[2,256,512]{2,1,0:T(8,128)(2,1)S(1)}, bf16[2,256,512]{2,1,0:T(8,128)(2,1)S(1)}, bf16[2,256,512]{2,1,0:T(8,128)(2,1)S(1)}, bf16[2,256,512]{2,1,0:T(8,128)(2,1)S(1)}) fusion(f32[2,1024,512]{2,1,0:T(8,128)} %param.16, s32[]{:T(128)S(6)} %select_n.191, s32[]{:T(128)S(6)} %select_n.190, s32[]{:T(128)S(6)} %select_n.193, ...), kind=kLoop, calls=%fused_computation.62 | loop fusion | bytes 4194320 | tf_op jit(solution)/shard_map/convert.14
  10.2 2.2 %pad_maximum_fusion = (bf16[2,1024,512]{2,1,0:T(8,128)(2,1)}, bf16[2,1024,512]{2,1,0:T(8,128)(2,1)}) fusion(bf16[2,256,512]{2,1,0:T(8,128)(2,1)S(1)} %get-tuple-element.208, bf16[2,256,512]{2,1,0:T(8,128)(2,1)S(1)} %get-tuple-element.207, bf16[2,256,512]{2,1,0:T(8,128)(2,1)S(1)} %get-tuple-element.206, bf16[2,256,512]{2,1,0:T(8,128)(2,1)S(1)} %get-tuple-element.209), kind=kLoop, calls=%fused_computation | loop fusion | flops 14680064 | bytes 6291456 | tf_op jit(solution)/shard_map/concatenate | solution.py:833
  14.2 1.9 %collective-permute-start.6 = (bf16[2,256,256]{2,1,0:T(8,128)(2,1)S(1)}, bf16[2,256,256]{2,1,0:T(8,128)(2,1)S(1)}, u32[]{:S(2)}, u32[]{:S(2)}) collective-permute-start(bf16[2,256,256]{2,1,0:T(8,128)(2,1)S(1)} %convert_element_type.205), channel_id=1, source_target_pairs={{0,2},{1,3},{2,0},{3,1},{4,6},{5,7},{6,4},{7,5},{8,10},{9,11},{10,... | collective-permute-start | bytes 786440 | tf_op jit(solution)/shard_map/ppermute | solution.py:22
  16.5 3.4 %collective-permute-start.5 = (bf16[2,8,1024]{2,1,0:T(8,128)(2,1)S(1)}, bf16[2,8,1024]{2,1,0:T(8,128)(2,1)S(1)}, u32[]{:S(2)}, u32[]{:S(2)}) collective-permute-start(bf16[2,8,1024]{2,1,0:T(8,128)(2,1)S(1)} %slice.107), channel_id=1, source_target_pairs={{0,4},{4,8},{8,12},{12,16},{16,20},{20,24},{24,28},{1,5},{5,9},{9,... | collective-permute-start | bytes 98312 | tf_op jit(solution)/shard_map/ppermute | solution.py:28
  23.0 1.6 fusion.74
  27.8 1.9 %fusion.10 = f32[2,256,512]{2,1,0:T(8,128)S(1)} fusion(bf16[2,256,1024]{2,1,0:T(8,128)(2,1)S(1)} %multiply_convert_fusion, bf16[2,1024,512]{2,1,0:T(8,128)(2,1)} %get-tuple-element.217), kind=kOutput, calls=%fused_computation.34 | convolution fusion | flops 536870912 | bytes 3145728 | tf_op jit(solution)/shard_map/ltd,de->lte/dot_general | solution.py:869
  29.7 1.8 %collective-permute-start.8 = (bf16[2,256,128]{2,1,0:T(8,128)(2,1)S(1)}, bf16[2,256,128]{2,1,0:T(8,128)(2,1)S(1)}, u32[]{:S(2)}, u32[]{:S(2)}) collective-permute-start(bf16[2,256,128]{2,1,0:T(8,128)(2,1)S(1)} %add_convert_fusion.4.sent_ref), channel_id=1, source_target_pairs={{0,2},{1,3},{2,0},{3,1},{4,6},{5,7},{6,4},{7,5},{8,10},{9,11},{10,... | collective-permute-start | bytes 393224 | tf_op jit(solution)/shard_map/ppermute | solution.py:22
  31.9 1.9 %multiply_reduce_fusion = (f32[512]{0:T(512)S(1)}, f32[2,256,512]{2,1,0:T(8,128)S(1)}, f32[2,256,512]{2,1,0:T(8,128)}) fusion(f32[2,256,512]{2,1,0:T(8,128)S(1)} %get-tuple-element.204.mixed_ref, f32[2,256,512]{2,1,0:T(8,128)S(1)} %fusion.10, f32[512,1024]{1,0:T(8,128)S(1)} %copy-done.33, bf16[2,256,256]{2,1,0:T(8,128)(2,1)S(1)} %get-tuple-element.225, ...), kind=kOutput, calls=%fused_computation.44 | convolution fusion | flops 543424000 | bytes 7342080 | tf_op jit(solution)/shard_map/ltd,ed->lte/dot_general | solution.py:896
  35.3 9.0 %scan_ends.1 = (f32[2,16,512]{2,1,0:T(8,128)S(1)}, f32[2,16,512]{2,1,0:T(8,128)S(1)}, f32[2,1,512]{2,1,0:T(1,128)S(1)}, f32[2,256,512]{2,1,0:T(8,128)}, f32[2,25...) custom-call(bf16[2,256,128]{2,1,0:T(8,128)(2,1)S(1)} %add_convert_fusion.4.sent_ref, ...), custom_call_target="tpu_custom_call" | custom-call | flops 536870912 | bytes 8388608 | tf_op jit(solution)/shard_map/scan_ends/pallas_call | solution.py:549
  45.4 6.0 %all-to-all-start = ((bf16[8,40,512]{2,1,0:T(8,128)(2,1)}), bf16[8,40,512]{2,1,0:T(8,128)(2,1)}, u32[]{:S(2)}, u32[]{:S(2)}) async-start(bf16[8,40,512]{2,1,0:T(8,128)(2,1)} %fusion.44), calls=%async_computation | async-start | bytes 655360 | tf_op jit(solution)/shard_map/all_to_all | solution.py:909
  51.4 1.7 dynamic-slice_convert_fusion.7
  56.5 4.8 %all-to-all-done.got_ref = bf16[8,40,512]{2,1,0:T(8,128)(2,1)} async-done(((bf16[8,40,512]{2,1,0:T(8,128)(2,1)}), bf16[8,40,512]{2,1,0:T(8,128)(2,1)}, u32[]{:S(2)}, u32[]{:S(2)}) %all-to-all-start) | async-done | bytes 327712 | tf_op jit(solution)/shard_map/all_to_all | solution.py:909
  62.5 8.3 %scan_forward.1 = (f32[2,256,512]{2,1,0:T(8,128)S(1)}, f32[2,256,128]{2,1,0:T(8,128)S(1)}, f32[2,16,512]{2,1,0:T(8,128)S(1)}, bf16[2,4096,512]{2,1,0:T(8,128)(2,1)S(1)}) custom-call(s32[3]{0:T(128)S(1)} %pad_add_fusion.1.place_ref, f32[2,256,128]{2,1,0:T(8,128)S(1)} %get-tuple-element.108.proj_ref, f32[16,512]{1,0:T(8,128)S(1)} %copy-done.3, ...), custom_call_target="tpu_custom_call" | custom-call | flops 536870912 | bytes 8388608 | tf_op jit(solution)/shard_map/scan_forward/pallas_call | solution.py:664
  75.6 11.0 %scan_backward.1 = (f32[2,256,512]{2,1,0:T(8,128)S(1)}, f32[2,256,512]{2,1,0:T(8,128)S(1)}, f32[2,256,128]{2,1,0:T(8,128)S(1)}, f32[2,16,512]{2,1,0:T(8,128)S(1)}) custom-call(f32[2,256,128]{2,1,0:T(8,128)S(1)} %get-tuple-element.108.proj_ref, f32[16,512]{1,0:T(8,128)S(1)} %copy-done.3, f32[2,256,512]{2,1,0:T(8,128)S(1)} %copy-done, ...), custom_call_target="tpu_custom_call" | custom-call | flops 805306368 | bytes 8388608 | tf_op jit(solution)/shard_map/scan_backward/pallas_call | solution.py:779
  91.1 3.6 %collective-permute-done.13 = bf16[2,256,128]{2,1,0:T(8,128)(2,1)S(1)} collective-permute-done((bf16[2,256,128]{2,1,0:T(8,128)(2,1)S(1)}, bf16[2,256,128]{2,1,0:T(8,128)(2,1)S(1)}, u32[]{:S(2)}, u32[]{:S(2)}) %collective-permute-start.13) | collective-permute-done | bytes 131104 | tf_op jit(solution)/shard_map/ppermute | solution.py:22
  103.5 6.1 %collective-permute-done.15 = f32[2,3,512]{2,1,0:T(4,128)S(1)} collective-permute-done((f32[2,3,512]{2,1,0:T(4,128)S(1)}, f32[2,3,512]{2,1,0:T(4,128)S(1)}, u32[]{:S(2)}, u32[]{:S(2)}) %collective-permute-start.15) | collective-permute-done | bytes 12320 | tf_op jit(solution)/shard_map/ppermute | solution.py:28
  112.2 1.8 collective-permute-done.16.refs_1_
  115.0 1.6 collective-permute-start.19
  116.7 7.9 %collective-permute-done.20.refs_1_ = bf16[304,512]{1,0:T(8,128)(2,1)S(1)} collective-permute-done((bf16[304,512]{1,0:T(8,128)(2,1)S(1)}, bf16[304,512]{1,0:T(8,128)(2,1)S(1)}, u32[]{:S(2)}, u32[]{:S(2)}) %collective-permute-start.20) | collective-permute-done | bytes 311328 | tf_op jit(solution)/shard_map/ppermute | solution.py:64
  124.6 5.4 %collective-permute-done.19.refs_1_ = bf16[256,512]{1,0:T(8,128)(2,1)S(1)} collective-permute-done((bf16[256,512]{1,0:T(8,128)(2,1)S(1)}, bf16[256,512]{1,0:T(8,128)(2,1)S(1)}, u32[]{:S(2)}, u32[]{:S(2)}) %collective-permute-start.19) | collective-permute-done | bytes 262176 | tf_op jit(solution)/shard_map/ppermute | solution.py:64
  130.3 2.2 %collective-permute-start.23 = (bf16[2,272,256]{2,1,0:T(8,128)(2,1)S(1)}, bf16[2,272,256]{2,1,0:T(8,128)(2,1)S(1)}, u32[]{:S(2)}, u32[]{:S(2)}) collective-permute-start(bf16[2,272,256]{2,1,0:T(8,128)(2,1)S(1)} %get-tuple-element.163), channel_id=1, source_target_pairs={{0,2},{1,3},{2,0},{3,1},{4,6},{5,7},{6,4},{7,5},{8,10},{9,11},{10,... | collective-permute-start | bytes 835592 | tf_op jit(solution)/shard_map/ppermute | solution.py:22
  132.5 3.0 %collective-permute-start.25 = (bf16[512,512]{1,0:T(8,128)(2,1)S(1)}, bf16[512,512]{1,0:T(8,128)(2,1)S(1)}, u32[]{:S(2)}, u32[]{:S(2)}) collective-permute-start(bf16[512,512]{1,0:T(8,128)(2,1)S(1)} %advance.15.refs_0_), channel_id=1, source_target_pairs={{0,8},{1,5},{2,10},{3,7},{4,12},{5,1},{6,14},{7,3},{8,0},{9,13},{1... | collective-permute-start | bytes 1572872 | tf_op jit(solution)/shard_map/ppermute | solution.py:64
  136.5 3.6 %collective-permute-done.23 = bf16[2,272,256]{2,1,0:T(8,128)(2,1)S(1)} collective-permute-done((bf16[2,272,256]{2,1,0:T(8,128)(2,1)S(1)}, bf16[2,272,256]{2,1,0:T(8,128)(2,1)S(1)}, u32[]{:S(2)}, u32[]{:S(2)}) %collective-permute-start.23) | collective-permute-done | bytes 278560 | tf_op jit(solution)/shard_map/ppermute | solution.py:22
  141.2 2.2 %collective-permute-done.22.refs_1_ = bf16[176,512]{1,0:T(8,128)(2,1)S(1)} collective-permute-done((bf16[176,512]{1,0:T(8,128)(2,1)S(1)}, bf16[176,512]{1,0:T(8,128)(2,1)S(1)}, u32[]{:S(2)}, u32[]{:S(2)}) %collective-permute-start.22) | collective-permute-done | bytes 180256 | tf_op jit(solution)/shard_map/ppermute | solution.py:64
  143.5 3.0 %collective-permute-done.25.refs_1_ = bf16[512,512]{1,0:T(8,128)(2,1)S(1)} collective-permute-done((bf16[512,512]{1,0:T(8,128)(2,1)S(1)}, bf16[512,512]{1,0:T(8,128)(2,1)S(1)}, u32[]{:S(2)}, u32[]{:S(2)}) %collective-permute-start.25) | collective-permute-done | bytes 524320 | tf_op jit(solution)/shard_map/ppermute | solution.py:64
  146.6 1.7 collective-permute-start.28
  148.2 4.4 %collective-permute-done.24.refs_1_ = bf16[144,512]{1,0:T(8,128)(2,1)S(1)} collective-permute-done((bf16[144,512]{1,0:T(8,128)(2,1)S(1)}, bf16[144,512]{1,0:T(8,128)(2,1)S(1)}, u32[]{:S(2)}, u32[]{:S(2)}) %collective-permute-start.24) | collective-permute-done | bytes 147488 | tf_op jit(solution)/shard_map/ppermute | solution.py:64
  153.6 9.7 %collective-permute-done.26.refs_1_ = bf16[320,512]{1,0:T(8,128)(2,1)S(1)} collective-permute-done((bf16[320,512]{1,0:T(8,128)(2,1)S(1)}, bf16[320,512]{1,0:T(8,128)(2,1)S(1)}, u32[]{:S(2)}, u32[]{:S(2)}) %collective-permute-start.26) | collective-permute-done | bytes 327712 | tf_op jit(solution)/shard_map/ppermute | solution.py:64
  164.9 2.7 %settle.2 = (f32[2,1024,512]{2,1,0:T(8,128)}, f32[512,1024]{1,0:T(8,128)}) custom-call(s32[12]{0:T(128)S(1)} %concatenate.56.order_ref, bf16[1024,512]{1,0:T(8,128)(2,1)S(1)} %advance.17.refs_0_.refs_2_, bf16[1024,512]{1,0:T(8,128)(2,1)S(1)} %collective-permute-done.28.refs_1_.refs_3_, bf16[1024,512]{1,0:T(8,128)(2,1)S(1)} %advance.17.refs_0_.refs_2_, ...), custom_call_target="tpu_custom_call" | custom-call | tf_op jit(solution)/shard_map/settle/pallas_call | solution.py:252
  169.2 4.6 %collective-permute-done.27.late_ref = bf16[624,512]{1,0:T(8,128)(2,1)S(1)} collective-permute-done((bf16[624,512]{1,0:T(8,128)(2,1)S(1)}, bf16[624,512]{1,0:T(8,128)(2,1)S(1)}, u32[]{:S(2)}, u32[]{:S(2)}) %collective-permute-start.27) | collective-permute-done | bytes 639008 | tf_op jit(solution)/shard_map/ppermute | solution.py:64
  173.8 2.3 %finish.1 = (f32[2,1024,512]{2,1,0:T(8,128)}, f32[4,512]{1,0:T(4,128)}, f32[1,512]{1,0:T(1,128)}, f32[1,512]{1,0:T(1,128)}, f32[1,512]{1,0:T(1,128)}, /*index=5*...) custom-call(s32[12]{0:T(128)S(1)} %concatenate.56.order_ref, ...), custom_call_target="tpu_custom_call", output_to_operand_aliasing={{0}: (4, {})} | custom-call | tf_op jit(solution)/shard_map/finish/pallas_call | solution.py:294
  (239 shorter events, 48.1 us)
Async XLA Ops:
  2.0 10.8 %collective-permute-start.1 = (bf16[2,256,256]{2,1,0:T(8,128)(2,1)S(1)}, bf16[2,256,256]{2,1,0:T(8,128)(2,1)S(1)}, u32[]{:S(2)}, u32[]{:S(2)}) collective-permute-start(bf16[2,256,256]{2,1,0:T(8,128)(2,1)S(1)} %get-tuple-element.228), channel_id=1, source_target_pairs={{0,2},{1,3},{2,0},{3,1},{4,6},{5,7},{6,4},{7,5},{8,10},{9,11},{10,... | collective-permute-start | bytes 786440 | tf_op jit(solution)/shard_map/ppermute | solution.py:22
  5.1 11.1 %collective-permute-start = (bf16[2,256,256]{2,1,0:T(8,128)(2,1)S(1)}, bf16[2,256,256]{2,1,0:T(8,128)(2,1)S(1)}, u32[]{:S(2)}, u32[]{:S(2)}) collective-permute-start(bf16[2,256,256]{2,1,0:T(8,128)(2,1)S(1)} %get-tuple-element.228), channel_id=1, source_target_pairs={{0,1},{1,0},{2,3},{3,2},{4,5},{5,4},{6,7},{7,6},{8,9},{9,8},{10,11... | collective-permute-start | bytes 786440 | tf_op jit(solution)/shard_map/ppermute | solution.py:22
  5.1 7.3 %collective-permute-start.3 = (f32[2,256]{1,0:T(2,128)S(1)}, f32[2,256]{1,0:T(2,128)S(1)}, u32[]{:S(2)}, u32[]{:S(2)}) collective-permute-start(f32[2,256]{1,0:T(2,128)S(1)} %get-tuple-element.227), channel_id=1, source_target_pairs={{0,2},{1,3},{2,0},{3,1},{4,6},{5,7},{6,4},{7,5},{8,10},{9,11},{10,... | collective-permute-start | bytes 6152 | tf_op jit(solution)/shard_map/ppermute | solution.py:22
  5.9 38.5 %copy-start.51 = (f32[2]{0:T(128)}, f32[2]{0:T(128)S(1)}, u32[]{:S(2)}) copy-start(f32[2]{0:T(128)S(1)} %get-tuple-element.238) | copy-start | bytes 28
  6.7 16.2 %copy-start.43 = (f32[1,512]{1,0:T(1,128)}, f32[1,512]{1,0:T(1,128)S(1)}, u32[]{:S(2)}) copy-start(f32[1,512]{1,0:T(1,128)S(1)} %get-tuple-element.229) | copy-start | bytes 6148
  12.4 1.8 collective-permute-start.4
  12.9 3.3 %collective-permute-start.2 = (bf16[2,256,256]{2,1,0:T(8,128)(2,1)S(1)}, bf16[2,256,256]{2,1,0:T(8,128)(2,1)S(1)}, u32[]{:S(2)}, u32[]{:S(2)}) collective-permute-start(bf16[2,256,256]{2,1,0:T(8,128)(2,1)S(1)} %collective-permute-done.1), channel_id=1, source_target_pairs={{0,1},{1,0},{2,3},{3,2},{4,5},{5,4},{6,7},{7,6},{8,9},{9,8},{10,11... | collective-permute-start | bytes 786440 | tf_op jit(solution)/shard_map/ppermute | solution.py:22
  14.2 8.6 %collective-permute-start.6 = (bf16[2,256,256]{2,1,0:T(8,128)(2,1)S(1)}, bf16[2,256,256]{2,1,0:T(8,128)(2,1)S(1)}, u32[]{:S(2)}, u32[]{:S(2)}) collective-permute-start(bf16[2,256,256]{2,1,0:T(8,128)(2,1)S(1)} %convert_element_type.205), channel_id=1, source_target_pairs={{0,2},{1,3},{2,0},{3,1},{4,6},{5,7},{6,4},{7,5},{8,10},{9,11},{10,... | collective-permute-start | bytes 786440 | tf_op jit(solution)/shard_map/ppermute | solution.py:22
  16.5 5.0 %collective-permute-start.5 = (bf16[2,8,1024]{2,1,0:T(8,128)(2,1)S(1)}, bf16[2,8,1024]{2,1,0:T(8,128)(2,1)S(1)}, u32[]{:S(2)}, u32[]{:S(2)}) collective-permute-start(bf16[2,8,1024]{2,1,0:T(8,128)(2,1)S(1)} %slice.107), channel_id=1, source_target_pairs={{0,4},{4,8},{8,12},{12,16},{16,20},{20,24},{24,28},{1,5},{5,9},{9,... | collective-permute-start | bytes 98312 | tf_op jit(solution)/shard_map/ppermute | solution.py:28
  25.7 1.4 collective-permute-start.7
  27.2 4.3 %collective-permute-start.9 = (bf16[2,256,256]{2,1,0:T(8,128)(2,1)S(1)}, bf16[2,256,256]{2,1,0:T(8,128)(2,1)S(1)}, u32[]{:S(2)}, u32[]{:S(2)}) collective-permute-start(bf16[2,256,256]{2,1,0:T(8,128)(2,1)S(1)} %convert_element_type.205), channel_id=1, source_target_pairs={{0,1},{1,0},{2,3},{3,2},{4,5},{5,4},{6,7},{7,6},{8,9},{9,8},{10,11... | collective-permute-start | bytes 786440 | tf_op jit(solution)/shard_map/ppermute | solution.py:22
  27.4 4.1 %collective-permute-start.10 = (bf16[2,256,256]{2,1,0:T(8,128)(2,1)S(1)}, bf16[2,256,256]{2,1,0:T(8,128)(2,1)S(1)}, u32[]{:S(2)}, u32[]{:S(2)}) collective-permute-start(bf16[2,256,256]{2,1,0:T(8,128)(2,1)S(1)} %collective-permute-done.6), channel_id=1, source_target_pairs={{0,1},{1,0},{2,3},{3,2},{4,5},{5,4},{6,7},{7,6},{8,9},{9,8},{10,11... | collective-permute-start | bytes 786440 | tf_op jit(solution)/shard_map/ppermute | solution.py:22
  29.7 5.6 %collective-permute-start.8 = (bf16[2,256,128]{2,1,0:T(8,128)(2,1)S(1)}, bf16[2,256,128]{2,1,0:T(8,128)(2,1)S(1)}, u32[]{:S(2)}, u32[]{:S(2)}) collective-permute-start(bf16[2,256,128]{2,1,0:T(8,128)(2,1)S(1)} %add_convert_fusion.4.sent_ref), channel_id=1, source_target_pairs={{0,2},{1,3},{2,0},{3,1},{4,6},{5,7},{6,4},{7,5},{8,10},{9,11},{10,... | collective-permute-start | bytes 393224 | tf_op jit(solution)/shard_map/ppermute | solution.py:22
  45.4 15.9 %all-to-all-start = ((bf16[8,40,512]{2,1,0:T(8,128)(2,1)}), bf16[8,40,512]{2,1,0:T(8,128)(2,1)}, u32[]{:S(2)}, u32[]{:S(2)}) async-start(bf16[8,40,512]{2,1,0:T(8,128)(2,1)} %fusion.44), calls=%async_computation | async-start | bytes 655360 | tf_op jit(solution)/shard_map/all_to_all | solution.py:909
  73.1 14.9 %collective-permute-start.12 = (bf16[1024,512]{1,0:T(8,128)(2,1)S(1)}, bf16[1024,512]{1,0:T(8,128)(2,1)S(1)}, u32[]{:S(2)}, u32[]{:S(2)}) collective-permute-start(bf16[1024,512]{1,0:T(8,128)(2,1)S(1)} %pad_maximum_fusion.7.refs_0_), channel_id=1, source_target_pairs={{0,4},{1,9},{2,6},{3,11},{4,0},{5,13},{6,2},{7,15},{8,12},{9,1},{1... | collective-permute-start | bytes 3145736 | tf_op jit(solution)/shard_map/ppermute | solution.py:64
  87.6 1.4 collective-permute-start.11
  89.1 5.6 %collective-permute-start.13 = (bf16[2,256,128]{2,1,0:T(8,128)(2,1)S(1)}, bf16[2,256,128]{2,1,0:T(8,128)(2,1)S(1)}, u32[]{:S(2)}, u32[]{:S(2)}) collective-permute-start(bf16[2,256,128]{2,1,0:T(8,128)(2,1)S(1)} %add_convert_fusion.2), channel_id=1, source_target_pairs={{0,2},{1,3},{2,0},{3,1},{4,6},{5,7},{6,4},{7,5},{8,10},{9,11},{10,... | collective-permute-start | bytes 393224 | tf_op jit(solution)/shard_map/ppermute | solution.py:22
  90.7 9.2 %collective-permute-start.14 = (bf16[512,512]{1,0:T(8,128)(2,1)S(1)}, bf16[512,512]{1,0:T(8,128)(2,1)S(1)}, u32[]{:S(2)}, u32[]{:S(2)}) collective-permute-start(bf16[512,512]{1,0:T(8,128)(2,1)S(1)} %get-tuple-element.127.refs_0_), channel_id=1, source_target_pairs={{0,8},{1,5},{2,10},{3,7},{4,12},{5,1},{6,14},{7,3},{8,0},{9,13},{1... | collective-permute-start | bytes 1572872 | tf_op jit(solution)/shard_map/ppermute | solution.py:64
  98.9 13.2 %collective-permute-start.17 = (bf16[608,512]{1,0:T(8,128)(2,1)S(1)}, bf16[608,512]{1,0:T(8,128)(2,1)S(1)}, u32[]{:S(2)}, u32[]{:S(2)}) collective-permute-start(bf16[608,512]{1,0:T(8,128)(2,1)S(1)} %get-tuple-element.134.refs_0_), channel_id=1, source_target_pairs={{0,4},{1,9},{2,6},{3,11},{4,0},{5,13},{6,2},{7,15},{8,12},{9,1},{1... | collective-permute-start | bytes 1867784 | tf_op jit(solution)/shard_map/ppermute | solution.py:64
  99.9 14.0 %collective-permute-start.16 = (bf16[256,512]{1,0:T(8,128)(2,1)S(1)}, bf16[256,512]{1,0:T(8,128)(2,1)S(1)}, u32[]{:S(2)}, u32[]{:S(2)}) collective-permute-start(bf16[256,512]{1,0:T(8,128)(2,1)S(1)} %get-tuple-element.138.refs_0_), channel_id=1, source_target_pairs={{0,16},{1,17},{2,18},{3,19},{4,20},{5,21},{6,22},{7,23},{8,24},{9,... | collective-permute-start | bytes 786440 | tf_op jit(solution)/shard_map/ppermute | solution.py:64
  101.3 8.3 %collective-permute-start.15 = (f32[2,3,512]{2,1,0:T(4,128)S(1)}, f32[2,3,512]{2,1,0:T(4,128)S(1)}, u32[]{:S(2)}, u32[]{:S(2)}) collective-permute-start(f32[2,3,512]{2,1,0:T(4,128)S(1)} %get-tuple-element.142), channel_id=1, source_target_pairs={{4,0},{8,4},{12,8},{16,12},{20,16},{24,20},{28,24},{5,1},{9,5},{13... | collective-permute-start | bytes 36872 | tf_op jit(solution)/shard_map/ppermute | solution.py:28
  114.0 16.1 %collective-permute-start.18 = (bf16[2,528,512]{2,1,0:T(8,128)(2,1)S(1)}, bf16[2,528,512]{2,1,0:T(8,128)(2,1)S(1)}, u32[]{:S(2)}, u32[]{:S(2)}) collective-permute-start(bf16[2,528,512]{2,1,0:T(8,128)(2,1)S(1)} %fusion.7), channel_id=1, source_target_pairs={{0,1},{1,0},{2,3},{3,2},{4,5},{5,4},{6,7},{7,6},{8,9},{9,8},{10,11... | collective-permute-start | bytes 3244040 | tf_op jit(solution)/shard_map/ppermute | solution.py:22
  114.1 10.5 %collective-permute-start.20 = (bf16[304,512]{1,0:T(8,128)(2,1)S(1)}, bf16[304,512]{1,0:T(8,128)(2,1)S(1)}, u32[]{:S(2)}, u32[]{:S(2)}) collective-permute-start(bf16[304,512]{1,0:T(8,128)(2,1)S(1)} %get-tuple-element.150.refs_0_), channel_id=1, source_target_pairs={{0,8},{1,5},{2,10},{3,7},{4,12},{5,1},{6,14},{7,3},{8,0},{9,13},{1... | collective-permute-start | bytes 933896 | tf_op jit(solution)/shard_map/ppermute | solution.py:64
  115.0 15.0 %collective-permute-start.19 = (bf16[256,512]{1,0:T(8,128)(2,1)S(1)}, bf16[256,512]{1,0:T(8,128)(2,1)S(1)}, u32[]{:S(2)}, u32[]{:S(2)}) collective-permute-start(bf16[256,512]{1,0:T(8,128)(2,1)S(1)} %advance.13.refs_0_), channel_id=1, source_target_pairs={{0,16},{1,17},{2,18},{3,19},{4,20},{5,21},{6,22},{7,23},{8,24},{9,... | collective-permute-start | bytes 786440 | tf_op jit(solution)/shard_map/ppermute | solution.py:64
  130.3 9.7 %collective-permute-start.23 = (bf16[2,272,256]{2,1,0:T(8,128)(2,1)S(1)}, bf16[2,272,256]{2,1,0:T(8,128)(2,1)S(1)}, u32[]{:S(2)}, u32[]{:S(2)}) collective-permute-start(bf16[2,272,256]{2,1,0:T(8,128)(2,1)S(1)} %get-tuple-element.163), channel_id=1, source_target_pairs={{0,2},{1,3},{2,0},{3,1},{4,6},{5,7},{6,4},{7,5},{8,10},{9,11},{10,... | collective-permute-start | bytes 835592 | tf_op jit(solution)/shard_map/ppermute | solution.py:22
  132.5 10.9 %collective-permute-start.22 = (bf16[176,512]{1,0:T(8,128)(2,1)S(1)}, bf16[176,512]{1,0:T(8,128)(2,1)S(1)}, u32[]{:S(2)}, u32[]{:S(2)}) collective-permute-start(bf16[176,512]{1,0:T(8,128)(2,1)S(1)} %get-tuple-element.158.refs_0_), channel_id=1, source_target_pairs={{0,16},{1,17},{2,18},{3,19},{4,20},{5,21},{6,22},{7,23},{8,24},{9,... | collective-permute-start | bytes 540680 | tf_op jit(solution)/shard_map/ppermute | solution.py:64
  132.5 14.0 %collective-permute-start.25 = (bf16[512,512]{1,0:T(8,128)(2,1)S(1)}, bf16[512,512]{1,0:T(8,128)(2,1)S(1)}, u32[]{:S(2)}, u32[]{:S(2)}) collective-permute-start(bf16[512,512]{1,0:T(8,128)(2,1)S(1)} %advance.15.refs_0_), channel_id=1, source_target_pairs={{0,8},{1,5},{2,10},{3,7},{4,12},{5,1},{6,14},{7,3},{8,0},{9,13},{1... | collective-permute-start | bytes 1572872 | tf_op jit(solution)/shard_map/ppermute | solution.py:64
  135.6 17.1 %collective-permute-start.21 = (bf16[2,256,256]{2,1,0:T(8,128)(2,1)S(1)}, bf16[2,256,256]{2,1,0:T(8,128)(2,1)S(1)}, u32[]{:S(2)}, u32[]{:S(2)}) collective-permute-start(bf16[2,256,256]{2,1,0:T(8,128)(2,1)S(1)} %get-tuple-element.164), channel_id=1, source_target_pairs={{0,2},{1,3},{2,0},{3,1},{4,6},{5,7},{6,4},{7,5},{8,10},{9,11},{10,... | collective-permute-start | bytes 786440 | tf_op jit(solution)/shard_map/ppermute | solution.py:22
  143.4 9.1 %collective-permute-start.24 = (bf16[144,512]{1,0:T(8,128)(2,1)S(1)}, bf16[144,512]{1,0:T(8,128)(2,1)S(1)}, u32[]{:S(2)}, u32[]{:S(2)}) collective-permute-start(bf16[144,512]{1,0:T(8,128)(2,1)S(1)} %get-tuple-element.170.refs_0_), channel_id=1, source_target_pairs={{0,16},{1,17},{2,18},{3,19},{4,20},{5,21},{6,22},{7,23},{8,24},{9,... | collective-permute-start | bytes 442376 | tf_op jit(solution)/shard_map/ppermute | solution.py:64
  146.6 18.4 %collective-permute-start.28 = (bf16[1024,512]{1,0:T(8,128)(2,1)S(1)}, bf16[1024,512]{1,0:T(8,128)(2,1)S(1)}, u32[]{:S(2)}, u32[]{:S(2)}) collective-permute-start(bf16[1024,512]{1,0:T(8,128)(2,1)S(1)} %advance.17.refs_0_.refs_2_), channel_id=1, source_target_pairs={{0,4},{1,9},{2,6},{3,11},{4,0},{5,13},{6,2},{7,15},{8,12},{9,1},{1... | collective-permute-start | bytes 3145736 | tf_op jit(solution)/shard_map/ppermute | solution.py:64
  152.6 10.7 %collective-permute-start.26 = (bf16[320,512]{1,0:T(8,128)(2,1)S(1)}, bf16[320,512]{1,0:T(8,128)(2,1)S(1)}, u32[]{:S(2)}, u32[]{:S(2)}) collective-permute-start(bf16[320,512]{1,0:T(8,128)(2,1)S(1)} %advance.18.refs_0_), channel_id=1, source_target_pairs={{0,8},{1,5},{2,10},{3,7},{4,12},{5,1},{6,14},{7,3},{8,0},{9,13},{1... | collective-permute-start | bytes 983048 | tf_op jit(solution)/shard_map/ppermute | solution.py:64
  163.4 10.5 %collective-permute-start.27 = (bf16[624,512]{1,0:T(8,128)(2,1)S(1)}, bf16[624,512]{1,0:T(8,128)(2,1)S(1)}, u32[]{:S(2)}, u32[]{:S(2)}) collective-permute-start(bf16[624,512]{1,0:T(8,128)(2,1)S(1)} %advance.19.refs_0_.own_ref), channel_id=1, source_target_pairs={{0,4},{1,9},{2,6},{3,11},{4,0},{5,13},{6,2},{7,15},{8,12},{9,1},{1... | collective-permute-start | bytes 1916936 | tf_op jit(solution)/shard_map/ppermute | solution.py:64
  (54 other events, 300.4 us)

commit v4 on v3

--- a/solution.py
+++ b/solution.py
@@ -403,6 +403,59 @@
         compiler_params=pltpu.CompilerParams(vmem_limit_bytes=8 << 20),
         name="pack",
     )(flag, sent, *parts)
+
+
+def join_kernel(lanes, short, up_ref, got_ref, log_ref, total_ref, window_ref, message, total, window):
+    states, width = log_ref.shape
+    rate = -jnp.exp(log_ref[...]) * LOG2E
+    upper = up_ref[0] != 0
+    count = lanes * states
+    spans = got_ref[got_ref.shape[0] - 16 :, :].astype(F32)
+    upper_next = up_ref[1] != 0
+    sums, befores, behinds = [], [], []
+    for l in range(lanes):
+        s = slice(l * states, (l + 1) * states)
+        g = slice(count + l * states, count + (l + 1) * states)
+        span, came = total_ref[2 * count + l : 2 * count + l + 1, :], spans[l : l + 1]
+        before = window_ref[2 * count + l : 2 * count + l + 1, :]
+        behind = window_ref[2 * count + lanes + l : 2 * count + lanes + l + 1, :]
+        through, through_came = jnp.exp2(span * rate), jnp.exp2(came * rate)
+        end, pull = total_ref[s, :], total_ref[g, :]
+        end_came = got_ref[s, :].astype(F32)
+        pull_came = end_came if short[0] else got_ref[g, :].astype(F32)
+        end_new = jnp.where(upper, end + through * end_came, end_came + through_came * end)
+        pull_new = jnp.where(upper, pull_came + through_came * pull, pull + through * pull_came)
+        total[s, :], total[g, :] = end_new, pull_new
+        if short[1]:
+            message[s, :] = jnp.where(upper_next, pull_new, end_new).astype(BF16)
+        else:
+            message[s, :], message[g, :] = end_new.astype(BF16), pull_new.astype(BF16)
+        enter = window_ref[s, :] + jnp.exp2(before * rate) * end_came
+        leave = window_ref[g, :] + jnp.exp2(behind * rate) * pull_came
+        window[s, :] = jnp.where(upper, enter, window_ref[s, :])
+        window[g, :] = jnp.where(upper, window_ref[g, :], leave)
+        sums.append(span + came)
+        befores.append(jnp.where(upper, before + came, before))
+        behinds.append(jnp.where(upper, behind, behind + came))
+    fill = jnp.zeros((8 - lanes, width), F32)
+    rows = jnp.concatenate([*sums, fill], axis=0)
+    total[2 * count :, :] = rows
+    message[message.shape[0] - 16 :, :] = jnp.concatenate([rows, jnp.zeros((8, width), F32)], axis=0).astype(BF16)
+    fill = jnp.zeros((8 - 2 * lanes, width), F32)
+    window[2 * count :, :] = jnp.concatenate([*befores, *behinds, fill], axis=0)
+
+
+def join(lanes, short, up, got, log, total, window):
+    shape = jax.ShapeDtypeStruct
+    rows = 16 + lanes * log.shape[0] * (1 if short[1] else 2)
+    return pl.pallas_call(
+        functools.partial(join_kernel, lanes, short),
+        in_specs=[pl.BlockSpec(memory_space=pltpu.SMEM)] + [VMEM] * 4,
+        out_specs=[VMEM] * 3,
+        out_shape=[shape((rows, got.shape[1]), BF16), shape(total.shape, F32), shape(window.shape, F32)],
+        compiler_params=pltpu.CompilerParams(vmem_limit_bytes=8 << 20),
+        name="join",
+    )(up, got, log, total, window)
 
 
 def iota(shape, dim):
@@ -572,8 +625,8 @@
 
 
 def forward_kernel(
-    low_rank, lanes, place_ref, proj_ref, log_ref, dt_ref, u_ref, gy_ref, got_ref,
-    y_ref, gc_ref, last_ref, hs_ref,
+    low_rank, lanes, starts_ref, proj_ref, log_ref, dt_ref, u_ref, gy_ref, begin_ref,
+    y_ref, gc_ref, hs_ref,
     kept, pa, pb, cols, left_c, masked, sems,
 ):
     length, width = dt_ref.shape
@@ -583,8 +636,6 @@
     _, per_step = selectors(states)
     wide = CHUNK * states
     chunks = length // CHUNK
-    groups = got_ref.shape[0]
-    place = place_ref[0]
 
     half = chunks // 2 * wide
 
@@ -592,22 +643,7 @@
         rows = pl.ds(part * half, half)
         return pltpu.make_async_copy(kept.at[slot, rows, :], hs_ref.at[slot, rows, :], sems.at[slot, part])
 
-    zero = jnp.zeros((states, width), F32)
-
-    def join(g, total, use):
-        at = lanes * states
-        spans = got_ref[g, at : at + lanes, :].astype(F32)
-        span = jnp.sum(jnp.where(iota(spans.shape, 0) == l, spans, 0.0), axis=0, keepdims=True)
-        factor = jnp.exp2(span * rate)
-        return jnp.where(use, total * factor + got_ref[g, rows_of(l, states), :].astype(F32), total)
-
-    begin = last = zero
-    for g in range(groups):
-        begin = join(g, begin, g < place)
-        h = groups - 1 - g
-        last = join(h, last, h > place)
-    last_ref[...] = last
-    begin = jnp.where(place_ref[1 + l] != 0, 0.0, begin)
+    begin = jnp.where(starts_ref[l] != 0, 0.0, begin_ref[...])
     proj = proj_ref[...]
     cols[...] = jnp.transpose(proj)[low_rank : low_rank + states]
     spread = by_step(proj.astype(BF16), from_lanes(low_rank + states, states), per_step)
@@ -656,7 +692,7 @@
                 leave(slot, part).wait()
 
 
-def scan_forward(low_rank, place, proj, log, dt, u, gy, got):
+def scan_forward(low_rank, starts, proj, log, dt, u, gy, begin):
     lanes, length, width = dt.shape
     states = log.shape[0]
     shape = jax.ShapeDtypeStruct
@@ -671,13 +707,12 @@
             tokens,
             tokens,
             tokens,
-            whole_spec(*got.shape),
+            state_spec,
         ],
-        out_specs=[tokens, narrow, state_spec, pl.BlockSpec(memory_space=pltpu.HBM)],
+        out_specs=[tokens, narrow, pl.BlockSpec(memory_space=pltpu.HBM)],
         out_shape=[
             shape((lanes, length, width), F32),
             shape(proj.shape, F32),
-            shape((lanes, states, width), F32),
             shape((lanes, length * states, width), BF16),
         ],
         scratch_shapes=[pltpu.VMEM((lanes, length * states, width), BF16)]
@@ -691,7 +726,7 @@
         compiler_params=pltpu.CompilerParams(vmem_limit_bytes=20 << 20),
         cost_estimate=cost(8, lanes, length, width, states),
         name="scan_forward",
-    )(place, proj, log, dt, u, gy, got)
+    )(starts, proj, log, dt, u, gy, begin)
 
 
 def backward_kernel(
@@ -846,27 +881,25 @@
     over = Reduction()
     per = shard_width * seq_size // model_width
     halves = seq_size // 2
-    place = jnp.concatenate([seq_index[None].astype(jnp.int32), row_starts[:, 0]])
+    ups = ((seq_index & jnp.array([*seq_bits, 0])) != 0).astype(jnp.int32)
+    ups = [ups[step : step + 2] for step in range(len(seq_bits))]
     orders = jnp.concatenate([over.order(per, mp_index), over.order(1, 0)])
     flat_order = over.flat_order()
     flags = [over.own(step)[None] for step in range(len(seq_bits))]
     span_more = FAR * starts[:, :, None]
-    to_later = (jnp.arange(seq_size) > seq_index)[:, None, None]
     w_in = blocks(in_weight, 1, near).astype(BF16)
-    w_back = blocks(in_weight, 1, near_first).astype(BF16)
-    w_out = out_weight.astype(BF16)
-    w_spread = blocks(out_weight, 1, near_first).astype(BF16)
+    w_out = lax.optimization_barrier(out_weight.astype(BF16))
     gain = blocks(norm_gain, 0, near)
     w_x = jnp.pad(xproj_weight.astype(BF16), ((0, 0), (0, -xproj_weight.shape[1] % LANE)))
     w_dt = jnp.pad(dtproj_weight.astype(BF16), ((0, -low_rank % LANE), (0, 0)))
+    w_dt = lax.optimization_barrier(w_dt)
     inv_rms = lax.rsqrt(square[:, :, None] / model_width + 1e-05)
-    x_parts[near[-1]] = after(x_parts[near[-1]], place, orders, flat_order, span_more, *flags)
+    x_parts[near[-1]] = after(x_parts[near[-1]], orders, flat_order, span_more, *flags, *ups, w_out, w_dt)
     x_whole = jnp.concatenate([x_parts[k] for k in near], axis=2)
     normed = (x_whole.astype(F32) * inv_rms * gain).astype(BF16)
     rim_count = 8
     rim_normed = from_behind(normed[:, length - rim_count :, :], "seq", 1)
     inner_act = jnp.einsum("ltd,de->lte", normed, w_in[0], preferred_element_type=F32).astype(BF16)
-    gate_in = jnp.einsum("ltd,de->lte", normed, w_in[1], preferred_element_type=F32)
     rim_rows = jnp.einsum("ltd,de->lte", rim_normed, w_in[0], preferred_element_type=F32).astype(BF16)
     rim_rows = after(rim_rows, *grad_parts.values())
     rim_rows = (rim_rows.astype(F32) * carry_mask)[:, rim_count - (tap_count - 1) :]
@@ -880,6 +913,7 @@
     for bit in mp_bits[:-1]:
         sent = (sent.astype(F32) + swap(sent, "mp", bit).astype(F32)).astype(BF16)
     got = swap(sent, "mp", mp_bits[-1])
+    gate_in = jnp.einsum("ltd,de->lte", after(normed, sent), w_in[1], preferred_element_type=F32)
     for k in list(grad_parts):
         grad_parts[k] = after(grad_parts[k], sent)
         grad_parts[k | 1] = swap(grad_parts[k], "mp", 1)
@@ -899,19 +933,38 @@
         low_rank, sent, got, w_dt, dt_bias[None], decay_log, mixed, grad_scan
     )
     span = span + span_more
-    flat = (1, lane_count * state_count, inner_width)
-    edge = jnp.where(to_later, end_state.reshape(flat), (pulled * carry_mask).reshape(flat))
-    spans = jnp.broadcast_to(
-        span.reshape(1, lane_count, inner_width), (seq_size, lane_count, inner_width)
-    )
-    message = jnp.concatenate([edge, spans], axis=1).astype(BF16)
-    message = jnp.pad(message, ((0, 0), (0, -message.shape[1] % 8), (0, 0)))
-    groups = lax.all_to_all(message, "seq", 0, 0, tiled=True)
+    count = lane_count * state_count
+    flat = (count, inner_width)
+    total = jnp.concatenate(
+        [
+            end_state.reshape(flat),
+            (pulled * carry_mask).reshape(flat),
+            span.reshape(lane_count, inner_width),
+            jnp.zeros((8 - lane_count, inner_width), F32),
+        ],
+        axis=0,
+    )
+    message = jnp.pad(total.astype(BF16), ((0, 8), (0, 0)))
+    window = jnp.zeros_like(total)
+    for step, bit in enumerate(seq_bits):
+        short = (step == len(seq_bits) - 1, step == len(seq_bits) - 2)
+        if step == 0:
+            w_late = after(w_out, message)
+            w_spread = blocks(w_late, 1, near_first)
+            w_late = after(w_in, message)
+            w_back = jnp.concatenate(
+                [w_late[:, k * shard_width : (k + 1) * shard_width] for k in near_first], axis=1
+            )
+        got = swap(message, "seq", bit)
+        message, total, window = join(lane_count, short, ups[step], got, decay_log, total, window)
+    window = window.reshape(-1, inner_width)
+    begin = window[:count].reshape(end_state.shape)
+    last = window[count : 2 * count].reshape(end_state.shape)
     projected, normed_more, w_back, w_spread = lax.optimization_barrier(
         (projected, normed_more, w_back, w_spread)
     )
-    y, grad_read, last, states_all = scan_forward(
-        low_rank, place, projected, decay_log, dt, source, grad_scan, groups
+    y, grad_read, states_all = scan_forward(
+        low_rank, row_starts[:, 0], projected, decay_log, dt, source, grad_scan, begin
     )
     scan_out = y + skip_gain * mixed
     gated = (scan_out * jax.nn.silu(gate_in)).astype(BF16)

time: 177 us -> 176 us (level)
  waiting for transfers between devices: 64.8 us -> 57.4 us
  starting transfers between devices: 34.2 us -> 41.5 us
  matrix products: 13 us -> 11 us
  Pallas kernels: 36 us -> 38 us
  local copies, waits for them, and re-layouts: 10.5 us -> 8.63 us
    ppermute x12, starting transfers between devices: 10.5 us -> 17.1 us  [swap(): return lax.ppermute(block, ('seq', 'mp'), route)]
    ppermute x15 -> x18, starting transfers between devices: 12.9 us -> 19.4 us  [swap(): return lax.ppermute(block, axis, [(i, i ^ bit) for i in range(devices)])]
    all_to_all x1 -> x0, starting transfers between devices: 6.03 us -> none  [per_device(): groups = lax.all_to_all(message, 'seq', 0, 0, tiled=True)]
    all_to_all x1 -> x0, waiting for transfers between devices: 4.76 us -> none  [per_device(): groups = lax.all_to_all(message, 'seq', 0, 0, tiled=True)]
    ppermute x15 -> x18, waiting for transfers between devices: 12 us -> 15.6 us  [swap(): return lax.ppermute(block, axis, [(i, i ^ bit) for i in range(devices)])]
    convert_element_type x0 -> x3, other arithmetic: none -> 3.57 us  [the longest x1 2.84 us: per_device(): w_out = lax.optimization_barrier(out_weight.astype(BF16))]
    ppermute x12, waiting for transfers between devices: 41.1 us -> 37.7 us  [swap(): return lax.ppermute(block, ('seq', 'mp'), route)]
    concatenate x3, other arithmetic: 3.32 us -> 0.28 us  [blocks(): return jnp.concatenate(parts, axis=axis)]
  transfers between devices with their start and end apart: 30 -> 32, of which waited for: 20 -> 20; matrix products, arithmetic and copies ran while one was open for 17% -> 15% of each run, Pallas kernels for 9% -> 9%
where the time goes in v4:
time: 176 us; the launch traced here: 175 us
  waiting for transfers between devices  57.4 us (33%)
  starting transfers between devices  41.5 us (24%)
  Pallas kernels  38 us (22%)
  other arithmetic  17.1 us (10%)
  matrix products  11 us (6%)
  local copies, waits for them, and re-layouts  8.63 us (5%)
    ppermute x12, waiting for transfers between devices, swap(): return lax.ppermute(block, ('seq', 'mp'), route)  37.7 us
    ppermute x18, starting transfers between devices, swap(): return lax.ppermute(block, axis, [(i, i ^ bit) for i in range(devices)])  19.4 us
    ppermute x12, starting transfers between devices, swap(): return lax.ppermute(block, ('seq', 'mp'), route)  17.1 us
    ppermute x18, waiting for transfers between devices, swap(): return lax.ppermute(block, axis, [(i, i ^ bit) for i in range(devices)])  15.6 us
    pallas_call x1, Pallas kernels, scan_backward(): pl.pallas_call(functools.partial(backward_kernel, low_rank, lanes), grid=...  11 us
    pallas_call x1, Pallas kernels, scan_ends(): pl.pallas_call(functools.partial(ends_kernel, low_rank), grid=(lanes,), i...  9.06 us
    pallas_call x1, Pallas kernels, scan_forward(): pl.pallas_call(functools.partial(forward_kernel, low_rank, lanes), grid=(...  7.67 us
    ppermute x2, starting transfers between devices, from_behind(): return lax.ppermute(block, axis, route)  5.04 us
  transfers between devices with their start and end apart: 32, of which 20 were waited for; matrix products, arithmetic and copies ran while one was open for 15% of the time, Pallas kernels for 9%

profile of v4, /device:TPU:0, one launch (start us, length us, event | category | flops | bytes accessed | tf_op | source)
XLA Modules:
  0.0 175.3 jit_solution(2162585244241158956)
XLA Ops:
  2.0 3.0 %collective-permute-start.1 = (bf16[2,256,256]{2,1,0:T(8,128)(2,1)S(1)}, bf16[2,256,256]{2,1,0:T(8,128)(2,1)}, u32[]{:S(2)}, u32[]{:S(2)}) collective-permute-start(bf16[2,256,256]{2,1,0:T(8,128)(2,1)S(1)} %get-tuple-element.246), channel_id=1, source_target_pairs={{0,2},{1,3},{2,0},{3,1},{4,6},{5,7},{6,4},{7,5},{8,10},{9,11},{10,... | collective-permute-start | bytes 786440 | tf_op jit(solution)/shard_map/ppermute | solution.py:22
  8.0 2.5 %dynamic-slice_convert_fusion.3 = (bf16[2,256,512]{2,1,0:T(8,128)(2,1)S(1)}, bf16[2,256,512]{2,1,0:T(8,128)(2,1)S(1)}, bf16[2,256,512]{2,1,0:T(8,128)(2,1)S(1)}, bf16[2,256,512]{2,1,0:T(8,128)(2,1)S(1)}) fusion(f32[2,1024,512]{2,1,0:T(8,128)} %param.17, s32[]{:T(128)S(6)} %select_n.182, s32[]{:T(128)S(6)} %select_n.183, s32[]{:T(128)S(6)} %select_n.185, ...), kind=kLoop, calls=%fused_computation.58 | loop fusion | bytes 4194320 | tf_op jit(solution)/shard_map/convert.3
  12.1 2.8 %convert_element_type.206 = bf16[512,1024]{1,0:T(8,128)(2,1)} convert(f32[512,1024]{1,0:T(8,128)} %param.25) | non-fusion elementwise | flops 524288 | bytes 3145728 | tf_op jit(solution)/shard_map/convert_element_type | solution.py:891
  15.0 1.8 %collective-permute-start.6 = (bf16[2,256,256]{2,1,0:T(8,128)(2,1)S(1)}, bf16[2,256,256]{2,1,0:T(8,128)(2,1)S(1)}, u32[]{:S(2)}, u32[]{:S(2)}) collective-permute-start(bf16[2,256,256]{2,1,0:T(8,128)(2,1)S(1)} %convert_element_type.211), channel_id=1, source_target_pairs={{0,2},{1,3},{2,0},{3,1},{4,6},{5,7},{6,4},{7,5},{8,10},{9,11},{10,... | collective-permute-start | bytes 786440 | tf_op jit(solution)/shard_map/ppermute | solution.py:22
  18.4 3.5 %collective-permute-start.5 = (bf16[2,8,1024]{2,1,0:T(8,128)(2,1)S(1)}, bf16[2,8,1024]{2,1,0:T(8,128)(2,1)S(1)}, u32[]{:S(2)}, u32[]{:S(2)}) collective-permute-start(bf16[2,8,1024]{2,1,0:T(8,128)(2,1)S(1)} %slice.143), channel_id=1, source_target_pairs={{0,4},{4,8},{8,12},{12,16},{16,20},{20,24},{24,28},{1,5},{5,9},{9,... | collective-permute-start | bytes 98312 | tf_op jit(solution)/shard_map/ppermute | solution.py:28
  24.5 1.6 fusion.68
  29.7 1.6 collective-permute-start.8
  36.1 9.1 %scan_ends.1 = (f32[2,16,512]{2,1,0:T(8,128)S(1)}, f32[2,16,512]{2,1,0:T(8,128)S(1)}, f32[2,1,512]{2,1,0:T(1,128)S(1)}, f32[2,256,512]{2,1,0:T(8,128)}, f32[2,25...) custom-call(bf16[2,256,128]{2,1,0:T(8,128)(2,1)S(1)} %add_convert_fusion.4.sent_ref, ...), custom_call_target="tpu_custom_call" | custom-call | flops 536870912 | bytes 8388608 | tf_op jit(solution)/shard_map/scan_ends/pallas_call | solution.py:602
  47.6 2.4 %collective-permute-done.11.got_ref = bf16[80,512]{1,0:T(8,128)(2,1)S(1)} collective-permute-done((bf16[80,512]{1,0:T(8,128)(2,1)S(1)}, bf16[80,512]{1,0:T(8,128)(2,1)S(1)}, u32[]{:S(2)}, u32[]{:S(2)}) %collective-permute-start.11) | collective-permute-done | bytes 81952 | tf_op jit(solution)/shard_map/ppermute | solution.py:22
  50.7 2.5 %collective-permute-start.12 = (bf16[80,512]{1,0:T(8,128)(2,1)S(1)}, bf16[80,512]{1,0:T(8,128)(2,1)S(1)}, u32[]{:S(2)}, u32[]{:S(2)}) collective-permute-start(bf16[80,512]{1,0:T(8,128)(2,1)S(1)} %get-tuple-element.124), channel_id=1, source_target_pairs={{0,8},{4,12},{8,0},{12,4},{16,24},{20,28},{24,16},{28,20},{1,9},{5... | collective-permute-start | bytes 245768 | tf_op jit(solution)/shard_map/ppermute | solution.py:22
  53.4 2.2 %collective-permute-done.12.got_ref = bf16[80,512]{1,0:T(8,128)(2,1)S(1)} collective-permute-done((bf16[80,512]{1,0:T(8,128)(2,1)S(1)}, bf16[80,512]{1,0:T(8,128)(2,1)S(1)}, u32[]{:S(2)}, u32[]{:S(2)}) %collective-permute-start.12) | collective-permute-done | bytes 81952 | tf_op jit(solution)/shard_map/ppermute | solution.py:22
  56.3 3.1 %collective-permute-start.13 = (bf16[48,512]{1,0:T(8,128)(2,1)S(1)}, bf16[48,512]{1,0:T(8,128)(2,1)S(1)}, u32[]{:S(2)}, u32[]{:S(2)}) collective-permute-start(bf16[48,512]{1,0:T(8,128)(2,1)S(1)} %get-tuple-element.127), channel_id=1, source_target_pairs={{0,16},{4,20},{8,24},{12,28},{16,0},{20,4},{24,8},{28,12},{1,17},{... | collective-permute-start | bytes 147464 | tf_op jit(solution)/shard_map/ppermute | solution.py:22
  59.5 1.9 %collective-permute-done.13.got_ref = bf16[48,512]{1,0:T(8,128)(2,1)S(1)} collective-permute-done((bf16[48,512]{1,0:T(8,128)(2,1)S(1)}, bf16[48,512]{1,0:T(8,128)(2,1)S(1)}, u32[]{:S(2)}, u32[]{:S(2)}) %collective-permute-start.13) | collective-permute-done | bytes 49184 | tf_op jit(solution)/shard_map/ppermute | solution.py:22
  62.8 7.7 %scan_forward.1 = (f32[2,256,512]{2,1,0:T(8,128)S(1)}, f32[2,256,128]{2,1,0:T(8,128)S(1)}, bf16[2,4096,512]{2,1,0:T(8,128)(2,1)S(1)}) custom-call(s32[2]{0:T(128)S(1)} %bitcast.152, f32[2,256,128]{2,1,0:T(8,128)S(1)} %get-tuple-element.121.proj_ref, f32[16,512]{1,0:T(8,128)S(1)} %copy-done.2, f32[2,256,512]{2,1,0:T(8,128)S(1)} %copy-done, ...), custom_call_target="tpu_custom_call" | custom-call | flops 536870912 | bytes 8388608 | tf_op jit(solution)/shard_map/scan_forward/pallas_call | solution.py:700
  74.2 11.0 %scan_backward.1 = (f32[2,256,512]{2,1,0:T(8,128)S(1)}, f32[2,256,512]{2,1,0:T(8,128)S(1)}, f32[2,256,128]{2,1,0:T(8,128)S(1)}, f32[2,16,512]{2,1,0:T(8,128)S(1)}) custom-call(f32[2,256,128]{2,1,0:T(8,128)S(1)} %get-tuple-element.121.proj_ref, f32[16,512]{1,0:T(8,128)S(1)} %copy-done.2, f32[2,256,512]{2,1,0:T(8,128)S(1)} %copy-done, ...), custom_call_target="tpu_custom_call" | custom-call | flops 805306368 | bytes 8388608 | tf_op jit(solution)/shard_map/scan_backward/pallas_call | solution.py:814
  90.8 2.5 %collective-permute-done.16 = bf16[2,256,128]{2,1,0:T(8,128)(2,1)S(1)} collective-permute-done((bf16[2,256,128]{2,1,0:T(8,128)(2,1)S(1)}, bf16[2,256,128]{2,1,0:T(8,128)(2,1)S(1)}, u32[]{:S(2)}, u32[]{:S(2)}) %collective-permute-start.16) | collective-permute-done | bytes 131104 | tf_op jit(solution)/shard_map/ppermute | solution.py:22
  98.6 3.0 %collective-permute-start.19 = (bf16[256,512]{1,0:T(8,128)(2,1)S(1)}, bf16[256,512]{1,0:T(8,128)(2,1)S(1)}, u32[]{:S(2)}, u32[]{:S(2)}) collective-permute-start(bf16[256,512]{1,0:T(8,128)(2,1)S(1)} %get-tuple-element.154.refs_0_), channel_id=1, source_target_pairs={{0,16},{1,17},{2,18},{3,19},{4,20},{5,21},{6,22},{7,23},{8,24},{9,... | collective-permute-start | bytes 786440 | tf_op jit(solution)/shard_map/ppermute | solution.py:64
  104.7 3.3 %collective-permute-done.18 = f32[2,3,512]{2,1,0:T(4,128)S(1)} collective-permute-done((f32[2,3,512]{2,1,0:T(4,128)S(1)}, f32[2,3,512]{2,1,0:T(4,128)S(1)}, u32[]{:S(2)}, u32[]{:S(2)}) %collective-permute-start.18) | collective-permute-done | bytes 12320 | tf_op jit(solution)/shard_map/ppermute | solution.py:28
  111.9 2.7 %collective-permute-start.23 = (bf16[304,512]{1,0:T(8,128)(2,1)S(1)}, bf16[304,512]{1,0:T(8,128)(2,1)S(1)}, u32[]{:S(2)}, u32[]{:S(2)}) collective-permute-start(bf16[304,512]{1,0:T(8,128)(2,1)S(1)} %get-tuple-element.166.refs_0_), channel_id=1, source_target_pairs={{0,8},{1,5},{2,10},{3,7},{4,12},{5,1},{6,14},{7,3},{8,0},{9,13},{1... | collective-permute-start | bytes 933896 | tf_op jit(solution)/shard_map/ppermute | solution.py:64
  114.5 2.7 %collective-permute-start.22 = (bf16[256,512]{1,0:T(8,128)(2,1)S(1)}, bf16[256,512]{1,0:T(8,128)(2,1)S(1)}, u32[]{:S(2)}, u32[]{:S(2)}) collective-permute-start(bf16[256,512]{1,0:T(8,128)(2,1)S(1)} %advance.13.refs_0_), channel_id=1, source_target_pairs={{0,16},{1,17},{2,18},{3,19},{4,20},{5,21},{6,22},{7,23},{8,24},{9,... | collective-permute-start | bytes 786440 | tf_op jit(solution)/shard_map/ppermute | solution.py:64
  117.2 2.6 %collective-permute-done.23.refs_1_ = bf16[304,512]{1,0:T(8,128)(2,1)S(1)} collective-permute-done((bf16[304,512]{1,0:T(8,128)(2,1)S(1)}, bf16[304,512]{1,0:T(8,128)(2,1)S(1)}, u32[]{:S(2)}, u32[]{:S(2)}) %collective-permute-start.23) | collective-permute-done | bytes 311328 | tf_op jit(solution)/shard_map/ppermute | solution.py:64
  119.9 10.0 %collective-permute-done.22.refs_1_ = bf16[256,512]{1,0:T(8,128)(2,1)S(1)} collective-permute-done((bf16[256,512]{1,0:T(8,128)(2,1)S(1)}, bf16[256,512]{1,0:T(8,128)(2,1)S(1)}, u32[]{:S(2)}, u32[]{:S(2)}) %collective-permute-start.22) | collective-permute-done | bytes 262176 | tf_op jit(solution)/shard_map/ppermute | solution.py:64
  131.5 3.0 %collective-permute-start.28 = (bf16[512,512]{1,0:T(8,128)(2,1)S(1)}, bf16[512,512]{1,0:T(8,128)(2,1)S(1)}, u32[]{:S(2)}, u32[]{:S(2)}) collective-permute-start(bf16[512,512]{1,0:T(8,128)(2,1)S(1)} %advance.15.refs_0_), channel_id=1, source_target_pairs={{0,8},{1,5},{2,10},{3,7},{4,12},{5,1},{6,14},{7,3},{8,0},{9,13},{1... | collective-permute-start | bytes 1572872 | tf_op jit(solution)/shard_map/ppermute | solution.py:64
  135.0 4.7 %collective-permute-done.26 = bf16[2,272,256]{2,1,0:T(8,128)(2,1)S(1)} collective-permute-done((bf16[2,272,256]{2,1,0:T(8,128)(2,1)S(1)}, bf16[2,272,256]{2,1,0:T(8,128)(2,1)S(1)}, u32[]{:S(2)}, u32[]{:S(2)}) %collective-permute-start.26) | collective-permute-done | bytes 278560 | tf_op jit(solution)/shard_map/ppermute | solution.py:22
  142.5 3.1 %collective-permute-done.28.refs_1_ = bf16[512,512]{1,0:T(8,128)(2,1)S(1)} collective-permute-done((bf16[512,512]{1,0:T(8,128)(2,1)S(1)}, bf16[512,512]{1,0:T(8,128)(2,1)S(1)}, u32[]{:S(2)}, u32[]{:S(2)}) %collective-permute-start.28) | collective-permute-done | bytes 524320 | tf_op jit(solution)/shard_map/ppermute | solution.py:64
  145.6 1.9 %collective-permute-start.31 = (bf16[1024,512]{1,0:T(8,128)(2,1)S(1)}, bf16[1024,512]{1,0:T(8,128)(2,1)S(1)}, u32[]{:S(2)}, u32[]{:S(2)}) collective-permute-start(bf16[1024,512]{1,0:T(8,128)(2,1)S(1)} %advance.17.refs_0_.refs_2_), channel_id=1, source_target_pairs={{0,4},{1,9},{2,6},{3,11},{4,0},{5,13},{6,2},{7,15},{8,12},{9,1},{1... | collective-permute-start | bytes 3145736 | tf_op jit(solution)/shard_map/ppermute | solution.py:64
  147.4 3.7 %collective-permute-done.27.refs_1_ = bf16[144,512]{1,0:T(8,128)(2,1)S(1)} collective-permute-done((bf16[144,512]{1,0:T(8,128)(2,1)S(1)}, bf16[144,512]{1,0:T(8,128)(2,1)S(1)}, u32[]{:S(2)}, u32[]{:S(2)}) %collective-permute-start.27) | collective-permute-done | bytes 147488 | tf_op jit(solution)/shard_map/ppermute | solution.py:64
  152.2 9.7 %collective-permute-done.29.refs_1_ = bf16[320,512]{1,0:T(8,128)(2,1)S(1)} collective-permute-done((bf16[320,512]{1,0:T(8,128)(2,1)S(1)}, bf16[320,512]{1,0:T(8,128)(2,1)S(1)}, u32[]{:S(2)}, u32[]{:S(2)}) %collective-permute-start.29) | collective-permute-done | bytes 327712 | tf_op jit(solution)/shard_map/ppermute | solution.py:64
  162.1 1.9 %collective-permute-done.31.refs_1_.refs_3_ = bf16[1024,512]{1,0:T(8,128)(2,1)S(1)} collective-permute-done((bf16[1024,512]{1,0:T(8,128)(2,1)S(1)}, bf16[1024,512]{1,0:T(8,128)(2,1)S(1)}, u32[]{:S(2)}, u32[]{:S(2)}) %collective-permute-start.31) | collective-permute-done | bytes 1048608 | tf_op jit(solution)/shard_map/ppermute | solution.py:64
  164.0 2.7 %settle.2 = (f32[2,1024,512]{2,1,0:T(8,128)}, f32[512,1024]{1,0:T(8,128)}) custom-call(s32[12]{0:T(128)S(1)} %concatenate.49.order_ref, bf16[1024,512]{1,0:T(8,128)(2,1)S(1)} %advance.17.refs_0_.refs_2_, bf16[1024,512]{1,0:T(8,128)(2,1)S(1)} %collective-permute-done.31.refs_1_.refs_3_, bf16[1024,512]{1,0:T(8,128)(2,1)S(1)} %advance.17.refs_0_.refs_2_, ...), custom_call_target="tpu_custom_call" | custom-call | tf_op jit(solution)/shard_map/settle/pallas_call | solution.py:252
  168.3 4.2 %collective-permute-done.30.late_ref = bf16[624,512]{1,0:T(8,128)(2,1)S(1)} collective-permute-done((bf16[624,512]{1,0:T(8,128)(2,1)S(1)}, bf16[624,512]{1,0:T(8,128)(2,1)S(1)}, u32[]{:S(2)}, u32[]{:S(2)}) %collective-permute-start.30) | collective-permute-done | bytes 639008 | tf_op jit(solution)/shard_map/ppermute | solution.py:64
  172.5 2.3 %finish.1 = (f32[2,1024,512]{2,1,0:T(8,128)}, f32[4,512]{1,0:T(4,128)}, f32[1,512]{1,0:T(1,128)}, f32[1,512]{1,0:T(1,128)}, f32[1,512]{1,0:T(1,128)}, /*index=5*...) custom-call(s32[12]{0:T(128)S(1)} %concatenate.49.order_ref, ...), custom_call_target="tpu_custom_call", output_to_operand_aliasing={{0}: (4, {})} | custom-call | tf_op jit(solution)/shard_map/finish/pallas_call | solution.py:294
  (212 shorter events, 52.7 us)
Async XLA Ops:
  2.0 9.7 %collective-permute-start.1 = (bf16[2,256,256]{2,1,0:T(8,128)(2,1)S(1)}, bf16[2,256,256]{2,1,0:T(8,128)(2,1)}, u32[]{:S(2)}, u32[]{:S(2)}) collective-permute-start(bf16[2,256,256]{2,1,0:T(8,128)(2,1)S(1)} %get-tuple-element.246), channel_id=1, source_target_pairs={{0,2},{1,3},{2,0},{3,1},{4,6},{5,7},{6,4},{7,5},{8,10},{9,11},{10,... | collective-permute-start | bytes 786440 | tf_op jit(solution)/shard_map/ppermute | solution.py:22
  5.0 11.9 %collective-permute-start = (bf16[2,256,256]{2,1,0:T(8,128)(2,1)S(1)}, bf16[2,256,256]{2,1,0:T(8,128)(2,1)}, u32[]{:S(2)}, u32[]{:S(2)}) collective-permute-start(bf16[2,256,256]{2,1,0:T(8,128)(2,1)S(1)} %get-tuple-element.246), channel_id=1, source_target_pairs={{0,1},{1,0},{2,3},{3,2},{4,5},{5,4},{6,7},{7,6},{8,9},{9,8},{10,11... | collective-permute-start | bytes 786440 | tf_op jit(solution)/shard_map/ppermute | solution.py:22
  5.0 6.4 %collective-permute-start.3 = (f32[2,256]{1,0:T(2,128)S(1)}, f32[2,256]{1,0:T(2,128)S(1)}, u32[]{:S(2)}, u32[]{:S(2)}) collective-permute-start(f32[2,256]{1,0:T(2,128)S(1)} %get-tuple-element.245), channel_id=1, source_target_pairs={{0,2},{1,3},{2,0},{3,1},{4,6},{5,7},{6,4},{7,5},{8,10},{9,11},{10,... | collective-permute-start | bytes 6152 | tf_op jit(solution)/shard_map/ppermute | solution.py:22
  11.5 3.6 %collective-permute-start.4 = (f32[2,256]{1,0:T(2,128)S(1)}, f32[2,256]{1,0:T(2,128)S(1)}, u32[]{:S(2)}, u32[]{:S(2)}) collective-permute-start(f32[2,256]{1,0:T(2,128)S(1)} %add.238), channel_id=1, source_target_pairs={{0,1},{1,0},{2,3},{3,2},{4,5},{5,4},{6,7},{7,6},{8,9},{9,8},{10,11... | collective-permute-start | bytes 6152 | tf_op jit(solution)/shard_map/ppermute | solution.py:22
  11.7 5.2 %collective-permute-start.2 = (bf16[2,256,256]{2,1,0:T(8,128)(2,1)}, bf16[2,256,256]{2,1,0:T(8,128)(2,1)}, u32[]{:S(2)}, u32[]{:S(2)}) collective-permute-start(bf16[2,256,256]{2,1,0:T(8,128)(2,1)} %collective-permute-done.1), channel_id=1, source_target_pairs={{0,1},{1,0},{2,3},{3,2},{4,5},{5,4},{6,7},{7,6},{8,9},{9,8},{10,11... | collective-permute-start | bytes 786440 | tf_op jit(solution)/shard_map/ppermute | solution.py:22
  15.0 8.7 %collective-permute-start.6 = (bf16[2,256,256]{2,1,0:T(8,128)(2,1)S(1)}, bf16[2,256,256]{2,1,0:T(8,128)(2,1)S(1)}, u32[]{:S(2)}, u32[]{:S(2)}) collective-permute-start(bf16[2,256,256]{2,1,0:T(8,128)(2,1)S(1)} %convert_element_type.211), channel_id=1, source_target_pairs={{0,2},{1,3},{2,0},{3,1},{4,6},{5,7},{6,4},{7,5},{8,10},{9,11},{10,... | collective-permute-start | bytes 786440 | tf_op jit(solution)/shard_map/ppermute | solution.py:22
  18.4 5.1 %collective-permute-start.5 = (bf16[2,8,1024]{2,1,0:T(8,128)(2,1)S(1)}, bf16[2,8,1024]{2,1,0:T(8,128)(2,1)S(1)}, u32[]{:S(2)}, u32[]{:S(2)}) collective-permute-start(bf16[2,8,1024]{2,1,0:T(8,128)(2,1)S(1)} %slice.143), channel_id=1, source_target_pairs={{0,4},{4,8},{8,12},{12,16},{16,20},{20,24},{24,28},{1,5},{5,9},{9,... | collective-permute-start | bytes 98312 | tf_op jit(solution)/shard_map/ppermute | solution.py:28
  27.2 1.5 collective-permute-start.7
  29.7 6.4 %collective-permute-start.8 = (bf16[2,256,128]{2,1,0:T(8,128)(2,1)S(1)}, bf16[2,256,128]{2,1,0:T(8,128)(2,1)S(1)}, u32[]{:S(2)}, u32[]{:S(2)}) collective-permute-start(bf16[2,256,128]{2,1,0:T(8,128)(2,1)S(1)} %add_convert_fusion.4.sent_ref), channel_id=1, source_target_pairs={{0,2},{1,3},{2,0},{3,1},{4,6},{5,7},{6,4},{7,5},{8,10},{9,11},{10,... | collective-permute-start | bytes 393224 | tf_op jit(solution)/shard_map/ppermute | solution.py:22
  31.3 2.6 %collective-permute-start.9 = (bf16[2,256,256]{2,1,0:T(8,128)(2,1)}, bf16[2,256,256]{2,1,0:T(8,128)(2,1)S(1)}, u32[]{:S(2)}, u32[]{:S(2)}) collective-permute-start(bf16[2,256,256]{2,1,0:T(8,128)(2,1)} %copy-done.13), channel_id=1, source_target_pairs={{0,1},{1,0},{2,3},{3,2},{4,5},{5,4},{6,7},{7,6},{8,9},{9,8},{10,11... | collective-permute-start | bytes 786440 | tf_op jit(solution)/shard_map/ppermute | solution.py:22
  31.3 2.6 %collective-permute-start.10 = (bf16[2,256,256]{2,1,0:T(8,128)(2,1)}, bf16[2,256,256]{2,1,0:T(8,128)(2,1)S(1)}, u32[]{:S(2)}, u32[]{:S(2)}) collective-permute-start(bf16[2,256,256]{2,1,0:T(8,128)(2,1)} %copy-done.18), channel_id=1, source_target_pairs={{0,1},{1,0},{2,3},{3,2},{4,5},{5,4},{6,7},{7,6},{8,9},{9,8},{10,11... | collective-permute-start | bytes 786440 | tf_op jit(solution)/shard_map/ppermute | solution.py:22
  45.5 4.5 %collective-permute-start.11 = (bf16[80,512]{1,0:T(8,128)(2,1)S(1)}, bf16[80,512]{1,0:T(8,128)(2,1)S(1)}, u32[]{:S(2)}, u32[]{:S(2)}) collective-permute-start(bf16[80,512]{1,0:T(8,128)(2,1)S(1)} %pad.45), channel_id=1, source_target_pairs={{0,4},{4,0},{8,12},{12,8},{16,20},{20,16},{24,28},{28,24},{1,5},{5... | collective-permute-start | bytes 245768 | tf_op jit(solution)/shard_map/ppermute | solution.py:22
  50.7 5.0 %collective-permute-start.12 = (bf16[80,512]{1,0:T(8,128)(2,1)S(1)}, bf16[80,512]{1,0:T(8,128)(2,1)S(1)}, u32[]{:S(2)}, u32[]{:S(2)}) collective-permute-start(bf16[80,512]{1,0:T(8,128)(2,1)S(1)} %get-tuple-element.124), channel_id=1, source_target_pairs={{0,8},{4,12},{8,0},{12,4},{16,24},{20,28},{24,16},{28,20},{1,9},{5... | collective-permute-start | bytes 245768 | tf_op jit(solution)/shard_map/ppermute | solution.py:22
  56.3 5.2 %collective-permute-start.13 = (bf16[48,512]{1,0:T(8,128)(2,1)S(1)}, bf16[48,512]{1,0:T(8,128)(2,1)S(1)}, u32[]{:S(2)}, u32[]{:S(2)}) collective-permute-start(bf16[48,512]{1,0:T(8,128)(2,1)S(1)} %get-tuple-element.127), channel_id=1, source_target_pairs={{0,16},{4,20},{8,24},{12,28},{16,0},{20,4},{24,8},{28,12},{1,17},{... | collective-permute-start | bytes 147464 | tf_op jit(solution)/shard_map/ppermute | solution.py:22
  72.2 14.9 %collective-permute-start.15 = (bf16[1024,512]{1,0:T(8,128)(2,1)S(1)}, bf16[1024,512]{1,0:T(8,128)(2,1)S(1)}, u32[]{:S(2)}, u32[]{:S(2)}) collective-permute-start(bf16[1024,512]{1,0:T(8,128)(2,1)S(1)} %pad_maximum_fusion.5.refs_0_), channel_id=1, source_target_pairs={{0,4},{1,9},{2,6},{3,11},{4,0},{5,13},{6,2},{7,15},{8,12},{9,1},{1... | collective-permute-start | bytes 3145736 | tf_op jit(solution)/shard_map/ppermute | solution.py:64
  86.2 1.4 collective-permute-start.14
  87.6 5.6 %collective-permute-start.16 = (bf16[2,256,128]{2,1,0:T(8,128)(2,1)S(1)}, bf16[2,256,128]{2,1,0:T(8,128)(2,1)S(1)}, u32[]{:S(2)}, u32[]{:S(2)}) collective-permute-start(bf16[2,256,128]{2,1,0:T(8,128)(2,1)S(1)} %add_convert_fusion.2), channel_id=1, source_target_pairs={{0,2},{1,3},{2,0},{3,1},{4,6},{5,7},{6,4},{7,5},{8,10},{9,11},{10,... | collective-permute-start | bytes 393224 | tf_op jit(solution)/shard_map/ppermute | solution.py:22
  89.0 9.6 %collective-permute-start.17 = (bf16[512,512]{1,0:T(8,128)(2,1)S(1)}, bf16[512,512]{1,0:T(8,128)(2,1)S(1)}, u32[]{:S(2)}, u32[]{:S(2)}) collective-permute-start(bf16[512,512]{1,0:T(8,128)(2,1)S(1)} %get-tuple-element.143.refs_0_), channel_id=1, source_target_pairs={{0,8},{1,5},{2,10},{3,7},{4,12},{5,1},{6,14},{7,3},{8,0},{9,13},{1... | collective-permute-start | bytes 1572872 | tf_op jit(solution)/shard_map/ppermute | solution.py:64
  97.3 13.1 %collective-permute-start.20 = (bf16[608,512]{1,0:T(8,128)(2,1)S(1)}, bf16[608,512]{1,0:T(8,128)(2,1)S(1)}, u32[]{:S(2)}, u32[]{:S(2)}) collective-permute-start(bf16[608,512]{1,0:T(8,128)(2,1)S(1)} %get-tuple-element.150.refs_0_), channel_id=1, source_target_pairs={{0,4},{1,9},{2,6},{3,11},{4,0},{5,13},{6,2},{7,15},{8,12},{9,1},{1... | collective-permute-start | bytes 1867784 | tf_op jit(solution)/shard_map/ppermute | solution.py:64
  98.6 12.1 %collective-permute-start.19 = (bf16[256,512]{1,0:T(8,128)(2,1)S(1)}, bf16[256,512]{1,0:T(8,128)(2,1)S(1)}, u32[]{:S(2)}, u32[]{:S(2)}) collective-permute-start(bf16[256,512]{1,0:T(8,128)(2,1)S(1)} %get-tuple-element.154.refs_0_), channel_id=1, source_target_pairs={{0,16},{1,17},{2,18},{3,19},{4,20},{5,21},{6,22},{7,23},{8,24},{9,... | collective-permute-start | bytes 786440 | tf_op jit(solution)/shard_map/ppermute | solution.py:64
  102.3 5.7 %collective-permute-start.18 = (f32[2,3,512]{2,1,0:T(4,128)S(1)}, f32[2,3,512]{2,1,0:T(4,128)S(1)}, u32[]{:S(2)}, u32[]{:S(2)}) collective-permute-start(f32[2,3,512]{2,1,0:T(4,128)S(1)} %get-tuple-element.158), channel_id=1, source_target_pairs={{4,0},{8,4},{12,8},{16,12},{20,16},{24,20},{28,24},{5,1},{9,5},{13... | collective-permute-start | bytes 36872 | tf_op jit(solution)/shard_map/ppermute | solution.py:28
  110.8 19.1 %collective-permute-start.21 = (bf16[2,528,512]{2,1,0:T(8,128)(2,1)S(1)}, bf16[2,528,512]{2,1,0:T(8,128)(2,1)S(1)}, u32[]{:S(2)}, u32[]{:S(2)}) collective-permute-start(bf16[2,528,512]{2,1,0:T(8,128)(2,1)S(1)} %fusion.5), channel_id=1, source_target_pairs={{0,1},{1,0},{2,3},{3,2},{4,5},{5,4},{6,7},{7,6},{8,9},{9,8},{10,11... | collective-permute-start | bytes 3244040 | tf_op jit(solution)/shard_map/ppermute | solution.py:22
  111.9 7.9 %collective-permute-start.23 = (bf16[304,512]{1,0:T(8,128)(2,1)S(1)}, bf16[304,512]{1,0:T(8,128)(2,1)S(1)}, u32[]{:S(2)}, u32[]{:S(2)}) collective-permute-start(bf16[304,512]{1,0:T(8,128)(2,1)S(1)} %get-tuple-element.166.refs_0_), channel_id=1, source_target_pairs={{0,8},{1,5},{2,10},{3,7},{4,12},{5,1},{6,14},{7,3},{8,0},{9,13},{1... | collective-permute-start | bytes 933896 | tf_op jit(solution)/shard_map/ppermute | solution.py:64
  114.5 15.3 %collective-permute-start.22 = (bf16[256,512]{1,0:T(8,128)(2,1)S(1)}, bf16[256,512]{1,0:T(8,128)(2,1)S(1)}, u32[]{:S(2)}, u32[]{:S(2)}) collective-permute-start(bf16[256,512]{1,0:T(8,128)(2,1)S(1)} %advance.13.refs_0_), channel_id=1, source_target_pairs={{0,16},{1,17},{2,18},{3,19},{4,20},{5,21},{6,22},{7,23},{8,24},{9,... | collective-permute-start | bytes 786440 | tf_op jit(solution)/shard_map/ppermute | solution.py:64
  130.2 9.6 %collective-permute-start.26 = (bf16[2,272,256]{2,1,0:T(8,128)(2,1)S(1)}, bf16[2,272,256]{2,1,0:T(8,128)(2,1)S(1)}, u32[]{:S(2)}, u32[]{:S(2)}) collective-permute-start(bf16[2,272,256]{2,1,0:T(8,128)(2,1)S(1)} %get-tuple-element.179), channel_id=1, source_target_pairs={{0,2},{1,3},{2,0},{3,1},{4,6},{5,7},{6,4},{7,5},{8,10},{9,11},{10,... | collective-permute-start | bytes 835592 | tf_op jit(solution)/shard_map/ppermute | solution.py:22
  131.5 10.8 %collective-permute-start.25 = (bf16[176,512]{1,0:T(8,128)(2,1)S(1)}, bf16[176,512]{1,0:T(8,128)(2,1)S(1)}, u32[]{:S(2)}, u32[]{:S(2)}) collective-permute-start(bf16[176,512]{1,0:T(8,128)(2,1)S(1)} %get-tuple-element.174.refs_0_), channel_id=1, source_target_pairs={{0,16},{1,17},{2,18},{3,19},{4,20},{5,21},{6,22},{7,23},{8,24},{9,... | collective-permute-start | bytes 540680 | tf_op jit(solution)/shard_map/ppermute | solution.py:64
  131.5 14.0 %collective-permute-start.28 = (bf16[512,512]{1,0:T(8,128)(2,1)S(1)}, bf16[512,512]{1,0:T(8,128)(2,1)S(1)}, u32[]{:S(2)}, u32[]{:S(2)}) collective-permute-start(bf16[512,512]{1,0:T(8,128)(2,1)S(1)} %advance.15.refs_0_), channel_id=1, source_target_pairs={{0,8},{1,5},{2,10},{3,7},{4,12},{5,1},{6,14},{7,3},{8,0},{9,13},{1... | collective-permute-start | bytes 1572872 | tf_op jit(solution)/shard_map/ppermute | solution.py:64
  134.5 16.8 %collective-permute-start.24 = (bf16[2,256,256]{2,1,0:T(8,128)(2,1)S(1)}, bf16[2,256,256]{2,1,0:T(8,128)(2,1)S(1)}, u32[]{:S(2)}, u32[]{:S(2)}) collective-permute-start(bf16[2,256,256]{2,1,0:T(8,128)(2,1)S(1)} %get-tuple-element.180), channel_id=1, source_target_pairs={{0,2},{1,3},{2,0},{3,1},{4,6},{5,7},{6,4},{7,5},{8,10},{9,11},{10,... | collective-permute-start | bytes 786440 | tf_op jit(solution)/shard_map/ppermute | solution.py:22
  142.4 8.8 %collective-permute-start.27 = (bf16[144,512]{1,0:T(8,128)(2,1)S(1)}, bf16[144,512]{1,0:T(8,128)(2,1)S(1)}, u32[]{:S(2)}, u32[]{:S(2)}) collective-permute-start(bf16[144,512]{1,0:T(8,128)(2,1)S(1)} %get-tuple-element.186.refs_0_), channel_id=1, source_target_pairs={{0,16},{1,17},{2,18},{3,19},{4,20},{5,21},{6,22},{7,23},{8,24},{9,... | collective-permute-start | bytes 442376 | tf_op jit(solution)/shard_map/ppermute | solution.py:64
  145.6 18.4 %collective-permute-start.31 = (bf16[1024,512]{1,0:T(8,128)(2,1)S(1)}, bf16[1024,512]{1,0:T(8,128)(2,1)S(1)}, u32[]{:S(2)}, u32[]{:S(2)}) collective-permute-start(bf16[1024,512]{1,0:T(8,128)(2,1)S(1)} %advance.17.refs_0_.refs_2_), channel_id=1, source_target_pairs={{0,4},{1,9},{2,6},{3,11},{4,0},{5,13},{6,2},{7,15},{8,12},{9,1},{1... | collective-permute-start | bytes 3145736 | tf_op jit(solution)/shard_map/ppermute | solution.py:64
  151.2 10.7 %collective-permute-start.29 = (bf16[320,512]{1,0:T(8,128)(2,1)S(1)}, bf16[320,512]{1,0:T(8,128)(2,1)S(1)}, u32[]{:S(2)}, u32[]{:S(2)}) collective-permute-start(bf16[320,512]{1,0:T(8,128)(2,1)S(1)} %advance.18.refs_0_), channel_id=1, source_target_pairs={{0,8},{1,5},{2,10},{3,7},{4,12},{5,1},{6,14},{7,3},{8,0},{9,13},{1... | collective-permute-start | bytes 983048 | tf_op jit(solution)/shard_map/ppermute | solution.py:64
  162.0 10.5 %collective-permute-start.30 = (bf16[624,512]{1,0:T(8,128)(2,1)S(1)}, bf16[624,512]{1,0:T(8,128)(2,1)S(1)}, u32[]{:S(2)}, u32[]{:S(2)}) collective-permute-start(bf16[624,512]{1,0:T(8,128)(2,1)S(1)} %advance.19.refs_0_.own_ref), channel_id=1, source_target_pairs={{0,4},{1,9},{2,6},{3,11},{4,0},{5,13},{6,2},{7,15},{8,12},{9,1},{1... | collective-permute-start | bytes 1916936 | tf_op jit(solution)/shard_map/ppermute | solution.py:64
  (36 other events, 229.2 us)

commit v5 on v4

--- a/solution.py
+++ b/solution.py
@@ -283,11 +283,12 @@
     out, small, (total, rows, wide, sems) = refs[0], refs[1:-4], refs[-4:]
     settle_kernel(1, layout, order_ref, late_ref, out, wide, sems, waits=False)
     deal_rows(sizes, offset, flat_ref, own_ref, late_ref, small, rows)
-    total[...] = own_ref[last : last + 16, :].astype(F32) + late_ref[last : last + 16, :].astype(F32)
+    rider = own_ref[last : last + 16, :].astype(F32) + late_ref[last : last + 16, :].astype(F32)
+    total[...] = rider[0:1, : total.shape[1]]
     settle_kernel(1, layout, order_ref, late_ref, out, wide, sems, starts=False)
 
 
-def finish(orders, flat_order, own, late, layout, offset, count, sizes, into):
+def finish(orders, flat_order, own, late, layout, offset, count, sizes, gain_width, into):
     width = own.shape[1]
     any_space, smem = pl.BlockSpec(memory_space=pl.ANY), pl.BlockSpec(memory_space=pltpu.SMEM)
     shape = jax.ShapeDtypeStruct
@@ -295,7 +296,7 @@
         functools.partial(finish_kernel, sizes, layout, offset, offset + count),
         in_specs=[smem, smem, VMEM, VMEM, any_space],
         out_specs=[any_space] + [VMEM] * (len(sizes) + 1),
-        out_shape=[shape(into.shape, F32)] + [shape((n, width), F32) for n in sizes] + [shape((16, width), F32)],
+        out_shape=[shape(into.shape, F32)] + [shape((n, width), F32) for n in sizes] + [shape((1, gain_width), F32)],
         input_output_aliases={4: 0},
         scratch_shapes=[
             pltpu.VMEM((2 * count, width), F32),
@@ -517,7 +518,7 @@
 
 def ends_kernel(
     low_rank, sent_ref, got_ref, wdt_ref, bias_ref, log_ref, mixed_ref, gy_ref,
-    end_ref, pull_ref, span_ref, dt_ref, u_ref, sig_ref, proj_ref,
+    end_ref, pull_ref, span_ref, dt_ref, u_ref, proj_ref,
     ahead, behind, left_b, left_c, xa, xb, ya, yb,
 ):
     length, width = dt_ref.shape
@@ -545,7 +546,6 @@
         dt = jnp.maximum(pre, 0.0) + jnp.where(small < 1e-3, series, jnp.log(one))
         dt_ref[o, :] = dt
         u_ref[o, :] = dt * mixed_ref[o, :]
-        sig_ref[o, :] = jnp.where(pre >= 0.0, 1.0, small) / one
     dt = dt_ref[...]
     high = dt.astype(BF16)
     low = (dt - high.astype(F32)).astype(BF16)
@@ -611,9 +611,9 @@
             tokens,
             tokens,
         ],
-        out_specs=[state_spec, state_spec, lane_spec(1, width), tokens, tokens, tokens, narrow],
+        out_specs=[state_spec, state_spec, lane_spec(1, width), tokens, tokens, narrow],
         out_shape=[state, state, shape((lanes, 1, width), F32)]
-        + [pltpu.HBM((lanes, length, width), F32)] * 3
+        + [pltpu.HBM((lanes, length, width), F32)] * 2
         + [shape(sent.shape, F32)],
         scratch_shapes=[pltpu.VMEM((length, width), F32)] * 2
         + [pltpu.VMEM((length // CHUNK * states, CHUNK * states), BF16)] * 2
@@ -929,7 +929,7 @@
     )
     grad_gated = jnp.einsum("ltd,ed->lte", grad_whole, w_out, preferred_element_type=F32)
     grad_scan = grad_gated * jax.nn.silu(gate_in)
-    end_state, pulled, span, dt, source, slope_dt, projected = scan_ends(
+    end_state, pulled, span, dt, source, projected = scan_ends(
         low_rank, sent, got, w_dt, dt_bias[None], decay_log, mixed, grad_scan
     )
     span = span + span_more
@@ -978,7 +978,7 @@
     turn, pull, part, grad_log = scan_backward(
         low_rank, projected, decay_log, dt, source, grad_scan, last, grad_read, states_all, *sum_first.kept
     )
-    grad_slope = (turn + pull * mixed) * slope_dt
+    grad_slope = (turn + pull * mixed) * -jnp.expm1(-dt)
     grad_pre = grad_slope.astype(BF16)
     part = part + jnp.einsum("lte,re->ltr", grad_pre, w_dt, preferred_element_type=F32)
     sent = part.astype(BF16)
@@ -1117,12 +1117,12 @@
     in_w = settle(orders, ends[:1], [(0, 0, 0, 0, halves, False, 0, half)], [in_shape], [in_w])
     count = small_half
     in_w, *parts, grad_gain = finish(
-        orders, flat_order, *ends, [(0, 0, 0, 1, halves, False, 0, half)], half, count, sizes, in_w[0]
+        orders, flat_order, *ends, [(0, 0, 0, 1, halves, False, 0, half)], half, count, sizes, shard_width, in_w[0]
     )
     return (
         output,
         input_grad,
-        grad_gain[0, :shard_width],
+        grad_gain[0],
         in_w,
         parts[0],
         parts[1][0],

time: 176 us -> 175 us (level)
    unnamed x74 -> x72, local copies, waits for them, and re-layouts: 3.89 us -> 3.88 us
where the time goes in v5:
time: 175 us; the launch traced here: 174 us
  waiting for transfers between devices  57.4 us (33%)
  starting transfers between devices  41.7 us (24%)
  Pallas kernels  37.3 us (21%)
  other arithmetic  17.2 us (10%)
  matrix products  10.9 us (6%)
  local copies, waits for them, and re-layouts  7.98 us (5%)
  between operations  1.85 us (1%)
    ppermute x12, waiting for transfers between devices, swap(): return lax.ppermute(block, ('seq', 'mp'), route)  37.6 us
    ppermute x18, starting transfers between devices, swap(): return lax.ppermute(block, axis, [(i, i ^ bit) for i in range(devices)])  19.4 us
    ppermute x12, starting transfers between devices, swap(): return lax.ppermute(block, ('seq', 'mp'), route)  17.2 us
    ppermute x18, waiting for transfers between devices, swap(): return lax.ppermute(block, axis, [(i, i ^ bit) for i in range(devices)])  15.6 us
    pallas_call x1, Pallas kernels, scan_backward(): pl.pallas_call(functools.partial(backward_kernel, low_rank, lanes), grid=...  11 us
    pallas_call x1, Pallas kernels, scan_ends(): pl.pallas_call(functools.partial(ends_kernel, low_rank), grid=(lanes,), i...  8.54 us
    pallas_call x1, Pallas kernels, scan_forward(): pl.pallas_call(functools.partial(forward_kernel, low_rank, lanes), grid=(...  7.66 us
    ppermute x2, starting transfers between devices, from_behind(): return lax.ppermute(block, axis, route)  5.04 us
  transfers between devices with their start and end apart: 32, of which 20 were waited for; matrix products, arithmetic and copies ran while one was open for 15% of the time, Pallas kernels for 9%

profile of v5, /device:TPU:0, one launch (start us, length us, event | category | flops | bytes accessed | tf_op | source)
XLA Modules:
  0.0 174.4 jit_solution(3299165280253846223)
XLA Ops:
  2.0 3.0 %collective-permute-start.1 = (bf16[2,256,256]{2,1,0:T(8,128)(2,1)S(1)}, bf16[2,256,256]{2,1,0:T(8,128)(2,1)}, u32[]{:S(2)}, u32[]{:S(2)}) collective-permute-start(bf16[2,256,256]{2,1,0:T(8,128)(2,1)S(1)} %get-tuple-element.244), channel_id=1, source_target_pairs={{0,2},{1,3},{2,0},{3,1},{4,6},{5,7},{6,4},{7,5},{8,10},{9,11},{10,... | collective-permute-start | bytes 786440 | tf_op jit(solution)/shard_map/ppermute | solution.py:22
  8.0 2.5 %dynamic-slice_convert_fusion.3 = (bf16[2,256,512]{2,1,0:T(8,128)(2,1)S(1)}, bf16[2,256,512]{2,1,0:T(8,128)(2,1)S(1)}, bf16[2,256,512]{2,1,0:T(8,128)(2,1)S(1)}, bf16[2,256,512]{2,1,0:T(8,128)(2,1)S(1)}) fusion(f32[2,1024,512]{2,1,0:T(8,128)} %param.17, s32[]{:T(128)S(6)} %select_n.182, s32[]{:T(128)S(6)} %select_n.183, s32[]{:T(128)S(6)} %select_n.185, ...), kind=kLoop, calls=%fused_computation.58 | loop fusion | bytes 4194320 | tf_op jit(solution)/shard_map/convert.3
  12.1 2.9 %convert_element_type.206 = bf16[512,1024]{1,0:T(8,128)(2,1)} convert(f32[512,1024]{1,0:T(8,128)} %param.25) | non-fusion elementwise | flops 524288 | bytes 3145728 | tf_op jit(solution)/shard_map/convert_element_type | solution.py:891
  15.1 1.8 %collective-permute-start.6 = (bf16[2,256,256]{2,1,0:T(8,128)(2,1)S(1)}, bf16[2,256,256]{2,1,0:T(8,128)(2,1)S(1)}, u32[]{:S(2)}, u32[]{:S(2)}) collective-permute-start(bf16[2,256,256]{2,1,0:T(8,128)(2,1)S(1)} %convert_element_type.211), channel_id=1, source_target_pairs={{0,2},{1,3},{2,0},{3,1},{4,6},{5,7},{6,4},{7,5},{8,10},{9,11},{10,... | collective-permute-start | bytes 786440 | tf_op jit(solution)/shard_map/ppermute | solution.py:22
  18.4 3.5 %collective-permute-start.5 = (bf16[2,8,1024]{2,1,0:T(8,128)(2,1)S(1)}, bf16[2,8,1024]{2,1,0:T(8,128)(2,1)S(1)}, u32[]{:S(2)}, u32[]{:S(2)}) collective-permute-start(bf16[2,8,1024]{2,1,0:T(8,128)(2,1)S(1)} %slice.139), channel_id=1, source_target_pairs={{0,4},{4,8},{8,12},{12,16},{16,20},{20,24},{24,28},{1,5},{5,9},{9,... | collective-permute-start | bytes 98312 | tf_op jit(solution)/shard_map/ppermute | solution.py:28
  24.5 1.6 fusion.68
  29.7 1.6 collective-permute-start.8
  36.2 8.5 %scan_ends.1 = (f32[2,16,512]{2,1,0:T(8,128)S(1)}, f32[2,16,512]{2,1,0:T(8,128)S(1)}, f32[2,1,512]{2,1,0:T(1,128)S(1)}, f32[2,256,512]{2,1,0:T(8,128)}, f32[2,25...) custom-call(bf16[2,256,128]{2,1,0:T(8,128)(2,1)S(1)} %add_convert_fusion.4.sent_ref, ...), custom_call_target="tpu_custom_call" | custom-call | flops 536870912 | bytes 8388608 | tf_op jit(solution)/shard_map/scan_ends/pallas_call | solution.py:602
  47.0 2.5 %collective-permute-done.11.got_ref = bf16[80,512]{1,0:T(8,128)(2,1)S(1)} collective-permute-done((bf16[80,512]{1,0:T(8,128)(2,1)S(1)}, bf16[80,512]{1,0:T(8,128)(2,1)S(1)}, u32[]{:S(2)}, u32[]{:S(2)}) %collective-permute-start.11) | collective-permute-done | bytes 81952 | tf_op jit(solution)/shard_map/ppermute | solution.py:22
  50.2 2.5 %collective-permute-start.12 = (bf16[80,512]{1,0:T(8,128)(2,1)S(1)}, bf16[80,512]{1,0:T(8,128)(2,1)S(1)}, u32[]{:S(2)}, u32[]{:S(2)}) collective-permute-start(bf16[80,512]{1,0:T(8,128)(2,1)S(1)} %get-tuple-element.123), channel_id=1, source_target_pairs={{0,8},{4,12},{8,0},{12,4},{16,24},{20,28},{24,16},{28,20},{1,9},{5... | collective-permute-start | bytes 245768 | tf_op jit(solution)/shard_map/ppermute | solution.py:22
  52.9 2.2 %collective-permute-done.12.got_ref = bf16[80,512]{1,0:T(8,128)(2,1)S(1)} collective-permute-done((bf16[80,512]{1,0:T(8,128)(2,1)S(1)}, bf16[80,512]{1,0:T(8,128)(2,1)S(1)}, u32[]{:S(2)}, u32[]{:S(2)}) %collective-permute-start.12) | collective-permute-done | bytes 81952 | tf_op jit(solution)/shard_map/ppermute | solution.py:22
  55.8 3.1 %collective-permute-start.13 = (bf16[48,512]{1,0:T(8,128)(2,1)S(1)}, bf16[48,512]{1,0:T(8,128)(2,1)S(1)}, u32[]{:S(2)}, u32[]{:S(2)}) collective-permute-start(bf16[48,512]{1,0:T(8,128)(2,1)S(1)} %get-tuple-element.126), channel_id=1, source_target_pairs={{0,16},{4,20},{8,24},{12,28},{16,0},{20,4},{24,8},{28,12},{1,17},{... | collective-permute-start | bytes 147464 | tf_op jit(solution)/shard_map/ppermute | solution.py:22
  59.0 1.9 %collective-permute-done.13.got_ref = bf16[48,512]{1,0:T(8,128)(2,1)S(1)} collective-permute-done((bf16[48,512]{1,0:T(8,128)(2,1)S(1)}, bf16[48,512]{1,0:T(8,128)(2,1)S(1)}, u32[]{:S(2)}, u32[]{:S(2)}) %collective-permute-start.13) | collective-permute-done | bytes 49184 | tf_op jit(solution)/shard_map/ppermute | solution.py:22
  62.3 7.7 %scan_forward.1 = (f32[2,256,512]{2,1,0:T(8,128)S(1)}, f32[2,256,128]{2,1,0:T(8,128)S(1)}, bf16[2,4096,512]{2,1,0:T(8,128)(2,1)S(1)}) custom-call(s32[2]{0:T(128)S(1)} %bitcast.152, f32[2,256,128]{2,1,0:T(8,128)S(1)} %get-tuple-element.120.proj_ref, f32[16,512]{1,0:T(8,128)S(1)} %copy-done.2, f32[2,256,512]{2,1,0:T(8,128)S(1)} %copy-done, ...), custom_call_target="tpu_custom_call" | custom-call | flops 536870912 | bytes 8388608 | tf_op jit(solution)/shard_map/scan_forward/pallas_call | solution.py:700
  73.7 11.0 %scan_backward.1 = (f32[2,256,512]{2,1,0:T(8,128)S(1)}, f32[2,256,512]{2,1,0:T(8,128)S(1)}, f32[2,256,128]{2,1,0:T(8,128)S(1)}, f32[2,16,512]{2,1,0:T(8,128)S(1)}) custom-call(f32[2,256,128]{2,1,0:T(8,128)S(1)} %get-tuple-element.120.proj_ref, f32[16,512]{1,0:T(8,128)S(1)} %copy-done.2, f32[2,256,512]{2,1,0:T(8,128)S(1)} %copy-done, ...), custom_call_target="tpu_custom_call" | custom-call | flops 805306368 | bytes 8388608 | tf_op jit(solution)/shard_map/scan_backward/pallas_call | solution.py:814
  90.3 2.4 %collective-permute-done.16 = bf16[2,256,128]{2,1,0:T(8,128)(2,1)S(1)} collective-permute-done((bf16[2,256,128]{2,1,0:T(8,128)(2,1)S(1)}, bf16[2,256,128]{2,1,0:T(8,128)(2,1)S(1)}, u32[]{:S(2)}, u32[]{:S(2)}) %collective-permute-start.16) | collective-permute-done | bytes 131104 | tf_op jit(solution)/shard_map/ppermute | solution.py:22
  98.1 3.0 %collective-permute-start.19 = (bf16[256,512]{1,0:T(8,128)(2,1)S(1)}, bf16[256,512]{1,0:T(8,128)(2,1)S(1)}, u32[]{:S(2)}, u32[]{:S(2)}) collective-permute-start(bf16[256,512]{1,0:T(8,128)(2,1)S(1)} %get-tuple-element.152.refs_0_), channel_id=1, source_target_pairs={{0,16},{1,17},{2,18},{3,19},{4,20},{5,21},{6,22},{7,23},{8,24},{9,... | collective-permute-start | bytes 786440 | tf_op jit(solution)/shard_map/ppermute | solution.py:64
  104.1 3.3 %collective-permute-done.18 = f32[2,3,512]{2,1,0:T(4,128)S(1)} collective-permute-done((f32[2,3,512]{2,1,0:T(4,128)S(1)}, f32[2,3,512]{2,1,0:T(4,128)S(1)}, u32[]{:S(2)}, u32[]{:S(2)}) %collective-permute-start.18) | collective-permute-done | bytes 12320 | tf_op jit(solution)/shard_map/ppermute | solution.py:28
  111.3 2.7 %collective-permute-start.23 = (bf16[304,512]{1,0:T(8,128)(2,1)S(1)}, bf16[304,512]{1,0:T(8,128)(2,1)S(1)}, u32[]{:S(2)}, u32[]{:S(2)}) collective-permute-start(bf16[304,512]{1,0:T(8,128)(2,1)S(1)} %get-tuple-element.164.refs_0_), channel_id=1, source_target_pairs={{0,8},{1,5},{2,10},{3,7},{4,12},{5,1},{6,14},{7,3},{8,0},{9,13},{1... | collective-permute-start | bytes 933896 | tf_op jit(solution)/shard_map/ppermute | solution.py:64
  114.0 2.7 %collective-permute-start.22 = (bf16[256,512]{1,0:T(8,128)(2,1)S(1)}, bf16[256,512]{1,0:T(8,128)(2,1)S(1)}, u32[]{:S(2)}, u32[]{:S(2)}) collective-permute-start(bf16[256,512]{1,0:T(8,128)(2,1)S(1)} %advance.13.refs_0_), channel_id=1, source_target_pairs={{0,16},{1,17},{2,18},{3,19},{4,20},{5,21},{6,22},{7,23},{8,24},{9,... | collective-permute-start | bytes 786440 | tf_op jit(solution)/shard_map/ppermute | solution.py:64
  116.7 2.6 %collective-permute-done.23.refs_1_ = bf16[304,512]{1,0:T(8,128)(2,1)S(1)} collective-permute-done((bf16[304,512]{1,0:T(8,128)(2,1)S(1)}, bf16[304,512]{1,0:T(8,128)(2,1)S(1)}, u32[]{:S(2)}, u32[]{:S(2)}) %collective-permute-start.23) | collective-permute-done | bytes 311328 | tf_op jit(solution)/shard_map/ppermute | solution.py:64
  119.4 10.0 %collective-permute-done.22.refs_1_ = bf16[256,512]{1,0:T(8,128)(2,1)S(1)} collective-permute-done((bf16[256,512]{1,0:T(8,128)(2,1)S(1)}, bf16[256,512]{1,0:T(8,128)(2,1)S(1)}, u32[]{:S(2)}, u32[]{:S(2)}) %collective-permute-start.22) | collective-permute-done | bytes 262176 | tf_op jit(solution)/shard_map/ppermute | solution.py:64
  130.9 3.0 %collective-permute-start.28 = (bf16[512,512]{1,0:T(8,128)(2,1)S(1)}, bf16[512,512]{1,0:T(8,128)(2,1)S(1)}, u32[]{:S(2)}, u32[]{:S(2)}) collective-permute-start(bf16[512,512]{1,0:T(8,128)(2,1)S(1)} %advance.15.refs_0_), channel_id=1, source_target_pairs={{0,8},{1,5},{2,10},{3,7},{4,12},{5,1},{6,14},{7,3},{8,0},{9,13},{1... | collective-permute-start | bytes 1572872 | tf_op jit(solution)/shard_map/ppermute | solution.py:64
  134.5 4.7 %collective-permute-done.26 = bf16[2,272,256]{2,1,0:T(8,128)(2,1)S(1)} collective-permute-done((bf16[2,272,256]{2,1,0:T(8,128)(2,1)S(1)}, bf16[2,272,256]{2,1,0:T(8,128)(2,1)S(1)}, u32[]{:S(2)}, u32[]{:S(2)}) %collective-permute-start.26) | collective-permute-done | bytes 278560 | tf_op jit(solution)/shard_map/ppermute | solution.py:22
  141.8 3.1 %collective-permute-done.28.refs_1_ = bf16[512,512]{1,0:T(8,128)(2,1)S(1)} collective-permute-done((bf16[512,512]{1,0:T(8,128)(2,1)S(1)}, bf16[512,512]{1,0:T(8,128)(2,1)S(1)}, u32[]{:S(2)}, u32[]{:S(2)}) %collective-permute-start.28) | collective-permute-done | bytes 524320 | tf_op jit(solution)/shard_map/ppermute | solution.py:64
  145.0 1.9 %collective-permute-start.31 = (bf16[1024,512]{1,0:T(8,128)(2,1)S(1)}, bf16[1024,512]{1,0:T(8,128)(2,1)S(1)}, u32[]{:S(2)}, u32[]{:S(2)}) collective-permute-start(bf16[1024,512]{1,0:T(8,128)(2,1)S(1)} %advance.17.refs_0_.refs_2_), channel_id=1, source_target_pairs={{0,4},{1,9},{2,6},{3,11},{4,0},{5,13},{6,2},{7,15},{8,12},{9,1},{1... | collective-permute-start | bytes 3145736 | tf_op jit(solution)/shard_map/ppermute | solution.py:64
  146.9 3.7 %collective-permute-done.27.refs_1_ = bf16[144,512]{1,0:T(8,128)(2,1)S(1)} collective-permute-done((bf16[144,512]{1,0:T(8,128)(2,1)S(1)}, bf16[144,512]{1,0:T(8,128)(2,1)S(1)}, u32[]{:S(2)}, u32[]{:S(2)}) %collective-permute-start.27) | collective-permute-done | bytes 147488 | tf_op jit(solution)/shard_map/ppermute | solution.py:64
  151.6 9.7 %collective-permute-done.29.refs_1_ = bf16[320,512]{1,0:T(8,128)(2,1)S(1)} collective-permute-done((bf16[320,512]{1,0:T(8,128)(2,1)S(1)}, bf16[320,512]{1,0:T(8,128)(2,1)S(1)}, u32[]{:S(2)}, u32[]{:S(2)}) %collective-permute-start.29) | collective-permute-done | bytes 327712 | tf_op jit(solution)/shard_map/ppermute | solution.py:64
  161.5 1.9 %collective-permute-done.31.refs_1_.refs_3_ = bf16[1024,512]{1,0:T(8,128)(2,1)S(1)} collective-permute-done((bf16[1024,512]{1,0:T(8,128)(2,1)S(1)}, bf16[1024,512]{1,0:T(8,128)(2,1)S(1)}, u32[]{:S(2)}, u32[]{:S(2)}) %collective-permute-start.31) | collective-permute-done | bytes 1048608 | tf_op jit(solution)/shard_map/ppermute | solution.py:64
  163.3 2.7 %settle.2 = (f32[2,1024,512]{2,1,0:T(8,128)}, f32[512,1024]{1,0:T(8,128)}) custom-call(s32[12]{0:T(128)S(1)} %concatenate.49.order_ref, bf16[1024,512]{1,0:T(8,128)(2,1)S(1)} %advance.17.refs_0_.refs_2_, bf16[1024,512]{1,0:T(8,128)(2,1)S(1)} %collective-permute-done.31.refs_1_.refs_3_, bf16[1024,512]{1,0:T(8,128)(2,1)S(1)} %advance.17.refs_0_.refs_2_, ...), custom_call_target="tpu_custom_call" | custom-call | tf_op jit(solution)/shard_map/settle/pallas_call | solution.py:252
  167.6 4.2 %collective-permute-done.30.late_ref = bf16[624,512]{1,0:T(8,128)(2,1)S(1)} collective-permute-done((bf16[624,512]{1,0:T(8,128)(2,1)S(1)}, bf16[624,512]{1,0:T(8,128)(2,1)S(1)}, u32[]{:S(2)}, u32[]{:S(2)}) %collective-permute-start.30) | collective-permute-done | bytes 639008 | tf_op jit(solution)/shard_map/ppermute | solution.py:64
  171.9 2.3 %finish.1 = (f32[2,1024,512]{2,1,0:T(8,128)}, f32[4,512]{1,0:T(4,128)}, f32[1,512]{1,0:T(1,128)}, f32[1,512]{1,0:T(1,128)}, f32[1,512]{1,0:T(1,128)}, /*index=5*...) custom-call(s32[12]{0:T(128)S(1)} %concatenate.49.order_ref, ...), custom_call_target="tpu_custom_call", output_to_operand_aliasing={{0}: (4, {})} | custom-call | tf_op jit(solution)/shard_map/finish/pallas_call | solution.py:295
  (209 shorter events, 52.0 us)
Async XLA Ops:
  2.0 9.7 %collective-permute-start.1 = (bf16[2,256,256]{2,1,0:T(8,128)(2,1)S(1)}, bf16[2,256,256]{2,1,0:T(8,128)(2,1)}, u32[]{:S(2)}, u32[]{:S(2)}) collective-permute-start(bf16[2,256,256]{2,1,0:T(8,128)(2,1)S(1)} %get-tuple-element.244), channel_id=1, source_target_pairs={{0,2},{1,3},{2,0},{3,1},{4,6},{5,7},{6,4},{7,5},{8,10},{9,11},{10,... | collective-permute-start | bytes 786440 | tf_op jit(solution)/shard_map/ppermute | solution.py:22
  5.0 11.9 %collective-permute-start = (bf16[2,256,256]{2,1,0:T(8,128)(2,1)S(1)}, bf16[2,256,256]{2,1,0:T(8,128)(2,1)}, u32[]{:S(2)}, u32[]{:S(2)}) collective-permute-start(bf16[2,256,256]{2,1,0:T(8,128)(2,1)S(1)} %get-tuple-element.244), channel_id=1, source_target_pairs={{0,1},{1,0},{2,3},{3,2},{4,5},{5,4},{6,7},{7,6},{8,9},{9,8},{10,11... | collective-permute-start | bytes 786440 | tf_op jit(solution)/shard_map/ppermute | solution.py:22
  5.0 6.4 %collective-permute-start.3 = (f32[2,256]{1,0:T(2,128)S(1)}, f32[2,256]{1,0:T(2,128)S(1)}, u32[]{:S(2)}, u32[]{:S(2)}) collective-permute-start(f32[2,256]{1,0:T(2,128)S(1)} %get-tuple-element.243), channel_id=1, source_target_pairs={{0,2},{1,3},{2,0},{3,1},{4,6},{5,7},{6,4},{7,5},{8,10},{9,11},{10,... | collective-permute-start | bytes 6152 | tf_op jit(solution)/shard_map/ppermute | solution.py:22
  11.5 3.6 %collective-permute-start.4 = (f32[2,256]{1,0:T(2,128)S(1)}, f32[2,256]{1,0:T(2,128)S(1)}, u32[]{:S(2)}, u32[]{:S(2)}) collective-permute-start(f32[2,256]{1,0:T(2,128)S(1)} %add.238), channel_id=1, source_target_pairs={{0,1},{1,0},{2,3},{3,2},{4,5},{5,4},{6,7},{7,6},{8,9},{9,8},{10,11... | collective-permute-start | bytes 6152 | tf_op jit(solution)/shard_map/ppermute | solution.py:22
  11.7 5.2 %collective-permute-start.2 = (bf16[2,256,256]{2,1,0:T(8,128)(2,1)}, bf16[2,256,256]{2,1,0:T(8,128)(2,1)}, u32[]{:S(2)}, u32[]{:S(2)}) collective-permute-start(bf16[2,256,256]{2,1,0:T(8,128)(2,1)} %collective-permute-done.1), channel_id=1, source_target_pairs={{0,1},{1,0},{2,3},{3,2},{4,5},{5,4},{6,7},{7,6},{8,9},{9,8},{10,11... | collective-permute-start | bytes 786440 | tf_op jit(solution)/shard_map/ppermute | solution.py:22
  15.1 8.7 %collective-permute-start.6 = (bf16[2,256,256]{2,1,0:T(8,128)(2,1)S(1)}, bf16[2,256,256]{2,1,0:T(8,128)(2,1)S(1)}, u32[]{:S(2)}, u32[]{:S(2)}) collective-permute-start(bf16[2,256,256]{2,1,0:T(8,128)(2,1)S(1)} %convert_element_type.211), channel_id=1, source_target_pairs={{0,2},{1,3},{2,0},{3,1},{4,6},{5,7},{6,4},{7,5},{8,10},{9,11},{10,... | collective-permute-start | bytes 786440 | tf_op jit(solution)/shard_map/ppermute | solution.py:22
  18.4 5.1 %collective-permute-start.5 = (bf16[2,8,1024]{2,1,0:T(8,128)(2,1)S(1)}, bf16[2,8,1024]{2,1,0:T(8,128)(2,1)S(1)}, u32[]{:S(2)}, u32[]{:S(2)}) collective-permute-start(bf16[2,8,1024]{2,1,0:T(8,128)(2,1)S(1)} %slice.139), channel_id=1, source_target_pairs={{0,4},{4,8},{8,12},{12,16},{16,20},{20,24},{24,28},{1,5},{5,9},{9,... | collective-permute-start | bytes 98312 | tf_op jit(solution)/shard_map/ppermute | solution.py:28
  27.2 1.5 collective-permute-start.7
  29.7 6.4 %collective-permute-start.8 = (bf16[2,256,128]{2,1,0:T(8,128)(2,1)S(1)}, bf16[2,256,128]{2,1,0:T(8,128)(2,1)S(1)}, u32[]{:S(2)}, u32[]{:S(2)}) collective-permute-start(bf16[2,256,128]{2,1,0:T(8,128)(2,1)S(1)} %add_convert_fusion.4.sent_ref), channel_id=1, source_target_pairs={{0,2},{1,3},{2,0},{3,1},{4,6},{5,7},{6,4},{7,5},{8,10},{9,11},{10,... | collective-permute-start | bytes 393224 | tf_op jit(solution)/shard_map/ppermute | solution.py:22
  31.4 2.6 %collective-permute-start.9 = (bf16[2,256,256]{2,1,0:T(8,128)(2,1)}, bf16[2,256,256]{2,1,0:T(8,128)(2,1)S(1)}, u32[]{:S(2)}, u32[]{:S(2)}) collective-permute-start(bf16[2,256,256]{2,1,0:T(8,128)(2,1)} %copy-done.13), channel_id=1, source_target_pairs={{0,1},{1,0},{2,3},{3,2},{4,5},{5,4},{6,7},{7,6},{8,9},{9,8},{10,11... | collective-permute-start | bytes 786440 | tf_op jit(solution)/shard_map/ppermute | solution.py:22
  31.4 2.6 %collective-permute-start.10 = (bf16[2,256,256]{2,1,0:T(8,128)(2,1)}, bf16[2,256,256]{2,1,0:T(8,128)(2,1)S(1)}, u32[]{:S(2)}, u32[]{:S(2)}) collective-permute-start(bf16[2,256,256]{2,1,0:T(8,128)(2,1)} %copy-done.18), channel_id=1, source_target_pairs={{0,1},{1,0},{2,3},{3,2},{4,5},{5,4},{6,7},{7,6},{8,9},{9,8},{10,11... | collective-permute-start | bytes 786440 | tf_op jit(solution)/shard_map/ppermute | solution.py:22
  45.0 4.5 %collective-permute-start.11 = (bf16[80,512]{1,0:T(8,128)(2,1)S(1)}, bf16[80,512]{1,0:T(8,128)(2,1)S(1)}, u32[]{:S(2)}, u32[]{:S(2)}) collective-permute-start(bf16[80,512]{1,0:T(8,128)(2,1)S(1)} %pad.45), channel_id=1, source_target_pairs={{0,4},{4,0},{8,12},{12,8},{16,20},{20,16},{24,28},{28,24},{1,5},{5... | collective-permute-start | bytes 245768 | tf_op jit(solution)/shard_map/ppermute | solution.py:22
  50.2 5.0 %collective-permute-start.12 = (bf16[80,512]{1,0:T(8,128)(2,1)S(1)}, bf16[80,512]{1,0:T(8,128)(2,1)S(1)}, u32[]{:S(2)}, u32[]{:S(2)}) collective-permute-start(bf16[80,512]{1,0:T(8,128)(2,1)S(1)} %get-tuple-element.123), channel_id=1, source_target_pairs={{0,8},{4,12},{8,0},{12,4},{16,24},{20,28},{24,16},{28,20},{1,9},{5... | collective-permute-start | bytes 245768 | tf_op jit(solution)/shard_map/ppermute | solution.py:22
  55.8 5.2 %collective-permute-start.13 = (bf16[48,512]{1,0:T(8,128)(2,1)S(1)}, bf16[48,512]{1,0:T(8,128)(2,1)S(1)}, u32[]{:S(2)}, u32[]{:S(2)}) collective-permute-start(bf16[48,512]{1,0:T(8,128)(2,1)S(1)} %get-tuple-element.126), channel_id=1, source_target_pairs={{0,16},{4,20},{8,24},{12,28},{16,0},{20,4},{24,8},{28,12},{1,17},{... | collective-permute-start | bytes 147464 | tf_op jit(solution)/shard_map/ppermute | solution.py:22
  71.7 14.9 %collective-permute-start.15 = (bf16[1024,512]{1,0:T(8,128)(2,1)S(1)}, bf16[1024,512]{1,0:T(8,128)(2,1)S(1)}, u32[]{:S(2)}, u32[]{:S(2)}) collective-permute-start(bf16[1024,512]{1,0:T(8,128)(2,1)S(1)} %pad_maximum_fusion.5.refs_0_), channel_id=1, source_target_pairs={{0,4},{1,9},{2,6},{3,11},{4,0},{5,13},{6,2},{7,15},{8,12},{9,1},{1... | collective-permute-start | bytes 3145736 | tf_op jit(solution)/shard_map/ppermute | solution.py:64
  85.7 1.4 collective-permute-start.14
  87.1 5.6 %collective-permute-start.16 = (bf16[2,256,128]{2,1,0:T(8,128)(2,1)S(1)}, bf16[2,256,128]{2,1,0:T(8,128)(2,1)S(1)}, u32[]{:S(2)}, u32[]{:S(2)}) collective-permute-start(bf16[2,256,128]{2,1,0:T(8,128)(2,1)S(1)} %add_convert_fusion.2), channel_id=1, source_target_pairs={{0,2},{1,3},{2,0},{3,1},{4,6},{5,7},{6,4},{7,5},{8,10},{9,11},{10,... | collective-permute-start | bytes 393224 | tf_op jit(solution)/shard_map/ppermute | solution.py:22
  88.4 9.6 %collective-permute-start.17 = (bf16[512,512]{1,0:T(8,128)(2,1)S(1)}, bf16[512,512]{1,0:T(8,128)(2,1)S(1)}, u32[]{:S(2)}, u32[]{:S(2)}) collective-permute-start(bf16[512,512]{1,0:T(8,128)(2,1)S(1)} %get-tuple-element.141.refs_0_), channel_id=1, source_target_pairs={{0,8},{1,5},{2,10},{3,7},{4,12},{5,1},{6,14},{7,3},{8,0},{9,13},{1... | collective-permute-start | bytes 1572872 | tf_op jit(solution)/shard_map/ppermute | solution.py:64
  96.8 13.1 %collective-permute-start.20 = (bf16[608,512]{1,0:T(8,128)(2,1)S(1)}, bf16[608,512]{1,0:T(8,128)(2,1)S(1)}, u32[]{:S(2)}, u32[]{:S(2)}) collective-permute-start(bf16[608,512]{1,0:T(8,128)(2,1)S(1)} %get-tuple-element.148.refs_0_), channel_id=1, source_target_pairs={{0,4},{1,9},{2,6},{3,11},{4,0},{5,13},{6,2},{7,15},{8,12},{9,1},{1... | collective-permute-start | bytes 1867784 | tf_op jit(solution)/shard_map/ppermute | solution.py:64
  98.1 12.1 %collective-permute-start.19 = (bf16[256,512]{1,0:T(8,128)(2,1)S(1)}, bf16[256,512]{1,0:T(8,128)(2,1)S(1)}, u32[]{:S(2)}, u32[]{:S(2)}) collective-permute-start(bf16[256,512]{1,0:T(8,128)(2,1)S(1)} %get-tuple-element.152.refs_0_), channel_id=1, source_target_pairs={{0,16},{1,17},{2,18},{3,19},{4,20},{5,21},{6,22},{7,23},{8,24},{9,... | collective-permute-start | bytes 786440 | tf_op jit(solution)/shard_map/ppermute | solution.py:64
  101.7 5.7 %collective-permute-start.18 = (f32[2,3,512]{2,1,0:T(4,128)S(1)}, f32[2,3,512]{2,1,0:T(4,128)S(1)}, u32[]{:S(2)}, u32[]{:S(2)}) collective-permute-start(f32[2,3,512]{2,1,0:T(4,128)S(1)} %get-tuple-element.156), channel_id=1, source_target_pairs={{4,0},{8,4},{12,8},{16,12},{20,16},{24,20},{28,24},{5,1},{9,5},{13... | collective-permute-start | bytes 36872 | tf_op jit(solution)/shard_map/ppermute | solution.py:28
  110.3 19.1 %collective-permute-start.21 = (bf16[2,528,512]{2,1,0:T(8,128)(2,1)S(1)}, bf16[2,528,512]{2,1,0:T(8,128)(2,1)S(1)}, u32[]{:S(2)}, u32[]{:S(2)}) collective-permute-start(bf16[2,528,512]{2,1,0:T(8,128)(2,1)S(1)} %fusion.5), channel_id=1, source_target_pairs={{0,1},{1,0},{2,3},{3,2},{4,5},{5,4},{6,7},{7,6},{8,9},{9,8},{10,11... | collective-permute-start | bytes 3244040 | tf_op jit(solution)/shard_map/ppermute | solution.py:22
  111.3 8.0 %collective-permute-start.23 = (bf16[304,512]{1,0:T(8,128)(2,1)S(1)}, bf16[304,512]{1,0:T(8,128)(2,1)S(1)}, u32[]{:S(2)}, u32[]{:S(2)}) collective-permute-start(bf16[304,512]{1,0:T(8,128)(2,1)S(1)} %get-tuple-element.164.refs_0_), channel_id=1, source_target_pairs={{0,8},{1,5},{2,10},{3,7},{4,12},{5,1},{6,14},{7,3},{8,0},{9,13},{1... | collective-permute-start | bytes 933896 | tf_op jit(solution)/shard_map/ppermute | solution.py:64
  114.0 15.3 %collective-permute-start.22 = (bf16[256,512]{1,0:T(8,128)(2,1)S(1)}, bf16[256,512]{1,0:T(8,128)(2,1)S(1)}, u32[]{:S(2)}, u32[]{:S(2)}) collective-permute-start(bf16[256,512]{1,0:T(8,128)(2,1)S(1)} %advance.13.refs_0_), channel_id=1, source_target_pairs={{0,16},{1,17},{2,18},{3,19},{4,20},{5,21},{6,22},{7,23},{8,24},{9,... | collective-permute-start | bytes 786440 | tf_op jit(solution)/shard_map/ppermute | solution.py:64
  129.6 9.6 %collective-permute-start.26 = (bf16[2,272,256]{2,1,0:T(8,128)(2,1)S(1)}, bf16[2,272,256]{2,1,0:T(8,128)(2,1)S(1)}, u32[]{:S(2)}, u32[]{:S(2)}) collective-permute-start(bf16[2,272,256]{2,1,0:T(8,128)(2,1)S(1)} %get-tuple-element.177), channel_id=1, source_target_pairs={{0,2},{1,3},{2,0},{3,1},{4,6},{5,7},{6,4},{7,5},{8,10},{9,11},{10,... | collective-permute-start | bytes 835592 | tf_op jit(solution)/shard_map/ppermute | solution.py:22
  130.9 10.8 %collective-permute-start.25 = (bf16[176,512]{1,0:T(8,128)(2,1)S(1)}, bf16[176,512]{1,0:T(8,128)(2,1)S(1)}, u32[]{:S(2)}, u32[]{:S(2)}) collective-permute-start(bf16[176,512]{1,0:T(8,128)(2,1)S(1)} %get-tuple-element.172.refs_0_), channel_id=1, source_target_pairs={{0,16},{1,17},{2,18},{3,19},{4,20},{5,21},{6,22},{7,23},{8,24},{9,... | collective-permute-start | bytes 540680 | tf_op jit(solution)/shard_map/ppermute | solution.py:64
  130.9 14.0 %collective-permute-start.28 = (bf16[512,512]{1,0:T(8,128)(2,1)S(1)}, bf16[512,512]{1,0:T(8,128)(2,1)S(1)}, u32[]{:S(2)}, u32[]{:S(2)}) collective-permute-start(bf16[512,512]{1,0:T(8,128)(2,1)S(1)} %advance.15.refs_0_), channel_id=1, source_target_pairs={{0,8},{1,5},{2,10},{3,7},{4,12},{5,1},{6,14},{7,3},{8,0},{9,13},{1... | collective-permute-start | bytes 1572872 | tf_op jit(solution)/shard_map/ppermute | solution.py:64
  133.9 16.8 %collective-permute-start.24 = (bf16[2,256,256]{2,1,0:T(8,128)(2,1)S(1)}, bf16[2,256,256]{2,1,0:T(8,128)(2,1)S(1)}, u32[]{:S(2)}, u32[]{:S(2)}) collective-permute-start(bf16[2,256,256]{2,1,0:T(8,128)(2,1)S(1)} %get-tuple-element.178), channel_id=1, source_target_pairs={{0,2},{1,3},{2,0},{3,1},{4,6},{5,7},{6,4},{7,5},{8,10},{9,11},{10,... | collective-permute-start | bytes 786440 | tf_op jit(solution)/shard_map/ppermute | solution.py:22
  141.7 8.9 %collective-permute-start.27 = (bf16[144,512]{1,0:T(8,128)(2,1)S(1)}, bf16[144,512]{1,0:T(8,128)(2,1)S(1)}, u32[]{:S(2)}, u32[]{:S(2)}) collective-permute-start(bf16[144,512]{1,0:T(8,128)(2,1)S(1)} %get-tuple-element.184.refs_0_), channel_id=1, source_target_pairs={{0,16},{1,17},{2,18},{3,19},{4,20},{5,21},{6,22},{7,23},{8,24},{9,... | collective-permute-start | bytes 442376 | tf_op jit(solution)/shard_map/ppermute | solution.py:64
  145.0 18.4 %collective-permute-start.31 = (bf16[1024,512]{1,0:T(8,128)(2,1)S(1)}, bf16[1024,512]{1,0:T(8,128)(2,1)S(1)}, u32[]{:S(2)}, u32[]{:S(2)}) collective-permute-start(bf16[1024,512]{1,0:T(8,128)(2,1)S(1)} %advance.17.refs_0_.refs_2_), channel_id=1, source_target_pairs={{0,4},{1,9},{2,6},{3,11},{4,0},{5,13},{6,2},{7,15},{8,12},{9,1},{1... | collective-permute-start | bytes 3145736 | tf_op jit(solution)/shard_map/ppermute | solution.py:64
  150.6 10.7 %collective-permute-start.29 = (bf16[320,512]{1,0:T(8,128)(2,1)S(1)}, bf16[320,512]{1,0:T(8,128)(2,1)S(1)}, u32[]{:S(2)}, u32[]{:S(2)}) collective-permute-start(bf16[320,512]{1,0:T(8,128)(2,1)S(1)} %advance.18.refs_0_), channel_id=1, source_target_pairs={{0,8},{1,5},{2,10},{3,7},{4,12},{5,1},{6,14},{7,3},{8,0},{9,13},{1... | collective-permute-start | bytes 983048 | tf_op jit(solution)/shard_map/ppermute | solution.py:64
  161.4 10.5 %collective-permute-start.30 = (bf16[624,512]{1,0:T(8,128)(2,1)S(1)}, bf16[624,512]{1,0:T(8,128)(2,1)S(1)}, u32[]{:S(2)}, u32[]{:S(2)}) collective-permute-start(bf16[624,512]{1,0:T(8,128)(2,1)S(1)} %advance.19.refs_0_.own_ref), channel_id=1, source_target_pairs={{0,4},{1,9},{2,6},{3,11},{4,0},{5,13},{6,2},{7,15},{8,12},{9,1},{1... | collective-permute-start | bytes 1916936 | tf_op jit(solution)/shard_map/ppermute | solution.py:64
  (35 other events, 217.1 us)

commit v6 on v5

--- a/solution.py
+++ b/solution.py
@@ -569,8 +569,8 @@
             y[s, :] = (to_here * row_of(gy_ref, t, states)).astype(BF16)
 
     def body(k, sums):
-        for i in range(0, ROUND, 2):
-            at = ROUND * k + i
+        for i in range(0, chunks, 2):
+            at = chunks * k + i
             sums = flush(at - 1, xb, yb, sums)
             fill(at, xa, ya)
             sums = flush(at, xa, ya, sums)
@@ -578,7 +578,7 @@
         return sums
 
     zero = jnp.zeros((states, width), F32)
-    sums = lax.fori_loop(0, chunks // ROUND, body, (zero, zero))
+    sums = body(0, (zero, zero))
     sums = flush(chunks - 1, xb, yb, sums)
     end_ref[...] = sums[0]
     pull_ref[...] = sums[1]

time: 175 us -> 174 us (level)
  no operation moved by 1% of the time
where the time goes in v6:
time: 174 us
  waiting for transfers between devices  57.4 us (33%)
  starting transfers between devices  41.8 us (24%)
  Pallas kernels  36.6 us (21%)
  other arithmetic  17.2 us (10%)
  matrix products  10.9 us (6%)
  local copies, waits for them, and re-layouts  7.98 us (5%)
  between operations  1.87 us (1%)
    ppermute x12, waiting for transfers between devices, swap(): return lax.ppermute(block, ('seq', 'mp'), route)  37.5 us
    ppermute x18, starting transfers between devices, swap(): return lax.ppermute(block, axis, [(i, i ^ bit) for i in range(devices)])  19.4 us
    ppermute x12, starting transfers between devices, swap(): return lax.ppermute(block, ('seq', 'mp'), route)  17.2 us
    ppermute x18, waiting for transfers between devices, swap(): return lax.ppermute(block, axis, [(i, i ^ bit) for i in range(devices)])  15.7 us
    pallas_call x1, Pallas kernels, scan_backward(): pl.pallas_call(functools.partial(backward_kernel, low_rank, lanes), grid=...  11.1 us
    pallas_call x1, Pallas kernels, scan_ends(): pl.pallas_call(functools.partial(ends_kernel, low_rank), grid=(lanes,), i...  7.76 us
    pallas_call x1, Pallas kernels, scan_forward(): pl.pallas_call(functools.partial(forward_kernel, low_rank, lanes), grid=(...  7.66 us
    ppermute x2, starting transfers between devices, from_behind(): return lax.ppermute(block, axis, route)  5.08 us
  transfers between devices with their start and end apart: 32, of which 20 were waited for; matrix products, arithmetic and copies ran while one was open for 15% of the time, Pallas kernels for 9%

profile of v6, /device:TPU:0, one launch (start us, length us, event | category | flops | bytes accessed | tf_op | source)
XLA Modules:
  0.0 173.7 jit_solution(18435772187573213915)
XLA Ops:
  2.0 3.0 %collective-permute-start.1 = (bf16[2,256,256]{2,1,0:T(8,128)(2,1)S(1)}, bf16[2,256,256]{2,1,0:T(8,128)(2,1)}, u32[]{:S(2)}, u32[]{:S(2)}) collective-permute-start(bf16[2,256,256]{2,1,0:T(8,128)(2,1)S(1)} %get-tuple-element.244), channel_id=1, source_target_pairs={{0,2},{1,3},{2,0},{3,1},{4,6},{5,7},{6,4},{7,5},{8,10},{9,11},{10,... | collective-permute-start | bytes 786440 | tf_op jit(solution)/shard_map/ppermute | solution.py:22
  8.0 2.5 %dynamic-slice_convert_fusion.3 = (bf16[2,256,512]{2,1,0:T(8,128)(2,1)S(1)}, bf16[2,256,512]{2,1,0:T(8,128)(2,1)S(1)}, bf16[2,256,512]{2,1,0:T(8,128)(2,1)S(1)}, bf16[2,256,512]{2,1,0:T(8,128)(2,1)S(1)}) fusion(f32[2,1024,512]{2,1,0:T(8,128)} %param.17, s32[]{:T(128)S(6)} %select_n.182, s32[]{:T(128)S(6)} %select_n.183, s32[]{:T(128)S(6)} %select_n.185, ...), kind=kLoop, calls=%fused_computation.58 | loop fusion | bytes 4194320 | tf_op jit(solution)/shard_map/convert.3
  12.1 2.9 %convert_element_type.206 = bf16[512,1024]{1,0:T(8,128)(2,1)} convert(f32[512,1024]{1,0:T(8,128)} %param.25) | non-fusion elementwise | flops 524288 | bytes 3145728 | tf_op jit(solution)/shard_map/convert_element_type | solution.py:891
  15.1 1.8 %collective-permute-start.6 = (bf16[2,256,256]{2,1,0:T(8,128)(2,1)S(1)}, bf16[2,256,256]{2,1,0:T(8,128)(2,1)S(1)}, u32[]{:S(2)}, u32[]{:S(2)}) collective-permute-start(bf16[2,256,256]{2,1,0:T(8,128)(2,1)S(1)} %convert_element_type.211), channel_id=1, source_target_pairs={{0,2},{1,3},{2,0},{3,1},{4,6},{5,7},{6,4},{7,5},{8,10},{9,11},{10,... | collective-permute-start | bytes 786440 | tf_op jit(solution)/shard_map/ppermute | solution.py:22
  18.4 3.5 %collective-permute-start.5 = (bf16[2,8,1024]{2,1,0:T(8,128)(2,1)S(1)}, bf16[2,8,1024]{2,1,0:T(8,128)(2,1)S(1)}, u32[]{:S(2)}, u32[]{:S(2)}) collective-permute-start(bf16[2,8,1024]{2,1,0:T(8,128)(2,1)S(1)} %slice.139), channel_id=1, source_target_pairs={{0,4},{4,8},{8,12},{12,16},{16,20},{20,24},{24,28},{1,5},{5,9},{9,... | collective-permute-start | bytes 98312 | tf_op jit(solution)/shard_map/ppermute | solution.py:28
  24.5 1.6 fusion.68
  29.7 1.6 collective-permute-start.8
  36.2 7.8 %scan_ends.1 = (f32[2,16,512]{2,1,0:T(8,128)S(1)}, f32[2,16,512]{2,1,0:T(8,128)S(1)}, f32[2,1,512]{2,1,0:T(1,128)S(1)}, f32[2,256,512]{2,1,0:T(8,128)}, f32[2,25...) custom-call(bf16[2,256,128]{2,1,0:T(8,128)(2,1)S(1)} %add_convert_fusion.4.sent_ref, ...), custom_call_target="tpu_custom_call" | custom-call | flops 536870912 | bytes 8388608 | tf_op jit(solution)/shard_map/scan_ends/pallas_call | solution.py:602
  46.3 2.5 %collective-permute-done.11.got_ref = bf16[80,512]{1,0:T(8,128)(2,1)S(1)} collective-permute-done((bf16[80,512]{1,0:T(8,128)(2,1)S(1)}, bf16[80,512]{1,0:T(8,128)(2,1)S(1)}, u32[]{:S(2)}, u32[]{:S(2)}) %collective-permute-start.11) | collective-permute-done | bytes 81952 | tf_op jit(solution)/shard_map/ppermute | solution.py:22
  49.4 2.6 %collective-permute-start.12 = (bf16[80,512]{1,0:T(8,128)(2,1)S(1)}, bf16[80,512]{1,0:T(8,128)(2,1)S(1)}, u32[]{:S(2)}, u32[]{:S(2)}) collective-permute-start(bf16[80,512]{1,0:T(8,128)(2,1)S(1)} %get-tuple-element.123), channel_id=1, source_target_pairs={{0,8},{4,12},{8,0},{12,4},{16,24},{20,28},{24,16},{28,20},{1,9},{5... | collective-permute-start | bytes 245768 | tf_op jit(solution)/shard_map/ppermute | solution.py:22
  52.1 2.2 %collective-permute-done.12.got_ref = bf16[80,512]{1,0:T(8,128)(2,1)S(1)} collective-permute-done((bf16[80,512]{1,0:T(8,128)(2,1)S(1)}, bf16[80,512]{1,0:T(8,128)(2,1)S(1)}, u32[]{:S(2)}, u32[]{:S(2)}) %collective-permute-start.12) | collective-permute-done | bytes 81952 | tf_op jit(solution)/shard_map/ppermute | solution.py:22
  55.0 3.1 %collective-permute-start.13 = (bf16[48,512]{1,0:T(8,128)(2,1)S(1)}, bf16[48,512]{1,0:T(8,128)(2,1)S(1)}, u32[]{:S(2)}, u32[]{:S(2)}) collective-permute-start(bf16[48,512]{1,0:T(8,128)(2,1)S(1)} %get-tuple-element.126), channel_id=1, source_target_pairs={{0,16},{4,20},{8,24},{12,28},{16,0},{20,4},{24,8},{28,12},{1,17},{... | collective-permute-start | bytes 147464 | tf_op jit(solution)/shard_map/ppermute | solution.py:22
  58.2 1.9 %collective-permute-done.13.got_ref = bf16[48,512]{1,0:T(8,128)(2,1)S(1)} collective-permute-done((bf16[48,512]{1,0:T(8,128)(2,1)S(1)}, bf16[48,512]{1,0:T(8,128)(2,1)S(1)}, u32[]{:S(2)}, u32[]{:S(2)}) %collective-permute-start.13) | collective-permute-done | bytes 49184 | tf_op jit(solution)/shard_map/ppermute | solution.py:22
  61.5 7.7 %scan_forward.1 = (f32[2,256,512]{2,1,0:T(8,128)S(1)}, f32[2,256,128]{2,1,0:T(8,128)S(1)}, bf16[2,4096,512]{2,1,0:T(8,128)(2,1)S(1)}) custom-call(s32[2]{0:T(128)S(1)} %bitcast.152, f32[2,256,128]{2,1,0:T(8,128)S(1)} %get-tuple-element.120.proj_ref, f32[16,512]{1,0:T(8,128)S(1)} %copy-done.2, f32[2,256,512]{2,1,0:T(8,128)S(1)} %copy-done, ...), custom_call_target="tpu_custom_call" | custom-call | flops 536870912 | bytes 8388608 | tf_op jit(solution)/shard_map/scan_forward/pallas_call | solution.py:700
  72.9 11.1 %scan_backward.1 = (f32[2,256,512]{2,1,0:T(8,128)S(1)}, f32[2,256,512]{2,1,0:T(8,128)S(1)}, f32[2,256,128]{2,1,0:T(8,128)S(1)}, f32[2,16,512]{2,1,0:T(8,128)S(1)}) custom-call(f32[2,256,128]{2,1,0:T(8,128)S(1)} %get-tuple-element.120.proj_ref, f32[16,512]{1,0:T(8,128)S(1)} %copy-done.2, f32[2,256,512]{2,1,0:T(8,128)S(1)} %copy-done, ...), custom_call_target="tpu_custom_call" | custom-call | flops 805306368 | bytes 8388608 | tf_op jit(solution)/shard_map/scan_backward/pallas_call | solution.py:814
  89.5 2.5 %collective-permute-done.16 = bf16[2,256,128]{2,1,0:T(8,128)(2,1)S(1)} collective-permute-done((bf16[2,256,128]{2,1,0:T(8,128)(2,1)S(1)}, bf16[2,256,128]{2,1,0:T(8,128)(2,1)S(1)}, u32[]{:S(2)}, u32[]{:S(2)}) %collective-permute-start.16) | collective-permute-done | bytes 131104 | tf_op jit(solution)/shard_map/ppermute | solution.py:22
  97.3 3.0 %collective-permute-start.19 = (bf16[256,512]{1,0:T(8,128)(2,1)S(1)}, bf16[256,512]{1,0:T(8,128)(2,1)S(1)}, u32[]{:S(2)}, u32[]{:S(2)}) collective-permute-start(bf16[256,512]{1,0:T(8,128)(2,1)S(1)} %get-tuple-element.152.refs_0_), channel_id=1, source_target_pairs={{0,16},{1,17},{2,18},{3,19},{4,20},{5,21},{6,22},{7,23},{8,24},{9,... | collective-permute-start | bytes 786440 | tf_op jit(solution)/shard_map/ppermute | solution.py:64
  103.4 3.3 %collective-permute-done.18 = f32[2,3,512]{2,1,0:T(4,128)S(1)} collective-permute-done((f32[2,3,512]{2,1,0:T(4,128)S(1)}, f32[2,3,512]{2,1,0:T(4,128)S(1)}, u32[]{:S(2)}, u32[]{:S(2)}) %collective-permute-start.18) | collective-permute-done | bytes 12320 | tf_op jit(solution)/shard_map/ppermute | solution.py:28
  110.6 2.7 %collective-permute-start.23 = (bf16[304,512]{1,0:T(8,128)(2,1)S(1)}, bf16[304,512]{1,0:T(8,128)(2,1)S(1)}, u32[]{:S(2)}, u32[]{:S(2)}) collective-permute-start(bf16[304,512]{1,0:T(8,128)(2,1)S(1)} %get-tuple-element.164.refs_0_), channel_id=1, source_target_pairs={{0,8},{1,5},{2,10},{3,7},{4,12},{5,1},{6,14},{7,3},{8,0},{9,13},{1... | collective-permute-start | bytes 933896 | tf_op jit(solution)/shard_map/ppermute | solution.py:64
  113.3 2.7 %collective-permute-start.22 = (bf16[256,512]{1,0:T(8,128)(2,1)S(1)}, bf16[256,512]{1,0:T(8,128)(2,1)S(1)}, u32[]{:S(2)}, u32[]{:S(2)}) collective-permute-start(bf16[256,512]{1,0:T(8,128)(2,1)S(1)} %advance.13.refs_0_), channel_id=1, source_target_pairs={{0,16},{1,17},{2,18},{3,19},{4,20},{5,21},{6,22},{7,23},{8,24},{9,... | collective-permute-start | bytes 786440 | tf_op jit(solution)/shard_map/ppermute | solution.py:64
  115.9 2.6 %collective-permute-done.23.refs_1_ = bf16[304,512]{1,0:T(8,128)(2,1)S(1)} collective-permute-done((bf16[304,512]{1,0:T(8,128)(2,1)S(1)}, bf16[304,512]{1,0:T(8,128)(2,1)S(1)}, u32[]{:S(2)}, u32[]{:S(2)}) %collective-permute-start.23) | collective-permute-done | bytes 311328 | tf_op jit(solution)/shard_map/ppermute | solution.py:64
  118.6 10.0 %collective-permute-done.22.refs_1_ = bf16[256,512]{1,0:T(8,128)(2,1)S(1)} collective-permute-done((bf16[256,512]{1,0:T(8,128)(2,1)S(1)}, bf16[256,512]{1,0:T(8,128)(2,1)S(1)}, u32[]{:S(2)}, u32[]{:S(2)}) %collective-permute-start.22) | collective-permute-done | bytes 262176 | tf_op jit(solution)/shard_map/ppermute | solution.py:64
  130.2 2.9 %collective-permute-start.28 = (bf16[512,512]{1,0:T(8,128)(2,1)S(1)}, bf16[512,512]{1,0:T(8,128)(2,1)S(1)}, u32[]{:S(2)}, u32[]{:S(2)}) collective-permute-start(bf16[512,512]{1,0:T(8,128)(2,1)S(1)} %advance.15.refs_0_), channel_id=1, source_target_pairs={{0,8},{1,5},{2,10},{3,7},{4,12},{5,1},{6,14},{7,3},{8,0},{9,13},{1... | collective-permute-start | bytes 1572872 | tf_op jit(solution)/shard_map/ppermute | solution.py:64
  133.8 4.7 %collective-permute-done.26 = bf16[2,272,256]{2,1,0:T(8,128)(2,1)S(1)} collective-permute-done((bf16[2,272,256]{2,1,0:T(8,128)(2,1)S(1)}, bf16[2,272,256]{2,1,0:T(8,128)(2,1)S(1)}, u32[]{:S(2)}, u32[]{:S(2)}) %collective-permute-start.26) | collective-permute-done | bytes 278560 | tf_op jit(solution)/shard_map/ppermute | solution.py:22
  141.0 3.1 %collective-permute-done.28.refs_1_ = bf16[512,512]{1,0:T(8,128)(2,1)S(1)} collective-permute-done((bf16[512,512]{1,0:T(8,128)(2,1)S(1)}, bf16[512,512]{1,0:T(8,128)(2,1)S(1)}, u32[]{:S(2)}, u32[]{:S(2)}) %collective-permute-start.28) | collective-permute-done | bytes 524320 | tf_op jit(solution)/shard_map/ppermute | solution.py:64
  144.2 2.0 %collective-permute-start.31 = (bf16[1024,512]{1,0:T(8,128)(2,1)S(1)}, bf16[1024,512]{1,0:T(8,128)(2,1)S(1)}, u32[]{:S(2)}, u32[]{:S(2)}) collective-permute-start(bf16[1024,512]{1,0:T(8,128)(2,1)S(1)} %advance.17.refs_0_.refs_2_), channel_id=1, source_target_pairs={{0,4},{1,9},{2,6},{3,11},{4,0},{5,13},{6,2},{7,15},{8,12},{9,1},{1... | collective-permute-start | bytes 3145736 | tf_op jit(solution)/shard_map/ppermute | solution.py:64
  146.2 3.7 %collective-permute-done.27.refs_1_ = bf16[144,512]{1,0:T(8,128)(2,1)S(1)} collective-permute-done((bf16[144,512]{1,0:T(8,128)(2,1)S(1)}, bf16[144,512]{1,0:T(8,128)(2,1)S(1)}, u32[]{:S(2)}, u32[]{:S(2)}) %collective-permute-start.27) | collective-permute-done | bytes 147488 | tf_op jit(solution)/shard_map/ppermute | solution.py:64
  150.9 9.7 %collective-permute-done.29.refs_1_ = bf16[320,512]{1,0:T(8,128)(2,1)S(1)} collective-permute-done((bf16[320,512]{1,0:T(8,128)(2,1)S(1)}, bf16[320,512]{1,0:T(8,128)(2,1)S(1)}, u32[]{:S(2)}, u32[]{:S(2)}) %collective-permute-start.29) | collective-permute-done | bytes 327712 | tf_op jit(solution)/shard_map/ppermute | solution.py:64
  160.8 1.8 %collective-permute-done.31.refs_1_.refs_3_ = bf16[1024,512]{1,0:T(8,128)(2,1)S(1)} collective-permute-done((bf16[1024,512]{1,0:T(8,128)(2,1)S(1)}, bf16[1024,512]{1,0:T(8,128)(2,1)S(1)}, u32[]{:S(2)}, u32[]{:S(2)}) %collective-permute-start.31) | collective-permute-done | bytes 1048608 | tf_op jit(solution)/shard_map/ppermute | solution.py:64
  162.6 2.7 %settle.2 = (f32[2,1024,512]{2,1,0:T(8,128)}, f32[512,1024]{1,0:T(8,128)}) custom-call(s32[12]{0:T(128)S(1)} %concatenate.49.order_ref, bf16[1024,512]{1,0:T(8,128)(2,1)S(1)} %advance.17.refs_0_.refs_2_, bf16[1024,512]{1,0:T(8,128)(2,1)S(1)} %collective-permute-done.31.refs_1_.refs_3_, bf16[1024,512]{1,0:T(8,128)(2,1)S(1)} %advance.17.refs_0_.refs_2_, ...), custom_call_target="tpu_custom_call" | custom-call | tf_op jit(solution)/shard_map/settle/pallas_call | solution.py:252
  166.9 4.3 %collective-permute-done.30.late_ref = bf16[624,512]{1,0:T(8,128)(2,1)S(1)} collective-permute-done((bf16[624,512]{1,0:T(8,128)(2,1)S(1)}, bf16[624,512]{1,0:T(8,128)(2,1)S(1)}, u32[]{:S(2)}, u32[]{:S(2)}) %collective-permute-start.30) | collective-permute-done | bytes 639008 | tf_op jit(solution)/shard_map/ppermute | solution.py:64
  171.1 2.3 %finish.1 = (f32[2,1024,512]{2,1,0:T(8,128)}, f32[4,512]{1,0:T(4,128)}, f32[1,512]{1,0:T(1,128)}, f32[1,512]{1,0:T(1,128)}, f32[1,512]{1,0:T(1,128)}, /*index=5*...) custom-call(s32[12]{0:T(128)S(1)} %concatenate.49.order_ref, ...), custom_call_target="tpu_custom_call", output_to_operand_aliasing={{0}: (4, {})} | custom-call | tf_op jit(solution)/shard_map/finish/pallas_call | solution.py:295
  (209 shorter events, 52.0 us)
Async XLA Ops:
  2.0 9.7 %collective-permute-start.1 = (bf16[2,256,256]{2,1,0:T(8,128)(2,1)S(1)}, bf16[2,256,256]{2,1,0:T(8,128)(2,1)}, u32[]{:S(2)}, u32[]{:S(2)}) collective-permute-start(bf16[2,256,256]{2,1,0:T(8,128)(2,1)S(1)} %get-tuple-element.244), channel_id=1, source_target_pairs={{0,2},{1,3},{2,0},{3,1},{4,6},{5,7},{6,4},{7,5},{8,10},{9,11},{10,... | collective-permute-start | bytes 786440 | tf_op jit(solution)/shard_map/ppermute | solution.py:22
  5.0 11.9 %collective-permute-start = (bf16[2,256,256]{2,1,0:T(8,128)(2,1)S(1)}, bf16[2,256,256]{2,1,0:T(8,128)(2,1)}, u32[]{:S(2)}, u32[]{:S(2)}) collective-permute-start(bf16[2,256,256]{2,1,0:T(8,128)(2,1)S(1)} %get-tuple-element.244), channel_id=1, source_target_pairs={{0,1},{1,0},{2,3},{3,2},{4,5},{5,4},{6,7},{7,6},{8,9},{9,8},{10,11... | collective-permute-start | bytes 786440 | tf_op jit(solution)/shard_map/ppermute | solution.py:22
  5.0 6.4 %collective-permute-start.3 = (f32[2,256]{1,0:T(2,128)S(1)}, f32[2,256]{1,0:T(2,128)S(1)}, u32[]{:S(2)}, u32[]{:S(2)}) collective-permute-start(f32[2,256]{1,0:T(2,128)S(1)} %get-tuple-element.243), channel_id=1, source_target_pairs={{0,2},{1,3},{2,0},{3,1},{4,6},{5,7},{6,4},{7,5},{8,10},{9,11},{10,... | collective-permute-start | bytes 6152 | tf_op jit(solution)/shard_map/ppermute | solution.py:22
  11.5 3.6 %collective-permute-start.4 = (f32[2,256]{1,0:T(2,128)S(1)}, f32[2,256]{1,0:T(2,128)S(1)}, u32[]{:S(2)}, u32[]{:S(2)}) collective-permute-start(f32[2,256]{1,0:T(2,128)S(1)} %add.238), channel_id=1, source_target_pairs={{0,1},{1,0},{2,3},{3,2},{4,5},{5,4},{6,7},{7,6},{8,9},{9,8},{10,11... | collective-permute-start | bytes 6152 | tf_op jit(solution)/shard_map/ppermute | solution.py:22
  11.7 5.2 %collective-permute-start.2 = (bf16[2,256,256]{2,1,0:T(8,128)(2,1)}, bf16[2,256,256]{2,1,0:T(8,128)(2,1)}, u32[]{:S(2)}, u32[]{:S(2)}) collective-permute-start(bf16[2,256,256]{2,1,0:T(8,128)(2,1)} %collective-permute-done.1), channel_id=1, source_target_pairs={{0,1},{1,0},{2,3},{3,2},{4,5},{5,4},{6,7},{7,6},{8,9},{9,8},{10,11... | collective-permute-start | bytes 786440 | tf_op jit(solution)/shard_map/ppermute | solution.py:22
  15.1 8.7 %collective-permute-start.6 = (bf16[2,256,256]{2,1,0:T(8,128)(2,1)S(1)}, bf16[2,256,256]{2,1,0:T(8,128)(2,1)S(1)}, u32[]{:S(2)}, u32[]{:S(2)}) collective-permute-start(bf16[2,256,256]{2,1,0:T(8,128)(2,1)S(1)} %convert_element_type.211), channel_id=1, source_target_pairs={{0,2},{1,3},{2,0},{3,1},{4,6},{5,7},{6,4},{7,5},{8,10},{9,11},{10,... | collective-permute-start | bytes 786440 | tf_op jit(solution)/shard_map/ppermute | solution.py:22
  18.4 5.1 %collective-permute-start.5 = (bf16[2,8,1024]{2,1,0:T(8,128)(2,1)S(1)}, bf16[2,8,1024]{2,1,0:T(8,128)(2,1)S(1)}, u32[]{:S(2)}, u32[]{:S(2)}) collective-permute-start(bf16[2,8,1024]{2,1,0:T(8,128)(2,1)S(1)} %slice.139), channel_id=1, source_target_pairs={{0,4},{4,8},{8,12},{12,16},{16,20},{20,24},{24,28},{1,5},{5,9},{9,... | collective-permute-start | bytes 98312 | tf_op jit(solution)/shard_map/ppermute | solution.py:28
  27.2 1.5 collective-permute-start.7
  29.7 6.4 %collective-permute-start.8 = (bf16[2,256,128]{2,1,0:T(8,128)(2,1)S(1)}, bf16[2,256,128]{2,1,0:T(8,128)(2,1)S(1)}, u32[]{:S(2)}, u32[]{:S(2)}) collective-permute-start(bf16[2,256,128]{2,1,0:T(8,128)(2,1)S(1)} %add_convert_fusion.4.sent_ref), channel_id=1, source_target_pairs={{0,2},{1,3},{2,0},{3,1},{4,6},{5,7},{6,4},{7,5},{8,10},{9,11},{10,... | collective-permute-start | bytes 393224 | tf_op jit(solution)/shard_map/ppermute | solution.py:22
  31.4 2.6 %collective-permute-start.9 = (bf16[2,256,256]{2,1,0:T(8,128)(2,1)}, bf16[2,256,256]{2,1,0:T(8,128)(2,1)S(1)}, u32[]{:S(2)}, u32[]{:S(2)}) collective-permute-start(bf16[2,256,256]{2,1,0:T(8,128)(2,1)} %copy-done.13), channel_id=1, source_target_pairs={{0,1},{1,0},{2,3},{3,2},{4,5},{5,4},{6,7},{7,6},{8,9},{9,8},{10,11... | collective-permute-start | bytes 786440 | tf_op jit(solution)/shard_map/ppermute | solution.py:22
  31.4 2.6 %collective-permute-start.10 = (bf16[2,256,256]{2,1,0:T(8,128)(2,1)}, bf16[2,256,256]{2,1,0:T(8,128)(2,1)S(1)}, u32[]{:S(2)}, u32[]{:S(2)}) collective-permute-start(bf16[2,256,256]{2,1,0:T(8,128)(2,1)} %copy-done.18), channel_id=1, source_target_pairs={{0,1},{1,0},{2,3},{3,2},{4,5},{5,4},{6,7},{7,6},{8,9},{9,8},{10,11... | collective-permute-start | bytes 786440 | tf_op jit(solution)/shard_map/ppermute | solution.py:22
  44.3 4.5 %collective-permute-start.11 = (bf16[80,512]{1,0:T(8,128)(2,1)S(1)}, bf16[80,512]{1,0:T(8,128)(2,1)S(1)}, u32[]{:S(2)}, u32[]{:S(2)}) collective-permute-start(bf16[80,512]{1,0:T(8,128)(2,1)S(1)} %pad.45), channel_id=1, source_target_pairs={{0,4},{4,0},{8,12},{12,8},{16,20},{20,16},{24,28},{28,24},{1,5},{5... | collective-permute-start | bytes 245768 | tf_op jit(solution)/shard_map/ppermute | solution.py:22
  49.4 5.0 %collective-permute-start.12 = (bf16[80,512]{1,0:T(8,128)(2,1)S(1)}, bf16[80,512]{1,0:T(8,128)(2,1)S(1)}, u32[]{:S(2)}, u32[]{:S(2)}) collective-permute-start(bf16[80,512]{1,0:T(8,128)(2,1)S(1)} %get-tuple-element.123), channel_id=1, source_target_pairs={{0,8},{4,12},{8,0},{12,4},{16,24},{20,28},{24,16},{28,20},{1,9},{5... | collective-permute-start | bytes 245768 | tf_op jit(solution)/shard_map/ppermute | solution.py:22
  55.0 5.2 %collective-permute-start.13 = (bf16[48,512]{1,0:T(8,128)(2,1)S(1)}, bf16[48,512]{1,0:T(8,128)(2,1)S(1)}, u32[]{:S(2)}, u32[]{:S(2)}) collective-permute-start(bf16[48,512]{1,0:T(8,128)(2,1)S(1)} %get-tuple-element.126), channel_id=1, source_target_pairs={{0,16},{4,20},{8,24},{12,28},{16,0},{20,4},{24,8},{28,12},{1,17},{... | collective-permute-start | bytes 147464 | tf_op jit(solution)/shard_map/ppermute | solution.py:22
  70.9 14.9 %collective-permute-start.15 = (bf16[1024,512]{1,0:T(8,128)(2,1)S(1)}, bf16[1024,512]{1,0:T(8,128)(2,1)S(1)}, u32[]{:S(2)}, u32[]{:S(2)}) collective-permute-start(bf16[1024,512]{1,0:T(8,128)(2,1)S(1)} %pad_maximum_fusion.5.refs_0_), channel_id=1, source_target_pairs={{0,4},{1,9},{2,6},{3,11},{4,0},{5,13},{6,2},{7,15},{8,12},{9,1},{1... | collective-permute-start | bytes 3145736 | tf_op jit(solution)/shard_map/ppermute | solution.py:64
  84.9 1.4 collective-permute-start.14
  86.4 5.6 %collective-permute-start.16 = (bf16[2,256,128]{2,1,0:T(8,128)(2,1)S(1)}, bf16[2,256,128]{2,1,0:T(8,128)(2,1)S(1)}, u32[]{:S(2)}, u32[]{:S(2)}) collective-permute-start(bf16[2,256,128]{2,1,0:T(8,128)(2,1)S(1)} %add_convert_fusion.2), channel_id=1, source_target_pairs={{0,2},{1,3},{2,0},{3,1},{4,6},{5,7},{6,4},{7,5},{8,10},{9,11},{10,... | collective-permute-start | bytes 393224 | tf_op jit(solution)/shard_map/ppermute | solution.py:22
  87.7 9.6 %collective-permute-start.17 = (bf16[512,512]{1,0:T(8,128)(2,1)S(1)}, bf16[512,512]{1,0:T(8,128)(2,1)S(1)}, u32[]{:S(2)}, u32[]{:S(2)}) collective-permute-start(bf16[512,512]{1,0:T(8,128)(2,1)S(1)} %get-tuple-element.141.refs_0_), channel_id=1, source_target_pairs={{0,8},{1,5},{2,10},{3,7},{4,12},{5,1},{6,14},{7,3},{8,0},{9,13},{1... | collective-permute-start | bytes 1572872 | tf_op jit(solution)/shard_map/ppermute | solution.py:64
  96.1 13.1 %collective-permute-start.20 = (bf16[608,512]{1,0:T(8,128)(2,1)S(1)}, bf16[608,512]{1,0:T(8,128)(2,1)S(1)}, u32[]{:S(2)}, u32[]{:S(2)}) collective-permute-start(bf16[608,512]{1,0:T(8,128)(2,1)S(1)} %get-tuple-element.148.refs_0_), channel_id=1, source_target_pairs={{0,4},{1,9},{2,6},{3,11},{4,0},{5,13},{6,2},{7,15},{8,12},{9,1},{1... | collective-permute-start | bytes 1867784 | tf_op jit(solution)/shard_map/ppermute | solution.py:64
  97.3 12.1 %collective-permute-start.19 = (bf16[256,512]{1,0:T(8,128)(2,1)S(1)}, bf16[256,512]{1,0:T(8,128)(2,1)S(1)}, u32[]{:S(2)}, u32[]{:S(2)}) collective-permute-start(bf16[256,512]{1,0:T(8,128)(2,1)S(1)} %get-tuple-element.152.refs_0_), channel_id=1, source_target_pairs={{0,16},{1,17},{2,18},{3,19},{4,20},{5,21},{6,22},{7,23},{8,24},{9,... | collective-permute-start | bytes 786440 | tf_op jit(solution)/shard_map/ppermute | solution.py:64
  101.0 5.7 %collective-permute-start.18 = (f32[2,3,512]{2,1,0:T(4,128)S(1)}, f32[2,3,512]{2,1,0:T(4,128)S(1)}, u32[]{:S(2)}, u32[]{:S(2)}) collective-permute-start(f32[2,3,512]{2,1,0:T(4,128)S(1)} %get-tuple-element.156), channel_id=1, source_target_pairs={{4,0},{8,4},{12,8},{16,12},{20,16},{24,20},{28,24},{5,1},{9,5},{13... | collective-permute-start | bytes 36872 | tf_op jit(solution)/shard_map/ppermute | solution.py:28
  109.5 19.1 %collective-permute-start.21 = (bf16[2,528,512]{2,1,0:T(8,128)(2,1)S(1)}, bf16[2,528,512]{2,1,0:T(8,128)(2,1)S(1)}, u32[]{:S(2)}, u32[]{:S(2)}) collective-permute-start(bf16[2,528,512]{2,1,0:T(8,128)(2,1)S(1)} %fusion.5), channel_id=1, source_target_pairs={{0,1},{1,0},{2,3},{3,2},{4,5},{5,4},{6,7},{7,6},{8,9},{9,8},{10,11... | collective-permute-start | bytes 3244040 | tf_op jit(solution)/shard_map/ppermute | solution.py:22
  110.6 8.0 %collective-permute-start.23 = (bf16[304,512]{1,0:T(8,128)(2,1)S(1)}, bf16[304,512]{1,0:T(8,128)(2,1)S(1)}, u32[]{:S(2)}, u32[]{:S(2)}) collective-permute-start(bf16[304,512]{1,0:T(8,128)(2,1)S(1)} %get-tuple-element.164.refs_0_), channel_id=1, source_target_pairs={{0,8},{1,5},{2,10},{3,7},{4,12},{5,1},{6,14},{7,3},{8,0},{9,13},{1... | collective-permute-start | bytes 933896 | tf_op jit(solution)/shard_map/ppermute | solution.py:64
  113.3 15.3 %collective-permute-start.22 = (bf16[256,512]{1,0:T(8,128)(2,1)S(1)}, bf16[256,512]{1,0:T(8,128)(2,1)S(1)}, u32[]{:S(2)}, u32[]{:S(2)}) collective-permute-start(bf16[256,512]{1,0:T(8,128)(2,1)S(1)} %advance.13.refs_0_), channel_id=1, source_target_pairs={{0,16},{1,17},{2,18},{3,19},{4,20},{5,21},{6,22},{7,23},{8,24},{9,... | collective-permute-start | bytes 786440 | tf_op jit(solution)/shard_map/ppermute | solution.py:64
  128.9 9.6 %collective-permute-start.26 = (bf16[2,272,256]{2,1,0:T(8,128)(2,1)S(1)}, bf16[2,272,256]{2,1,0:T(8,128)(2,1)S(1)}, u32[]{:S(2)}, u32[]{:S(2)}) collective-permute-start(bf16[2,272,256]{2,1,0:T(8,128)(2,1)S(1)} %get-tuple-element.177), channel_id=1, source_target_pairs={{0,2},{1,3},{2,0},{3,1},{4,6},{5,7},{6,4},{7,5},{8,10},{9,11},{10,... | collective-permute-start | bytes 835592 | tf_op jit(solution)/shard_map/ppermute | solution.py:22
  130.2 10.7 %collective-permute-start.25 = (bf16[176,512]{1,0:T(8,128)(2,1)S(1)}, bf16[176,512]{1,0:T(8,128)(2,1)S(1)}, u32[]{:S(2)}, u32[]{:S(2)}) collective-permute-start(bf16[176,512]{1,0:T(8,128)(2,1)S(1)} %get-tuple-element.172.refs_0_), channel_id=1, source_target_pairs={{0,16},{1,17},{2,18},{3,19},{4,20},{5,21},{6,22},{7,23},{8,24},{9,... | collective-permute-start | bytes 540680 | tf_op jit(solution)/shard_map/ppermute | solution.py:64
  130.2 13.9 %collective-permute-start.28 = (bf16[512,512]{1,0:T(8,128)(2,1)S(1)}, bf16[512,512]{1,0:T(8,128)(2,1)S(1)}, u32[]{:S(2)}, u32[]{:S(2)}) collective-permute-start(bf16[512,512]{1,0:T(8,128)(2,1)S(1)} %advance.15.refs_0_), channel_id=1, source_target_pairs={{0,8},{1,5},{2,10},{3,7},{4,12},{5,1},{6,14},{7,3},{8,0},{9,13},{1... | collective-permute-start | bytes 1572872 | tf_op jit(solution)/shard_map/ppermute | solution.py:64
  133.1 16.9 %collective-permute-start.24 = (bf16[2,256,256]{2,1,0:T(8,128)(2,1)S(1)}, bf16[2,256,256]{2,1,0:T(8,128)(2,1)S(1)}, u32[]{:S(2)}, u32[]{:S(2)}) collective-permute-start(bf16[2,256,256]{2,1,0:T(8,128)(2,1)S(1)} %get-tuple-element.178), channel_id=1, source_target_pairs={{0,2},{1,3},{2,0},{3,1},{4,6},{5,7},{6,4},{7,5},{8,10},{9,11},{10,... | collective-permute-start | bytes 786440 | tf_op jit(solution)/shard_map/ppermute | solution.py:22
  141.0 8.9 %collective-permute-start.27 = (bf16[144,512]{1,0:T(8,128)(2,1)S(1)}, bf16[144,512]{1,0:T(8,128)(2,1)S(1)}, u32[]{:S(2)}, u32[]{:S(2)}) collective-permute-start(bf16[144,512]{1,0:T(8,128)(2,1)S(1)} %get-tuple-element.184.refs_0_), channel_id=1, source_target_pairs={{0,16},{1,17},{2,18},{3,19},{4,20},{5,21},{6,22},{7,23},{8,24},{9,... | collective-permute-start | bytes 442376 | tf_op jit(solution)/shard_map/ppermute | solution.py:64
  144.2 18.4 %collective-permute-start.31 = (bf16[1024,512]{1,0:T(8,128)(2,1)S(1)}, bf16[1024,512]{1,0:T(8,128)(2,1)S(1)}, u32[]{:S(2)}, u32[]{:S(2)}) collective-permute-start(bf16[1024,512]{1,0:T(8,128)(2,1)S(1)} %advance.17.refs_0_.refs_2_), channel_id=1, source_target_pairs={{0,4},{1,9},{2,6},{3,11},{4,0},{5,13},{6,2},{7,15},{8,12},{9,1},{1... | collective-permute-start | bytes 3145736 | tf_op jit(solution)/shard_map/ppermute | solution.py:64
  149.9 10.7 %collective-permute-start.29 = (bf16[320,512]{1,0:T(8,128)(2,1)S(1)}, bf16[320,512]{1,0:T(8,128)(2,1)S(1)}, u32[]{:S(2)}, u32[]{:S(2)}) collective-permute-start(bf16[320,512]{1,0:T(8,128)(2,1)S(1)} %advance.18.refs_0_), channel_id=1, source_target_pairs={{0,8},{1,5},{2,10},{3,7},{4,12},{5,1},{6,14},{7,3},{8,0},{9,13},{1... | collective-permute-start | bytes 983048 | tf_op jit(solution)/shard_map/ppermute | solution.py:64
  160.7 10.5 %collective-permute-start.30 = (bf16[624,512]{1,0:T(8,128)(2,1)S(1)}, bf16[624,512]{1,0:T(8,128)(2,1)S(1)}, u32[]{:S(2)}, u32[]{:S(2)}) collective-permute-start(bf16[624,512]{1,0:T(8,128)(2,1)S(1)} %advance.19.refs_0_.own_ref), channel_id=1, source_target_pairs={{0,4},{1,9},{2,6},{3,11},{4,0},{5,13},{6,2},{7,15},{8,12},{9,1},{1... | collective-permute-start | bytes 1916936 | tf_op jit(solution)/shard_map/ppermute | solution.py:64
  (35 other events, 215.6 us)
